TPU v7x, 128 devices: a whole 4x4x4 slice. The times are simulated.
128 devices in a mesh: lx: 8 (over z, core), ly: 8 (over y_hi, x), af: 2 (over y_lo).
Axes of the slice: x: 4, y: 4 (y_hi: 2, y_lo: 2; y = y_hi * 2 + y_lo), z: 4, core: 2. Of those that a mesh axis runs over, the one named last changes fastest.
Arguments:
- grad_out: bfloat16 [16, 64, 128, 320], P('af', 'lx', 'ly'), may hold values from -6 to 6
- inputs: bfloat16 [16, 64, 128, 320], P('af', 'lx', 'ly'), may hold values from -6 to 6
- weight: bfloat16 [27, 320, 320], P(None, 'af'), may hold values from -0.0625 to 0.0625
Outputs:
- grad_input: bfloat16 [16, 64, 128, 320], P('af', 'lx', 'ly')
- grad_weight: float32 [27, 320, 320], P(None, 'af', ('lx', 'ly'))
All inputs are finite; a program needn't handle non-finite values.
Results may differ from a plain program's by a relative error of at most 0.01.
Values may be sent and summed in bfloat16 or wider, within the bound.
No kernel may reach another device: no remote copies, remote signals or barrier semaphores. Data moves between devices by JAX's collectives and lax.ppermute only.
A program may use at most 128 MiB of HBM per device.

v0:
```python
import math

import jax
import jax.numpy as jnp
from jax import lax
from jax.sharding import PartitionSpec as P


def with_halo(value, sides, width):
    for axis, dim in sides:
        count, length = (lax.axis_size(axis), value.shape[dim])
        up = [(i, (i + 1) % count) for i in range(count - 1)]
        down = [(j, i) for i, j in up]
        last = lax.slice_in_dim(value, length - width, length, axis=dim)
        initial = lax.slice_in_dim(value, 0, width, axis=dim)
        before = lax.ppermute(last, axis, up)
        after = lax.ppermute(initial, axis, down)
        value = jnp.concatenate([before, value, after], axis=dim)
    return value


def offsets():
    return [
        (depth_off, row_off, col_off)
        for depth_off in range(3)
        for row_off in range(3)
        for col_off in range(3)
    ]


def accumulate(padded_in, padded_grad, kernel, scale):
    chans = padded_in.shape[3]
    filters = padded_grad.shape[3]
    depth = padded_in.shape[0] - 2
    rows = padded_in.shape[1] - 2
    cols = padded_in.shape[2] - 2
    cells = depth * rows * cols
    center = padded_grad[1 : 1 + depth, 1 : 1 + rows, 1 : 1 + cols, :].reshape(cells, filters)
    total = jnp.zeros((cells, chans), jnp.float32)
    pieces = []
    for index, (depth_off, row_off, col_off) in enumerate(offsets()):
        shifted = padded_in[
            depth_off : depth_off + depth, row_off : row_off + rows, col_off : col_off + cols, :
        ].reshape(cells, chans)
        pieces.append(
            lax.dot_general(
                center, shifted, (((0,), (0,)), ((), ())), preferred_element_type=jnp.float32
            )
            * scale
        )
        moved = padded_grad[
            2 - depth_off : 2 - depth_off + depth,
            2 - row_off : 2 - row_off + rows,
            2 - col_off : 2 - col_off + cols,
            :,
        ].reshape(cells, filters)
        total = total + jnp.dot(moved, kernel[index], preferred_element_type=jnp.float32)
    return (total.reshape(depth, rows, cols, chans), jnp.stack(pieces))


def body(grad_out, inputs, weight):
    rows = inputs.shape[1]
    cols = inputs.shape[2]
    whole_depth = inputs.shape[0] * lax.axis_size("af")
    scale = 1.0 / math.sqrt(whole_depth * rows * lax.axis_size("lx") * cols * lax.axis_size("ly"))
    depth_pad = ((1, 1), (0, 0), (0, 0), (0, 0))
    own_filters = weight.shape[1]
    full_in = lax.all_gather(inputs, "af", axis=0, tiled=True)
    every_grad = lax.all_gather(grad_out, "af", axis=0, tiled=True)
    own_grad = lax.dynamic_slice_in_dim(
        every_grad, lax.axis_index("af") * own_filters, own_filters, 3
    )
    padded_in = with_halo(full_in, (("lx", 1), ("ly", 2)), 1)
    padded_grad = with_halo(own_grad, (("lx", 1), ("ly", 2)), 1)
    padded_in = jnp.pad(padded_in, depth_pad)
    padded_grad = jnp.pad(padded_grad, depth_pad)
    partial_in, weight_terms = accumulate(padded_in, padded_grad, weight, scale)
    grad_input = lax.psum_scatter(partial_in, "af", scatter_dimension=0, tiled=True).astype(
        jnp.bfloat16
    )
    grad_weight = lax.psum_scatter(weight_terms, ("lx", "ly"), scatter_dimension=2, tiled=True)
    return (grad_input, grad_weight)


def solution(mesh):
    placed = (P("af", "lx", "ly", None), P("af", "lx", "ly", None), P(None, "af", None))
    return jax.shard_map(
        body,
        mesh=mesh,
        in_specs=placed,
        out_specs=(P("af", "lx", "ly", None), P(None, "af", ("lx", "ly"))),
        check_vma=False,
    )
```

profile of v0, /device:TPU:0, one launch (start us, length us, event | category | flops | bytes accessed | tf_op | source)
XLA Modules:
  0.0 579.6 jit_solution(14016585664518089393)
XLA Ops:
  8.7 33.2 %all-gather.5.cloned.1.call-done = bf16[16,8,16,320]{3,2,1,0:T(8,128)(2,1)} async-done(((bf16[8,8,16,320]{3,2,1,0:T(8,128)(2,1)}), bf16[16,8,16,320]{3,2,1,0:T(8,128)(2,1)}) %all-gather.5.cloned.1.call-update) | async-done | bytes 1310736 | tf_op jit(solution)/shard_map/all_gather | solution.py:68
  41.9 1.8 fusion.422
  43.7 2.4 collective-permute-start.4
  47.4 26.9 %all-gather.3.cloned.1.call-done = bf16[16,8,16,320]{3,2,1,0:T(8,128)(2,1)} async-done(((bf16[8,8,16,320]{3,2,1,0:T(8,128)(2,1)}), bf16[16,8,16,320]{3,2,1,0:T(8,128)(2,1)}) %all-gather.3.cloned.1.call-update) | async-done | bytes 1310736 | tf_op jit(solution)/shard_map/all_gather | solution.py:69
  75.4 1.7 collective-permute-start
  77.2 1.3 collective-permute-start.1
  78.5 1.8 constant_dynamic-slice_fusion.2
  80.4 1.4 collective-permute-done.1
  82.1 3.4 collective-permute-start.2
  85.5 1.3 collective-permute-start.3
  86.8 1.7 pad_maximum_fusion.41
  88.4 4.2 collective-permute-done.3
  92.7 1.3 select_maximum_fusion
  94.0 7.3 %fusion.418 = (bf16[16,8,16,160]{3,2,1,0:T(8,128)(2,1)S(1)}, bf16[16,8,16,160]{3,2,1,0:T(8,128)(2,1)S(1)}, bf16[16,8,16,160]{3,2,1,0:T(8,128)(2,1)S(1)}, bf16[16...) fusion(bf16[18,10,18,160]{3,2,1,0:T(8,128)(2,1)S(1)} %select_ma, ...), kind=kLoop, calls=%fused_computation.294 | loop fusion | bytes 23592960 | tf_op jit(solution)/shard_map/slice | solution.py:51
  101.4 1.8 fusion.381
  103.1 1.7 pad_maximum_fusion
  104.9 1.7 fusion.420
  128.6 1.7 constant_dynamic-update-slice_fusion.2
  130.3 1.4 constant_dynamic-update-slice_fusion.1
  132.4 2.6 fusion.419
  135.0 3.4 collective-permute-start.6
  138.3 1.3 collective-permute-start.7
  139.6 2.1 convolution_add_fusion
  141.7 3.4 copy.9
  145.2 2.6 collective-permute-done.7
  147.8 3.2 fusion.6
  152.3 1.4 fusion.155
  153.7 1.4 fusion.167
  156.4 1.4 fusion.191
  157.8 1.4 fusion.203
  160.5 1.4 fusion.227
  161.9 1.4 fusion.239
  163.4 3.2 fusion.95
  166.6 2.2 fusion.73
  168.8 3.1 fusion.119
  171.9 3.0 fusion.107
  176.1 3.1 fusion.131
  179.2 3.0 fusion.77
  183.5 3.1 fusion.85
  187.9 1.6 fusion.263
  189.5 1.4 fusion.275
  192.2 1.4 fusion.299
  193.6 1.4 fusion.311
  196.3 1.4 fusion.335
  197.8 1.4 fusion.347
  199.2 11.5 %copy.10 = f32[27,160,320]{1,0,2:T(8,128)} copy(f32[27,160,320]{2,1,0:T(8,128)} %fusion.347) | data formatting | bytes 11059200 | tf_op jit(solution)/shard_map/stack | solution.py:58
  210.7 2.4 convert_element_type.7
  213.1 359.5 %reduce-scatter.5.cloned.1.call-done = f32[27,160,5]{1,0,2:T(8,128)} async-done(((f32[27,160,320]{1,0,2:T(8,128)}), f32[27,160,5]{1,0,2:T(8,128)}) %reduce-scatter.5.cloned.1.call-update) | async-done | bytes 86416 | tf_op jit(solution)/shard_map/reduce_scatter | solution.py:81
  (79 shorter events, 37.1 us)
Async XLA Ops:
  7.2 34.7 %all-gather.5.cloned.1.call-start = ((), (), s32[]{:S(2)}) async-start(), calls=%async_computation.4 | async-start | bytes 2359296 | tf_op jit(solution)/shard_map/all_gather | solution.py:68
  7.9 66.4 %all-gather.3.cloned.1.call-start = ((), (), s32[]{:S(2)}) async-start(), calls=%async_computation.2 | async-start | bytes 2359296 | tf_op jit(solution)/shard_map/all_gather | solution.py:69
  8.6 202.0 %reduce-scatter.3.cloned.1.call-start = ((), (), s32[]{:S(2)}) async-start(), calls=%async_computation.3 | async-start | bytes 4718592 | tf_op jit(solution)/shard_map/reduce_scatter | solution.py:78
  43.7 85.0 %collective-permute-start.4 = (bf16[16,1,16,320]{3,2,1,0:T(8,128)(2,1)}, bf16[16,1,16,320]{3,2,1,0:T(8,128)(2,1)}, u32[]{:S(2)}, u32[]{:S(2)}) collective-permute-start(bf16[16,1,16,320]{3,2,1,0:T(8,128)(2,1)} %get-tuple-element.33), channel_id=1, source_target_pairs={{0,16},{16,32},{32,48},{48,64},{64,80},{80,96},{96,112},{1,17},{17... | collective-permute-start | bytes 491528 | tf_op jit(solution)/shard_map/ppermute | solution.py:16
  46.1 85.6 %collective-permute-start.5 = (bf16[16,1,16,320]{3,2,1,0:T(8,128)(2,1)}, bf16[16,1,16,320]{3,2,1,0:T(8,128)(2,1)S(1)}, u32[]{:S(2)}, u32[]{:S(2)}) collective-permute-start(bf16[16,1,16,320]{3,2,1,0:T(8,128)(2,1)} %get-tuple-element.32), channel_id=1, source_target_pairs={{16,0},{32,16},{48,32},{64,48},{80,64},{96,80},{112,96},{17,1},{33... | collective-permute-start | bytes 491528 | tf_op jit(solution)/shard_map/ppermute | solution.py:17
  75.4 4.9 collective-permute-start
  77.2 4.6 collective-permute-start.1
  82.1 6.4 %collective-permute-start.2 = (bf16[16,10,1,160]{3,2,1,0:T(2,128)(2,1)S(1)}, bf16[16,10,1,160]{3,2,1,0:T(2,128)(2,1)S(1)}, u32[]{:S(2)}, u32[]{:S(2)}) collective-permute-start(bf16[16,10,1,160]{3,2,1,0:T(2,128)(2,1)S(1)} %get-tuple-element.39), channel_id=1, source_target_pairs={{0,2},{2,4},{4,6},{6,8},{8,10},{10,12},{12,14},{1,3},{3,5},{5,7},{... | collective-permute-start | bytes 153608 | tf_op jit(solution)/shard_map/ppermute | solution.py:16
  85.5 7.2 %collective-permute-start.3 = (bf16[16,10,1,160]{3,2,1,0:T(2,128)(2,1)S(1)}, bf16[16,10,1,160]{3,2,1,0:T(2,128)(2,1)S(1)}, u32[]{:S(2)}, u32[]{:S(2)}) collective-permute-start(bf16[16,10,1,160]{3,2,1,0:T(2,128)(2,1)S(1)} %get-tuple-element.38), channel_id=1, source_target_pairs={{2,0},{4,2},{6,4},{8,6},{10,8},{12,10},{14,12},{3,1},{5,3},{7,5},{... | collective-permute-start | bytes 153608 | tf_op jit(solution)/shard_map/ppermute | solution.py:17
  104.8 1.9 copy-start.13
  106.8 1.2 copy-start.10
  108.0 1.2 copy-start.9
  109.2 1.2 copy-start.8
  110.5 1.2 copy-start.7
  111.7 1.2 copy-start.6
  112.9 1.2 copy-start.5
  114.1 1.2 copy-start.4
  115.4 1.2 copy-start.3
  117.2 1.2 copy-start.12
  120.7 1.2 copy-start.11
  121.9 1.2 copy-start.2
  123.2 1.2 copy-start.1
  128.0 2.3 copy-start
  135.0 10.2 %collective-permute-start.6 = (bf16[16,10,1,320]{3,2,1,0:T(2,128)(2,1)}, bf16[16,10,1,320]{3,2,1,0:T(2,128)(2,1)S(1)}, u32[]{:S(2)}, u32[]{:S(2)}) collective-permute-start(bf16[16,10,1,320]{3,2,1,0:T(2,128)(2,1)} %get-tuple-element.24), channel_id=1, source_target_pairs={{0,2},{2,4},{4,6},{6,8},{8,10},{10,12},{12,14},{1,3},{3,5},{5,7},{... | collective-permute-start | bytes 307208 | tf_op jit(solution)/shard_map/ppermute | solution.py:16
  138.3 9.4 %collective-permute-start.7 = (bf16[16,10,1,320]{3,2,1,0:T(2,128)(2,1)S(1)}, bf16[16,10,1,320]{3,2,1,0:T(2,128)(2,1)S(1)}, u32[]{:S(2)}, u32[]{:S(2)}) collective-permute-start(bf16[16,10,1,320]{3,2,1,0:T(2,128)(2,1)S(1)} %get-tuple-element.25), channel_id=1, source_target_pairs={{2,0},{4,2},{6,4},{8,6},{10,8},{12,10},{14,12},{3,1},{5,3},{7,5},{... | collective-permute-start | bytes 307208 | tf_op jit(solution)/shard_map/ppermute | solution.py:17
  145.1 427.4 %reduce-scatter.5.cloned.1.call-start = ((), (), s32[]{:S(2)}) async-start(), calls=%async_computation.5 | async-start | bytes 10649600 | tf_op jit(solution)/shard_map/reduce_scatter | solution.py:81
Sparse Core Ops, SparseCore 0:
  9.6 32.1 all-gather.4
  43.5 30.6 all-gather.2
  145.3 54.5 reduce-scatter.2
  210.8 361.7 reduce-scatter.4
where the time goes:
time: 586 us; the launch traced here: 580 us
  waiting for transfers between devices  429 us (73%)
  matrix products  66.3 us (11%)
  local copies, waits for them, and re-layouts  42.5 us (7%)
  starting transfers between devices  16.2 us (3%)
  between operations  14.6 us (2%)
  other arithmetic  10.6 us (2%)
    reduce_scatter x1, waiting for transfers between devices, body(): lax.psum_scatter(weight_terms, ('lx', 'ly'), scatter_dimension=2, tiled=T...  360 us
    dot_general x27, matrix products, accumulate(): lax.dot_general(center, shifted, (((0,), (0,)), ((), ())), preferred_elem...  48.1 us
    all_gather x1, waiting for transfers between devices, body(): full_in = lax.all_gather(inputs, 'af', axis=0, tiled=True)  33.2 us
    all_gather x1, waiting for transfers between devices, body(): every_grad = lax.all_gather(grad_out, 'af', axis=0, tiled=True)  26.9 us
    dot_general x27, matrix products, accumulate(): jnp.dot(moved, kernel[index], preferred_element_type=jnp.float32)  18.2 us
  transfers between devices with their start and end apart: 12, of which 6 were waited for; matrix products, arithmetic and copies ran while one was open for 19% of the time, Pallas kernels for 0%

commit v1 on v0

v1 whole, which is shorter than its diff:
```python
import functools
import math

import jax
import jax.numpy as jnp
import numpy as np
from jax import lax
from jax.experimental import pallas as pl
from jax.experimental.pallas import tpu as pltpu
from jax.sharding import PartitionSpec as P

AXES = ("lx", "ly", "af")
BF, F32 = jnp.bfloat16, jnp.float32
C = 320
LIMIT = 56 * 2**20

STREAM_A = (0, 1, 2, 3, 4)
STREAM_B = (5, 6, 7, 8)


def routes(to):
    pairs = []
    for a in range(8):
        for b in range(8):
            for c in range(2):
                u, v, w = to(a, b, c)
                if 0 <= u < 8 and 0 <= v < 8:
                    pairs.append(((a * 8 + b) * 2 + c, (u * 8 + v) * 2 + w))
    return pairs


def send(value, to):
    return lax.ppermute(value, AXES, routes(to))


def swap_core(v):
    return send(v, lambda a, b, c: (a ^ 1, b, c))


def row_order():
    out = np.zeros((2, 4, 4, 2, 5, 2), np.int32)
    for first in range(4):
        for second in range(4):
            for d in range(2):
                for j in range(5):
                    out[0, first, second, d, j] = (first * 16 + d * 4 + second, j)
                    out[1, first, second, d, j] = (second * 16 + d * 4 + first, j)
    return out.reshape(320, 2)


def params():
    return pltpu.CompilerParams(vmem_limit_bytes=LIMIT)


def cost(flops, moved):
    return pl.CostEstimate(flops=flops, bytes_accessed=moved, transcendentals=0)


def sds(shape, dtype):
    return jax.ShapeDtypeStruct(shape, dtype)


def edges_kernel(g, first, last, plane, plane_first, plane_last):
    af = lax.axis_index("af")
    cells = g[...].reshape(1024, C)
    row = lax.broadcasted_iota(jnp.int32, (128, 1024), 0)
    col = lax.broadcasted_iota(jnp.int32, (128, 1024), 1)
    want = jnp.where(row < 64, row * 16, (row - 64) * 16 + 15)
    pick = jnp.where(col == want, 1.0, 0.0).astype(BF)
    both = jnp.dot(pick, cells, preferred_element_type=F32)
    low = both[:64].reshape(8, 8, C)
    high = both[64:].reshape(8, 8, C)
    first[...] = low.astype(BF)
    last[...] = high.astype(BF)
    at = (1 - af) * 7
    plane[...] = g[pl.ds(at, 1)].reshape(8, 16, C)
    plane_first[...] = jnp.where(af == 0, low[7], low[0]).astype(BF)
    plane_last[...] = jnp.where(af == 0, high[7], high[0]).astype(BF)


def edges(g):
    return pl.pallas_call(
        edges_kernel,
        out_shape=(
            sds((8, 8, C), BF),
            sds((8, 8, C), BF),
            sds((8, 16, C), BF),
            sds((8, C), BF),
            sds((8, C), BF),
        ),
        compiler_params=params(),
        cost_estimate=cost(100_000_000, 1_000_000),
        name="edges",
    )(g)


def rim_kernel(g, left, right, plane, plane_left, plane_right, halo, outer):
    core = lax.axis_index("lx") % 2
    lf, rf = left[...].astype(F32), right[...].astype(F32)
    pf, qf = plane_left[...].astype(F32), plane_right[...].astype(F32)
    for d in range(8):
        halo[d] = jnp.concatenate([lf[d], rf[d]], axis=0).astype(BF)
    halo[8:16] = plane[...]
    halo[16] = jnp.concatenate([pf, qf], axis=0).astype(BF)
    at = core * 7
    outer[0:8] = g[:, pl.ds(at, 1)].reshape(8, 16, C)
    outer[8] = plane[pl.ds(at, 1)].reshape(16, C)
    pad = jnp.zeros((7, C), F32)
    for n, (body, cap) in enumerate(((lf, pf), (rf, qf))):
        lo = jnp.concatenate([body[d, 0:1] for d in range(8)] + [cap[0:1], pad], axis=0)
        hi = jnp.concatenate([body[d, 7:8] for d in range(8)] + [cap[7:8], pad], axis=0)
        outer[9 + n] = jnp.where(core == 0, lo, hi).astype(BF)


def rim(g, left, right, plane, plane_left, plane_right):
    return pl.pallas_call(
        rim_kernel,
        out_shape=(sds((17, 16, C), BF), sds((11, 16, C), BF)),
        compiler_params=params(),
        cost_estimate=cost(1_000_000, 1_000_000),
        name="rim",
    )(g, left, right, plane, plane_left, plane_right)


def turn_kernel(order, own, other, out, both):
    core = lax.axis_index("lx") % 2
    mine = lax.axis_index("lx") * 8 + lax.axis_index("ly")
    both[:, pl.ds(core * 8, 8)] = own[...]
    both[:, pl.ds(8 - core * 8, 8)] = other[...]
    target = (order[:, 0:1] ^ mine) * 5 + order[:, 1:2]
    lane = lax.broadcasted_iota(jnp.int32, (320, C), 1)
    pick = jnp.where(lane == target, 1.0, 0.0).astype(BF)
    cells = both[...].reshape(2048, C)
    out[...] = lax.dot_general(
        pick, cells, (((1,), (1,)), ((), ())), preferred_element_type=F32
    ).astype(BF)


def turn(order, own, other):
    return pl.pallas_call(
        turn_kernel,
        out_shape=sds((320, 2048), BF),
        scratch_shapes=[pltpu.VMEM((8, 16, 16, C), BF)],
        compiler_params=params(),
        cost_estimate=cost(420_000_000, 2_600_000),
        name="turn",
    )(order, own, other)


def spread(tile, left, right):
    n = tile.shape[0]
    flat = tile.astype(F32).reshape(n * 16, C)
    col = lax.broadcasted_iota(jnp.int32, (n, 16, C), 1).reshape(n * 16, C)
    ends = jnp.broadcast_to(right.reshape(n, 1, C), (n, 16, C)).reshape(n * 16, C)
    heads = jnp.broadcast_to(left.reshape(n, 1, C), (n, 16, C)).reshape(n * 16, C)
    up = jnp.where(col == 15, ends, pltpu.roll(flat, n * 16 - 1, 0))
    down = jnp.where(col == 0, heads, pltpu.roll(flat, 1, 0))
    return jnp.concatenate([up, flat, down], axis=1).astype(BF).reshape(n, 16, 3 * C)


def weight_tiles(groups, turned, shifted, keep, sends):
    for n, pq in enumerate(groups):
        p, q = pq // 3, pq % 3
        cells = shifted[2 - p : 10 - p, 2 - q : 18 - q].reshape(2048, 3 * C)
        tile = jnp.dot(turned[...], cells, preferred_element_type=F32)
        keep[n] = tile[0:40]
        for b, ref in enumerate(sends):
            ref[n] = tile[40 * b + 40 : 40 * b + 80].astype(BF)


def first_kernel(g, other, halo, halo_other, alpha, beta, turned, kept_shifted, keep, s1, s2, s3, shifted, sem):
    core = lax.axis_index("lx") % 2
    af = lax.axis_index("af")
    for src, lines, at in ((g, halo, core * 8 + 1), (other, halo_other, 9 - core * 8)):

        def plane(d, carry, src=src, lines=lines, at=at):
            edge = lines[d].astype(F32)
            shifted[pl.ds(d + 1, 1), pl.ds(at, 8)] = spread(src[d], edge[0:8], edge[8:16])[None]
            return carry

        lax.fori_loop(0, 8, plane, 0)
        edge = lines[16].astype(F32)
        shifted[pl.ds(9 - af * 9, 1), pl.ds(at, 8)] = spread(lines[8:16], edge[0:8], edge[8:16])[None]
    for outer, at in ((alpha, core * 17), (beta, 17 - core * 17)):
        lf, rf = outer[9].astype(F32), outer[10].astype(F32)
        shifted[1:9, pl.ds(at, 1)] = spread(outer[0:8], lf[0:8], rf[0:8])[:, None]
        shifted[pl.ds(9 - af * 9, 1), pl.ds(at, 1)] = spread(outer[8:9], lf[8:9], rf[8:9])[None]
    shifted[pl.ds(af * 9, 1)] = jnp.zeros((1, 18, 16, 3 * C), BF)
    copy = pltpu.make_async_copy(shifted, kept_shifted, sem)
    copy.start()
    weight_tiles(STREAM_A, turned, shifted, keep, (s1, s2, s3))
    copy.wait()


def first_tiles(*operands):
    n = len(STREAM_A)
    piece = sds((n, 40, 3 * C), BF)
    spec = pl.BlockSpec(memory_space=pltpu.VMEM)
    return pl.pallas_call(
        first_kernel,
        out_shape=(sds((10, 18, 16, 3 * C), BF), sds((n, 40, 3 * C), F32), piece, piece, piece),
        in_specs=[spec] * 7,
        out_specs=(pl.BlockSpec(memory_space=pl.ANY),) + (spec,) * 4,
        scratch_shapes=[pltpu.VMEM((10, 18, 16, 3 * C), BF), pltpu.SemaphoreType.DMA],
        compiler_params=params(),
        cost_estimate=cost(2 * n * 160 * 2048 * 960, 14_000_000),
        name="first_tiles",
    )(*operands)


def second_kernel(shifted, turned, keep, s1, s2, s3):
    weight_tiles(STREAM_B, turned, shifted, keep, (s1, s2, s3))


def second_tiles(shifted, turned):
    n = len(STREAM_B)
    piece = sds((n, 40, 3 * C), BF)
    return pl.pallas_call(
        second_kernel,
        out_shape=(sds((n, 40, 3 * C), F32), piece, piece, piece),
        compiler_params=params(),
        cost_estimate=cost(2 * n * 160 * 2048 * 960, 10_000_000),
        name="second_tiles",
    )(shifted, turned)


def input_kernel(shifted_hbm, own_hbm, far_hbm, near_hbm, out, shifted, weight, sems):
    core = lax.axis_index("lx") % 2
    af = lax.axis_index("af")
    other = 160 - af * 160
    copies = [
        pltpu.make_async_copy(shifted_hbm.at[:, pl.ds(core * 8, 10)], shifted, sems.at[0]),
        pltpu.make_async_copy(own_hbm, weight.at[:, pl.ds(pl.multiple_of(af * 160, 16), 160)], sems.at[1]),
        pltpu.make_async_copy(far_hbm, weight.at[:, pl.ds(pl.multiple_of(other + core * 80, 16), 80)], sems.at[2]),
        pltpu.make_async_copy(
            near_hbm, weight.at[:, pl.ds(pl.multiple_of(other + 80 - core * 80, 16), 80)], sems.at[3]
        ),
    ]
    for copy in copies:
        copy.start()
    for copy in copies:
        copy.wait()

    def block(m, carry):
        total = jnp.zeros((256, C), F32)
        for p in range(3):
            for q in range(3):
                cells = shifted[pl.ds(2 * m + 2 - p, 2), 2 - q : 10 - q].reshape(256, 3 * C)
                taps = weight[9 * p + 3 * q : 9 * p + 3 * q + 3].reshape(3 * C, C)
                total = total + jnp.dot(cells, taps, preferred_element_type=F32)
        out[pl.ds(2 * m, 2)] = total.astype(BF).reshape(2, 8, 16, C)
        return carry

    lax.fori_loop(0, 4, block, 0)


def input_gradient(shifted, own, far, near):
    return pl.pallas_call(
        input_kernel,
        out_shape=sds((8, 8, 16, C), BF),
        in_specs=[pl.BlockSpec(memory_space=pl.ANY)] * 4,
        out_specs=pl.BlockSpec(memory_space=pltpu.VMEM),
        scratch_shapes=[
            pltpu.VMEM((10, 10, 16, 3 * C), BF),
            pltpu.VMEM((27, C, C), BF),
            pltpu.SemaphoreType.DMA((4,)),
        ],
        compiler_params=params(),
        cost_estimate=cost(2 * 1024 * 8640 * 320, 10_000_000),
        name="input_gradient",
    )(shifted, own, far, near)


def fold_kernel(n, keep, r1, r2, r3, out, s1, s2, s3):
    parts = [[], [], [], []]
    for g in range(n):
        total = keep[g] + r1[g].astype(F32) + r2[g].astype(F32) + r3[g].astype(F32)
        for b in range(4):
            parts[b].append(total[10 * b : 10 * b + 10])
    out[...] = jnp.concatenate(parts[0], axis=0)
    for b, ref in enumerate((s1, s2, s3)):
        ref[...] = jnp.concatenate(parts[b + 1], axis=0).astype(BF)


def fold(keep, r1, r2, r3):
    n = keep.shape[0]
    piece = sds((n * 10, 3 * C), BF)
    return pl.pallas_call(
        functools.partial(fold_kernel, n),
        out_shape=(sds((n * 10, 3 * C), F32), piece, piece, piece),
        compiler_params=params(),
        cost_estimate=cost(1_000_000, 2_500_000),
        name="fold",
    )(keep, r1, r2, r3)


def cut_kernel(a0, a1, a2, a3, b0, b1, b2, b3, out, s1, s2, s3):
    af = lax.axis_index("af")
    same, flip = [[], []], [[], []]
    for refs, n in (((a0, a1, a2, a3), len(STREAM_A)), ((b0, b1, b2, b3), len(STREAM_B))):
        total = refs[0][...]
        for ref in refs[1:]:
            total = total + ref[...].astype(F32)
        low = jnp.concatenate([total[:, C * r : C * r + 160] for r in range(3)], axis=1)
        high = jnp.concatenate([total[:, C * r + 160 : C * r + 320] for r in range(3)], axis=1)
        mine = jnp.where(af == 0, low, high)
        theirs = jnp.where(af == 0, high, low)
        for g in range(n):
            for d in range(2):
                same[d].append(mine[10 * g + 5 * d : 10 * g + 5 * d + 5])
                flip[d].append(theirs[10 * g + 5 * d : 10 * g + 5 * d + 5])
    out[...] = jnp.concatenate(same[0], axis=0)
    s1[...] = jnp.concatenate(flip[0], axis=0).astype(BF)
    s2[...] = jnp.concatenate(same[1], axis=0).astype(BF)
    s3[...] = jnp.concatenate(flip[1], axis=0).astype(BF)


def cut(*operands):
    piece = sds((45, 480), BF)
    return pl.pallas_call(
        cut_kernel,
        out_shape=(sds((45, 480), F32), piece, piece, piece),
        compiler_params=params(),
        cost_estimate=cost(1_000_000, 1_500_000),
        name="cut",
    )(*operands)


def last_kernel(scale, keep, r1, r2, r3, out):
    total = (keep[...] + r1[...].astype(F32) + r2[...].astype(F32) + r3[...].astype(F32)) * scale
    for n, pq in enumerate(STREAM_A + STREAM_B):
        for r in range(3):
            out[:, 3 * pq + r, :] = total[5 * n : 5 * n + 5, 160 * r : 160 * r + 160]


def last(scale, *operands):
    return pl.pallas_call(
        functools.partial(last_kernel, scale),
        out_shape=sds((5, 27, 160), F32),
        compiler_params=params(),
        cost_estimate=cost(100_000, 400_000),
        name="last",
    )(*operands)


def body(grad_out, inputs, weight):
    core = lax.axis_index("lx") % 2
    scale = 1.0 / math.sqrt(16 * 64 * 128)

    first, final, plane, plane_first, plane_final = edges(grad_out)
    left = send(final, lambda a, b, c: (a, b + 1, c))
    right = send(first, lambda a, b, c: (a, b - 1, c))
    plane = send(plane, lambda a, b, c: (a, b, c ^ 1))
    plane_left = send(plane_final, lambda a, b, c: (a, b + 1, c ^ 1))
    plane_right = send(plane_first, lambda a, b, c: (a, b - 1, c ^ 1))
    grad_other = swap_core(grad_out)
    inputs_other = swap_core(inputs)

    quarter = lax.dynamic_slice_in_dim(weight, core * 80, 80, 1)
    far = send(quarter, lambda a, b, c: (a, b ^ (4 * (a % 2)), c ^ 1))
    near = swap_core(far)

    halo, outer = rim(grad_out, left, right, plane, plane_left, plane_right)
    halo_other = swap_core(halo)
    alpha = send(outer, lambda a, b, c: (a + 2 * (a % 2) - 1, b, c))
    beta = send(outer, lambda a, b, c: (a + 4 * (a % 2) - 2, b, c))

    turned = turn(jnp.asarray(row_order()), inputs, inputs_other)
    shifted, a0, *a_out = first_tiles(
        grad_out, grad_other, halo, halo_other, alpha, beta, turned[:160]
    )
    along_z = [lambda a, b, c, s=s: (a ^ (2 * s), b, c) for s in (1, 2, 3)]
    along_x = [lambda a, b, c, s=s: (a, b ^ s, c) for s in (1, 2, 3)]
    along_y = [
        lambda a, b, c: (a, b, c ^ 1),
        lambda a, b, c: (a, b ^ 4, c),
        lambda a, b, c: (a, b ^ 4, c ^ 1),
    ]
    a_in = [send(v, to) for v, to in zip(a_out, along_z)]
    b0, *b_out = second_tiles(shifted, turned[160:])
    b_in = [send(v, to) for v, to in zip(b_out, along_x)]

    grad_input = input_gradient(shifted, weight, far, near)

    a0, *a_out = fold(a0, *a_in)
    a_in = [send(v, to) for v, to in zip(a_out, along_x)]
    b0, *b_out = fold(b0, *b_in)
    b_in = [send(v, to) for v, to in zip(b_out, along_z)]
    keep, *outs = cut(a0, *a_in, b0, *b_in)
    ins = [send(v, to) for v, to in zip(outs, along_y)]
    grad_weight = last(scale, keep, *ins)
    return (grad_input, jnp.transpose(grad_weight, (1, 2, 0)))


def solution(mesh):
    placed = (P("af", "lx", "ly", None), P("af", "lx", "ly", None), P(None, "af", None))
    return jax.shard_map(
        body,
        mesh=mesh,
        in_specs=placed,
        out_specs=(P("af", "lx", "ly", None), P(None, "af", ("lx", "ly"))),
        check_vma=False,
    )
```

time: 586 us -> 146 us (0.25)
  waiting for transfers between devices: 429 us -> 34.8 us
  matrix products: 66.3 us -> 0 us
  Pallas kernels: 0 us -> 47.1 us
  starting transfers between devices: 16.2 us -> 52 us
  local copies, waits for them, and re-layouts: 42.5 us -> 10 us
  between operations: 14.6 us -> 1.11 us
  other arithmetic: 10.6 us -> 0 us
    reduce_scatter x2 -> x0, waiting for transfers between devices: 360 us -> none  [the longest x1 360 us: body(): lax.psum_scatter(weight_terms, ('lx', 'ly'), scatter_dimension=2, tiled=T...]
    dot_general x54 -> x0, matrix products: 66.3 us -> none  [the longest x27 48.1 us: accumulate(): lax.dot_general(center, shifted, (((0,), (0,)), ((), ())), preferred_elem...]
    all_gather x2 -> x0, waiting for transfers between devices: 60.1 us -> none  [the longest x1 33.2 us: body(): full_in = lax.all_gather(inputs, 'af', axis=0, tiled=True)]
    pallas_call x0 -> x10, Pallas kernels: none -> 47.1 us  [the longest x1 15.2 us: input_gradient(): pl.pallas_call(input_kernel, out_shape=sds((8, 8, 16, C), BF), in_specs=[...]
    ppermute x8 -> x27, starting transfers between devices: 16.1 us -> 52 us  [send(): return lax.ppermute(value, AXES, routes(to))]
    ppermute x8 -> x27, waiting for transfers between devices: 8.24 us -> 34.8 us  [send(): return lax.ppermute(value, AXES, routes(to))]
    slice x5 -> x1, local copies, waits for them, and re-layouts: 14.6 us -> 2.49 us  [body(): b0, *b_out = second_tiles(shifted, turned[160:])]
    another operation x1 -> x0, local copies, waits for them, and re-layouts: 11.5 us -> none  [accumulate(): return (total.reshape(depth, rows, cols, chans), jnp.stack(pieces))]
  transfers between devices with their start and end apart: 12 -> 27, of which waited for: 6 -> 9; matrix products, arithmetic and copies ran while one was open for 19% -> 2% of each run, Pallas kernels for 0% -> 22%
where the time goes in v1:
time: 146 us; the launch traced here: 145 us
  starting transfers between devices  52 us (36%)
  Pallas kernels  47.1 us (32%)
  waiting for transfers between devices  34.8 us (24%)
  local copies, waits for them, and re-layouts  10 us (7%)
    ppermute x27, starting transfers between devices, send(): return lax.ppermute(value, AXES, routes(to))  52 us
    ppermute x27, waiting for transfers between devices, send(): return lax.ppermute(value, AXES, routes(to))  34.8 us
    pallas_call x1, Pallas kernels, input_gradient(): pl.pallas_call(input_kernel, out_shape=sds((8, 8, 16, C), BF), in_specs=[...  15.2 us
    pallas_call x1, Pallas kernels, first_tiles(): pl.pallas_call(first_kernel, out_shape=(sds((10, 18, 16, 3 * C), BF), sds...  8.76 us
    pallas_call x1, Pallas kernels, second_tiles(): pl.pallas_call(second_kernel, out_shape=(sds((n, 40, 3 * C), F32), piece,...  6.92 us
    unnamed x66, local copies, waits for them, and re-layouts  5.81 us
    pallas_call x2, Pallas kernels, fold(): pl.pallas_call(functools.partial(fold_kernel, n), out_shape=(sds((n * 10,...  4.61 us
    pallas_call x1, Pallas kernels, turn(): pl.pallas_call(turn_kernel, out_shape=sds((320, 2048), BF), scratch_shape...  3.57 us
  transfers between devices with their start and end apart: 27, of which 9 were waited for; matrix products, arithmetic and copies ran while one was open for 2% of the time, Pallas kernels for 22%

profile of v1, /device:TPU:0, one launch (start us, length us, event | category | flops | bytes accessed | tf_op | source)
XLA Modules:
  0.0 145.0 jit_solution(10155067158365683220)
XLA Ops:
  0.7 1.7 %constant_dynamic-slice_fusion = bf16[27,80,320]{2,1,0:T(8,128)(2,1)S(1)} fusion(bf16[27,160,320]{2,1,0:T(8,128)(2,1)} %own_hbm.1, s32[]{:T(128)S(6)} %select_n.11), kind=kLoop, calls=%fused_computation | loop fusion | bytes 2764804 | tf_op jit(solution)/shard_map/dynamic_slice | solution.py:359
  2.4 1.7 %collective-permute-start.10 = (bf16[27,80,320]{2,1,0:T(8,128)(2,1)S(1)}, bf16[27,80,320]{2,1,0:T(8,128)(2,1)S(1)}, u32[]{:S(2)}, u32[]{:S(2)}) collective-permute-start(bf16[27,80,320]{2,1,0:T(8,128)(2,1)S(1)} %constant_dynamic-slice_fusion), channel_id=1, source_target_pairs={{0,1},{1,0},{2,3},{3,2},{4,5},{5,4},{6,7},{7,6},{8,9},{9,8},{10,11... | collective-permute-start | bytes 4147208 | tf_op jit(solution)/shard_map/ppermute | solution.py:33
  4.1 1.0 collective-permute-start.9
  5.2 2.1 %edges.1 = (bf16[8,8,320]{2,1,0:T(8,128)(2,1)}, bf16[8,8,320]{2,1,0:T(8,128)(2,1)}, bf16[8,16,320]{2,1,0:T(8,128)(2,1)}, bf16[8,320]{1,0:T(8,128)(2,1)}, bf16[8,320]{1,0:T(8,128)(2,1)}) custom-call(bf16[8,8,16,320]{3,2,1,0:T(8,128)(2,1)} %g.5), custom_call_target="tpu_custom_call" | custom-call | flops 100000000 | bytes 1000000 | tf_op jit(solution)/shard_map/edges/pallas_call | solution.py:82
  7.3 3.0 %collective-permute-start.4 = (bf16[8,320]{1,0:T(8,128)(2,1)}, bf16[8,320]{1,0:T(8,128)(2,1)S(1)}, u32[]{:S(2)}, u32[]{:S(2)}) collective-permute-start(bf16[8,320]{1,0:T(8,128)(2,1)} %get-tuple-element.33), channel_id=1, source_target_pairs={{0,3},{1,2},{2,5},{3,4},{4,7},{5,6},{6,9},{7,8},{8,11},{9,10},{10,... | collective-permute-start | bytes 15368 | tf_op jit(solution)/shard_map/ppermute | solution.py:33
  10.3 1.3 collective-permute-start.5
  11.8 5.6 %collective-permute-start.1 = (bf16[8,8,320]{2,1,0:T(8,128)(2,1)}, bf16[8,8,320]{2,1,0:T(8,128)(2,1)S(1)}, u32[]{:S(2)}, u32[]{:S(2)}) collective-permute-start(bf16[8,8,320]{2,1,0:T(8,128)(2,1)} %get-tuple-element.30), channel_id=1, source_target_pairs={{0,2},{1,3},{2,4},{3,5},{4,6},{5,7},{6,8},{7,9},{8,10},{9,11},{10,... | collective-permute-start | bytes 122888 | tf_op jit(solution)/shard_map/ppermute | solution.py:33
  17.5 1.4 collective-permute-start.3
  18.9 0.6 collective-permute-done.1.left
  19.5 1.3 collective-permute-start.2
  20.8 5.1 %collective-permute-done.2.right = bf16[8,8,320]{2,1,0:T(8,128)(2,1)S(1)} collective-permute-done((bf16[8,8,320]{2,1,0:T(8,128)(2,1)}, bf16[8,8,320]{2,1,0:T(8,128)(2,1)S(1)}, u32[]{:S(2)}, u32[]{:S(2)}) %collective-permute-start.2) | collective-permute-done | bytes 40992 | tf_op jit(solution)/shard_map/ppermute | solution.py:33
  25.9 1.2 collective-permute-done.3.plane
  27.1 0.6 copy-done.12
  27.8 2.0 %rim.1 = (bf16[17,16,320]{2,1,0:T(8,128)(2,1)}, bf16[11,16,320]{2,1,0:T(8,128)(2,1)}) custom-call(bf16[8,8,16,320]{3,2,1,0:T(8,128)(2,1)} %g.5, bf16[8,8,320]{2,1,0:T(8,128)(2,1)} %copy-done.16, bf16[8,8,320]{2,1,0:T(8,128)(2,1)} %copy-done.17, bf16[8,16,320]{2,1,0:T(8,128)(2,1)} %copy-done.12, bf16[8,320]{1,0:T(8,128)(2,1)} %copy-done.21, ...), custom_call_target="tpu_custom_call" | custom-call | flops 1000000 | bytes 1000000 | tf_op jit(solution)/shard_map/rim/pallas_call | solution.py:116
  29.8 0.7 collective-permute-start.7
  30.4 1.3 collective-permute-start.8
  31.8 5.7 %collective-permute-start.6 = (bf16[17,16,320]{2,1,0:T(8,128)(2,1)}, bf16[17,16,320]{2,1,0:T(8,128)(2,1)S(1)}, u32[]{:S(2)}, u32[]{:S(2)}) collective-permute-start(bf16[17,16,320]{2,1,0:T(8,128)(2,1)} %get-tuple-element.35.halo), channel_id=1, source_target_pairs={{0,16},{1,17},{2,18},{3,19},{4,20},{5,21},{6,22},{7,23},{8,24},{9,... | collective-permute-start | bytes 522248 | tf_op jit(solution)/shard_map/ppermute | solution.py:33
  37.4 3.6 %turn.1 = bf16[320,2048]{1,0:T(8,128)(2,1)} custom-call(s32[320,2]{1,0:T(8,128)} %constant.26.clone.order, bf16[8,8,16,320]{3,2,1,0:T(8,128)(2,1)} %own.1, bf16[8,8,16,320]{3,2,1,0:T(8,128)(2,1)} %copy-done.2), custom_call_target="tpu_custom_call" | custom-call | flops 420000000 | bytes 2600000 | tf_op jit(solution)/shard_map/turn/pallas_call | solution.py:140
  41.0 0.8 collective-permute-start.11
  41.8 2.5 %fusion = (bf16[160,2048]{1,0:T(8,128)(2,1)}, bf16[160,2048]{1,0:T(8,128)(2,1)}) fusion(bf16[320,2048]{1,0:T(8,128)(2,1)} %turn.1), kind=kLoop, calls=%fused_computation.1 | loop fusion | bytes 2621440 | tf_op jit(solution)/shard_map/slice | solution.py:380
  44.4 0.6 copy-done.30
  45.3 8.8 %first_tiles.1 = (bf16[10,18,16,960]{3,2,1,0:T(8,128)(2,1)}, f32[5,40,960]{2,1,0:T(8,128)}, bf16[5,40,960]{2,1,0:T(8,128)(2,1)}, bf16[5,40,960]{2,1,0:T(8,128)(2,1)}, bf16[5,40,960]{2,1,0:T(8,128)(2,1)}) custom-call(bf16[8,8,16,320]{3,2,1,0:T(8,128)(2,1)} %g.5, bf16[8,8,16,320]{3,2,1,0:T(8,128)(2,1)} %copy-done.25, ...), custom_call_target="tpu_custom_call" | custom-call | flops 3145728000 | bytes 14000000 | tf_op jit(solution)/shard_map/first_tiles/pallas_call | solution.py:199
  54.1 6.9 %second_tiles.1 = (f32[4,40,960]{2,1,0:T(8,128)}, bf16[4,40,960]{2,1,0:T(8,128)(2,1)}, bf16[4,40,960]{2,1,0:T(8,128)(2,1)}, bf16[4,40,960]{2,1,0:T(8,128)(2,1)}) custom-call(bf16[10,18,16,960]{3,2,1,0:T(8,128)(2,1)} %get-tuple-element.37.shifted_hbm.shifted, bf16[160,2048]{1,0:T(8,128)(2,1)} %get-tuple-element.58.turned), custom_call_target="tpu_custom_call" | custom-call | flops 2516582400 | bytes 10000000 | tf_op jit(solution)/shard_map/second_tiles/pallas_call | solution.py:218
  61.1 1.4 collective-permute-start.18
  62.4 7.9 %collective-permute-start.19 = (bf16[4,40,960]{2,1,0:T(8,128)(2,1)}, bf16[4,40,960]{2,1,0:T(8,128)(2,1)S(1)}, u32[]{:S(2)}, u32[]{:S(2)}) collective-permute-start(bf16[4,40,960]{2,1,0:T(8,128)(2,1)} %get-tuple-element.48), channel_id=1, source_target_pairs={{0,4},{1,5},{2,6},{3,7},{4,0},{5,1},{6,2},{7,3},{8,12},{9,13},{10,... | collective-permute-start | bytes 921608 | tf_op jit(solution)/shard_map/ppermute | solution.py:33
  70.3 1.6 %collective-permute-start.12 = (bf16[5,40,960]{2,1,0:T(8,128)(2,1)S(1)}, bf16[5,40,960]{2,1,0:T(8,128)(2,1)S(1)}, u32[]{:S(2)}, u32[]{:S(2)}) collective-permute-start(bf16[5,40,960]{2,1,0:T(8,128)(2,1)S(1)} %copy-done.28), channel_id=1, source_target_pairs={{0,32},{1,33},{2,34},{3,35},{4,36},{5,37},{6,38},{7,39},{8,40},{9,... | collective-permute-start | bytes 1152008 | tf_op jit(solution)/shard_map/ppermute | solution.py:33
  71.9 1.2 collective-permute-start.13
  73.2 1.9 %collective-permute-start.14 = (bf16[5,40,960]{2,1,0:T(8,128)(2,1)S(1)}, bf16[5,40,960]{2,1,0:T(8,128)(2,1)S(1)}, u32[]{:S(2)}, u32[]{:S(2)}) collective-permute-start(bf16[5,40,960]{2,1,0:T(8,128)(2,1)S(1)} %copy-done.26), channel_id=1, source_target_pairs={{0,96},{1,97},{2,98},{3,99},{4,100},{5,101},{6,102},{7,103},{8,104... | collective-permute-start | bytes 1152008 | tf_op jit(solution)/shard_map/ppermute | solution.py:33
  75.1 10.6 %collective-permute-done.19.r2 = bf16[4,40,960]{2,1,0:T(8,128)(2,1)S(1)} collective-permute-done((bf16[4,40,960]{2,1,0:T(8,128)(2,1)}, bf16[4,40,960]{2,1,0:T(8,128)(2,1)S(1)}, u32[]{:S(2)}, u32[]{:S(2)}) %collective-permute-start.19) | collective-permute-done | bytes 307232 | tf_op jit(solution)/shard_map/ppermute | solution.py:33
  85.7 10.9 %collective-permute-done.20.r3 = bf16[4,40,960]{2,1,0:T(8,128)(2,1)S(1)} collective-permute-done((bf16[4,40,960]{2,1,0:T(8,128)(2,1)}, bf16[4,40,960]{2,1,0:T(8,128)(2,1)S(1)}, u32[]{:S(2)}, u32[]{:S(2)}) %collective-permute-start.20) | collective-permute-done | bytes 307232 | tf_op jit(solution)/shard_map/ppermute | solution.py:33
  96.6 0.7 copy-done.8
  97.4 2.2 %fold.3 = (f32[40,960]{1,0:T(8,128)}, bf16[40,960]{1,0:T(8,128)(2,1)}, bf16[40,960]{1,0:T(8,128)(2,1)}, bf16[40,960]{1,0:T(8,128)(2,1)}) custom-call(f32[4,40,960]{2,1,0:T(8,128)} %get-tuple-element.46.keep, bf16[4,40,960]{2,1,0:T(8,128)(2,1)} %copy-done.6, bf16[4,40,960]{2,1,0:T(8,128)(2,1)} %copy-done.7, bf16[4,40,960]{2,1,0:T(8,128)(2,1)} %copy-done.8), custom_call_target="tpu_custom_call" | custom-call | flops 1000000 | bytes 2500000 | tf_op jit(solution)/shard_map/fold/pallas_call | solution.py:288
  99.6 1.6 %collective-permute-start.21 = (bf16[40,960]{1,0:T(8,128)(2,1)}, bf16[40,960]{1,0:T(8,128)(2,1)S(1)}, u32[]{:S(2)}, u32[]{:S(2)}) collective-permute-start(bf16[40,960]{1,0:T(8,128)(2,1)} %get-tuple-element.51), channel_id=1, source_target_pairs={{0,32},{1,33},{2,34},{3,35},{4,36},{5,37},{6,38},{7,39},{8,40},{9,... | collective-permute-start | bytes 230408 | tf_op jit(solution)/shard_map/ppermute | solution.py:33
  102.5 2.4 %fold.2 = (f32[50,960]{1,0:T(8,128)}, bf16[50,960]{1,0:T(8,128)(2,1)}, bf16[50,960]{1,0:T(8,128)(2,1)}, bf16[50,960]{1,0:T(8,128)(2,1)}) custom-call(f32[5,40,960]{2,1,0:T(8,128)} %get-tuple-element.38.keep, bf16[5,40,960]{2,1,0:T(8,128)(2,1)} %copy-done.3, bf16[5,40,960]{2,1,0:T(8,128)(2,1)} %copy-done.4, bf16[5,40,960]{2,1,0:T(8,128)(2,1)} %copy-done.5), custom_call_target="tpu_custom_call" | custom-call | flops 1000000 | bytes 2500000 | tf_op jit(solution)/shard_map/fold/pallas_call | solution.py:288
  104.9 1.7 %collective-permute-start.16 = (bf16[50,960]{1,0:T(8,128)(2,1)}, bf16[50,960]{1,0:T(8,128)(2,1)S(1)}, u32[]{:S(2)}, u32[]{:S(2)}) collective-permute-start(bf16[50,960]{1,0:T(8,128)(2,1)} %get-tuple-element.44), channel_id=1, source_target_pairs={{0,4},{1,5},{2,6},{3,7},{4,0},{5,1},{6,2},{7,3},{8,12},{9,13},{10,... | collective-permute-start | bytes 288008 | tf_op jit(solution)/shard_map/ppermute | solution.py:33
  106.7 3.0 %collective-permute-start.17 = (bf16[50,960]{1,0:T(8,128)(2,1)}, bf16[50,960]{1,0:T(8,128)(2,1)S(1)}, u32[]{:S(2)}, u32[]{:S(2)}) collective-permute-start(bf16[50,960]{1,0:T(8,128)(2,1)} %get-tuple-element.45), channel_id=1, source_target_pairs={{0,6},{1,7},{2,4},{3,5},{4,2},{5,3},{6,0},{7,1},{8,14},{9,15},{10,... | collective-permute-start | bytes 288008 | tf_op jit(solution)/shard_map/ppermute | solution.py:33
  109.6 2.7 %collective-permute-start.23 = (bf16[40,960]{1,0:T(8,128)(2,1)S(1)}, bf16[40,960]{1,0:T(8,128)(2,1)S(1)}, u32[]{:S(2)}, u32[]{:S(2)}) collective-permute-start(bf16[40,960]{1,0:T(8,128)(2,1)S(1)} %copy-done.32), channel_id=1, source_target_pairs={{0,96},{1,97},{2,98},{3,99},{4,100},{5,101},{6,102},{7,103},{8,104... | collective-permute-start | bytes 230408 | tf_op jit(solution)/shard_map/ppermute | solution.py:33
  112.4 3.0 %collective-permute-done.23.b3 = bf16[40,960]{1,0:T(8,128)(2,1)S(1)} collective-permute-done((bf16[40,960]{1,0:T(8,128)(2,1)S(1)}, bf16[40,960]{1,0:T(8,128)(2,1)S(1)}, u32[]{:S(2)}, u32[]{:S(2)}) %collective-permute-start.23) | collective-permute-done | bytes 76832 | tf_op jit(solution)/shard_map/ppermute | solution.py:33
  115.4 0.6 copy-done.15
  116.1 2.2 %cut.1 = (f32[45,480]{1,0:T(8,128)}, bf16[45,480]{1,0:T(8,128)(2,1)}, bf16[45,480]{1,0:T(8,128)(2,1)}, bf16[45,480]{1,0:T(8,128)(2,1)}) custom-call(f32[50,960]{1,0:T(8,128)} %get-tuple-element.42.a0, bf16[50,960]{1,0:T(8,128)(2,1)} %copy-done.9, bf16[50,960]{1,0:T(8,128)(2,1)} %copy-done.10, bf16[50,960]{1,0:T(8,128)(2,1)} %copy-done.11, ...), custom_call_target="tpu_custom_call" | custom-call | flops 1000000 | bytes 1500000 | tf_op jit(solution)/shard_map/cut/pallas_call | solution.py:320
  118.3 1.4 collective-permute-start.24
  120.0 3.0 %collective-permute-start.26 = (bf16[45,480]{1,0:T(8,128)(2,1)}, bf16[45,480]{1,0:T(8,128)(2,1)S(1)}, u32[]{:S(2)}, u32[]{:S(2)}) collective-permute-start(bf16[45,480]{1,0:T(8,128)(2,1)} %get-tuple-element.57), channel_id=1, source_target_pairs={{0,9},{1,8},{2,11},{3,10},{4,13},{5,12},{6,15},{7,14},{8,1},{9,0},... | collective-permute-start | bytes 129608 | tf_op jit(solution)/shard_map/ppermute | solution.py:33
  123.0 2.6 %collective-permute-done.25.r2 = bf16[45,480]{1,0:T(8,128)(2,1)S(1)} collective-permute-done((bf16[45,480]{1,0:T(8,128)(2,1)}, bf16[45,480]{1,0:T(8,128)(2,1)S(1)}, u32[]{:S(2)}, u32[]{:S(2)}) %collective-permute-start.25) | collective-permute-done | bytes 43232 | tf_op jit(solution)/shard_map/ppermute | solution.py:33
  125.5 0.5 collective-permute-done.26.r3
  126.1 0.5 copy-done.20
  126.6 1.8 %last.1 = f32[5,27,160]{2,1,0:T(8,128)} custom-call(f32[45,480]{1,0:T(8,128)} %get-tuple-element.54.keep, bf16[45,480]{1,0:T(8,128)(2,1)} %copy-done.18, bf16[45,480]{1,0:T(8,128)(2,1)} %copy-done.19, bf16[45,480]{1,0:T(8,128)(2,1)} %copy-done.20), custom_call_target="tpu_custom_call" | custom-call | flops 100000 | bytes 400000 | tf_op jit(solution)/shard_map/last/pallas_call | solution.py:337
  128.4 1.2 copy-done.24
  129.6 15.2 %input_gradient.1 = bf16[8,8,16,320]{3,2,1,0:T(8,128)(2,1)} custom-call(bf16[10,18,16,960]{3,2,1,0:T(8,128)(2,1)} %get-tuple-element.37.shifted_hbm.shifted, bf16[27,160,320]{2,1,0:T(8,128)(2,1)} %own_hbm.1, bf16[27,80,320]{2,1,0:T(8,128)(2,1)} %copy-done.23, bf16[27,80,320]{2,1,0:T(8,128)(2,1)} %copy-done.24), custom_call_target="tpu_custom_call" | custom-call | flops 5662310400 | bytes 10000000 | tf_op jit(solution)/shard_map/input_gradient/pallas_call | solution.py:258
  (84 shorter events, 2.7 us)
Async XLA Ops:
  0.6 3.5 %copy-start.1 = (bf16[8,8,16,320]{3,2,1,0:T(8,128)(2,1)S(1)}, bf16[8,8,16,320]{3,2,1,0:T(8,128)(2,1)}, u32[]{:S(2)}) copy-start(bf16[8,8,16,320]{3,2,1,0:T(8,128)(2,1)} %own.1) | copy-start | bytes 1966084
  0.7 4.5 %copy-start = (bf16[8,8,16,320]{3,2,1,0:T(8,128)(2,1)S(1)}, bf16[8,8,16,320]{3,2,1,0:T(8,128)(2,1)}, u32[]{:S(2)}) copy-start(bf16[8,8,16,320]{3,2,1,0:T(8,128)(2,1)} %g.5) | copy-start | bytes 1966084
  2.4 38.6 %collective-permute-start.10 = (bf16[27,80,320]{2,1,0:T(8,128)(2,1)S(1)}, bf16[27,80,320]{2,1,0:T(8,128)(2,1)S(1)}, u32[]{:S(2)}, u32[]{:S(2)}) collective-permute-start(bf16[27,80,320]{2,1,0:T(8,128)(2,1)S(1)} %constant_dynamic-slice_fusion), channel_id=1, source_target_pairs={{0,1},{1,0},{2,3},{3,2},{4,5},{5,4},{6,7},{7,6},{8,9},{9,8},{10,11... | collective-permute-start | bytes 4147208 | tf_op jit(solution)/shard_map/ppermute | solution.py:33
  4.1 27.6 %collective-permute-start.9 = (bf16[8,8,16,320]{3,2,1,0:T(8,128)(2,1)S(1)}, bf16[8,8,16,320]{3,2,1,0:T(8,128)(2,1)S(1)}, u32[]{:S(2)}, u32[]{:S(2)}) collective-permute-start(bf16[8,8,16,320]{3,2,1,0:T(8,128)(2,1)S(1)} %copy-done.1), channel_id=1, source_target_pairs={{0,16},{1,17},{2,18},{3,19},{4,20},{5,21},{6,22},{7,23},{8,24},{9,... | collective-permute-start | bytes 1966088 | tf_op jit(solution)/shard_map/ppermute | solution.py:33
  5.1 39.2 %collective-permute-start = (bf16[8,8,16,320]{3,2,1,0:T(8,128)(2,1)S(1)}, bf16[8,8,16,320]{3,2,1,0:T(8,128)(2,1)S(1)}, u32[]{:S(2)}, u32[]{:S(2)}) collective-permute-start(bf16[8,8,16,320]{3,2,1,0:T(8,128)(2,1)S(1)} %copy-done), channel_id=1, source_target_pairs={{0,16},{1,17},{2,18},{3,19},{4,20},{5,21},{6,22},{7,23},{8,24},{9,... | collective-permute-start | bytes 1966088 | tf_op jit(solution)/shard_map/ppermute | solution.py:33
  7.3 4.5 %collective-permute-start.4 = (bf16[8,320]{1,0:T(8,128)(2,1)}, bf16[8,320]{1,0:T(8,128)(2,1)S(1)}, u32[]{:S(2)}, u32[]{:S(2)}) collective-permute-start(bf16[8,320]{1,0:T(8,128)(2,1)} %get-tuple-element.33), channel_id=1, source_target_pairs={{0,3},{1,2},{2,5},{3,4},{4,7},{5,6},{6,9},{7,8},{8,11},{9,10},{10,... | collective-permute-start | bytes 15368 | tf_op jit(solution)/shard_map/ppermute | solution.py:33
  10.3 7.2 %collective-permute-start.5 = (bf16[8,320]{1,0:T(8,128)(2,1)}, bf16[8,320]{1,0:T(8,128)(2,1)S(1)}, u32[]{:S(2)}, u32[]{:S(2)}) collective-permute-start(bf16[8,320]{1,0:T(8,128)(2,1)} %get-tuple-element.34), channel_id=1, source_target_pairs={{2,1},{3,0},{4,3},{5,2},{6,5},{7,4},{8,7},{9,6},{10,9},{11,8},{12,... | collective-permute-start | bytes 15368 | tf_op jit(solution)/shard_map/ppermute | solution.py:33
  11.8 15.3 %copy-start.21 = (bf16[8,320]{1,0:T(8,128)(2,1)}, bf16[8,320]{1,0:T(8,128)(2,1)S(1)}, u32[]{:S(2)}) copy-start(bf16[8,320]{1,0:T(8,128)(2,1)S(1)} %collective-permute-done.4.plane_left) | copy-start | bytes 15364
  11.8 7.7 %collective-permute-start.1 = (bf16[8,8,320]{2,1,0:T(8,128)(2,1)}, bf16[8,8,320]{2,1,0:T(8,128)(2,1)S(1)}, u32[]{:S(2)}, u32[]{:S(2)}) collective-permute-start(bf16[8,8,320]{2,1,0:T(8,128)(2,1)} %get-tuple-element.30), channel_id=1, source_target_pairs={{0,2},{1,3},{2,4},{3,5},{4,6},{5,7},{6,8},{7,9},{8,10},{9,11},{10,... | collective-permute-start | bytes 122888 | tf_op jit(solution)/shard_map/ppermute | solution.py:33
  17.5 9.6 %copy-start.22 = (bf16[8,320]{1,0:T(8,128)(2,1)}, bf16[8,320]{1,0:T(8,128)(2,1)S(1)}, u32[]{:S(2)}) copy-start(bf16[8,320]{1,0:T(8,128)(2,1)S(1)} %collective-permute-done.5.plane_right) | copy-start | bytes 15364
  17.5 9.6 %collective-permute-start.3 = (bf16[8,16,320]{2,1,0:T(8,128)(2,1)}, bf16[8,16,320]{2,1,0:T(8,128)(2,1)S(1)}, u32[]{:S(2)}, u32[]{:S(2)}) collective-permute-start(bf16[8,16,320]{2,1,0:T(8,128)(2,1)} %get-tuple-element.32), channel_id=1, source_target_pairs={{0,1},{1,0},{2,3},{3,2},{4,5},{5,4},{6,7},{7,6},{8,9},{9,8},{10,11... | collective-permute-start | bytes 245768 | tf_op jit(solution)/shard_map/ppermute | solution.py:33
  19.5 7.6 %copy-start.16 = (bf16[8,8,320]{2,1,0:T(8,128)(2,1)}, bf16[8,8,320]{2,1,0:T(8,128)(2,1)S(1)}, u32[]{:S(2)}) copy-start(bf16[8,8,320]{2,1,0:T(8,128)(2,1)S(1)} %collective-permute-done.1.left) | copy-start | bytes 122884
  19.5 6.4 %collective-permute-start.2 = (bf16[8,8,320]{2,1,0:T(8,128)(2,1)}, bf16[8,8,320]{2,1,0:T(8,128)(2,1)S(1)}, u32[]{:S(2)}, u32[]{:S(2)}) collective-permute-start(bf16[8,8,320]{2,1,0:T(8,128)(2,1)} %get-tuple-element.31), channel_id=1, source_target_pairs={{2,0},{3,1},{4,2},{5,3},{6,4},{7,5},{8,6},{9,7},{10,8},{11,9},{12,... | collective-permute-start | bytes 122888 | tf_op jit(solution)/shard_map/ppermute | solution.py:33
  25.9 1.2 copy-start.17
  29.8 14.5 %collective-permute-start.7 = (bf16[11,16,320]{2,1,0:T(8,128)(2,1)}, bf16[11,16,320]{2,1,0:T(8,128)(2,1)S(1)}, u32[]{:S(2)}, u32[]{:S(2)}) collective-permute-start(bf16[11,16,320]{2,1,0:T(8,128)(2,1)} %get-tuple-element.36), channel_id=1, source_target_pairs={{16,32},{17,33},{18,34},{19,35},{20,36},{21,37},{22,38},{23,39},{2... | collective-permute-start | bytes 337928 | tf_op jit(solution)/shard_map/ppermute | solution.py:33
  30.4 13.9 %collective-permute-start.8 = (bf16[11,16,320]{2,1,0:T(8,128)(2,1)}, bf16[11,16,320]{2,1,0:T(8,128)(2,1)S(1)}, u32[]{:S(2)}, u32[]{:S(2)}) collective-permute-start(bf16[11,16,320]{2,1,0:T(8,128)(2,1)} %get-tuple-element.36), channel_id=1, source_target_pairs={{16,48},{17,49},{18,50},{19,51},{20,52},{21,53},{22,54},{23,55},{2... | collective-permute-start | bytes 337928 | tf_op jit(solution)/shard_map/ppermute | solution.py:33
  31.7 5.7 %copy-start.2 = (bf16[8,8,16,320]{3,2,1,0:T(8,128)(2,1)}, bf16[8,8,16,320]{3,2,1,0:T(8,128)(2,1)S(1)}, u32[]{:S(2)}) copy-start(bf16[8,8,16,320]{3,2,1,0:T(8,128)(2,1)S(1)} %collective-permute-done.9.other) | copy-start | bytes 1966084
  31.8 12.6 %collective-permute-start.6 = (bf16[17,16,320]{2,1,0:T(8,128)(2,1)}, bf16[17,16,320]{2,1,0:T(8,128)(2,1)S(1)}, u32[]{:S(2)}, u32[]{:S(2)}) collective-permute-start(bf16[17,16,320]{2,1,0:T(8,128)(2,1)} %get-tuple-element.35.halo), channel_id=1, source_target_pairs={{0,16},{1,17},{2,18},{3,19},{4,20},{5,21},{6,22},{7,23},{8,24},{9,... | collective-permute-start | bytes 522248 | tf_op jit(solution)/shard_map/ppermute | solution.py:33
  41.0 13.1 %copy-start.23 = (bf16[27,80,320]{2,1,0:T(8,128)(2,1)}, bf16[27,80,320]{2,1,0:T(8,128)(2,1)S(1)}, u32[]{:S(2)}) copy-start(bf16[27,80,320]{2,1,0:T(8,128)(2,1)S(1)} %collective-permute-done.10.far_hbm) | copy-start | bytes 4147204
  41.0 87.4 %collective-permute-start.11 = (bf16[27,80,320]{2,1,0:T(8,128)(2,1)S(1)}, bf16[27,80,320]{2,1,0:T(8,128)(2,1)S(1)}, u32[]{:S(2)}, u32[]{:S(2)}) collective-permute-start(bf16[27,80,320]{2,1,0:T(8,128)(2,1)S(1)} %collective-permute-done.10.far_hbm), channel_id=1, source_target_pairs={{0,16},{1,17},{2,18},{3,19},{4,20},{5,21},{6,22},{7,23},{8,24},{9,... | collective-permute-start | bytes 4147208 | tf_op jit(solution)/shard_map/ppermute | solution.py:33
  44.3 1.0 copy-start.25
  54.1 16.2 %copy-start.28 = (bf16[5,40,960]{2,1,0:T(8,128)(2,1)S(1)}, bf16[5,40,960]{2,1,0:T(8,128)(2,1)}, u32[]{:S(2)}) copy-start(bf16[5,40,960]{2,1,0:T(8,128)(2,1)} %get-tuple-element.39) | copy-start | bytes 1152004
  54.1 17.8 %copy-start.27 = (bf16[5,40,960]{2,1,0:T(8,128)(2,1)S(1)}, bf16[5,40,960]{2,1,0:T(8,128)(2,1)}, u32[]{:S(2)}) copy-start(bf16[5,40,960]{2,1,0:T(8,128)(2,1)} %get-tuple-element.40) | copy-start | bytes 1152004
  54.1 19.1 %copy-start.26 = (bf16[5,40,960]{2,1,0:T(8,128)(2,1)S(1)}, bf16[5,40,960]{2,1,0:T(8,128)(2,1)}, u32[]{:S(2)}) copy-start(bf16[5,40,960]{2,1,0:T(8,128)(2,1)} %get-tuple-element.41) | copy-start | bytes 1152004
  61.1 12.1 %collective-permute-start.18 = (bf16[4,40,960]{2,1,0:T(8,128)(2,1)}, bf16[4,40,960]{2,1,0:T(8,128)(2,1)S(1)}, u32[]{:S(2)}, u32[]{:S(2)}) collective-permute-start(bf16[4,40,960]{2,1,0:T(8,128)(2,1)} %get-tuple-element.47), channel_id=1, source_target_pairs={{0,2},{1,3},{2,0},{3,1},{4,6},{5,7},{6,4},{7,5},{8,10},{9,11},{10,... | collective-permute-start | bytes 921608 | tf_op jit(solution)/shard_map/ppermute | solution.py:33
  62.4 23.3 %collective-permute-start.19 = (bf16[4,40,960]{2,1,0:T(8,128)(2,1)}, bf16[4,40,960]{2,1,0:T(8,128)(2,1)S(1)}, u32[]{:S(2)}, u32[]{:S(2)}) collective-permute-start(bf16[4,40,960]{2,1,0:T(8,128)(2,1)} %get-tuple-element.48), channel_id=1, source_target_pairs={{0,4},{1,5},{2,6},{3,7},{4,0},{5,1},{6,2},{7,3},{8,12},{9,13},{10,... | collective-permute-start | bytes 921608 | tf_op jit(solution)/shard_map/ppermute | solution.py:33
  70.3 30.9 %collective-permute-start.12 = (bf16[5,40,960]{2,1,0:T(8,128)(2,1)S(1)}, bf16[5,40,960]{2,1,0:T(8,128)(2,1)S(1)}, u32[]{:S(2)}, u32[]{:S(2)}) collective-permute-start(bf16[5,40,960]{2,1,0:T(8,128)(2,1)S(1)} %copy-done.28), channel_id=1, source_target_pairs={{0,32},{1,33},{2,34},{3,35},{4,36},{5,37},{6,38},{7,39},{8,40},{9,... | collective-permute-start | bytes 1152008 | tf_op jit(solution)/shard_map/ppermute | solution.py:33
  71.9 29.7 %collective-permute-start.13 = (bf16[5,40,960]{2,1,0:T(8,128)(2,1)S(1)}, bf16[5,40,960]{2,1,0:T(8,128)(2,1)S(1)}, u32[]{:S(2)}, u32[]{:S(2)}) collective-permute-start(bf16[5,40,960]{2,1,0:T(8,128)(2,1)S(1)} %copy-done.27), channel_id=1, source_target_pairs={{0,64},{1,65},{2,66},{3,67},{4,68},{5,69},{6,70},{7,71},{8,72},{9,... | collective-permute-start | bytes 1152008 | tf_op jit(solution)/shard_map/ppermute | solution.py:33
  73.2 23.4 %copy-start.6 = (bf16[4,40,960]{2,1,0:T(8,128)(2,1)}, bf16[4,40,960]{2,1,0:T(8,128)(2,1)S(1)}, u32[]{:S(2)}) copy-start(bf16[4,40,960]{2,1,0:T(8,128)(2,1)S(1)} %collective-permute-done.18.r1) | copy-start | bytes 921604
  73.2 28.4 %collective-permute-start.14 = (bf16[5,40,960]{2,1,0:T(8,128)(2,1)S(1)}, bf16[5,40,960]{2,1,0:T(8,128)(2,1)S(1)}, u32[]{:S(2)}, u32[]{:S(2)}) collective-permute-start(bf16[5,40,960]{2,1,0:T(8,128)(2,1)S(1)} %copy-done.26), channel_id=1, source_target_pairs={{0,96},{1,97},{2,98},{3,99},{4,100},{5,101},{6,102},{7,103},{8,104... | collective-permute-start | bytes 1152008 | tf_op jit(solution)/shard_map/ppermute | solution.py:33
  85.7 10.9 %copy-start.7 = (bf16[4,40,960]{2,1,0:T(8,128)(2,1)}, bf16[4,40,960]{2,1,0:T(8,128)(2,1)S(1)}, u32[]{:S(2)}) copy-start(bf16[4,40,960]{2,1,0:T(8,128)(2,1)S(1)} %collective-permute-done.19.r2) | copy-start | bytes 921604
  85.7 10.9 %collective-permute-start.20 = (bf16[4,40,960]{2,1,0:T(8,128)(2,1)}, bf16[4,40,960]{2,1,0:T(8,128)(2,1)S(1)}, u32[]{:S(2)}, u32[]{:S(2)}) collective-permute-start(bf16[4,40,960]{2,1,0:T(8,128)(2,1)} %get-tuple-element.49), channel_id=1, source_target_pairs={{0,6},{1,7},{2,4},{3,5},{4,2},{5,3},{6,0},{7,1},{8,14},{9,15},{10,... | collective-permute-start | bytes 921608 | tf_op jit(solution)/shard_map/ppermute | solution.py:33
  99.6 10.1 %copy-start.32 = (bf16[40,960]{1,0:T(8,128)(2,1)S(1)}, bf16[40,960]{1,0:T(8,128)(2,1)}, u32[]{:S(2)}) copy-start(bf16[40,960]{1,0:T(8,128)(2,1)} %get-tuple-element.53) | copy-start | bytes 230404
  99.6 7.1 %collective-permute-start.21 = (bf16[40,960]{1,0:T(8,128)(2,1)}, bf16[40,960]{1,0:T(8,128)(2,1)S(1)}, u32[]{:S(2)}, u32[]{:S(2)}) collective-permute-start(bf16[40,960]{1,0:T(8,128)(2,1)} %get-tuple-element.51), channel_id=1, source_target_pairs={{0,32},{1,33},{2,34},{3,35},{4,36},{5,37},{6,38},{7,39},{8,40},{9,... | collective-permute-start | bytes 230408 | tf_op jit(solution)/shard_map/ppermute | solution.py:33
  101.2 8.4 %collective-permute-start.22 = (bf16[40,960]{1,0:T(8,128)(2,1)}, bf16[40,960]{1,0:T(8,128)(2,1)S(1)}, u32[]{:S(2)}, u32[]{:S(2)}) collective-permute-start(bf16[40,960]{1,0:T(8,128)(2,1)} %get-tuple-element.52), channel_id=1, source_target_pairs={{0,64},{1,65},{2,66},{3,67},{4,68},{5,69},{6,70},{7,71},{8,72},{9,... | collective-permute-start | bytes 230408 | tf_op jit(solution)/shard_map/ppermute | solution.py:33
  101.6 0.8 copy-start.4
  101.6 0.9 copy-start.5
  104.9 10.4 %collective-permute-start.15 = (bf16[50,960]{1,0:T(8,128)(2,1)}, bf16[50,960]{1,0:T(8,128)(2,1)S(1)}, u32[]{:S(2)}, u32[]{:S(2)}) collective-permute-start(bf16[50,960]{1,0:T(8,128)(2,1)} %get-tuple-element.43), channel_id=1, source_target_pairs={{0,2},{1,3},{2,0},{3,1},{4,6},{5,7},{6,4},{7,5},{8,10},{9,11},{10,... | collective-permute-start | bytes 288008 | tf_op jit(solution)/shard_map/ppermute | solution.py:33
  104.9 10.4 %collective-permute-start.16 = (bf16[50,960]{1,0:T(8,128)(2,1)}, bf16[50,960]{1,0:T(8,128)(2,1)S(1)}, u32[]{:S(2)}, u32[]{:S(2)}) collective-permute-start(bf16[50,960]{1,0:T(8,128)(2,1)} %get-tuple-element.44), channel_id=1, source_target_pairs={{0,4},{1,5},{2,6},{3,7},{4,0},{5,1},{6,2},{7,3},{8,12},{9,13},{10,... | collective-permute-start | bytes 288008 | tf_op jit(solution)/shard_map/ppermute | solution.py:33
  106.7 8.7 %copy-start.13 = (bf16[40,960]{1,0:T(8,128)(2,1)}, bf16[40,960]{1,0:T(8,128)(2,1)S(1)}, u32[]{:S(2)}) copy-start(bf16[40,960]{1,0:T(8,128)(2,1)S(1)} %collective-permute-done.21.b1) | copy-start | bytes 230404
  106.7 8.7 %collective-permute-start.17 = (bf16[50,960]{1,0:T(8,128)(2,1)}, bf16[50,960]{1,0:T(8,128)(2,1)S(1)}, u32[]{:S(2)}, u32[]{:S(2)}) collective-permute-start(bf16[50,960]{1,0:T(8,128)(2,1)} %get-tuple-element.45), channel_id=1, source_target_pairs={{0,6},{1,7},{2,4},{3,5},{4,2},{5,3},{6,0},{7,1},{8,14},{9,15},{10,... | collective-permute-start | bytes 288008 | tf_op jit(solution)/shard_map/ppermute | solution.py:33
  109.6 5.8 %copy-start.14 = (bf16[40,960]{1,0:T(8,128)(2,1)}, bf16[40,960]{1,0:T(8,128)(2,1)S(1)}, u32[]{:S(2)}) copy-start(bf16[40,960]{1,0:T(8,128)(2,1)S(1)} %collective-permute-done.22.b2) | copy-start | bytes 230404
  109.6 5.7 %collective-permute-start.23 = (bf16[40,960]{1,0:T(8,128)(2,1)S(1)}, bf16[40,960]{1,0:T(8,128)(2,1)S(1)}, u32[]{:S(2)}, u32[]{:S(2)}) collective-permute-start(bf16[40,960]{1,0:T(8,128)(2,1)S(1)} %copy-done.32), channel_id=1, source_target_pairs={{0,96},{1,97},{2,98},{3,99},{4,100},{5,101},{6,102},{7,103},{8,104... | collective-permute-start | bytes 230408 | tf_op jit(solution)/shard_map/ppermute | solution.py:33
  118.3 4.7 %collective-permute-start.24 = (bf16[45,480]{1,0:T(8,128)(2,1)}, bf16[45,480]{1,0:T(8,128)(2,1)S(1)}, u32[]{:S(2)}, u32[]{:S(2)}) collective-permute-start(bf16[45,480]{1,0:T(8,128)(2,1)} %get-tuple-element.55), channel_id=1, source_target_pairs={{0,1},{1,0},{2,3},{3,2},{4,5},{5,4},{6,7},{7,6},{8,9},{9,8},{10,11... | collective-permute-start | bytes 129608 | tf_op jit(solution)/shard_map/ppermute | solution.py:33
  119.7 5.9 %collective-permute-start.25 = (bf16[45,480]{1,0:T(8,128)(2,1)}, bf16[45,480]{1,0:T(8,128)(2,1)S(1)}, u32[]{:S(2)}, u32[]{:S(2)}) collective-permute-start(bf16[45,480]{1,0:T(8,128)(2,1)} %get-tuple-element.56), channel_id=1, source_target_pairs={{0,8},{1,9},{2,10},{3,11},{4,12},{5,13},{6,14},{7,15},{8,0},{9,1},... | collective-permute-start | bytes 129608 | tf_op jit(solution)/shard_map/ppermute | solution.py:33
  120.0 6.0 %collective-permute-start.26 = (bf16[45,480]{1,0:T(8,128)(2,1)}, bf16[45,480]{1,0:T(8,128)(2,1)S(1)}, u32[]{:S(2)}, u32[]{:S(2)}) collective-permute-start(bf16[45,480]{1,0:T(8,128)(2,1)} %get-tuple-element.57), channel_id=1, source_target_pairs={{0,9},{1,8},{2,11},{3,10},{4,13},{5,12},{6,15},{7,14},{8,1},{9,0},... | collective-permute-start | bytes 129608 | tf_op jit(solution)/shard_map/ppermute | solution.py:33
  123.0 3.0 %copy-start.18 = (bf16[45,480]{1,0:T(8,128)(2,1)}, bf16[45,480]{1,0:T(8,128)(2,1)S(1)}, u32[]{:S(2)}) copy-start(bf16[45,480]{1,0:T(8,128)(2,1)S(1)} %collective-permute-done.24.r1) | copy-start | bytes 129604
  128.4 1.2 copy-start.24
  (12 other events, 8.1 us)

commit v2 on v1

v2 whole, which is shorter than its diff:
```python
import functools
import math

import jax
import jax.numpy as jnp
import numpy as np
from jax import lax
from jax.experimental import pallas as pl
from jax.experimental.pallas import tpu as pltpu
from jax.sharding import PartitionSpec as P

AXES = ("lx", "ly", "af")
BF, F32 = jnp.bfloat16, jnp.float32
C = 320

STREAM_A = (0, 1, 2, 3, 4)
STREAM_B = (5, 6, 7, 8)


def routes(to):
    pairs = []
    for a in range(8):
        for b in range(8):
            for c in range(2):
                u, v, w = to(a, b, c)
                pairs.append(((a * 8 + b) * 2 + c, (u * 8 + v) * 2 + w))
    return pairs


def send(value, to):
    return lax.ppermute(value, AXES, routes(to))


def swap_core(v):
    return send(v, lambda a, b, c: (a ^ 1, b, c))


def row_order():
    out = np.zeros((2, 4, 4, 2, 5, 2), np.int32)
    steps = (0, 1, 3, 2)
    for m, first in enumerate(steps):
        for n, second in enumerate(steps):
            for d in range(2):
                for j in range(5):
                    out[0, m, n, d, j] = (first * 16 + d * 4 + second, j)
                    out[1, m, n, d, j] = (second * 16 + d * 4 + first, j)
    return out.reshape(320, 2)


def params(mib=8):
    return pltpu.CompilerParams(vmem_limit_bytes=mib * 2**20)


BRIEF = pl.CostEstimate(flops=1, bytes_accessed=1, transcendentals=0)


def sds(shape, dtype):
    return jax.ShapeDtypeStruct(shape, dtype)


def edges_kernel(g, other, alpha, beta, line, half, corner, outer, plane):
    core = lax.axis_index("lx") % 2
    at = 7 - lax.axis_index("af") * 7
    column = jnp.where(lax.axis_index("ly") % 2 == core, 15, 0)

    def picker(rows, tiles):
        row = lax.broadcasted_iota(jnp.int32, (rows, 16 * tiles), 0)
        cell = lax.broadcasted_iota(jnp.int32, (rows, 16 * tiles), 1)
        return jnp.where(cell == row * 16 + column, 1.0, 0.0).astype(BF)

    pick = picker(8, 8)

    def ends(tile, to):
        got = jnp.dot(pick, tile.reshape(128, C), preferred_element_type=F32)
        line[pl.ds(to, 1)] = got.astype(BF)[None]

    for src, to in ((g, core * 8 + 1), (other, 9 - core * 8)):
        for n in range(8):
            ends(src[:, n], to + n)
        plane[pl.ds(to, 8)] = src[pl.ds(at, 1)].reshape(8, 16, C)
    z = lax.axis_index("lx") // 2
    for n, src in enumerate((alpha, beta)):
        to = 17 * (core ^ n)
        inside = jnp.where(to == 0, z > 0, z < 3)
        outer[n] = jnp.where(inside, src[...].astype(F32), 0.0).astype(BF)
        ends(outer[n], to)
        plane[pl.ds(to, 1)] = outer[n, pl.ds(at, 1)]
    half[...] = plane[pl.ds(9 * core, 9)]
    got = jnp.dot(picker(24, 18), plane[...].reshape(288, C), preferred_element_type=F32)
    corner[...] = got[:18].astype(BF)


def edges(g, other, alpha, beta):
    return pl.pallas_call(
        edges_kernel,
        out_shape=(
            sds((18, 8, C), BF),
            sds((9, 16, C), BF),
            sds((18, C), BF),
            sds((2, 8, 16, C), BF),
        ),
        scratch_shapes=[pltpu.VMEM((18, 16, C), BF)],
        compiler_params=params(10),
        cost_estimate=BRIEF,
        name="edges",
    )(g, other, alpha, beta)


def turn_kernel(order, own, other, out_a, out_b, both):
    core = lax.axis_index("lx") % 2
    mine = lax.axis_index("lx") * 8 + lax.axis_index("ly")
    both[:, pl.ds(core * 8, 8)] = own[...]
    both[:, pl.ds(8 - core * 8, 8)] = other[...]
    target = (order[:, 0:1] ^ mine) * 5 + order[:, 1:2]
    lane = lax.broadcasted_iota(jnp.int32, (320, C), 1)
    pick = jnp.where(lane == target, 1.0, 0.0).astype(BF)
    cells = both[...].reshape(2048, C)
    out = lax.dot_general(
        pick, cells, (((1,), (1,)), ((), ())), preferred_element_type=F32
    ).astype(BF)
    out_a[...] = out[:160]
    out_b[...] = out[160:]


def turn(order, own, other):
    return pl.pallas_call(
        turn_kernel,
        out_shape=(sds((160, 2048), BF), sds((160, 2048), BF)),
        scratch_shapes=[pltpu.VMEM((8, 16, 16, C), BF)],
        compiler_params=params(12),
        cost_estimate=BRIEF,
        name="turn",
    )(order, own, other)


def spread(tile, left, right):
    n = tile.shape[0]
    flat = tile.astype(F32).reshape(n * 16, C)
    col = lax.broadcasted_iota(jnp.int32, (n, 16, C), 1).reshape(n * 16, C)
    ends = jnp.broadcast_to(right.reshape(n, 1, C), (n, 16, C)).reshape(n * 16, C)
    heads = jnp.broadcast_to(left.reshape(n, 1, C), (n, 16, C)).reshape(n * 16, C)
    up = jnp.where(col == 15, ends, pltpu.roll(flat, n * 16 - 1, 0))
    down = jnp.where(col == 0, heads, pltpu.roll(flat, 1, 0))
    return jnp.concatenate([up, flat, down], axis=1).astype(BF).reshape(n, 16, 3 * C)


def weight_tiles(groups, turned, shifted, keep, sends):
    for n, pq in enumerate(groups):
        p, q = pq // 3, pq % 3
        cells = shifted[2 - p : 10 - p, 2 - q : 18 - q].reshape(2048, 3 * C)
        tile = jnp.dot(turned[...], cells, preferred_element_type=F32)
        keep[n] = tile[0:40]
        for b, ref in enumerate(sends):
            ref[n] = tile[40 * b + 40 : 40 * b + 80].astype(BF)


def first_kernel(
    g, other, outer, line, line_other, half, half_other, corner, corner_other, turned,
    kept_shifted, keep, s1, s2, s3, shifted, plane, sem,
):
    core = lax.axis_index("lx") % 2
    af = lax.axis_index("af")

    ly = lax.axis_index("ly")
    side = ly % 2

    def order(mine, theirs):
        mine, theirs = mine.astype(F32), theirs.astype(F32)
        left = jnp.where(side == core, theirs, mine)
        right = jnp.where(side == core, mine, theirs)
        return jnp.where(ly > 0, left, 0.0), jnp.where(ly < 7, right, 0.0)

    def put(tile, at):
        lines = order(line[pl.ds(at, 1)][0], line_other[pl.ds(at, 1)][0])
        shifted[1:9, pl.ds(at, 1)] = spread(tile, *lines)[:, None]

    for src, at in ((g, core * 8 + 1), (other, 9 - core * 8)):

        def row(n, carry, src=src, at=at):
            put(src[:, pl.ds(n, 1)].reshape(8, 16, C), at + n)
            return carry

        lax.fori_loop(0, 8, row, 0)
    put(outer[0], core * 17)
    put(outer[1], 17 - core * 17)
    plane[pl.ds(9 * core, 9)] = half[...]
    plane[pl.ds(9 - 9 * core, 9)] = half_other[...]
    lines = order(corner[...], corner_other[...])
    shifted[pl.ds(9 - af * 9, 1)] = spread(plane[...], *lines)[None]
    shifted[pl.ds(af * 9, 1)] = jnp.zeros((1, 18, 16, 3 * C), BF)
    copy = pltpu.make_async_copy(shifted, kept_shifted, sem)
    copy.start()
    weight_tiles(STREAM_A, turned, shifted, keep, (s1, s2, s3))
    copy.wait()


def first_tiles(*operands):
    n = len(STREAM_A)
    piece = sds((n, 40, 3 * C), BF)
    spec = pl.BlockSpec(memory_space=pltpu.VMEM)
    return pl.pallas_call(
        first_kernel,
        out_shape=(sds((10, 18, 16, 3 * C), BF), sds((n, 40, 3 * C), F32), piece, piece, piece),
        in_specs=[spec] * 10,
        out_specs=(pl.BlockSpec(memory_space=pl.ANY),) + (spec,) * 4,
        scratch_shapes=[
            pltpu.VMEM((10, 18, 16, 3 * C), BF),
            pltpu.VMEM((18, 16, C), BF),
            pltpu.SemaphoreType.DMA,
        ],
        compiler_params=params(24),
        cost_estimate=BRIEF,
        name="first_tiles",
    )(*operands)


def second_kernel(shifted, turned, keep, s1, s2, s3):
    weight_tiles(STREAM_B, turned, shifted, keep, (s1, s2, s3))


def second_tiles(shifted, turned):
    n = len(STREAM_B)
    piece = sds((n, 40, 3 * C), BF)
    return pl.pallas_call(
        second_kernel,
        out_shape=(sds((n, 40, 3 * C), F32), piece, piece, piece),
        compiler_params=params(16),
        cost_estimate=BRIEF,
        name="second_tiles",
    )(shifted, turned)


def input_kernel(start, planes, *refs):
    shifted_hbm, own_hbm, far_hbm, near_hbm = refs[:4]
    out, shifted, weight, total, done, sems = refs[-6:]
    core = lax.axis_index("lx") % 2
    af = lax.axis_index("af")
    other = 160 - af * 160
    rows = pl.ds(core * 8, 10)
    pieces = (
        (own_hbm, 160, af * 160),
        (far_hbm, 80, other + core * 80),
        (near_hbm, 80, other + 80 - core * 80),
    )
    copies = []
    for n, p in enumerate((2, 1, 0)):
        low, high = (0, planes) if n == 0 else (planes + n - 1, planes + n)
        some = [
            pltpu.make_async_copy(
                shifted_hbm.at[start + low : start + high, rows], shifted.at[low:high], sems.at[4 * n]
            )
        ]
        for m, (src, size, to) in enumerate(pieces):
            some.append(
                pltpu.make_async_copy(
                    src.at[9 * p : 9 * p + 9],
                    weight.at[9 * p : 9 * p + 9, pl.ds(pl.multiple_of(to, 16), size)],
                    sems.at[4 * n + 1 + m],
                )
            )
        for copy in some:
            copy.start()
        copies.append(some)
    for n, p in enumerate((2, 1, 0)):
        for copy in copies[n]:
            copy.wait()

        def block(m, carry, n=n, p=p):
            value = jnp.zeros((256, C), F32)
            for q in range(3):
                cells = shifted[pl.ds(2 * m + 2 - p, 2), 2 - q : 10 - q].reshape(256, 3 * C)
                taps = weight[9 * p + 3 * q : 9 * p + 3 * q + 3].reshape(3 * C, C)
                value = value + jnp.dot(cells, taps, preferred_element_type=F32)
            if n > 0:
                value = value + total[m]
            if n < 2:
                total[m] = value
            else:
                done[pl.ds(2 * m, 2)] = value.astype(BF).reshape(2, 8, 16, C)
            return carry

        lax.fori_loop(0, planes // 2, block, 0)
    copy = pltpu.make_async_copy(done, out.at[start : start + planes], sems.at[12])
    copy.start()
    copy.wait()


def input_gradient(start, planes, operands, so_far=None):
    operands = list(operands) + ([] if so_far is None else [so_far])
    spec = pl.BlockSpec(memory_space=pl.ANY)
    return pl.pallas_call(
        functools.partial(input_kernel, start, planes),
        out_shape=sds((8, 8, 16, C), BF),
        in_specs=[spec] * len(operands),
        out_specs=spec,
        input_output_aliases={} if so_far is None else {4: 0},
        scratch_shapes=[
            pltpu.VMEM((planes + 2, 10, 16, 3 * C), BF),
            pltpu.VMEM((27, C, C), BF),
            pltpu.VMEM((planes // 2, 256, C), F32),
            pltpu.VMEM((planes, 8, 16, C), BF),
            pltpu.SemaphoreType.DMA((13,)),
        ],
        compiler_params=params(18),
        cost_estimate=BRIEF,
        name="input_gradient",
    )(*operands)


def quarters(blocks):
    return [jnp.concatenate([v[10 * b : 10 * b + 10] for v in blocks], axis=0) for b in range(4)]


def fold_kernel(n, keep, r1, r2, r3, out, s1, s2, s3):
    blocks = [keep[g] + r1[g].astype(F32) + r2[g].astype(F32) + r3[g].astype(F32) for g in range(n)]
    parts = quarters(blocks)
    out[...] = parts[0]
    for b, ref in enumerate((s1, s2, s3)):
        ref[...] = parts[b + 1].astype(BF)


def fold(keep, ins):
    n = keep.shape[0]
    piece = sds((n * 10, 3 * C), BF)
    return pl.pallas_call(
        functools.partial(fold_kernel, n),
        out_shape=(sds((n * 10, 3 * C), F32), piece, piece, piece),
        compiler_params=params(),
        cost_estimate=BRIEF,
        name="fold",
    )(keep, *ins)


def cut_kernel(a0, a1, a2, a3, b0, b1, b2, b3, out, s1, s2, s3):
    af = lax.axis_index("af")
    same, flip = [[], []], [[], []]
    for refs, n in (((a0, a1, a2, a3), len(STREAM_A)), ((b0, b1, b2, b3), len(STREAM_B))):
        total = refs[0][...]
        for ref in refs[1:]:
            total = total + ref[...].astype(F32)
        low = jnp.concatenate([total[:, C * r : C * r + 160] for r in range(3)], axis=1)
        high = jnp.concatenate([total[:, C * r + 160 : C * r + 320] for r in range(3)], axis=1)
        mine = jnp.where(af == 0, low, high)
        theirs = jnp.where(af == 0, high, low)
        for g in range(n):
            for d in range(2):
                same[d].append(mine[10 * g + 5 * d : 10 * g + 5 * d + 5])
                flip[d].append(theirs[10 * g + 5 * d : 10 * g + 5 * d + 5])
    out[...] = jnp.concatenate(same[0], axis=0)
    s1[...] = jnp.concatenate(flip[0], axis=0).astype(BF)
    s2[...] = jnp.concatenate(same[1], axis=0).astype(BF)
    s3[...] = jnp.concatenate(flip[1], axis=0).astype(BF)


def cut(*operands):
    piece = sds((45, 480), BF)
    return pl.pallas_call(
        cut_kernel,
        out_shape=(sds((45, 480), F32), piece, piece, piece),
        compiler_params=params(),
        cost_estimate=BRIEF,
        name="cut",
    )(*operands)


def last_kernel(scale, keep, r1, r2, r3, out):
    total = (keep[...] + r1[...].astype(F32) + r2[...].astype(F32) + r3[...].astype(F32)) * scale
    for n, pq in enumerate(STREAM_A + STREAM_B):
        for r in range(3):
            out[:, 3 * pq + r, :] = total[5 * n : 5 * n + 5, 160 * r : 160 * r + 160]


def last(scale, *operands):
    return pl.pallas_call(
        functools.partial(last_kernel, scale),
        out_shape=sds((5, 27, 160), F32),
        compiler_params=params(),
        cost_estimate=BRIEF,
        name="last",
    )(*operands)


def body(grad_out, inputs, weight):
    core = lax.axis_index("lx") % 2
    scale = 1.0 / math.sqrt(16 * 64 * 128)

    grad_other = swap_core(grad_out)
    inputs_other = swap_core(inputs)
    outer = lax.dynamic_slice_in_dim(grad_out, core * 7, 1, 1).reshape(8, 16, C)
    weight_late, outer = lax.optimization_barrier((weight, outer))
    quarter = lax.dynamic_slice_in_dim(weight_late, core * 80, 80, 1)
    alpha = send(outer, lambda a, b, c: ((a + 2 * (a % 2) - 1) % 8, b, c))
    alpha, grad_other, inputs_other, _ = lax.optimization_barrier(
        (alpha, grad_other, inputs_other, quarter)
    )
    beta = swap_core(alpha)

    line, plane, corner, outer = edges(grad_out, grad_other, alpha, beta)

    def side(a, b):
        return b ^ 1 if a % 2 == 0 else (b + 2 * (b % 2) - 1) % 8

    line = send(line, lambda a, b, c: (a, side(a, b), c))
    corner = send(corner, lambda a, b, c: (a, side(a, b), c ^ 1))
    plane = send(plane, lambda a, b, c: (a, b, c ^ 1))
    turned_a, turned_b = turn(jnp.asarray(row_order()), inputs, inputs_other)
    line, corner, plane, turned_a = lax.optimization_barrier((line, corner, plane, turned_a))
    line_other, corner_other, plane_other = swap_core(line), swap_core(corner), swap_core(plane)

    quarter, line = lax.optimization_barrier((quarter, line))
    far = send(quarter, lambda a, b, c: (a, b ^ (4 * (a % 2)), c ^ 1))

    shifted, a0, *a_out = first_tiles(
        grad_out, grad_other, outer,
        line, line_other, plane, plane_other, corner, corner_other, turned_a,
    )
    along_z = [lambda a, b, c, s=s: (a ^ (2 * s), b, c) for s in (1, 3, 2)]
    along_x = [lambda a, b, c, s=s: (a, b ^ s, c) for s in (1, 3, 2)]
    along_y = [
        lambda a, b, c: (a, b, c ^ 1),
        lambda a, b, c: (a, b ^ 4, c),
        lambda a, b, c: (a, b ^ 4, c ^ 1),
    ]
    a_in = [send(v, to) for v, to in zip(a_out[:2], along_z)]
    b0, *b_out = second_tiles(shifted, turned_b)
    b_in = [send(v, to) for v, to in zip(b_out[:2], along_x)]
    a_late, b_late = a_out[2], b_out[2]
    far, b0, a_in[0], a_in[1], a_late, b_late = lax.optimization_barrier(
        (far, b0, a_in[0], a_in[1], a_late, b_late)
    )
    near = swap_core(far)
    a_in.append(send(a_late, along_z[2]))
    b_in.append(send(b_late, along_x[2]))

    operands = (shifted, weight, far, near)
    grad_input = input_gradient(0, 6, operands)
    grad_input, *a_in = lax.optimization_barrier((grad_input, *a_in))
    a0, *a_out = fold(a0, a_in)
    a0, *b_in = lax.optimization_barrier((a0, *b_in))
    a_in = [send(v, to) for v, to in zip(a_out, along_x)]
    b0, *b_out = fold(b0, b_in)
    b_in = [send(v, to) for v, to in zip(b_out, along_z)]
    grad_input, b0 = lax.optimization_barrier((grad_input, b0))
    grad_input = input_gradient(6, 2, operands, grad_input)
    grad_input, *b_in = lax.optimization_barrier((grad_input, *b_in))
    keep, *outs = cut(a0, *a_in, b0, *b_in)
    ins = [send(v, to) for v, to in zip(outs, along_y)]
    grad_weight = last(scale, keep, *ins)
    return (grad_input, jnp.transpose(grad_weight, (1, 2, 0)))


def solution(mesh):
    placed = (P("af", "lx", "ly", None), P("af", "lx", "ly", None), P(None, "af", None))
    return jax.shard_map(
        body,
        mesh=mesh,
        in_specs=placed,
        out_specs=(P("af", "lx", "ly", None), P(None, "af", ("lx", "ly"))),
        check_vma=False,
    )
```

time: 146 us -> 88 us (0.60)
  Pallas kernels: 47.1 us -> 27.8 us
  starting transfers between devices: 52 us -> 36 us
  waiting for transfers between devices: 34.8 us -> 20.7 us
  local copies, waits for them, and re-layouts: 10 us -> 2.61 us
    ppermute x27, starting transfers between devices: 52 us -> 36 us  [send(): return lax.ppermute(value, AXES, routes(to))]
    ppermute x27, waiting for transfers between devices: 34.8 us -> 20.7 us  [send(): return lax.ppermute(value, AXES, routes(to))]
    pallas_call x4, Pallas kernels: 22.9 us -> 17 us  [the longest x2 15.5 us: input_gradient(): pl.pallas_call(functools.partial(input_kernel, start, planes), out_shape=...]
    unnamed x66 -> x8, local copies, waits for them, and re-layouts: 5.81 us -> 0.02 us
    pallas_call x2, Pallas kernels: 4.61 us -> 0.46 us  [fold(): pl.pallas_call(functools.partial(fold_kernel, n), out_shape=(sds((n * 10,...]
    pallas_call x1, Pallas kernels: 6.92 us -> 2.96 us  [second_tiles(): pl.pallas_call(second_kernel, out_shape=(sds((n, 40, 3 * C), F32), piece,...]
    slice x1 -> x0, local copies, waits for them, and re-layouts: 2.49 us -> none  [body(): b0, *b_out = second_tiles(shifted, turned[160:])]
    pallas_call x1, Pallas kernels: 8.76 us -> 6.35 us  [first_tiles(): pl.pallas_call(first_kernel, out_shape=(sds((10, 18, 16, 3 * C), BF), sds...]
  transfers between devices with their start and end apart: 27 -> 27, of which waited for: 9 -> 9; matrix products, arithmetic and copies ran while one was open for 2% -> 3% of each run, Pallas kernels for 22% -> 30%
where the time goes in v2:
time: 88 us; the launch traced here: 87.9 us
  starting transfers between devices  36 us (41%)
  Pallas kernels  27.8 us (32%)
  waiting for transfers between devices  20.7 us (24%)
  local copies, waits for them, and re-layouts  2.61 us (3%)
    ppermute x27, starting transfers between devices, send(): return lax.ppermute(value, AXES, routes(to))  36 us
    ppermute x27, waiting for transfers between devices, send(): return lax.ppermute(value, AXES, routes(to))  20.7 us
    pallas_call x2, Pallas kernels, input_gradient(): pl.pallas_call(functools.partial(input_kernel, start, planes), out_shape=...  15.5 us
    pallas_call x1, Pallas kernels, first_tiles(): pl.pallas_call(first_kernel, out_shape=(sds((10, 18, 16, 3 * C), BF), sds...  6.35 us
    pallas_call x1, Pallas kernels, second_tiles(): pl.pallas_call(second_kernel, out_shape=(sds((n, 40, 3 * C), F32), piece,...  2.96 us
  transfers between devices with their start and end apart: 27, of which 9 were waited for; matrix products, arithmetic and copies ran while one was open for 3% of the time, Pallas kernels for 30%

profile of v2, /device:TPU:0, one launch (start us, length us, event | category | flops | bytes accessed | tf_op | source)
XLA Modules:
  0.0 87.9 jit_solution(460628560081625051)
XLA Ops:
  0.6 0.1 collective-permute-start.2
  0.7 0.5 collective-permute-start.1
  1.2 0.9 %dynamic-slice_bitcast_fusion = bf16[8,16,320]{2,1,0:T(8,128)(2,1)S(1)} fusion(bf16[8,8,16,320]{3,2,1,0:T(8,128)(2,1)} %g.3, s32[]{:T(128)S(6)} %select_n.14), kind=kLoop, calls=%fused_computation | loop fusion | bytes 163844 | tf_op jit(solution)/shard_map/reshape | solution.py:389
  2.1 3.9 %collective-permute-start = (bf16[8,16,320]{2,1,0:T(8,128)(2,1)S(1)}, bf16[8,16,320]{2,1,0:T(8,128)(2,1)S(1)}, u32[]{:S(2)}, u32[]{:S(2)}) collective-permute-start(bf16[8,16,320]{2,1,0:T(8,128)(2,1)S(1)} %dynamic-slice_bitcast_fusion), channel_id=1, source_target_pairs={{0,112},{1,113},{2,114},{3,115},{4,116},{5,117},{6,118},{7,119},{8... | collective-permute-start | bytes 245768 | tf_op jit(solution)/shard_map/ppermute | solution.py:31
  6.0 1.7 %constant_dynamic-slice_fusion = bf16[27,80,320]{2,1,0:T(8,128)(2,1)S(1)} fusion(bf16[27,160,320]{2,1,0:T(8,128)(2,1)} %refs_1_.3, s32[]{:T(128)S(6)} %select_n.15), kind=kLoop, calls=%fused_computation.1 | loop fusion | bytes 2764804 | tf_op jit(solution)/shard_map/dynamic_slice | solution.py:391
  7.7 0.0 copy-start.2
  7.7 0.0 copy-start.3
  7.7 0.6 collective-permute-done.alpha
  8.3 1.3 %collective-permute-done.3.beta = bf16[8,16,320]{2,1,0:T(8,128)(2,1)S(1)} collective-permute-done((bf16[8,16,320]{2,1,0:T(8,128)(2,1)S(1)}, bf16[8,16,320]{2,1,0:T(8,128)(2,1)S(1)}, u32[]{:S(2)}, u32[]{:S(2)}) %collective-permute-start.3) | collective-permute-done | bytes 81952 | tf_op jit(solution)/shard_map/ppermute | solution.py:31
  9.6 0.5 edges.1
  10.1 1.6 %collective-permute-start.4 = (bf16[18,8,320]{2,1,0:T(8,128)(2,1)S(1)}, bf16[18,8,320]{2,1,0:T(8,128)(2,1)S(1)}, u32[]{:S(2)}, u32[]{:S(2)}) collective-permute-start(bf16[18,8,320]{2,1,0:T(8,128)(2,1)S(1)} %get-tuple-element.65), channel_id=1, source_target_pairs={{0,2},{1,3},{2,0},{3,1},{4,6},{5,7},{6,4},{7,5},{8,10},{9,11},{10,... | collective-permute-start | bytes 276488 | tf_op jit(solution)/shard_map/ppermute | solution.py:31
  11.7 1.6 %collective-permute-start.6 = (bf16[9,16,320]{2,1,0:T(8,128)(2,1)S(1)}, bf16[9,16,320]{2,1,0:T(8,128)(2,1)S(1)}, u32[]{:S(2)}, u32[]{:S(2)}) collective-permute-start(bf16[9,16,320]{2,1,0:T(8,128)(2,1)S(1)} %get-tuple-element.67), channel_id=1, source_target_pairs={{0,1},{1,0},{2,3},{3,2},{4,5},{5,4},{6,7},{7,6},{8,9},{9,8},{10,11... | collective-permute-start | bytes 276488 | tf_op jit(solution)/shard_map/ppermute | solution.py:31
  13.3 0.4 collective-permute-start.5
  13.7 1.1 %turn.1 = (bf16[160,2048]{1,0:T(8,128)(2,1)S(1)}, bf16[160,2048]{1,0:T(8,128)(2,1)S(1)}) custom-call(s32[320,2]{1,0:T(8,128)S(1)} %copy-done.3, bf16[8,8,16,320]{3,2,1,0:T(8,128)(2,1)S(1)} %copy-done.2, bf16[8,8,16,320]{3,2,1,0:T(8,128)(2,1)S(1)} %collective-permute-done.2.other), custom_call_target="tpu_custom_call" | custom-call | flops 1 | bytes 1 | tf_op jit(solution)/shard_map/turn/pallas_call | solution.py:126
  14.8 3.4 %collective-permute-done.5.corner = bf16[18,320]{1,0:T(8,128)(2,1)S(1)} collective-permute-done((bf16[18,320]{1,0:T(8,128)(2,1)S(1)}, bf16[18,320]{1,0:T(8,128)(2,1)S(1)}, u32[]{:S(2)}, u32[]{:S(2)}) %collective-permute-start.5) | collective-permute-done | bytes 11552 | tf_op jit(solution)/shard_map/ppermute | solution.py:31
  18.1 0.4 collective-permute-start.10
  18.5 3.7 %collective-permute-start.7 = (bf16[18,8,320]{2,1,0:T(8,128)(2,1)S(1)}, bf16[18,8,320]{2,1,0:T(8,128)(2,1)S(1)}, u32[]{:S(2)}, u32[]{:S(2)}) collective-permute-start(bf16[18,8,320]{2,1,0:T(8,128)(2,1)S(1)} %collective-permute-done.4.line), channel_id=1, source_target_pairs={{0,16},{1,17},{2,18},{3,19},{4,20},{5,21},{6,22},{7,23},{8,24},{9,... | collective-permute-start | bytes 276488 | tf_op jit(solution)/shard_map/ppermute | solution.py:31
  22.2 0.5 collective-permute-start.9
  22.7 0.8 collective-permute-done.9.corner_other
  23.5 6.4 %first_tiles.1 = (bf16[10,18,16,960]{3,2,1,0:T(8,128)(2,1)S(1)}, f32[5,40,960]{2,1,0:T(8,128)S(1)}, bf16[5,40,960]{2,1,0:T(8,128)(2,1)S(1)}, bf16[5,40,960]{2,1,0:T(8,128)(2,1)S(1)}, bf16[5,40,960]{2,1,0:T(8,128)(2,1)S(1)}) custom-call(bf16[8,8,16,320]{3,2,1,0:T(8,128)(2,1)S(1)} %copy-done.1, bf16[8,8,16,320]{3,2,1,0:T(8,128)(2,1)S(1)} %collective-permute-done.1.other, ...), custom_call_target="tpu_custom_call" | custom-call | flops 1 | bytes 1 | tf_op jit(solution)/shard_map/first_tiles/pallas_call | solution.py:201
  29.9 0.1 collective-permute-start.11
  30.0 3.2 %collective-permute-start.12 = (bf16[5,40,960]{2,1,0:T(8,128)(2,1)S(1)}, bf16[5,40,960]{2,1,0:T(8,128)(2,1)S(1)}, u32[]{:S(2)}, u32[]{:S(2)}) collective-permute-start(bf16[5,40,960]{2,1,0:T(8,128)(2,1)S(1)} %get-tuple-element.80), channel_id=1, source_target_pairs={{0,96},{1,97},{2,98},{3,99},{4,100},{5,101},{6,102},{7,103},{8,104... | collective-permute-start | bytes 1152008 | tf_op jit(solution)/shard_map/ppermute | solution.py:31
  33.3 3.0 %second_tiles.1 = (f32[4,40,960]{2,1,0:T(8,128)S(1)}, bf16[4,40,960]{2,1,0:T(8,128)(2,1)S(1)}, bf16[4,40,960]{2,1,0:T(8,128)(2,1)S(1)}, bf16[4,40,960]{2,1,0:T(8,128)(2,1)S(1)}) custom-call(bf16[10,18,16,960]{3,2,1,0:T(8,128)(2,1)S(1)} %get-tuple-element.75.shifted.refs_0_, bf16[160,2048]{1,0:T(8,128)(2,1)S(1)} %get-tuple-element.77.turned), custom_call_target="tpu_custom_call" | custom-call | flops 1 | bytes 1 | tf_op jit(solution)/shard_map/second_tiles/pallas_call | solution.py:224
  36.3 5.4 %collective-permute-done.11.r1 = bf16[5,40,960]{2,1,0:T(8,128)(2,1)S(1)} collective-permute-done((bf16[5,40,960]{2,1,0:T(8,128)(2,1)S(1)}, bf16[5,40,960]{2,1,0:T(8,128)(2,1)S(1)}, u32[]{:S(2)}, u32[]{:S(2)}) %collective-permute-start.11) | collective-permute-done | bytes 384032 | tf_op jit(solution)/shard_map/ppermute | solution.py:31
  41.7 1.5 %collective-permute-done.12.r2 = bf16[5,40,960]{2,1,0:T(8,128)(2,1)S(1)} collective-permute-done((bf16[5,40,960]{2,1,0:T(8,128)(2,1)S(1)}, bf16[5,40,960]{2,1,0:T(8,128)(2,1)S(1)}, u32[]{:S(2)}, u32[]{:S(2)}) %collective-permute-start.12) | collective-permute-done | bytes 384032 | tf_op jit(solution)/shard_map/ppermute | solution.py:31
  43.2 0.1 collective-permute-start.13
  43.4 2.7 %collective-permute-start.14 = (bf16[5,40,960]{2,1,0:T(8,128)(2,1)S(1)}, bf16[5,40,960]{2,1,0:T(8,128)(2,1)S(1)}, u32[]{:S(2)}, u32[]{:S(2)}) collective-permute-start(bf16[5,40,960]{2,1,0:T(8,128)(2,1)S(1)} %get-tuple-element.86), channel_id=1, source_target_pairs={{0,64},{1,65},{2,66},{3,67},{4,68},{5,69},{6,70},{7,71},{8,72},{9,... | collective-permute-start | bytes 1152008 | tf_op jit(solution)/shard_map/ppermute | solution.py:31
  46.1 0.0 collective-permute-start.15
  46.1 1.3 %collective-permute-start.16 = (bf16[4,40,960]{2,1,0:T(8,128)(2,1)S(1)}, bf16[4,40,960]{2,1,0:T(8,128)(2,1)S(1)}, u32[]{:S(2)}, u32[]{:S(2)}) collective-permute-start(bf16[4,40,960]{2,1,0:T(8,128)(2,1)S(1)} %get-tuple-element.95), channel_id=1, source_target_pairs={{0,6},{1,7},{2,4},{3,5},{4,2},{5,3},{6,0},{7,1},{8,14},{9,15},{10,... | collective-permute-start | bytes 921608 | tf_op jit(solution)/shard_map/ppermute | solution.py:31
  47.4 2.8 %collective-permute-start.17 = (bf16[4,40,960]{2,1,0:T(8,128)(2,1)S(1)}, bf16[4,40,960]{2,1,0:T(8,128)(2,1)S(1)}, u32[]{:S(2)}, u32[]{:S(2)}) collective-permute-start(bf16[4,40,960]{2,1,0:T(8,128)(2,1)S(1)} %get-tuple-element.96), channel_id=1, source_target_pairs={{0,4},{1,5},{2,6},{3,7},{4,0},{5,1},{6,2},{7,3},{8,12},{9,13},{10,... | collective-permute-start | bytes 921608 | tf_op jit(solution)/shard_map/ppermute | solution.py:31
  50.2 10.8 %input_gradient.2.refs_4_ = bf16[8,8,16,320]{3,2,1,0:T(8,128)(2,1)} custom-call(bf16[10,18,16,960]{3,2,1,0:T(8,128)(2,1)S(1)} %get-tuple-element.75.shifted.refs_0_, bf16[27,160,320]{2,1,0:T(8,128)(2,1)S(1)} %copy-done, bf16[27,80,320]{2,1,0:T(8,128)(2,1)S(1)} %collective-permute-done.10.refs_2_, bf16[27,80,320]{2,1,0:T(8,128)(2,1)S(1)} %collective-permute-done.13.refs_3_), custom_call_target="tpu_custom_call" | custom-call | flops 1 | bytes 1 | tf_op jit(solution)/shard_map/input_gradient/pallas_call | solution.py:291
  61.0 0.3 fold.2
  61.3 2.9 %collective-permute-done.16.r2 = bf16[4,40,960]{2,1,0:T(8,128)(2,1)S(1)} collective-permute-done((bf16[4,40,960]{2,1,0:T(8,128)(2,1)S(1)}, bf16[4,40,960]{2,1,0:T(8,128)(2,1)S(1)}, u32[]{:S(2)}, u32[]{:S(2)}) %collective-permute-start.16) | collective-permute-done | bytes 307232 | tf_op jit(solution)/shard_map/ppermute | solution.py:31
  64.2 0.2 fold.3
  64.4 1.1 %collective-permute-start.18 = (bf16[40,960]{1,0:T(8,128)(2,1)S(1)}, bf16[40,960]{1,0:T(8,128)(2,1)S(1)}, u32[]{:S(2)}, u32[]{:S(2)}) collective-permute-start(bf16[40,960]{1,0:T(8,128)(2,1)S(1)} %get-tuple-element.102), channel_id=1, source_target_pairs={{0,32},{1,33},{2,34},{3,35},{4,36},{5,37},{6,38},{7,39},{8,40},{9,... | collective-permute-start | bytes 230408 | tf_op jit(solution)/shard_map/ppermute | solution.py:31
  65.4 0.5 collective-permute-start.21
  66.0 1.3 %collective-permute-start.22 = (bf16[50,960]{1,0:T(8,128)(2,1)S(1)}, bf16[50,960]{1,0:T(8,128)(2,1)S(1)}, u32[]{:S(2)}, u32[]{:S(2)}) collective-permute-start(bf16[50,960]{1,0:T(8,128)(2,1)S(1)} %get-tuple-element.108), channel_id=1, source_target_pairs={{0,6},{1,7},{2,4},{3,5},{4,2},{5,3},{6,0},{7,1},{8,14},{9,15},{10,... | collective-permute-start | bytes 288008 | tf_op jit(solution)/shard_map/ppermute | solution.py:31
  67.3 2.2 %collective-permute-start.23 = (bf16[50,960]{1,0:T(8,128)(2,1)S(1)}, bf16[50,960]{1,0:T(8,128)(2,1)S(1)}, u32[]{:S(2)}, u32[]{:S(2)}) collective-permute-start(bf16[50,960]{1,0:T(8,128)(2,1)S(1)} %get-tuple-element.109), channel_id=1, source_target_pairs={{0,4},{1,5},{2,6},{3,7},{4,0},{5,1},{6,2},{7,3},{8,12},{9,13},{10,... | collective-permute-start | bytes 288008 | tf_op jit(solution)/shard_map/ppermute | solution.py:31
  69.5 0.3 collective-permute-start.19
  69.8 2.8 %collective-permute-start.20 = (bf16[40,960]{1,0:T(8,128)(2,1)S(1)}, bf16[40,960]{1,0:T(8,128)(2,1)S(1)}, u32[]{:S(2)}, u32[]{:S(2)}) collective-permute-start(bf16[40,960]{1,0:T(8,128)(2,1)S(1)} %get-tuple-element.104), channel_id=1, source_target_pairs={{0,64},{1,65},{2,66},{3,67},{4,68},{5,69},{6,70},{7,71},{8,72},{9,... | collective-permute-start | bytes 230408 | tf_op jit(solution)/shard_map/ppermute | solution.py:31
  72.6 4.7 %input_gradient.3 = bf16[8,8,16,320]{3,2,1,0:T(8,128)(2,1)} custom-call(bf16[10,18,16,960]{3,2,1,0:T(8,128)(2,1)S(1)} %get-tuple-element.75.shifted.refs_0_, bf16[27,160,320]{2,1,0:T(8,128)(2,1)S(1)} %copy-done, bf16[27,80,320]{2,1,0:T(8,128)(2,1)S(1)} %collective-permute-done.10.refs_2_, ...), custom_call_target="tpu_custom_call", output_to_operand_aliasing={{}: (4, {})} | custom-call | flops 1 | bytes 1 | tf_op jit(solution)/shard_map/input_gradient/pallas_call | solution.py:291
  77.4 0.2 cut.1
  77.6 0.1 collective-permute-start.24
  77.7 4.0 %collective-permute-start.25 = (bf16[45,480]{1,0:T(8,128)(2,1)S(1)}, bf16[45,480]{1,0:T(8,128)(2,1)S(1)}, u32[]{:S(2)}, u32[]{:S(2)}) collective-permute-start(bf16[45,480]{1,0:T(8,128)(2,1)S(1)} %get-tuple-element.116), channel_id=1, source_target_pairs={{0,8},{1,9},{2,10},{3,11},{4,12},{5,13},{6,14},{7,15},{8,0},{9,1},... | collective-permute-start | bytes 129608 | tf_op jit(solution)/shard_map/ppermute | solution.py:31
  81.7 0.7 collective-permute-start.26
  82.4 1.9 %collective-permute-done.25.r2 = bf16[45,480]{1,0:T(8,128)(2,1)S(1)} collective-permute-done((bf16[45,480]{1,0:T(8,128)(2,1)S(1)}, bf16[45,480]{1,0:T(8,128)(2,1)S(1)}, u32[]{:S(2)}, u32[]{:S(2)}) %collective-permute-start.25) | collective-permute-done | bytes 43232 | tf_op jit(solution)/shard_map/ppermute | solution.py:31
  84.3 2.7 %collective-permute-done.26.r3 = bf16[45,480]{1,0:T(8,128)(2,1)S(1)} collective-permute-done((bf16[45,480]{1,0:T(8,128)(2,1)S(1)}, bf16[45,480]{1,0:T(8,128)(2,1)S(1)}, u32[]{:S(2)}, u32[]{:S(2)}) %collective-permute-start.26) | collective-permute-done | bytes 43232 | tf_op jit(solution)/shard_map/ppermute | solution.py:31
  87.0 0.8 last.1
  (26 shorter events, 0.1 us)
Async XLA Ops:
  0.6 7.7 %collective-permute-start.2 = (bf16[8,8,16,320]{3,2,1,0:T(8,128)(2,1)}, bf16[8,8,16,320]{3,2,1,0:T(8,128)(2,1)S(1)}, u32[]{:S(2)}, u32[]{:S(2)}) collective-permute-start(bf16[8,8,16,320]{3,2,1,0:T(8,128)(2,1)} %own.1), channel_id=1, source_target_pairs={{0,16},{1,17},{2,18},{3,19},{4,20},{5,21},{6,22},{7,23},{8,24},{9,... | collective-permute-start | bytes 1966088 | tf_op jit(solution)/shard_map/ppermute | solution.py:31
  0.7 7.6 %collective-permute-start.1 = (bf16[8,8,16,320]{3,2,1,0:T(8,128)(2,1)}, bf16[8,8,16,320]{3,2,1,0:T(8,128)(2,1)S(1)}, u32[]{:S(2)}, u32[]{:S(2)}) collective-permute-start(bf16[8,8,16,320]{3,2,1,0:T(8,128)(2,1)} %g.3), channel_id=1, source_target_pairs={{0,16},{1,17},{2,18},{3,19},{4,20},{5,21},{6,22},{7,23},{8,24},{9,... | collective-permute-start | bytes 1966088 | tf_op jit(solution)/shard_map/ppermute | solution.py:31
  2.1 6.2 %collective-permute-start = (bf16[8,16,320]{2,1,0:T(8,128)(2,1)S(1)}, bf16[8,16,320]{2,1,0:T(8,128)(2,1)S(1)}, u32[]{:S(2)}, u32[]{:S(2)}) collective-permute-start(bf16[8,16,320]{2,1,0:T(8,128)(2,1)S(1)} %dynamic-slice_bitcast_fusion), channel_id=1, source_target_pairs={{0,112},{1,113},{2,114},{3,115},{4,116},{5,117},{6,118},{7,119},{8... | collective-permute-start | bytes 245768 | tf_op jit(solution)/shard_map/ppermute | solution.py:31
  6.0 3.6 %copy-start.1 = (bf16[8,8,16,320]{3,2,1,0:T(8,128)(2,1)S(1)}, bf16[8,8,16,320]{3,2,1,0:T(8,128)(2,1)}, u32[]{:S(2)}) copy-start(bf16[8,8,16,320]{3,2,1,0:T(8,128)(2,1)} %g.3) | copy-start | bytes 1966084
  7.7 6.0 %copy-start.2 = (bf16[8,8,16,320]{3,2,1,0:T(8,128)(2,1)S(1)}, bf16[8,8,16,320]{3,2,1,0:T(8,128)(2,1)}, u32[]{:S(2)}) copy-start(bf16[8,8,16,320]{3,2,1,0:T(8,128)(2,1)} %own.1) | copy-start | bytes 1966084
  7.7 6.0 %copy-start.3 = (s32[320,2]{1,0:T(8,128)S(1)}, s32[320,2]{1,0:T(8,128)}, u32[]{:S(2)}) copy-start(s32[320,2]{1,0:T(8,128)} %constant.30.clone.order) | copy-start | bytes 7684
  8.3 1.3 %collective-permute-start.3 = (bf16[8,16,320]{2,1,0:T(8,128)(2,1)S(1)}, bf16[8,16,320]{2,1,0:T(8,128)(2,1)S(1)}, u32[]{:S(2)}, u32[]{:S(2)}) collective-permute-start(bf16[8,16,320]{2,1,0:T(8,128)(2,1)S(1)} %collective-permute-done.alpha), channel_id=1, source_target_pairs={{0,16},{1,17},{2,18},{3,19},{4,20},{5,21},{6,22},{7,23},{8,24},{9,... | collective-permute-start | bytes 245768 | tf_op jit(solution)/shard_map/ppermute | solution.py:31
  10.1 8.0 %collective-permute-start.4 = (bf16[18,8,320]{2,1,0:T(8,128)(2,1)S(1)}, bf16[18,8,320]{2,1,0:T(8,128)(2,1)S(1)}, u32[]{:S(2)}, u32[]{:S(2)}) collective-permute-start(bf16[18,8,320]{2,1,0:T(8,128)(2,1)S(1)} %get-tuple-element.65), channel_id=1, source_target_pairs={{0,2},{1,3},{2,0},{3,1},{4,6},{5,7},{6,4},{7,5},{8,10},{9,11},{10,... | collective-permute-start | bytes 276488 | tf_op jit(solution)/shard_map/ppermute | solution.py:31
  11.7 6.4 %collective-permute-start.6 = (bf16[9,16,320]{2,1,0:T(8,128)(2,1)S(1)}, bf16[9,16,320]{2,1,0:T(8,128)(2,1)S(1)}, u32[]{:S(2)}, u32[]{:S(2)}) collective-permute-start(bf16[9,16,320]{2,1,0:T(8,128)(2,1)S(1)} %get-tuple-element.67), channel_id=1, source_target_pairs={{0,1},{1,0},{2,3},{3,2},{4,5},{5,4},{6,7},{7,6},{8,9},{9,8},{10,11... | collective-permute-start | bytes 276488 | tf_op jit(solution)/shard_map/ppermute | solution.py:31
  13.3 4.9 %collective-permute-start.5 = (bf16[18,320]{1,0:T(8,128)(2,1)S(1)}, bf16[18,320]{1,0:T(8,128)(2,1)S(1)}, u32[]{:S(2)}, u32[]{:S(2)}) collective-permute-start(bf16[18,320]{1,0:T(8,128)(2,1)S(1)} %get-tuple-element.66), channel_id=1, source_target_pairs={{0,3},{1,2},{2,1},{3,0},{4,7},{5,6},{6,5},{7,4},{8,11},{9,10},{10,... | collective-permute-start | bytes 34568 | tf_op jit(solution)/shard_map/ppermute | solution.py:31
  18.1 25.1 %collective-permute-start.10 = (bf16[27,80,320]{2,1,0:T(8,128)(2,1)S(1)}, bf16[27,80,320]{2,1,0:T(8,128)(2,1)S(1)}, u32[]{:S(2)}, u32[]{:S(2)}) collective-permute-start(bf16[27,80,320]{2,1,0:T(8,128)(2,1)S(1)} %constant_dynamic-slice_fusion), channel_id=1, source_target_pairs={{0,1},{1,0},{2,3},{3,2},{4,5},{5,4},{6,7},{7,6},{8,9},{9,8},{10,11... | collective-permute-start | bytes 4147208 | tf_op jit(solution)/shard_map/ppermute | solution.py:31
  18.5 5.0 %collective-permute-start.7 = (bf16[18,8,320]{2,1,0:T(8,128)(2,1)S(1)}, bf16[18,8,320]{2,1,0:T(8,128)(2,1)S(1)}, u32[]{:S(2)}, u32[]{:S(2)}) collective-permute-start(bf16[18,8,320]{2,1,0:T(8,128)(2,1)S(1)} %collective-permute-done.4.line), channel_id=1, source_target_pairs={{0,16},{1,17},{2,18},{3,19},{4,20},{5,21},{6,22},{7,23},{8,24},{9,... | collective-permute-start | bytes 276488 | tf_op jit(solution)/shard_map/ppermute | solution.py:31
  22.2 1.4 %collective-permute-start.8 = (bf16[9,16,320]{2,1,0:T(8,128)(2,1)S(1)}, bf16[9,16,320]{2,1,0:T(8,128)(2,1)S(1)}, u32[]{:S(2)}, u32[]{:S(2)}) collective-permute-start(bf16[9,16,320]{2,1,0:T(8,128)(2,1)S(1)} %collective-permute-done.6.half), channel_id=1, source_target_pairs={{0,16},{1,17},{2,18},{3,19},{4,20},{5,21},{6,22},{7,23},{8,24},{9,... | collective-permute-start | bytes 276488 | tf_op jit(solution)/shard_map/ppermute | solution.py:31
  22.2 1.3 %collective-permute-start.9 = (bf16[18,320]{1,0:T(8,128)(2,1)S(1)}, bf16[18,320]{1,0:T(8,128)(2,1)S(1)}, u32[]{:S(2)}, u32[]{:S(2)}) collective-permute-start(bf16[18,320]{1,0:T(8,128)(2,1)S(1)} %collective-permute-done.5.corner), channel_id=1, source_target_pairs={{0,16},{1,17},{2,18},{3,19},{4,20},{5,21},{6,22},{7,23},{8,24},{9,... | collective-permute-start | bytes 34568 | tf_op jit(solution)/shard_map/ppermute | solution.py:31
  29.9 11.8 %collective-permute-start.11 = (bf16[5,40,960]{2,1,0:T(8,128)(2,1)S(1)}, bf16[5,40,960]{2,1,0:T(8,128)(2,1)S(1)}, u32[]{:S(2)}, u32[]{:S(2)}) collective-permute-start(bf16[5,40,960]{2,1,0:T(8,128)(2,1)S(1)} %get-tuple-element.79), channel_id=1, source_target_pairs={{0,32},{1,33},{2,34},{3,35},{4,36},{5,37},{6,38},{7,39},{8,40},{9,... | collective-permute-start | bytes 1152008 | tf_op jit(solution)/shard_map/ppermute | solution.py:31
  30.0 13.2 %collective-permute-start.12 = (bf16[5,40,960]{2,1,0:T(8,128)(2,1)S(1)}, bf16[5,40,960]{2,1,0:T(8,128)(2,1)S(1)}, u32[]{:S(2)}, u32[]{:S(2)}) collective-permute-start(bf16[5,40,960]{2,1,0:T(8,128)(2,1)S(1)} %get-tuple-element.80), channel_id=1, source_target_pairs={{0,96},{1,97},{2,98},{3,99},{4,100},{5,101},{6,102},{7,103},{8,104... | collective-permute-start | bytes 1152008 | tf_op jit(solution)/shard_map/ppermute | solution.py:31
  33.3 16.9 %copy-start = (bf16[27,160,320]{2,1,0:T(8,128)(2,1)S(1)}, bf16[27,160,320]{2,1,0:T(8,128)(2,1)}, u32[]{:S(2)}) copy-start(bf16[27,160,320]{2,1,0:T(8,128)(2,1)} %refs_1_.3) | copy-start | bytes 8294404
  43.2 6.9 %collective-permute-start.13 = (bf16[27,80,320]{2,1,0:T(8,128)(2,1)S(1)}, bf16[27,80,320]{2,1,0:T(8,128)(2,1)S(1)}, u32[]{:S(2)}, u32[]{:S(2)}) collective-permute-start(bf16[27,80,320]{2,1,0:T(8,128)(2,1)S(1)} %collective-permute-done.10.refs_2_), channel_id=1, source_target_pairs={{0,16},{1,17},{2,18},{3,19},{4,20},{5,21},{6,22},{7,23},{8,24},{9,... | collective-permute-start | bytes 4147208 | tf_op jit(solution)/shard_map/ppermute | solution.py:31
  43.4 17.6 %collective-permute-start.14 = (bf16[5,40,960]{2,1,0:T(8,128)(2,1)S(1)}, bf16[5,40,960]{2,1,0:T(8,128)(2,1)S(1)}, u32[]{:S(2)}, u32[]{:S(2)}) collective-permute-start(bf16[5,40,960]{2,1,0:T(8,128)(2,1)S(1)} %get-tuple-element.86), channel_id=1, source_target_pairs={{0,64},{1,65},{2,66},{3,67},{4,68},{5,69},{6,70},{7,71},{8,72},{9,... | collective-permute-start | bytes 1152008 | tf_op jit(solution)/shard_map/ppermute | solution.py:31
  46.1 15.2 %collective-permute-start.15 = (bf16[4,40,960]{2,1,0:T(8,128)(2,1)S(1)}, bf16[4,40,960]{2,1,0:T(8,128)(2,1)S(1)}, u32[]{:S(2)}, u32[]{:S(2)}) collective-permute-start(bf16[4,40,960]{2,1,0:T(8,128)(2,1)S(1)} %get-tuple-element.94), channel_id=1, source_target_pairs={{0,2},{1,3},{2,0},{3,1},{4,6},{5,7},{6,4},{7,5},{8,10},{9,11},{10,... | collective-permute-start | bytes 921608 | tf_op jit(solution)/shard_map/ppermute | solution.py:31
  46.1 18.1 %collective-permute-start.16 = (bf16[4,40,960]{2,1,0:T(8,128)(2,1)S(1)}, bf16[4,40,960]{2,1,0:T(8,128)(2,1)S(1)}, u32[]{:S(2)}, u32[]{:S(2)}) collective-permute-start(bf16[4,40,960]{2,1,0:T(8,128)(2,1)S(1)} %get-tuple-element.95), channel_id=1, source_target_pairs={{0,6},{1,7},{2,4},{3,5},{4,2},{5,3},{6,0},{7,1},{8,14},{9,15},{10,... | collective-permute-start | bytes 921608 | tf_op jit(solution)/shard_map/ppermute | solution.py:31
  47.4 16.7 %collective-permute-start.17 = (bf16[4,40,960]{2,1,0:T(8,128)(2,1)S(1)}, bf16[4,40,960]{2,1,0:T(8,128)(2,1)S(1)}, u32[]{:S(2)}, u32[]{:S(2)}) collective-permute-start(bf16[4,40,960]{2,1,0:T(8,128)(2,1)S(1)} %get-tuple-element.96), channel_id=1, source_target_pairs={{0,4},{1,5},{2,6},{3,7},{4,0},{5,1},{6,2},{7,3},{8,12},{9,13},{10,... | collective-permute-start | bytes 921608 | tf_op jit(solution)/shard_map/ppermute | solution.py:31
  64.4 5.5 %collective-permute-start.18 = (bf16[40,960]{1,0:T(8,128)(2,1)S(1)}, bf16[40,960]{1,0:T(8,128)(2,1)S(1)}, u32[]{:S(2)}, u32[]{:S(2)}) collective-permute-start(bf16[40,960]{1,0:T(8,128)(2,1)S(1)} %get-tuple-element.102), channel_id=1, source_target_pairs={{0,32},{1,33},{2,34},{3,35},{4,36},{5,37},{6,38},{7,39},{8,40},{9,... | collective-permute-start | bytes 230408 | tf_op jit(solution)/shard_map/ppermute | solution.py:31
  65.4 12.0 %collective-permute-start.21 = (bf16[50,960]{1,0:T(8,128)(2,1)S(1)}, bf16[50,960]{1,0:T(8,128)(2,1)S(1)}, u32[]{:S(2)}, u32[]{:S(2)}) collective-permute-start(bf16[50,960]{1,0:T(8,128)(2,1)S(1)} %get-tuple-element.107), channel_id=1, source_target_pairs={{0,2},{1,3},{2,0},{3,1},{4,6},{5,7},{6,4},{7,5},{8,10},{9,11},{10,... | collective-permute-start | bytes 288008 | tf_op jit(solution)/shard_map/ppermute | solution.py:31
  66.0 11.4 %collective-permute-start.22 = (bf16[50,960]{1,0:T(8,128)(2,1)S(1)}, bf16[50,960]{1,0:T(8,128)(2,1)S(1)}, u32[]{:S(2)}, u32[]{:S(2)}) collective-permute-start(bf16[50,960]{1,0:T(8,128)(2,1)S(1)} %get-tuple-element.108), channel_id=1, source_target_pairs={{0,6},{1,7},{2,4},{3,5},{4,2},{5,3},{6,0},{7,1},{8,14},{9,15},{10,... | collective-permute-start | bytes 288008 | tf_op jit(solution)/shard_map/ppermute | solution.py:31
  67.3 10.1 %collective-permute-start.23 = (bf16[50,960]{1,0:T(8,128)(2,1)S(1)}, bf16[50,960]{1,0:T(8,128)(2,1)S(1)}, u32[]{:S(2)}, u32[]{:S(2)}) collective-permute-start(bf16[50,960]{1,0:T(8,128)(2,1)S(1)} %get-tuple-element.109), channel_id=1, source_target_pairs={{0,4},{1,5},{2,6},{3,7},{4,0},{5,1},{6,2},{7,3},{8,12},{9,13},{10,... | collective-permute-start | bytes 288008 | tf_op jit(solution)/shard_map/ppermute | solution.py:31
  69.5 7.8 %collective-permute-start.19 = (bf16[40,960]{1,0:T(8,128)(2,1)S(1)}, bf16[40,960]{1,0:T(8,128)(2,1)S(1)}, u32[]{:S(2)}, u32[]{:S(2)}) collective-permute-start(bf16[40,960]{1,0:T(8,128)(2,1)S(1)} %get-tuple-element.103), channel_id=1, source_target_pairs={{0,96},{1,97},{2,98},{3,99},{4,100},{5,101},{6,102},{7,103},{8,104... | collective-permute-start | bytes 230408 | tf_op jit(solution)/shard_map/ppermute | solution.py:31
  69.8 7.5 %collective-permute-start.20 = (bf16[40,960]{1,0:T(8,128)(2,1)S(1)}, bf16[40,960]{1,0:T(8,128)(2,1)S(1)}, u32[]{:S(2)}, u32[]{:S(2)}) collective-permute-start(bf16[40,960]{1,0:T(8,128)(2,1)S(1)} %get-tuple-element.104), channel_id=1, source_target_pairs={{0,64},{1,65},{2,66},{3,67},{4,68},{5,69},{6,70},{7,71},{8,72},{9,... | collective-permute-start | bytes 230408 | tf_op jit(solution)/shard_map/ppermute | solution.py:31
  77.6 4.8 %collective-permute-start.24 = (bf16[45,480]{1,0:T(8,128)(2,1)S(1)}, bf16[45,480]{1,0:T(8,128)(2,1)S(1)}, u32[]{:S(2)}, u32[]{:S(2)}) collective-permute-start(bf16[45,480]{1,0:T(8,128)(2,1)S(1)} %get-tuple-element.115), channel_id=1, source_target_pairs={{0,1},{1,0},{2,3},{3,2},{4,5},{5,4},{6,7},{7,6},{8,9},{9,8},{10,11... | collective-permute-start | bytes 129608 | tf_op jit(solution)/shard_map/ppermute | solution.py:31
  77.7 6.6 %collective-permute-start.25 = (bf16[45,480]{1,0:T(8,128)(2,1)S(1)}, bf16[45,480]{1,0:T(8,128)(2,1)S(1)}, u32[]{:S(2)}, u32[]{:S(2)}) collective-permute-start(bf16[45,480]{1,0:T(8,128)(2,1)S(1)} %get-tuple-element.116), channel_id=1, source_target_pairs={{0,8},{1,9},{2,10},{3,11},{4,12},{5,13},{6,14},{7,15},{8,0},{9,1},... | collective-permute-start | bytes 129608 | tf_op jit(solution)/shard_map/ppermute | solution.py:31
  81.7 5.3 %collective-permute-start.26 = (bf16[45,480]{1,0:T(8,128)(2,1)S(1)}, bf16[45,480]{1,0:T(8,128)(2,1)S(1)}, u32[]{:S(2)}, u32[]{:S(2)}) collective-permute-start(bf16[45,480]{1,0:T(8,128)(2,1)S(1)} %get-tuple-element.117), channel_id=1, source_target_pairs={{0,9},{1,8},{2,11},{3,10},{4,13},{5,12},{6,15},{7,14},{8,1},{9,0},... | collective-permute-start | bytes 129608 | tf_op jit(solution)/shard_map/ppermute | solution.py:31

commit v3 on v2

v3 whole, which is shorter than its diff:
```python
import functools
import math

import jax
import jax.numpy as jnp
from jax import lax
from jax.experimental import pallas as pl
from jax.experimental.pallas import tpu as pltpu
from jax.sharding import PartitionSpec as P

AXES = ("lx", "ly", "af")
BF, F32 = jnp.bfloat16, jnp.float32
C = 320
HALF = 512
LANES = 2 * HALF

STREAM_A = (0, 1, 2, 3, 4)
STREAM_B = (5, 6, 7, 8)


def routes(to):
    pairs = []
    for a in range(8):
        for b in range(8):
            for c in range(2):
                u, v, w = to(a, b, c)
                pairs.append(((a * 8 + b) * 2 + c, (u * 8 + v) * 2 + w))
    return pairs


def send(value, to):
    return lax.ppermute(value, AXES, routes(to))


def swap_core(v):
    return send(v, lambda a, b, c: (a ^ 1, b, c))


def params(mib=8):
    return pltpu.CompilerParams(vmem_limit_bytes=mib * 2**20)


BRIEF = pl.CostEstimate(flops=1, bytes_accessed=1, transcendentals=0)


def sds(shape, dtype):
    return jax.ShapeDtypeStruct(shape, dtype)


def edges_kernel(g, other, alpha, beta, line, half, corner, outer, plane):
    core = lax.axis_index("lx") % 2
    at = 7 - lax.axis_index("af") * 7
    column = jnp.where(lax.axis_index("ly") % 2 == core, 15, 0)

    def picker(rows, tiles):
        row = lax.broadcasted_iota(jnp.int32, (rows, 16 * tiles), 0)
        cell = lax.broadcasted_iota(jnp.int32, (rows, 16 * tiles), 1)
        return jnp.where(cell == row * 16 + column, 1.0, 0.0).astype(BF)

    pick = picker(8, 8)

    def ends(tile, to):
        got = jnp.dot(pick, tile.reshape(128, C), preferred_element_type=F32)
        line[pl.ds(to, 1)] = got.astype(BF)[None]

    for src, to in ((g, core * 8 + 1), (other, 9 - core * 8)):
        for n in range(8):
            ends(src[:, n], to + n)
        plane[pl.ds(to, 8)] = src[pl.ds(at, 1)].reshape(8, 16, C)
    z = lax.axis_index("lx") // 2
    for n, src in enumerate((alpha, beta)):
        to = 17 * (core ^ n)
        inside = jnp.where(to == 0, z > 0, z < 3)
        outer[n] = jnp.where(inside, src[...].astype(F32), 0.0).astype(BF)
        ends(outer[n], to)
        plane[pl.ds(to, 1)] = outer[n, pl.ds(at, 1)]
    half[...] = plane[pl.ds(9 * core, 9)]
    got = jnp.dot(picker(24, 18), plane[...].reshape(288, C), preferred_element_type=F32)
    corner[...] = got[:18].astype(BF)


def edges(g, other, alpha, beta):
    return pl.pallas_call(
        edges_kernel,
        out_shape=(
            sds((18, 8, C), BF),
            sds((9, 16, C), BF),
            sds((18, C), BF),
            sds((2, 8, 16, C), BF),
        ),
        scratch_shapes=[pltpu.VMEM((18, 16, C), BF)],
        compiler_params=params(10),
        cost_estimate=BRIEF,
        name="edges",
    )(g, other, alpha, beta)


def turn_kernel(own, other, out_a, out_b, both):
    core = lax.axis_index("lx") % 2
    mine = lax.axis_index("lx") * 8 + lax.axis_index("ly")
    both[:, pl.ds(core * 8, 8)] = own[...]
    both[:, pl.ds(8 - core * 8, 8)] = other[...]
    cells = both[...].reshape(2048, C)
    row = lax.broadcasted_iota(jnp.int32, (160, C), 0)
    fives, tens, forties = row * 13108 >> 16, row * 6554 >> 16, row * 52429 >> 21
    first, second = forties, tens & 3
    first, second = first ^ (first >> 1), second ^ (second >> 1)
    lane = lax.broadcasted_iota(jnp.int32, (160, C), 1)
    for out, z, x in ((out_a, first, second), (out_b, second, first)):
        chunk = mine ^ (z * 16 + (fives & 1) * 4 + x)
        target = chunk * 5 + row - fives * 5
        pick = jnp.where(lane == target, 1.0, 0.0).astype(BF)
        out[...] = lax.dot_general(
            pick, cells, (((1,), (1,)), ((), ())), preferred_element_type=F32
        ).astype(BF)


def turn(own, other):
    return pl.pallas_call(
        turn_kernel,
        out_shape=(sds((160, 2048), BF), sds((160, 2048), BF)),
        scratch_shapes=[pltpu.VMEM((8, 16, 16, C), BF)],
        compiler_params=params(12),
        cost_estimate=BRIEF,
        name="turn",
    )(own, other)


def spread(tile, left, right):
    n = tile.shape[0]
    rows = n * 16
    flat = tile.astype(F32).reshape(rows, C)
    col = lax.broadcasted_iota(jnp.int32, (n, 16, C), 1).reshape(rows, C)
    ends = jnp.broadcast_to(right.reshape(n, 1, C), (n, 16, C)).reshape(rows, C)
    heads = jnp.broadcast_to(left.reshape(n, 1, C), (n, 16, C)).reshape(rows, C)
    up = jnp.where(col == 15, ends, pltpu.roll(flat, rows - 1, 0)).astype(BF)
    down = jnp.where(col == 0, heads, pltpu.roll(flat, 1, 0)).astype(BF)
    shifts = (up, tile.reshape(rows, C), down)
    pad = jnp.zeros((rows, HALF - 480), BF)
    lanes = [v[:, :160] for v in shifts] + [pad] + [v[:, 160:] for v in shifts] + [pad]
    return jnp.concatenate(lanes, axis=1).reshape(n, 16, LANES)


def tiles_kernel(
    g, other, outer, line, line_other, half, half_other, corner, corner_other, turned_a, turned_b,
    shifted, keep_a, a1, a3, a_low, a_high, keep_b, b1, b3, b_low, b_high, plane,
):
    core = lax.axis_index("lx") % 2
    af = lax.axis_index("af")
    ly = lax.axis_index("ly")
    side = ly % 2

    def order(mine, theirs):
        mine, theirs = mine.astype(F32), theirs.astype(F32)
        left = jnp.where(side == core, theirs, mine)
        right = jnp.where(side == core, mine, theirs)
        return jnp.where(ly > 0, left, 0.0), jnp.where(ly < 7, right, 0.0)

    def put(tile, at):
        lines = order(line[pl.ds(at, 1)][0], line_other[pl.ds(at, 1)][0])
        shifted[1:9, pl.ds(at, 1)] = spread(tile, *lines)[:, None]

    for src, at in ((g, core * 8 + 1), (other, 9 - core * 8)):

        def row(n, carry, src=src, at=at):
            put(src[:, pl.ds(n, 1)].reshape(8, 16, C), at + n)
            return carry

        lax.fori_loop(0, 8, row, 0, unroll=4)
    put(outer[0], core * 17)
    put(outer[1], 17 - core * 17)
    plane[pl.ds(9 * core, 9)] = half[...]
    plane[pl.ds(9 - 9 * core, 9)] = half_other[...]
    lines = order(corner[...], corner_other[...])
    shifted[pl.ds(9 - af * 9, 1)] = spread(plane[...], *lines)[None]
    shifted[pl.ds(af * 9, 1)] = jnp.zeros((1, 18, 16, LANES), BF)
    for groups, turned, keep, near, low, high in (
        (STREAM_A, turned_a, keep_a, (a1, a3), a_low, a_high),
        (STREAM_B, turned_b, keep_b, (b1, b3), b_low, b_high),
    ):
        for n, pq in enumerate(groups):
            p, q = pq // 3, pq % 3
            cells = shifted[2 - p : 10 - p, 2 - q : 18 - q].reshape(2048, LANES)
            tile = jnp.dot(turned[...], cells, preferred_element_type=F32)
            keep[n] = tile[0:40]
            for b, ref in enumerate(near):
                ref[n] = tile[40 * b + 40 : 40 * b + 80]
            low[n] = tile[120:160, :HALF].astype(BF)
            high[n] = tile[120:160, HALF:].astype(BF)


def tiles(*operands):
    outs = [sds((10, 18, 16, LANES), BF)]
    for stream in (STREAM_A, STREAM_B):
        n = len(stream)
        outs += [sds((n, 40, LANES), F32)] * 3 + [sds((n, 40, HALF), BF)] * 2
    return pl.pallas_call(
        tiles_kernel,
        out_shape=tuple(outs),
        scratch_shapes=[pltpu.VMEM((18, 16, C), BF)],
        compiler_params=params(28),
        cost_estimate=BRIEF,
        name="tiles",
    )(*operands)


def join_kernel(a1, a3, a_low, a_high, b1, b3, b_low, b_high, a1_out, a3_out, b1_out, b3_out):
    for one, three, low, high, one_out, three_out in (
        (a1, a3, a_low, a_high, a1_out, a3_out),
        (b1, b3, b_low, b_high, b1_out, b3_out),
    ):
        one_out[:, :, :HALF] = one[:, :, :HALF].astype(BF)
        one_out[:, :, HALF:] = (one[:, :, HALF:] + high[...].astype(F32)).astype(BF)
        three_out[:, :, :HALF] = (three[:, :, :HALF] + low[...].astype(F32)).astype(BF)
        three_out[:, :, HALF:] = three[:, :, HALF:].astype(BF)


def join(a1, a3, a_low, a_high, b1, b3, b_low, b_high):
    outs = [sds(v.shape, BF) for v in (a1, a3, b1, b3)]
    return pl.pallas_call(
        join_kernel,
        out_shape=tuple(outs),
        compiler_params=params(12),
        cost_estimate=BRIEF,
        name="join",
    )(a1, a3, a_low, a_high, b1, b3, b_low, b_high)


def flipped(weight, pq, start, rows):
    row = lax.broadcasted_iota(jnp.int32, (rows, C), 0)
    lane = lax.broadcasted_iota(jnp.int32, (rows, C), 1)
    pick = jnp.where(lane == row + start, 1.0, 0.0).astype(BF)
    taps = weight[3 * pq : 3 * pq + 3].reshape(480, C)
    turned = lax.dot_general(pick, taps, (((1,), (1,)), ((), ())), preferred_element_type=F32)
    return jnp.concatenate([turned.astype(BF), jnp.zeros((rows, HALF - 480), BF)], axis=1)


def flip_kernel(weight, out):
    core = lax.axis_index("lx") % 2
    for pq in range(9):
        out[pq] = flipped(weight, pq, core * 160, 160)


def flip(weight):
    return pl.pallas_call(
        flip_kernel,
        out_shape=sds((9, 160, HALF), BF),
        compiler_params=params(20),
        cost_estimate=BRIEF,
        name="flip",
    )(weight)


def half_sum(shifted, taps, first, emit):
    core = lax.axis_index("lx") % 2
    lanes = pl.ds(pl.multiple_of(first * HALF, HALF), HALF)
    for p in range(3):
        value = None
        for q in range(3):
            rows = pl.ds(core * 8 + 2 - q, 8)
            cells = shifted[2 - p : 10 - p, rows, :, lanes].reshape(1024, HALF)
            term = lax.dot_general(
                taps(3 * p + q), cells, (((1,), (1,)), ((), ())), preferred_element_type=F32
            )
            value = term if value is None else value + term
        emit(p, value)


def own_kernel(shifted, own, out):
    def emit(p, value):
        out[...] = value if p == 0 else out[...] + value

    half_sum(shifted, lambda pq: flipped(own, pq, 0, C), lax.axis_index("af"), emit)


def own_half(shifted, own):
    return pl.pallas_call(
        own_kernel,
        out_shape=sds((C, 1024), F32),
        compiler_params=params(20),
        cost_estimate=BRIEF,
        name="own_half",
    )(shifted, own)


def other_kernel(shifted, far, near, partial, out, total):
    core = lax.axis_index("lx") % 2

    def taps(pq):
        low = jnp.where(core == 0, far[pq].astype(F32), near[pq].astype(F32))
        high = jnp.where(core == 0, near[pq].astype(F32), far[pq].astype(F32))
        return jnp.concatenate([low, high], axis=0).astype(BF)

    def emit(p, value):
        value = value + (partial if p == 0 else total)[...]
        if p < 2:
            total[...] = value
        else:
            out[...] = value.T.astype(BF).reshape(8, 8, 16, C)

    half_sum(shifted, taps, 1 - lax.axis_index("af"), emit)


def other_half(shifted, far, near, partial):
    return pl.pallas_call(
        other_kernel,
        out_shape=sds((8, 8, 16, C), BF),
        scratch_shapes=[pltpu.VMEM((C, 1024), F32)],
        compiler_params=params(24),
        cost_estimate=BRIEF,
        name="other_half",
    )(shifted, far, near, partial)


def quarters(blocks):
    return [jnp.concatenate([v[10 * b : 10 * b + 10] for v in blocks], axis=0) for b in range(4)]


def fold_kernel(*refs):
    for stream, ins, outs in ((STREAM_A, refs[0:3], refs[6:10]), (STREAM_B, refs[3:6], refs[10:14])):
        blocks = []
        for g in range(len(stream)):
            total = ins[0][g]
            for ref in ins[1:]:
                total = total + ref[g].astype(F32)
            blocks.append(total)
        for part, ref in zip(quarters(blocks), outs):
            ref[...] = part.astype(ref.dtype)


def fold(a, b):
    outs = []
    for stream in (STREAM_A, STREAM_B):
        rows = 10 * len(stream)
        outs += [sds((rows, LANES), F32)] + [sds((rows, LANES), BF)] * 3
    return pl.pallas_call(
        fold_kernel,
        out_shape=tuple(outs),
        compiler_params=params(12),
        cost_estimate=BRIEF,
        name="fold",
    )(*a, *b)


def cut_kernel(a0, a1, a2, a3, b0, b1, b2, b3, out, s1, s2, s3):
    af = lax.axis_index("af")
    cuts = []
    for first in (af, 1 - af):
        lanes = pl.ds(pl.multiple_of(first * HALF, HALF), HALF)
        kept, given = [], []
        for refs, n in (((a0, a1, a2, a3), len(STREAM_A)), ((b0, b1, b2, b3), len(STREAM_B))):
            total = refs[0][:, lanes]
            for ref in refs[1:]:
                total = total + ref[:, lanes].astype(F32)
            for g in range(n):
                kept.append(total[10 * g : 10 * g + 5])
                given.append(total[10 * g + 5 : 10 * g + 10])
        cuts += [jnp.concatenate(kept, axis=0), jnp.concatenate(given, axis=0)]
    out[...] = cuts[0]
    s1[...] = cuts[2].astype(BF)
    s2[...] = cuts[1].astype(BF)
    s3[...] = cuts[3].astype(BF)


def cut(*operands):
    piece = sds((45, HALF), BF)
    return pl.pallas_call(
        cut_kernel,
        out_shape=(sds((45, HALF), F32), piece, piece, piece),
        compiler_params=params(),
        cost_estimate=BRIEF,
        name="cut",
    )(*operands)


def last_kernel(scale, keep, r1, r2, r3, out):
    total = (keep[...] + r1[...].astype(F32) + r2[...].astype(F32) + r3[...].astype(F32)) * scale
    for n, pq in enumerate(STREAM_A + STREAM_B):
        for r in range(3):
            out[:, 3 * pq + r, :] = total[5 * n : 5 * n + 5, 160 * r : 160 * r + 160]


def last(scale, *operands):
    return pl.pallas_call(
        functools.partial(last_kernel, scale),
        out_shape=sds((5, 27, 160), F32),
        compiler_params=params(),
        cost_estimate=BRIEF,
        name="last",
    )(*operands)


def body(grad_out, inputs, weight):
    core = lax.axis_index("lx") % 2
    scale = 1.0 / math.sqrt(16 * 64 * 128)

    grad_other = swap_core(grad_out)
    inputs_other = swap_core(inputs)
    outer = lax.dynamic_slice_in_dim(grad_out, core * 7, 1, 1).reshape(8, 16, C)
    alpha = send(outer, lambda a, b, c: ((a + 2 * (a % 2) - 1) % 8, b, c))
    quarter = flip(weight)
    alpha, grad_other, inputs_other, quarter = lax.optimization_barrier(
        (alpha, grad_other, inputs_other, quarter)
    )
    beta = swap_core(alpha)

    line, plane, corner, outer = edges(grad_out, grad_other, alpha, beta)

    def side(a, b):
        return b ^ 1 if a % 2 == 0 else (b + 2 * (b % 2) - 1) % 8

    line = send(line, lambda a, b, c: (a, side(a, b), c))
    corner = send(corner, lambda a, b, c: (a, side(a, b), c ^ 1))
    plane = send(plane, lambda a, b, c: (a, b, c ^ 1))
    turned_a, turned_b = turn(inputs, inputs_other)
    line, corner, plane, turned_a = lax.optimization_barrier((line, corner, plane, turned_a))
    line_other, corner_other, plane_other = swap_core(line), swap_core(corner), swap_core(plane)

    quarter, turned_a = lax.optimization_barrier((quarter, turned_a))
    far = send(quarter, lambda a, b, c: (a, b ^ (4 * (a % 2)), c ^ 1))

    shifted, *terms = tiles(
        grad_out, grad_other, outer,
        line, line_other, plane, plane_other, corner, corner_other, turned_a, turned_b,
    )
    a_keep, a1, a3, a_low, a_high, b_keep, b1, b3, b_low, b_high = terms
    along_z = [lambda a, b, c, s=s: (a ^ (2 * s), b, c) for s in (1, 3, 2)]
    along_x = [lambda a, b, c, s=s: (a, b ^ s, c) for s in (1, 3, 2)]
    along_y = [
        lambda a, b, c: (a, b, c ^ 1),
        lambda a, b, c: (a, b ^ 4, c),
        lambda a, b, c: (a, b ^ 4, c ^ 1),
    ]

    a_low, a_high = send(a_low, along_z[0]), send(a_high, along_z[1])
    b_low, b_high = send(b_low, along_x[0]), send(b_high, along_x[1])
    grad_input = own_half(shifted, weight)
    grad_input, far, a_low, a_high, b_low, b_high = lax.optimization_barrier(
        (grad_input, far, a_low, a_high, b_low, b_high)
    )
    near = swap_core(far)
    a1, a3, b1, b3 = join(a1, a3, a_low, a_high, b1, b3, b_low, b_high)
    a1, a3 = send(a1, along_z[0]), send(a3, along_z[1])
    b1, b3 = send(b1, along_x[0]), send(b3, along_x[1])
    grad_input = other_half(shifted, far, near, grad_input)
    grad_input, a1, a3, b1, b3 = lax.optimization_barrier((grad_input, a1, a3, b1, b3))

    both = fold((a_keep, a1, a3), (b_keep, b1, b3))
    a = [both[0]] + [send(v, to) for v, to in zip(both[1:4], along_x)]
    b = [both[4]] + [send(v, to) for v, to in zip(both[5:8], along_z)]
    keep, *outs = cut(*a, *b)
    ins = [send(v, to) for v, to in zip(outs, along_y)]
    grad_weight = last(scale, keep, *ins)
    return (grad_input, jnp.transpose(grad_weight, (1, 2, 0)))


def solution(mesh):
    placed = (P("af", "lx", "ly", None), P("af", "lx", "ly", None), P(None, "af", None))
    return jax.shard_map(
        body,
        mesh=mesh,
        in_specs=placed,
        out_specs=(P("af", "lx", "ly", None), P(None, "af", ("lx", "ly"))),
        check_vma=False,
    )
```

time: 88 us -> 79.9 us (0.908)
  Pallas kernels: 27.8 us -> 22.6 us
  waiting for transfers between devices: 20.7 us -> 18.9 us
  starting transfers between devices: 36 us -> 34.5 us
    pallas_call x7, Pallas kernels: 25.5 us -> 19.9 us  [the longest x1 8.48 us: tiles(): pl.pallas_call(tiles_kernel, out_shape=tuple(outs), scratch_shapes=[pltpu...]
    unnamed x8, local copies, waits for them, and re-layouts: 0.02 us -> 1.95 us
    ppermute x27 -> x29, waiting for transfers between devices: 20.7 us -> 18.9 us  [send(): return lax.ppermute(value, AXES, routes(to))]
    dynamic_slice x1 -> x0, local copies, waits for them, and re-layouts: 1.68 us -> none  [body(): quarter = lax.dynamic_slice_in_dim(weight_late, core * 80, 80, 1)]
    ppermute x27 -> x29, starting transfers between devices: 36 us -> 34.5 us  [send(): return lax.ppermute(value, AXES, routes(to))]
  transfers between devices with their start and end apart: 27 -> 29, of which waited for: 9 -> 11; matrix products, arithmetic and copies ran while one was open for 3% -> 1% of each run, Pallas kernels for 30% -> 26%
where the time goes in v3:
time: 79.9 us; the launch traced here: 79.8 us
  starting transfers between devices  34.5 us (43%)
  Pallas kernels  22.6 us (28%)
  waiting for transfers between devices  18.9 us (24%)
  local copies, waits for them, and re-layouts  2.86 us (4%)
    ppermute x29, starting transfers between devices, send(): return lax.ppermute(value, AXES, routes(to))  34.5 us
    ppermute x29, waiting for transfers between devices, send(): return lax.ppermute(value, AXES, routes(to))  18.9 us
    pallas_call x1, Pallas kernels, tiles(): pl.pallas_call(tiles_kernel, out_shape=tuple(outs), scratch_shapes=[pltpu...  8.48 us
    pallas_call x1, Pallas kernels, own_half(): pl.pallas_call(own_kernel, out_shape=sds((C, 1024), F32), compiler_params...  5.16 us
    pallas_call x1, Pallas kernels, other_half(): pl.pallas_call(other_kernel, out_shape=sds((8, 8, 16, C), BF), scratch_sh...  4.21 us
    unnamed x8, local copies, waits for them, and re-layouts  1.95 us
  transfers between devices with their start and end apart: 29, of which 11 were waited for; matrix products, arithmetic and copies ran while one was open for 1% of the time, Pallas kernels for 26%

profile of v3, /device:TPU:0, one launch (start us, length us, event | category | flops | bytes accessed | tf_op | source)
XLA Modules:
  0.0 79.8 jit_solution(16084017675528873812)
XLA Ops:
  0.6 0.1 collective-permute-start.2
  0.7 0.5 collective-permute-start.1
  1.2 0.9 %dynamic-slice_bitcast_fusion = bf16[8,16,320]{2,1,0:T(8,128)(2,1)S(1)} fusion(bf16[8,8,16,320]{3,2,1,0:T(8,128)(2,1)} %g.3, s32[]{:T(128)S(6)} %select_n.11), kind=kLoop, calls=%fused_computation | loop fusion | bytes 163844 | tf_op jit(solution)/shard_map/reshape | solution.py:399
  2.1 3.9 %collective-permute-start = (bf16[8,16,320]{2,1,0:T(8,128)(2,1)S(1)}, bf16[8,16,320]{2,1,0:T(8,128)(2,1)S(1)}, u32[]{:S(2)}, u32[]{:S(2)}) collective-permute-start(bf16[8,16,320]{2,1,0:T(8,128)(2,1)S(1)} %dynamic-slice_bitcast_fusion), channel_id=1, source_target_pairs={{0,112},{1,113},{2,114},{3,115},{4,116},{5,117},{6,118},{7,119},{8... | collective-permute-start | bytes 245768 | tf_op jit(solution)/shard_map/ppermute | solution.py:32
  6.0 1.9 %copy-done = bf16[27,160,320]{2,1,0:T(8,128)(2,1)S(1)} copy-done((bf16[27,160,320]{2,1,0:T(8,128)(2,1)S(1)}, bf16[27,160,320]{2,1,0:T(8,128)(2,1)}, u32[]{:S(2)}) %copy-start) | copy-done | bytes 2764824
  8.0 1.3 %flip.1 = bf16[9,160,512]{2,1,0:T(8,128)(2,1)S(1)} custom-call(bf16[27,160,320]{2,1,0:T(8,128)(2,1)S(1)} %copy-done), custom_call_target="tpu_custom_call" | custom-call | flops 1 | bytes 1 | tf_op jit(solution)/shard_map/flip/pallas_call | solution.py:245
  9.4 1.3 %collective-permute-done.3.beta = bf16[8,16,320]{2,1,0:T(8,128)(2,1)S(1)} collective-permute-done((bf16[8,16,320]{2,1,0:T(8,128)(2,1)S(1)}, bf16[8,16,320]{2,1,0:T(8,128)(2,1)S(1)}, u32[]{:S(2)}, u32[]{:S(2)}) %collective-permute-start.3) | collective-permute-done | bytes 81952 | tf_op jit(solution)/shard_map/ppermute | solution.py:32
  10.7 0.5 edges.1
  11.2 1.6 %collective-permute-start.4 = (bf16[18,8,320]{2,1,0:T(8,128)(2,1)S(1)}, bf16[18,8,320]{2,1,0:T(8,128)(2,1)S(1)}, u32[]{:S(2)}, u32[]{:S(2)}) collective-permute-start(bf16[18,8,320]{2,1,0:T(8,128)(2,1)S(1)} %get-tuple-element.59), channel_id=1, source_target_pairs={{0,2},{1,3},{2,0},{3,1},{4,6},{5,7},{6,4},{7,5},{8,10},{9,11},{10,... | collective-permute-start | bytes 276488 | tf_op jit(solution)/shard_map/ppermute | solution.py:32
  12.8 1.6 %collective-permute-start.6 = (bf16[9,16,320]{2,1,0:T(8,128)(2,1)S(1)}, bf16[9,16,320]{2,1,0:T(8,128)(2,1)S(1)}, u32[]{:S(2)}, u32[]{:S(2)}) collective-permute-start(bf16[9,16,320]{2,1,0:T(8,128)(2,1)S(1)} %get-tuple-element.61), channel_id=1, source_target_pairs={{0,1},{1,0},{2,3},{3,2},{4,5},{5,4},{6,7},{7,6},{8,9},{9,8},{10,11... | collective-permute-start | bytes 276488 | tf_op jit(solution)/shard_map/ppermute | solution.py:32
  14.4 0.4 collective-permute-start.5
  14.8 1.4 %turn.1 = (bf16[160,2048]{1,0:T(8,128)(2,1)S(1)}, bf16[160,2048]{1,0:T(8,128)(2,1)S(1)}) custom-call(bf16[8,8,16,320]{3,2,1,0:T(8,128)(2,1)S(1)} %copy-done.3, bf16[8,8,16,320]{3,2,1,0:T(8,128)(2,1)S(1)} %collective-permute-done.2.other), custom_call_target="tpu_custom_call" | custom-call | flops 1 | bytes 1 | tf_op jit(solution)/shard_map/turn/pallas_call | solution.py:119
  16.2 3.0 %collective-permute-done.5.corner = bf16[18,320]{1,0:T(8,128)(2,1)S(1)} collective-permute-done((bf16[18,320]{1,0:T(8,128)(2,1)S(1)}, bf16[18,320]{1,0:T(8,128)(2,1)S(1)}, u32[]{:S(2)}, u32[]{:S(2)}) %collective-permute-start.5) | collective-permute-done | bytes 11552 | tf_op jit(solution)/shard_map/ppermute | solution.py:32
  19.2 0.4 collective-permute-start.10
  19.6 3.7 %collective-permute-start.7 = (bf16[18,8,320]{2,1,0:T(8,128)(2,1)S(1)}, bf16[18,8,320]{2,1,0:T(8,128)(2,1)S(1)}, u32[]{:S(2)}, u32[]{:S(2)}) collective-permute-start(bf16[18,8,320]{2,1,0:T(8,128)(2,1)S(1)} %collective-permute-done.4.line), channel_id=1, source_target_pairs={{0,16},{1,17},{2,18},{3,19},{4,20},{5,21},{6,22},{7,23},{8,24},{9,... | collective-permute-start | bytes 276488 | tf_op jit(solution)/shard_map/ppermute | solution.py:32
  23.3 0.5 collective-permute-start.9
  23.8 0.8 %collective-permute-done.9.corner_other = bf16[18,320]{1,0:T(8,128)(2,1)S(1)} collective-permute-done((bf16[18,320]{1,0:T(8,128)(2,1)S(1)}, bf16[18,320]{1,0:T(8,128)(2,1)S(1)}, u32[]{:S(2)}, u32[]{:S(2)}) %collective-permute-start.9) | collective-permute-done | bytes 11552 | tf_op jit(solution)/shard_map/ppermute | solution.py:32
  24.6 8.5 %tiles.1 = (bf16[10,18,16,1024]{3,2,1,0:T(8,128)(2,1)S(1)}, f32[5,40,1024]{2,1,0:T(8,128)S(1)}, f32[5,40,1024]{2,1,0:T(8,128)S(1)}, f32[5,40,1024]{2,1,0:T(8,128...) custom-call(bf16[8,8,16,320]{3,2,1,0:T(8,128)(2,1)S(1)} %copy-done.2, ...), custom_call_target="tpu_custom_call" | custom-call | flops 1 | bytes 1 | tf_op jit(solution)/shard_map/tiles/pallas_call | solution.py:197
  33.1 0.1 collective-permute-start.11
  33.3 2.2 %collective-permute-start.12 = (bf16[5,40,512]{2,1,0:T(8,128)(2,1)S(1)}, bf16[5,40,512]{2,1,0:T(8,128)(2,1)S(1)}, u32[]{:S(2)}, u32[]{:S(2)}) collective-permute-start(bf16[5,40,512]{2,1,0:T(8,128)(2,1)S(1)} %get-tuple-element.74), channel_id=1, source_target_pairs={{0,96},{1,97},{2,98},{3,99},{4,100},{5,101},{6,102},{7,103},{8,104... | collective-permute-start | bytes 614408 | tf_op jit(solution)/shard_map/ppermute | solution.py:32
  35.5 1.3 %collective-permute-start.14 = (bf16[4,40,512]{2,1,0:T(8,128)(2,1)S(1)}, bf16[4,40,512]{2,1,0:T(8,128)(2,1)S(1)}, u32[]{:S(2)}, u32[]{:S(2)}) collective-permute-start(bf16[4,40,512]{2,1,0:T(8,128)(2,1)S(1)} %get-tuple-element.76), channel_id=1, source_target_pairs={{0,6},{1,7},{2,4},{3,5},{4,2},{5,3},{6,0},{7,1},{8,14},{9,15},{10,... | collective-permute-start | bytes 491528 | tf_op jit(solution)/shard_map/ppermute | solution.py:32
  36.8 5.2 %own_half.1.partial = f32[320,1024]{1,0:T(8,128)S(1)} custom-call(bf16[10,18,16,1024]{3,2,1,0:T(8,128)(2,1)S(1)} %get-tuple-element.71.shifted, bf16[27,160,320]{2,1,0:T(8,128)(2,1)S(1)} %copy-done.1), custom_call_target="tpu_custom_call" | custom-call | flops 1 | bytes 1 | tf_op jit(solution)/shard_map/own_half/pallas_call | solution.py:277
  42.0 0.8 collective-permute-done.14.b_high
  42.8 0.1 collective-permute-start.15
  42.9 0.2 join.1
  43.1 1.1 %collective-permute-start.16 = (bf16[5,40,1024]{2,1,0:T(8,128)(2,1)S(1)}, bf16[5,40,1024]{2,1,0:T(8,128)(2,1)S(1)}, u32[]{:S(2)}, u32[]{:S(2)}) collective-permute-start(bf16[5,40,1024]{2,1,0:T(8,128)(2,1)S(1)} %get-tuple-element.87), channel_id=1, source_target_pairs={{0,32},{1,33},{2,34},{3,35},{4,36},{5,37},{6,38},{7,39},{8,40},{9,... | collective-permute-start | bytes 1228808 | tf_op jit(solution)/shard_map/ppermute | solution.py:32
  44.2 1.1 %collective-permute-start.17 = (bf16[5,40,1024]{2,1,0:T(8,128)(2,1)S(1)}, bf16[5,40,1024]{2,1,0:T(8,128)(2,1)S(1)}, u32[]{:S(2)}, u32[]{:S(2)}) collective-permute-start(bf16[5,40,1024]{2,1,0:T(8,128)(2,1)S(1)} %get-tuple-element.88), channel_id=1, source_target_pairs={{0,96},{1,97},{2,98},{3,99},{4,100},{5,101},{6,102},{7,103},{8,104... | collective-permute-start | bytes 1228808 | tf_op jit(solution)/shard_map/ppermute | solution.py:32
  45.4 0.9 %collective-permute-start.18 = (bf16[4,40,1024]{2,1,0:T(8,128)(2,1)S(1)}, bf16[4,40,1024]{2,1,0:T(8,128)(2,1)S(1)}, u32[]{:S(2)}, u32[]{:S(2)}) collective-permute-start(bf16[4,40,1024]{2,1,0:T(8,128)(2,1)S(1)} %get-tuple-element.89), channel_id=1, source_target_pairs={{0,2},{1,3},{2,0},{3,1},{4,6},{5,7},{6,4},{7,5},{8,10},{9,11},{10,... | collective-permute-start | bytes 983048 | tf_op jit(solution)/shard_map/ppermute | solution.py:32
  46.2 1.9 %collective-permute-start.19 = (bf16[4,40,1024]{2,1,0:T(8,128)(2,1)S(1)}, bf16[4,40,1024]{2,1,0:T(8,128)(2,1)S(1)}, u32[]{:S(2)}, u32[]{:S(2)}) collective-permute-start(bf16[4,40,1024]{2,1,0:T(8,128)(2,1)S(1)} %get-tuple-element.90), channel_id=1, source_target_pairs={{0,6},{1,7},{2,4},{3,5},{4,2},{5,3},{6,0},{7,1},{8,14},{9,15},{10,... | collective-permute-start | bytes 983048 | tf_op jit(solution)/shard_map/ppermute | solution.py:32
  48.1 4.2 %other_half.1 = bf16[8,8,16,320]{3,2,1,0:T(8,128)(2,1)} custom-call(bf16[10,18,16,1024]{3,2,1,0:T(8,128)(2,1)S(1)} %get-tuple-element.71.shifted, bf16[9,160,512]{2,1,0:T(8,128)(2,1)S(1)} %collective-permute-done.10.far, bf16[9,160,512]{2,1,0:T(8,128)(2,1)S(1)} %collective-permute-done.15.near, f32[320,1024]{1,0:T(8,128)S(1)} %own_half.1.partial), custom_call_target="tpu_custom_call" | custom-call | flops 1 | bytes 1 | tf_op jit(solution)/shard_map/other_half/pallas_call | solution.py:305
  52.3 2.6 %collective-permute-done.18.refs_4_ = bf16[4,40,1024]{2,1,0:T(8,128)(2,1)S(1)} collective-permute-done((bf16[4,40,1024]{2,1,0:T(8,128)(2,1)S(1)}, bf16[4,40,1024]{2,1,0:T(8,128)(2,1)S(1)}, u32[]{:S(2)}, u32[]{:S(2)}) %collective-permute-start.18) | collective-permute-done | bytes 327712 | tf_op jit(solution)/shard_map/ppermute | solution.py:32
  54.9 1.8 %collective-permute-done.19.refs_5_ = bf16[4,40,1024]{2,1,0:T(8,128)(2,1)S(1)} collective-permute-done((bf16[4,40,1024]{2,1,0:T(8,128)(2,1)S(1)}, bf16[4,40,1024]{2,1,0:T(8,128)(2,1)S(1)}, u32[]{:S(2)}, u32[]{:S(2)}) %collective-permute-start.19) | collective-permute-done | bytes 327712 | tf_op jit(solution)/shard_map/ppermute | solution.py:32
  56.7 0.3 collective-permute-done.17.refs_2_
  57.0 0.3 fold.1
  57.4 0.1 collective-permute-start.23
  57.5 0.9 %collective-permute-start.20 = (bf16[50,1024]{1,0:T(8,128)(2,1)S(1)}, bf16[50,1024]{1,0:T(8,128)(2,1)S(1)}, u32[]{:S(2)}, u32[]{:S(2)}) collective-permute-start(bf16[50,1024]{1,0:T(8,128)(2,1)S(1)} %get-tuple-element.99), channel_id=1, source_target_pairs={{0,2},{1,3},{2,0},{3,1},{4,6},{5,7},{6,4},{7,5},{8,10},{9,11},{10,... | collective-permute-start | bytes 307208 | tf_op jit(solution)/shard_map/ppermute | solution.py:32
  58.4 1.9 %collective-permute-start.21 = (bf16[50,1024]{1,0:T(8,128)(2,1)S(1)}, bf16[50,1024]{1,0:T(8,128)(2,1)S(1)}, u32[]{:S(2)}, u32[]{:S(2)}) collective-permute-start(bf16[50,1024]{1,0:T(8,128)(2,1)S(1)} %get-tuple-element.100), channel_id=1, source_target_pairs={{0,6},{1,7},{2,4},{3,5},{4,2},{5,3},{6,0},{7,1},{8,14},{9,15},{10,... | collective-permute-start | bytes 307208 | tf_op jit(solution)/shard_map/ppermute | solution.py:32
  60.3 1.3 %collective-permute-start.22 = (bf16[50,1024]{1,0:T(8,128)(2,1)S(1)}, bf16[50,1024]{1,0:T(8,128)(2,1)S(1)}, u32[]{:S(2)}, u32[]{:S(2)}) collective-permute-start(bf16[50,1024]{1,0:T(8,128)(2,1)S(1)} %get-tuple-element.101), channel_id=1, source_target_pairs={{0,4},{1,5},{2,6},{3,7},{4,0},{5,1},{6,2},{7,3},{8,12},{9,13},{10,... | collective-permute-start | bytes 307208 | tf_op jit(solution)/shard_map/ppermute | solution.py:32
  61.6 1.9 %collective-permute-start.24 = (bf16[40,1024]{1,0:T(8,128)(2,1)S(1)}, bf16[40,1024]{1,0:T(8,128)(2,1)S(1)}, u32[]{:S(2)}, u32[]{:S(2)}) collective-permute-start(bf16[40,1024]{1,0:T(8,128)(2,1)S(1)} %get-tuple-element.104), channel_id=1, source_target_pairs={{0,96},{1,97},{2,98},{3,99},{4,100},{5,101},{6,102},{7,103},{8,104... | collective-permute-start | bytes 245768 | tf_op jit(solution)/shard_map/ppermute | solution.py:32
  63.5 2.1 %collective-permute-start.25 = (bf16[40,1024]{1,0:T(8,128)(2,1)S(1)}, bf16[40,1024]{1,0:T(8,128)(2,1)S(1)}, u32[]{:S(2)}, u32[]{:S(2)}) collective-permute-start(bf16[40,1024]{1,0:T(8,128)(2,1)S(1)} %get-tuple-element.105), channel_id=1, source_target_pairs={{0,64},{1,65},{2,66},{3,67},{4,68},{5,69},{6,70},{7,71},{8,72},{9,... | collective-permute-start | bytes 245768 | tf_op jit(solution)/shard_map/ppermute | solution.py:32
  65.7 1.6 %collective-permute-done.24.b2 = bf16[40,1024]{1,0:T(8,128)(2,1)S(1)} collective-permute-done((bf16[40,1024]{1,0:T(8,128)(2,1)S(1)}, bf16[40,1024]{1,0:T(8,128)(2,1)S(1)}, u32[]{:S(2)}, u32[]{:S(2)}) %collective-permute-start.24) | collective-permute-done | bytes 81952 | tf_op jit(solution)/shard_map/ppermute | solution.py:32
  67.3 2.2 %collective-permute-done.25.b3 = bf16[40,1024]{1,0:T(8,128)(2,1)S(1)} collective-permute-done((bf16[40,1024]{1,0:T(8,128)(2,1)S(1)}, bf16[40,1024]{1,0:T(8,128)(2,1)S(1)}, u32[]{:S(2)}, u32[]{:S(2)}) %collective-permute-start.25) | collective-permute-done | bytes 81952 | tf_op jit(solution)/shard_map/ppermute | solution.py:32
  69.5 0.1 cut.1
  69.7 3.9 %collective-permute-start.27 = (bf16[45,512]{1,0:T(8,128)(2,1)S(1)}, bf16[45,512]{1,0:T(8,128)(2,1)S(1)}, u32[]{:S(2)}, u32[]{:S(2)}) collective-permute-start(bf16[45,512]{1,0:T(8,128)(2,1)S(1)} %get-tuple-element.108), channel_id=1, source_target_pairs={{0,8},{1,9},{2,10},{3,11},{4,12},{5,13},{6,14},{7,15},{8,0},{9,1},... | collective-permute-start | bytes 138248 | tf_op jit(solution)/shard_map/ppermute | solution.py:32
  73.6 0.8 %collective-permute-start.28 = (bf16[45,512]{1,0:T(8,128)(2,1)S(1)}, bf16[45,512]{1,0:T(8,128)(2,1)S(1)}, u32[]{:S(2)}, u32[]{:S(2)}) collective-permute-start(bf16[45,512]{1,0:T(8,128)(2,1)S(1)} %get-tuple-element.109), channel_id=1, source_target_pairs={{0,9},{1,8},{2,11},{3,10},{4,13},{5,12},{6,15},{7,14},{8,1},{9,0},... | collective-permute-start | bytes 138248 | tf_op jit(solution)/shard_map/ppermute | solution.py:32
  74.4 1.8 %collective-permute-done.27.r2 = bf16[45,512]{1,0:T(8,128)(2,1)S(1)} collective-permute-done((bf16[45,512]{1,0:T(8,128)(2,1)S(1)}, bf16[45,512]{1,0:T(8,128)(2,1)S(1)}, u32[]{:S(2)}, u32[]{:S(2)}) %collective-permute-start.27) | collective-permute-done | bytes 46112 | tf_op jit(solution)/shard_map/ppermute | solution.py:32
  76.2 2.7 %collective-permute-done.28.r3 = bf16[45,512]{1,0:T(8,128)(2,1)S(1)} collective-permute-done((bf16[45,512]{1,0:T(8,128)(2,1)S(1)}, bf16[45,512]{1,0:T(8,128)(2,1)S(1)}, u32[]{:S(2)}, u32[]{:S(2)}) %collective-permute-start.28) | collective-permute-done | bytes 46112 | tf_op jit(solution)/shard_map/ppermute | solution.py:32
  78.9 0.8 %last.1 = f32[5,27,160]{2,1,0:T(8,128)} custom-call(f32[45,512]{1,0:T(8,128)S(1)} %get-tuple-element.106.keep, bf16[45,512]{1,0:T(8,128)(2,1)S(1)} %collective-permute-done.26.r1, bf16[45,512]{1,0:T(8,128)(2,1)S(1)} %collective-permute-done.27.r2, bf16[45,512]{1,0:T(8,128)(2,1)S(1)} %collective-permute-done.28.r3), custom_call_target="tpu_custom_call" | custom-call | flops 1 | bytes 1 | tf_op jit(solution)/shard_map/last/pallas_call | solution.py:384
  (29 shorter events, 0.2 us)
Async XLA Ops:
  0.6 8.7 %collective-permute-start.2 = (bf16[8,8,16,320]{3,2,1,0:T(8,128)(2,1)}, bf16[8,8,16,320]{3,2,1,0:T(8,128)(2,1)S(1)}, u32[]{:S(2)}, u32[]{:S(2)}) collective-permute-start(bf16[8,8,16,320]{3,2,1,0:T(8,128)(2,1)} %own.2), channel_id=1, source_target_pairs={{0,16},{1,17},{2,18},{3,19},{4,20},{5,21},{6,22},{7,23},{8,24},{9,... | collective-permute-start | bytes 1966088 | tf_op jit(solution)/shard_map/ppermute | solution.py:32
  0.7 8.6 %collective-permute-start.1 = (bf16[8,8,16,320]{3,2,1,0:T(8,128)(2,1)}, bf16[8,8,16,320]{3,2,1,0:T(8,128)(2,1)S(1)}, u32[]{:S(2)}, u32[]{:S(2)}) collective-permute-start(bf16[8,8,16,320]{3,2,1,0:T(8,128)(2,1)} %g.3), channel_id=1, source_target_pairs={{0,16},{1,17},{2,18},{3,19},{4,20},{5,21},{6,22},{7,23},{8,24},{9,... | collective-permute-start | bytes 1966088 | tf_op jit(solution)/shard_map/ppermute | solution.py:32
  2.1 7.2 %collective-permute-start = (bf16[8,16,320]{2,1,0:T(8,128)(2,1)S(1)}, bf16[8,16,320]{2,1,0:T(8,128)(2,1)S(1)}, u32[]{:S(2)}, u32[]{:S(2)}) collective-permute-start(bf16[8,16,320]{2,1,0:T(8,128)(2,1)S(1)} %dynamic-slice_bitcast_fusion), channel_id=1, source_target_pairs={{0,112},{1,113},{2,114},{3,115},{4,116},{5,117},{6,118},{7,119},{8... | collective-permute-start | bytes 245768 | tf_op jit(solution)/shard_map/ppermute | solution.py:32
  6.0 1.9 %copy-start = (bf16[27,160,320]{2,1,0:T(8,128)(2,1)S(1)}, bf16[27,160,320]{2,1,0:T(8,128)(2,1)}, u32[]{:S(2)}) copy-start(bf16[27,160,320]{2,1,0:T(8,128)(2,1)} %own.3) | copy-start | bytes 8294404
  8.0 2.8 %copy-start.2 = (bf16[8,8,16,320]{3,2,1,0:T(8,128)(2,1)S(1)}, bf16[8,8,16,320]{3,2,1,0:T(8,128)(2,1)}, u32[]{:S(2)}) copy-start(bf16[8,8,16,320]{3,2,1,0:T(8,128)(2,1)} %g.3) | copy-start | bytes 1966084
  9.3 5.5 %copy-start.3 = (bf16[8,8,16,320]{3,2,1,0:T(8,128)(2,1)S(1)}, bf16[8,8,16,320]{3,2,1,0:T(8,128)(2,1)}, u32[]{:S(2)}) copy-start(bf16[8,8,16,320]{3,2,1,0:T(8,128)(2,1)} %own.2) | copy-start | bytes 1966084
  9.3 1.4 %collective-permute-start.3 = (bf16[8,16,320]{2,1,0:T(8,128)(2,1)S(1)}, bf16[8,16,320]{2,1,0:T(8,128)(2,1)S(1)}, u32[]{:S(2)}, u32[]{:S(2)}) collective-permute-start(bf16[8,16,320]{2,1,0:T(8,128)(2,1)S(1)} %collective-permute-done.alpha), channel_id=1, source_target_pairs={{0,16},{1,17},{2,18},{3,19},{4,20},{5,21},{6,22},{7,23},{8,24},{9,... | collective-permute-start | bytes 245768 | tf_op jit(solution)/shard_map/ppermute | solution.py:32
  11.2 8.0 %collective-permute-start.4 = (bf16[18,8,320]{2,1,0:T(8,128)(2,1)S(1)}, bf16[18,8,320]{2,1,0:T(8,128)(2,1)S(1)}, u32[]{:S(2)}, u32[]{:S(2)}) collective-permute-start(bf16[18,8,320]{2,1,0:T(8,128)(2,1)S(1)} %get-tuple-element.59), channel_id=1, source_target_pairs={{0,2},{1,3},{2,0},{3,1},{4,6},{5,7},{6,4},{7,5},{8,10},{9,11},{10,... | collective-permute-start | bytes 276488 | tf_op jit(solution)/shard_map/ppermute | solution.py:32
  12.8 6.4 %collective-permute-start.6 = (bf16[9,16,320]{2,1,0:T(8,128)(2,1)S(1)}, bf16[9,16,320]{2,1,0:T(8,128)(2,1)S(1)}, u32[]{:S(2)}, u32[]{:S(2)}) collective-permute-start(bf16[9,16,320]{2,1,0:T(8,128)(2,1)S(1)} %get-tuple-element.61), channel_id=1, source_target_pairs={{0,1},{1,0},{2,3},{3,2},{4,5},{5,4},{6,7},{7,6},{8,9},{9,8},{10,11... | collective-permute-start | bytes 276488 | tf_op jit(solution)/shard_map/ppermute | solution.py:32
  14.4 4.9 %collective-permute-start.5 = (bf16[18,320]{1,0:T(8,128)(2,1)S(1)}, bf16[18,320]{1,0:T(8,128)(2,1)S(1)}, u32[]{:S(2)}, u32[]{:S(2)}) collective-permute-start(bf16[18,320]{1,0:T(8,128)(2,1)S(1)} %get-tuple-element.60), channel_id=1, source_target_pairs={{0,3},{1,2},{2,1},{3,0},{4,7},{5,6},{6,5},{7,4},{8,11},{9,10},{10,... | collective-permute-start | bytes 34568 | tf_op jit(solution)/shard_map/ppermute | solution.py:32
  19.2 23.6 %collective-permute-start.10 = (bf16[9,160,512]{2,1,0:T(8,128)(2,1)S(1)}, bf16[9,160,512]{2,1,0:T(8,128)(2,1)S(1)}, u32[]{:S(2)}, u32[]{:S(2)}) collective-permute-start(bf16[9,160,512]{2,1,0:T(8,128)(2,1)S(1)} %flip.1), channel_id=1, source_target_pairs={{0,1},{1,0},{2,3},{3,2},{4,5},{5,4},{6,7},{7,6},{8,9},{9,8},{10,11... | collective-permute-start | bytes 4423688 | tf_op jit(solution)/shard_map/ppermute | solution.py:32
  19.6 5.0 %collective-permute-start.7 = (bf16[18,8,320]{2,1,0:T(8,128)(2,1)S(1)}, bf16[18,8,320]{2,1,0:T(8,128)(2,1)S(1)}, u32[]{:S(2)}, u32[]{:S(2)}) collective-permute-start(bf16[18,8,320]{2,1,0:T(8,128)(2,1)S(1)} %collective-permute-done.4.line), channel_id=1, source_target_pairs={{0,16},{1,17},{2,18},{3,19},{4,20},{5,21},{6,22},{7,23},{8,24},{9,... | collective-permute-start | bytes 276488 | tf_op jit(solution)/shard_map/ppermute | solution.py:32
  23.3 1.4 %collective-permute-start.8 = (bf16[9,16,320]{2,1,0:T(8,128)(2,1)S(1)}, bf16[9,16,320]{2,1,0:T(8,128)(2,1)S(1)}, u32[]{:S(2)}, u32[]{:S(2)}) collective-permute-start(bf16[9,16,320]{2,1,0:T(8,128)(2,1)S(1)} %collective-permute-done.6.half), channel_id=1, source_target_pairs={{0,16},{1,17},{2,18},{3,19},{4,20},{5,21},{6,22},{7,23},{8,24},{9,... | collective-permute-start | bytes 276488 | tf_op jit(solution)/shard_map/ppermute | solution.py:32
  23.3 1.4 %collective-permute-start.9 = (bf16[18,320]{1,0:T(8,128)(2,1)S(1)}, bf16[18,320]{1,0:T(8,128)(2,1)S(1)}, u32[]{:S(2)}, u32[]{:S(2)}) collective-permute-start(bf16[18,320]{1,0:T(8,128)(2,1)S(1)} %collective-permute-done.5.corner), channel_id=1, source_target_pairs={{0,16},{1,17},{2,18},{3,19},{4,20},{5,21},{6,22},{7,23},{8,24},{9,... | collective-permute-start | bytes 34568 | tf_op jit(solution)/shard_map/ppermute | solution.py:32
  24.6 12.2 %copy-start.1 = (bf16[27,160,320]{2,1,0:T(8,128)(2,1)S(1)}, bf16[27,160,320]{2,1,0:T(8,128)(2,1)}, u32[]{:S(2)}) copy-start(bf16[27,160,320]{2,1,0:T(8,128)(2,1)} %own.3) | copy-start | bytes 8294404
  33.1 9.7 %collective-permute-start.11 = (bf16[5,40,512]{2,1,0:T(8,128)(2,1)S(1)}, bf16[5,40,512]{2,1,0:T(8,128)(2,1)S(1)}, u32[]{:S(2)}, u32[]{:S(2)}) collective-permute-start(bf16[5,40,512]{2,1,0:T(8,128)(2,1)S(1)} %get-tuple-element.73), channel_id=1, source_target_pairs={{0,32},{1,33},{2,34},{3,35},{4,36},{5,37},{6,38},{7,39},{8,40},{9,... | collective-permute-start | bytes 614408 | tf_op jit(solution)/shard_map/ppermute | solution.py:32
  33.3 9.5 %collective-permute-start.12 = (bf16[5,40,512]{2,1,0:T(8,128)(2,1)S(1)}, bf16[5,40,512]{2,1,0:T(8,128)(2,1)S(1)}, u32[]{:S(2)}, u32[]{:S(2)}) collective-permute-start(bf16[5,40,512]{2,1,0:T(8,128)(2,1)S(1)} %get-tuple-element.74), channel_id=1, source_target_pairs={{0,96},{1,97},{2,98},{3,99},{4,100},{5,101},{6,102},{7,103},{8,104... | collective-permute-start | bytes 614408 | tf_op jit(solution)/shard_map/ppermute | solution.py:32
  35.5 6.5 %collective-permute-start.13 = (bf16[4,40,512]{2,1,0:T(8,128)(2,1)S(1)}, bf16[4,40,512]{2,1,0:T(8,128)(2,1)S(1)}, u32[]{:S(2)}, u32[]{:S(2)}) collective-permute-start(bf16[4,40,512]{2,1,0:T(8,128)(2,1)S(1)} %get-tuple-element.75), channel_id=1, source_target_pairs={{0,2},{1,3},{2,0},{3,1},{4,6},{5,7},{6,4},{7,5},{8,10},{9,11},{10,... | collective-permute-start | bytes 491528 | tf_op jit(solution)/shard_map/ppermute | solution.py:32
  35.5 7.3 %collective-permute-start.14 = (bf16[4,40,512]{2,1,0:T(8,128)(2,1)S(1)}, bf16[4,40,512]{2,1,0:T(8,128)(2,1)S(1)}, u32[]{:S(2)}, u32[]{:S(2)}) collective-permute-start(bf16[4,40,512]{2,1,0:T(8,128)(2,1)S(1)} %get-tuple-element.76), channel_id=1, source_target_pairs={{0,6},{1,7},{2,4},{3,5},{4,2},{5,3},{6,0},{7,1},{8,14},{9,15},{10,... | collective-permute-start | bytes 491528 | tf_op jit(solution)/shard_map/ppermute | solution.py:32
  42.8 5.3 %collective-permute-start.15 = (bf16[9,160,512]{2,1,0:T(8,128)(2,1)S(1)}, bf16[9,160,512]{2,1,0:T(8,128)(2,1)S(1)}, u32[]{:S(2)}, u32[]{:S(2)}) collective-permute-start(bf16[9,160,512]{2,1,0:T(8,128)(2,1)S(1)} %collective-permute-done.10.far), channel_id=1, source_target_pairs={{0,16},{1,17},{2,18},{3,19},{4,20},{5,21},{6,22},{7,23},{8,24},{9,... | collective-permute-start | bytes 4423688 | tf_op jit(solution)/shard_map/ppermute | solution.py:32
  43.1 13.6 %collective-permute-start.16 = (bf16[5,40,1024]{2,1,0:T(8,128)(2,1)S(1)}, bf16[5,40,1024]{2,1,0:T(8,128)(2,1)S(1)}, u32[]{:S(2)}, u32[]{:S(2)}) collective-permute-start(bf16[5,40,1024]{2,1,0:T(8,128)(2,1)S(1)} %get-tuple-element.87), channel_id=1, source_target_pairs={{0,32},{1,33},{2,34},{3,35},{4,36},{5,37},{6,38},{7,39},{8,40},{9,... | collective-permute-start | bytes 1228808 | tf_op jit(solution)/shard_map/ppermute | solution.py:32
  44.2 12.8 %collective-permute-start.17 = (bf16[5,40,1024]{2,1,0:T(8,128)(2,1)S(1)}, bf16[5,40,1024]{2,1,0:T(8,128)(2,1)S(1)}, u32[]{:S(2)}, u32[]{:S(2)}) collective-permute-start(bf16[5,40,1024]{2,1,0:T(8,128)(2,1)S(1)} %get-tuple-element.88), channel_id=1, source_target_pairs={{0,96},{1,97},{2,98},{3,99},{4,100},{5,101},{6,102},{7,103},{8,104... | collective-permute-start | bytes 1228808 | tf_op jit(solution)/shard_map/ppermute | solution.py:32
  45.4 9.5 %collective-permute-start.18 = (bf16[4,40,1024]{2,1,0:T(8,128)(2,1)S(1)}, bf16[4,40,1024]{2,1,0:T(8,128)(2,1)S(1)}, u32[]{:S(2)}, u32[]{:S(2)}) collective-permute-start(bf16[4,40,1024]{2,1,0:T(8,128)(2,1)S(1)} %get-tuple-element.89), channel_id=1, source_target_pairs={{0,2},{1,3},{2,0},{3,1},{4,6},{5,7},{6,4},{7,5},{8,10},{9,11},{10,... | collective-permute-start | bytes 983048 | tf_op jit(solution)/shard_map/ppermute | solution.py:32
  46.2 10.5 %collective-permute-start.19 = (bf16[4,40,1024]{2,1,0:T(8,128)(2,1)S(1)}, bf16[4,40,1024]{2,1,0:T(8,128)(2,1)S(1)}, u32[]{:S(2)}, u32[]{:S(2)}) collective-permute-start(bf16[4,40,1024]{2,1,0:T(8,128)(2,1)S(1)} %get-tuple-element.90), channel_id=1, source_target_pairs={{0,6},{1,7},{2,4},{3,5},{4,2},{5,3},{6,0},{7,1},{8,14},{9,15},{10,... | collective-permute-start | bytes 983048 | tf_op jit(solution)/shard_map/ppermute | solution.py:32
  57.4 6.2 %collective-permute-start.23 = (bf16[40,1024]{1,0:T(8,128)(2,1)S(1)}, bf16[40,1024]{1,0:T(8,128)(2,1)S(1)}, u32[]{:S(2)}, u32[]{:S(2)}) collective-permute-start(bf16[40,1024]{1,0:T(8,128)(2,1)S(1)} %get-tuple-element.103), channel_id=1, source_target_pairs={{0,32},{1,33},{2,34},{3,35},{4,36},{5,37},{6,38},{7,39},{8,40},{9,... | collective-permute-start | bytes 245768 | tf_op jit(solution)/shard_map/ppermute | solution.py:32
  57.5 12.0 %collective-permute-start.20 = (bf16[50,1024]{1,0:T(8,128)(2,1)S(1)}, bf16[50,1024]{1,0:T(8,128)(2,1)S(1)}, u32[]{:S(2)}, u32[]{:S(2)}) collective-permute-start(bf16[50,1024]{1,0:T(8,128)(2,1)S(1)} %get-tuple-element.99), channel_id=1, source_target_pairs={{0,2},{1,3},{2,0},{3,1},{4,6},{5,7},{6,4},{7,5},{8,10},{9,11},{10,... | collective-permute-start | bytes 307208 | tf_op jit(solution)/shard_map/ppermute | solution.py:32
  58.4 11.1 %collective-permute-start.21 = (bf16[50,1024]{1,0:T(8,128)(2,1)S(1)}, bf16[50,1024]{1,0:T(8,128)(2,1)S(1)}, u32[]{:S(2)}, u32[]{:S(2)}) collective-permute-start(bf16[50,1024]{1,0:T(8,128)(2,1)S(1)} %get-tuple-element.100), channel_id=1, source_target_pairs={{0,6},{1,7},{2,4},{3,5},{4,2},{5,3},{6,0},{7,1},{8,14},{9,15},{10,... | collective-permute-start | bytes 307208 | tf_op jit(solution)/shard_map/ppermute | solution.py:32
  60.3 9.2 %collective-permute-start.22 = (bf16[50,1024]{1,0:T(8,128)(2,1)S(1)}, bf16[50,1024]{1,0:T(8,128)(2,1)S(1)}, u32[]{:S(2)}, u32[]{:S(2)}) collective-permute-start(bf16[50,1024]{1,0:T(8,128)(2,1)S(1)} %get-tuple-element.101), channel_id=1, source_target_pairs={{0,4},{1,5},{2,6},{3,7},{4,0},{5,1},{6,2},{7,3},{8,12},{9,13},{10,... | collective-permute-start | bytes 307208 | tf_op jit(solution)/shard_map/ppermute | solution.py:32
  61.6 5.7 %collective-permute-start.24 = (bf16[40,1024]{1,0:T(8,128)(2,1)S(1)}, bf16[40,1024]{1,0:T(8,128)(2,1)S(1)}, u32[]{:S(2)}, u32[]{:S(2)}) collective-permute-start(bf16[40,1024]{1,0:T(8,128)(2,1)S(1)} %get-tuple-element.104), channel_id=1, source_target_pairs={{0,96},{1,97},{2,98},{3,99},{4,100},{5,101},{6,102},{7,103},{8,104... | collective-permute-start | bytes 245768 | tf_op jit(solution)/shard_map/ppermute | solution.py:32
  63.5 5.9 %collective-permute-start.25 = (bf16[40,1024]{1,0:T(8,128)(2,1)S(1)}, bf16[40,1024]{1,0:T(8,128)(2,1)S(1)}, u32[]{:S(2)}, u32[]{:S(2)}) collective-permute-start(bf16[40,1024]{1,0:T(8,128)(2,1)S(1)} %get-tuple-element.105), channel_id=1, source_target_pairs={{0,64},{1,65},{2,66},{3,67},{4,68},{5,69},{6,70},{7,71},{8,72},{9,... | collective-permute-start | bytes 245768 | tf_op jit(solution)/shard_map/ppermute | solution.py:32
  69.6 4.8 %collective-permute-start.26 = (bf16[45,512]{1,0:T(8,128)(2,1)S(1)}, bf16[45,512]{1,0:T(8,128)(2,1)S(1)}, u32[]{:S(2)}, u32[]{:S(2)}) collective-permute-start(bf16[45,512]{1,0:T(8,128)(2,1)S(1)} %get-tuple-element.107), channel_id=1, source_target_pairs={{0,1},{1,0},{2,3},{3,2},{4,5},{5,4},{6,7},{7,6},{8,9},{9,8},{10,11... | collective-permute-start | bytes 138248 | tf_op jit(solution)/shard_map/ppermute | solution.py:32
  69.7 6.5 %collective-permute-start.27 = (bf16[45,512]{1,0:T(8,128)(2,1)S(1)}, bf16[45,512]{1,0:T(8,128)(2,1)S(1)}, u32[]{:S(2)}, u32[]{:S(2)}) collective-permute-start(bf16[45,512]{1,0:T(8,128)(2,1)S(1)} %get-tuple-element.108), channel_id=1, source_target_pairs={{0,8},{1,9},{2,10},{3,11},{4,12},{5,13},{6,14},{7,15},{8,0},{9,1},... | collective-permute-start | bytes 138248 | tf_op jit(solution)/shard_map/ppermute | solution.py:32
  73.6 5.3 %collective-permute-start.28 = (bf16[45,512]{1,0:T(8,128)(2,1)S(1)}, bf16[45,512]{1,0:T(8,128)(2,1)S(1)}, u32[]{:S(2)}, u32[]{:S(2)}) collective-permute-start(bf16[45,512]{1,0:T(8,128)(2,1)S(1)} %get-tuple-element.109), channel_id=1, source_target_pairs={{0,9},{1,8},{2,11},{3,10},{4,13},{5,12},{6,15},{7,14},{8,1},{9,0},... | collective-permute-start | bytes 138248 | tf_op jit(solution)/shard_map/ppermute | solution.py:32

commit v4 on v3

--- a/solution.py
+++ b/solution.py
@@ -11,6 +11,9 @@
 AXES = ("lx", "ly", "af")
 BF, F32 = jnp.bfloat16, jnp.float32
 C = 320
+HALF = 512
+LANES = 2 * HALF
+
 HALF = 512
 LANES = 2 * HALF
 
@@ -95,30 +98,29 @@
     )(g, other, alpha, beta)
 
 
-def turn_kernel(own, other, out_a, out_b, both):
+def turn_kernel(own, other, out, both):
     core = lax.axis_index("lx") % 2
     mine = lax.axis_index("lx") * 8 + lax.axis_index("ly")
     both[:, pl.ds(core * 8, 8)] = own[...]
     both[:, pl.ds(8 - core * 8, 8)] = other[...]
     cells = both[...].reshape(2048, C)
-    row = lax.broadcasted_iota(jnp.int32, (160, C), 0)
-    fives, tens, forties = row * 13108 >> 16, row * 6554 >> 16, row * 52429 >> 21
-    first, second = forties, tens & 3
+    row = lax.broadcasted_iota(jnp.int32, (C, C), 0)
+    fives, tens, twenties, eighties = row * 13108 >> 16, row * 6554 >> 16, row * 52429 >> 20, row * 52429 >> 22
+    first, second = eighties, twenties & 3
     first, second = first ^ (first >> 1), second ^ (second >> 1)
-    lane = lax.broadcasted_iota(jnp.int32, (160, C), 1)
-    for out, z, x in ((out_a, first, second), (out_b, second, first)):
-        chunk = mine ^ (z * 16 + (fives & 1) * 4 + x)
-        target = chunk * 5 + row - fives * 5
-        pick = jnp.where(lane == target, 1.0, 0.0).astype(BF)
-        out[...] = lax.dot_general(
-            pick, cells, (((1,), (1,)), ((), ())), preferred_element_type=F32
-        ).astype(BF)
+    z, x = jnp.where(core == 0, first, second), jnp.where(core == 0, second, first)
+    chunk = mine ^ (z * 16 + (tens & 1) * 8 + (fives & 1) * 4 + x)
+    lane = lax.broadcasted_iota(jnp.int32, (C, C), 1)
+    pick = jnp.where(lane == chunk * 5 + row - fives * 5, 1.0, 0.0).astype(BF)
+    out[...] = lax.dot_general(
+        pick, cells, (((1,), (1,)), ((), ())), preferred_element_type=F32
+    ).astype(BF)
 
 
 def turn(own, other):
     return pl.pallas_call(
         turn_kernel,
-        out_shape=(sds((160, 2048), BF), sds((160, 2048), BF)),
+        out_shape=sds((C, 2048), BF),
         scratch_shapes=[pltpu.VMEM((8, 16, 16, C), BF)],
         compiler_params=params(12),
         cost_estimate=BRIEF,
@@ -142,8 +144,8 @@
 
 
 def tiles_kernel(
-    g, other, outer, line, line_other, half, half_other, corner, corner_other, turned_a, turned_b,
-    shifted, keep_a, a1, a3, a_low, a_high, keep_b, b1, b3, b_low, b_high, plane,
+    g, other, outer, line, line_other, half, half_other, corner, corner_other, turned,
+    shifted, keep, one, three, far, plane,
 ):
     core = lax.axis_index("lx") % 2
     af = lax.axis_index("af")
@@ -174,56 +176,26 @@
     lines = order(corner[...], corner_other[...])
     shifted[pl.ds(9 - af * 9, 1)] = spread(plane[...], *lines)[None]
     shifted[pl.ds(af * 9, 1)] = jnp.zeros((1, 18, 16, LANES), BF)
-    for groups, turned, keep, near, low, high in (
-        (STREAM_A, turned_a, keep_a, (a1, a3), a_low, a_high),
-        (STREAM_B, turned_b, keep_b, (b1, b3), b_low, b_high),
-    ):
-        for n, pq in enumerate(groups):
-            p, q = pq // 3, pq % 3
-            cells = shifted[2 - p : 10 - p, 2 - q : 18 - q].reshape(2048, LANES)
-            tile = jnp.dot(turned[...], cells, preferred_element_type=F32)
-            keep[n] = tile[0:40]
-            for b, ref in enumerate(near):
-                ref[n] = tile[40 * b + 40 : 40 * b + 80]
-            low[n] = tile[120:160, :HALF].astype(BF)
-            high[n] = tile[120:160, HALF:].astype(BF)
+    lanes = pl.ds(pl.multiple_of(core * HALF, HALF), HALF)
+    for pq in range(9):
+        p, q = pq // 3, pq % 3
+        cells = shifted[2 - p : 10 - p, 2 - q : 18 - q, :, lanes].reshape(2048, HALF)
+        tile = jnp.dot(turned[...], cells, preferred_element_type=F32)
+        keep[pq] = tile[0:80]
+        for n, ref in enumerate((one, three, far)):
+            ref[pq] = tile[80 * n + 80 : 80 * n + 160].astype(BF)
 
 
 def tiles(*operands):
-    outs = [sds((10, 18, 16, LANES), BF)]
-    for stream in (STREAM_A, STREAM_B):
-        n = len(stream)
-        outs += [sds((n, 40, LANES), F32)] * 3 + [sds((n, 40, HALF), BF)] * 2
+    piece = sds((9, 80, HALF), BF)
     return pl.pallas_call(
         tiles_kernel,
-        out_shape=tuple(outs),
+        out_shape=(sds((10, 18, 16, LANES), BF), sds((9, 80, HALF), F32), piece, piece, piece),
         scratch_shapes=[pltpu.VMEM((18, 16, C), BF)],
         compiler_params=params(28),
         cost_estimate=BRIEF,
         name="tiles",
     )(*operands)
-
-
-def join_kernel(a1, a3, a_low, a_high, b1, b3, b_low, b_high, a1_out, a3_out, b1_out, b3_out):
-    for one, three, low, high, one_out, three_out in (
-        (a1, a3, a_low, a_high, a1_out, a3_out),
-        (b1, b3, b_low, b_high, b1_out, b3_out),
-    ):
-        one_out[:, :, :HALF] = one[:, :, :HALF].astype(BF)
-        one_out[:, :, HALF:] = (one[:, :, HALF:] + high[...].astype(F32)).astype(BF)
-        three_out[:, :, :HALF] = (three[:, :, :HALF] + low[...].astype(F32)).astype(BF)
-        three_out[:, :, HALF:] = three[:, :, HALF:].astype(BF)
-
-
-def join(a1, a3, a_low, a_high, b1, b3, b_low, b_high):
-    outs = [sds(v.shape, BF) for v in (a1, a3, b1, b3)]
-    return pl.pallas_call(
-        join_kernel,
-        out_shape=tuple(outs),
-        compiler_params=params(12),
-        cost_estimate=BRIEF,
-        name="join",
-    )(a1, a3, a_low, a_high, b1, b3, b_low, b_high)
 
 
 def flipped(weight, pq, start, rows):
@@ -283,12 +255,15 @@
     )(shifted, own)
 
 
-def other_kernel(shifted, far, near, partial, out, total):
-    core = lax.axis_index("lx") % 2
+def other_kernel(shifted, far, near_low, near_high, partial, out, total):
+    core = lax.axis_index("lx") % 2
+    pad = jnp.zeros((160, HALF - 480), F32)
 
     def taps(pq):
-        low = jnp.where(core == 0, far[pq].astype(F32), near[pq].astype(F32))
-        high = jnp.where(core == 0, near[pq].astype(F32), far[pq].astype(F32))
+        own = far[pq].astype(F32)
+        near = jnp.concatenate([near_low[pq], near_high[pq]], axis=0).astype(F32)
+        near = jnp.concatenate([near, pad], axis=1)
+        low, high = jnp.where(core == 0, own, near), jnp.where(core == 0, near, own)
         return jnp.concatenate([low, high], axis=0).astype(BF)
 
     def emit(p, value):
@@ -309,75 +284,81 @@
         compiler_params=params(24),
         cost_estimate=BRIEF,
         name="other_half",
-    )(shifted, far, near, partial)
-
-
-def quarters(blocks):
-    return [jnp.concatenate([v[10 * b : 10 * b + 10] for v in blocks], axis=0) for b in range(4)]
-
-
-def fold_kernel(*refs):
-    for stream, ins, outs in ((STREAM_A, refs[0:3], refs[6:10]), (STREAM_B, refs[3:6], refs[10:14])):
-        blocks = []
-        for g in range(len(stream)):
-            total = ins[0][g]
-            for ref in ins[1:]:
-                total = total + ref[g].astype(F32)
-            blocks.append(total)
-        for part, ref in zip(quarters(blocks), outs):
-            ref[...] = part.astype(ref.dtype)
-
-
-def fold(a, b):
-    outs = []
-    for stream in (STREAM_A, STREAM_B):
-        rows = 10 * len(stream)
-        outs += [sds((rows, LANES), F32)] + [sds((rows, LANES), BF)] * 3
+    )(shifted, far, *near, partial)
+
+
+def fold_kernel(keep, one, three, far, *outs):
+    parts = [[], [], [], []]
+    for pq in range(9):
+        total = keep[pq]
+        for ref in (one, three, far):
+            total = total + ref[pq].astype(F32)
+        for n in range(4):
+            parts[n].append(total[20 * n : 20 * n + 20])
+    for part, ref in zip(parts, outs):
+        ref[...] = jnp.concatenate(part, axis=0).astype(ref.dtype)
+
+
+def fold(*operands):
+    piece = sds((180, HALF), BF)
     return pl.pallas_call(
         fold_kernel,
-        out_shape=tuple(outs),
+        out_shape=(sds((180, HALF), F32), piece, piece, piece),
         compiler_params=params(12),
         cost_estimate=BRIEF,
         name="fold",
-    )(*a, *b)
-
-
-def cut_kernel(a0, a1, a2, a3, b0, b1, b2, b3, out, s1, s2, s3):
-    af = lax.axis_index("af")
-    cuts = []
-    for first in (af, 1 - af):
-        lanes = pl.ds(pl.multiple_of(first * HALF, HALF), HALF)
-        kept, given = [], []
-        for refs, n in (((a0, a1, a2, a3), len(STREAM_A)), ((b0, b1, b2, b3), len(STREAM_B))):
-            total = refs[0][:, lanes]
-            for ref in refs[1:]:
-                total = total + ref[:, lanes].astype(F32)
-            for g in range(n):
-                kept.append(total[10 * g : 10 * g + 5])
-                given.append(total[10 * g + 5 : 10 * g + 10])
-        cuts += [jnp.concatenate(kept, axis=0), jnp.concatenate(given, axis=0)]
-    out[...] = cuts[0]
-    s1[...] = cuts[2].astype(BF)
-    s2[...] = cuts[1].astype(BF)
-    s3[...] = cuts[3].astype(BF)
+    )(*operands)
+
+
+def cut_kernel(keep, r1, r2, r3, out, low, high, same):
+    total = keep[...]
+    for ref in (r1, r2, r3):
+        total = total + ref[...].astype(F32)
+    tens = [total[10 * n : 10 * n + 10] for n in range(18)]
+    part = jnp.concatenate([v[:5] for v in tens], axis=0)
+    out[...] = part
+    low[...] = part.astype(BF)
+    part = jnp.concatenate([v[5:] for v in tens], axis=0).astype(BF)
+    high[...] = part
+    same[...] = part
 
 
 def cut(*operands):
-    piece = sds((45, HALF), BF)
     return pl.pallas_call(
         cut_kernel,
-        out_shape=(sds((45, HALF), F32), piece, piece, piece),
+        out_shape=(sds((90, HALF), F32),) + (sds((90, HALF), BF),) * 3,
         compiler_params=params(),
         cost_estimate=BRIEF,
         name="cut",
     )(*operands)
 
 
-def last_kernel(scale, keep, r1, r2, r3, out):
-    total = (keep[...] + r1[...].astype(F32) + r2[...].astype(F32) + r3[...].astype(F32)) * scale
-    for n, pq in enumerate(STREAM_A + STREAM_B):
+def close_kernel(keep, r1, r2, r3, mine, theirs):
+    total = keep[...]
+    for ref in (r1, r2, r3):
+        total = total + ref[...].astype(F32)
+    tens = [total[10 * n : 10 * n + 10] for n in range(9)]
+    mine[...] = jnp.concatenate([v[:5] for v in tens], axis=0)
+    theirs[...] = jnp.concatenate([v[5:] for v in tens], axis=0)
+
+
+def close(*operands):
+    piece = sds((45, HALF), F32)
+    return pl.pallas_call(
+        close_kernel,
+        out_shape=(piece, piece),
+        compiler_params=params(),
+        cost_estimate=BRIEF,
+        name="close",
+    )(*operands)
+
+
+def last_kernel(scale, mine, theirs, out):
+    owner = lax.axis_index("af") == lax.axis_index("lx") % 2
+    total = jnp.where(owner, mine[...], theirs[...]) * scale
+    for pq in range(9):
         for r in range(3):
-            out[:, 3 * pq + r, :] = total[5 * n : 5 * n + 5, 160 * r : 160 * r + 160]
+            out[:, 3 * pq + r, :] = total[5 * pq : 5 * pq + 5, 160 * r : 160 * r + 160]
 
 
 def last(scale, *operands):
@@ -412,45 +393,36 @@
     line = send(line, lambda a, b, c: (a, side(a, b), c))
     corner = send(corner, lambda a, b, c: (a, side(a, b), c ^ 1))
     plane = send(plane, lambda a, b, c: (a, b, c ^ 1))
-    turned_a, turned_b = turn(inputs, inputs_other)
-    line, corner, plane, turned_a = lax.optimization_barrier((line, corner, plane, turned_a))
+    turned = turn(inputs, inputs_other)
+    line, corner, plane, turned = lax.optimization_barrier((line, corner, plane, turned))
     line_other, corner_other, plane_other = swap_core(line), swap_core(corner), swap_core(plane)
 
-    quarter, turned_a = lax.optimization_barrier((quarter, turned_a))
+    quarter, turned = lax.optimization_barrier((quarter, turned))
     far = send(quarter, lambda a, b, c: (a, b ^ (4 * (a % 2)), c ^ 1))
 
-    shifted, *terms = tiles(
+    shifted, keep, one, three, opposite = tiles(
         grad_out, grad_other, outer,
-        line, line_other, plane, plane_other, corner, corner_other, turned_a, turned_b,
+        line, line_other, plane, plane_other, corner, corner_other, turned,
     )
-    a_keep, a1, a3, a_low, a_high, b_keep, b1, b3, b_low, b_high = terms
-    along_z = [lambda a, b, c, s=s: (a ^ (2 * s), b, c) for s in (1, 3, 2)]
-    along_x = [lambda a, b, c, s=s: (a, b ^ s, c) for s in (1, 3, 2)]
-    along_y = [
-        lambda a, b, c: (a, b, c ^ 1),
-        lambda a, b, c: (a, b ^ 4, c),
-        lambda a, b, c: (a, b ^ 4, c ^ 1),
-    ]
-
-    a_low, a_high = send(a_low, along_z[0]), send(a_high, along_z[1])
-    b_low, b_high = send(b_low, along_x[0]), send(b_high, along_x[1])
+
+    def ring(s, second):
+        return lambda a, b, c: (a ^ (2 * s), b, c) if a % 2 == second else (a, b ^ s, c)
+
+    opposite, one, three = send(opposite, ring(2, 0)), send(one, ring(1, 0)), send(three, ring(3, 0))
     grad_input = own_half(shifted, weight)
-    grad_input, far, a_low, a_high, b_low, b_high = lax.optimization_barrier(
-        (grad_input, far, a_low, a_high, b_low, b_high)
-    )
-    near = swap_core(far)
-    a1, a3, b1, b3 = join(a1, a3, a_low, a_high, b1, b3, b_low, b_high)
-    a1, a3 = send(a1, along_z[0]), send(a3, along_z[1])
-    b1, b3 = send(b1, along_x[0]), send(b3, along_x[1])
+    grad_input, far = lax.optimization_barrier((grad_input, far))
+    near = [swap_core(far[:, n : n + 80, :480]) for n in (0, 80)]
     grad_input = other_half(shifted, far, near, grad_input)
-    grad_input, a1, a3, b1, b3 = lax.optimization_barrier((grad_input, a1, a3, b1, b3))
-
-    both = fold((a_keep, a1, a3), (b_keep, b1, b3))
-    a = [both[0]] + [send(v, to) for v, to in zip(both[1:4], along_x)]
-    b = [both[4]] + [send(v, to) for v, to in zip(both[5:8], along_z)]
-    keep, *outs = cut(*a, *b)
-    ins = [send(v, to) for v, to in zip(outs, along_y)]
-    grad_weight = last(scale, keep, *ins)
+    grad_input, opposite, one, three = lax.optimization_barrier((grad_input, opposite, one, three))
+
+    keep, one, three, far = fold(keep, one, three, opposite)
+    far, one, three = send(far, ring(2, 1)), send(one, ring(1, 1)), send(three, ring(3, 1))
+    keep, low, high, same = cut(keep, far, one, three)
+    far = send(high, lambda a, b, c: (a, b ^ 4, c))
+    one = send(low, lambda a, b, c: (a, b, c ^ 1))
+    three = send(same, lambda a, b, c: (a, b ^ 4, c ^ 1))
+    mine, theirs = close(keep, far, one, three)
+    grad_weight = last(scale, mine, swap_core(theirs))
     return (grad_input, jnp.transpose(grad_weight, (1, 2, 0)))
 
 

time: 79.9 us -> 76.8 us (0.961)
  the two profiles are of different devices: /device:TPU:0 before, /device:TPU:1 now
where the time goes in v4:
time: 76.8 us; the launch traced here: 76.6 us
  starting transfers between devices  26.5 us (35%)
  waiting for transfers between devices  24.5 us (32%)
  Pallas kernels  21.9 us (29%)
  local copies, waits for them, and re-layouts  2.97 us (4%)
    ppermute x23, starting transfers between devices, send(): return lax.ppermute(value, AXES, routes(to))  26.5 us
    ppermute x23, waiting for transfers between devices, send(): return lax.ppermute(value, AXES, routes(to))  24.5 us
    pallas_call x1, Pallas kernels, tiles(): pl.pallas_call(tiles_kernel, out_shape=(sds((10, 18, 16, LANES), BF), sds...  8.26 us
    pallas_call x1, Pallas kernels, own_half(): pl.pallas_call(own_kernel, out_shape=sds((C, 1024), F32), compiler_params...  5.16 us
    pallas_call x1, Pallas kernels, other_half(): pl.pallas_call(other_kernel, out_shape=sds((8, 8, 16, C), BF), scratch_sh...  4.21 us
    unnamed x8, local copies, waits for them, and re-layouts  1.95 us
  transfers between devices with their start and end apart: 23, of which 15 were waited for; matrix products, arithmetic and copies ran while one was open for 1% of the time, Pallas kernels for 26%

profile of v4, /device:TPU:1, one launch (start us, length us, event | category | flops | bytes accessed | tf_op | source)
XLA Modules:
  0.0 76.6 jit_solution(16586401880220929271)
XLA Ops:
  0.6 1.5 %collective-permute-start.2 = (bf16[8,8,16,320]{3,2,1,0:T(8,128)(2,1)}, bf16[8,8,16,320]{3,2,1,0:T(8,128)(2,1)S(1)}, u32[]{:S(2)}, u32[]{:S(2)}) collective-permute-start(bf16[8,8,16,320]{3,2,1,0:T(8,128)(2,1)} %own.2), channel_id=1, source_target_pairs={{0,16},{1,17},{2,18},{3,19},{4,20},{5,21},{6,22},{7,23},{8,24},{9,... | collective-permute-start | bytes 1966088 | tf_op jit(solution)/shard_map/ppermute | solution.py:35
  2.1 0.1 collective-permute-start.1
  2.2 0.9 %dynamic-slice_bitcast_fusion = bf16[8,16,320]{2,1,0:T(8,128)(2,1)S(1)} fusion(bf16[8,8,16,320]{3,2,1,0:T(8,128)(2,1)} %g.3, s32[]{:T(128)S(6)} %select_n.11), kind=kLoop, calls=%fused_computation | loop fusion | bytes 163844 | tf_op jit(solution)/shard_map/reshape | solution.py:380
  3.1 2.1 %collective-permute-start = (bf16[8,16,320]{2,1,0:T(8,128)(2,1)S(1)}, bf16[8,16,320]{2,1,0:T(8,128)(2,1)S(1)}, u32[]{:S(2)}, u32[]{:S(2)}) collective-permute-start(bf16[8,16,320]{2,1,0:T(8,128)(2,1)S(1)} %dynamic-slice_bitcast_fusion), channel_id=1, source_target_pairs={{0,112},{1,113},{2,114},{3,115},{4,116},{5,117},{6,118},{7,119},{8... | collective-permute-start | bytes 245768 | tf_op jit(solution)/shard_map/ppermute | solution.py:35
  5.2 1.9 %copy-done = bf16[27,160,320]{2,1,0:T(8,128)(2,1)S(1)} copy-done((bf16[27,160,320]{2,1,0:T(8,128)(2,1)S(1)}, bf16[27,160,320]{2,1,0:T(8,128)(2,1)}, u32[]{:S(2)}) %copy-start) | copy-done | bytes 2764824
  7.2 1.3 %flip.1 = bf16[9,160,512]{2,1,0:T(8,128)(2,1)S(1)} custom-call(bf16[27,160,320]{2,1,0:T(8,128)(2,1)S(1)} %copy-done), custom_call_target="tpu_custom_call" | custom-call | flops 1 | bytes 1 | tf_op jit(solution)/shard_map/flip/pallas_call | solution.py:217
  8.6 2.3 %collective-permute-start.3 = (bf16[8,16,320]{2,1,0:T(8,128)(2,1)S(1)}, bf16[8,16,320]{2,1,0:T(8,128)(2,1)S(1)}, u32[]{:S(2)}, u32[]{:S(2)}) collective-permute-start(bf16[8,16,320]{2,1,0:T(8,128)(2,1)S(1)} %collective-permute-done.alpha), channel_id=1, source_target_pairs={{0,16},{1,17},{2,18},{3,19},{4,20},{5,21},{6,22},{7,23},{8,24},{9,... | collective-permute-start | bytes 245768 | tf_op jit(solution)/shard_map/ppermute | solution.py:35
  10.8 0.9 %collective-permute-done.3.beta = bf16[8,16,320]{2,1,0:T(8,128)(2,1)S(1)} collective-permute-done((bf16[8,16,320]{2,1,0:T(8,128)(2,1)S(1)}, bf16[8,16,320]{2,1,0:T(8,128)(2,1)S(1)}, u32[]{:S(2)}, u32[]{:S(2)}) %collective-permute-start.3) | collective-permute-done | bytes 81952 | tf_op jit(solution)/shard_map/ppermute | solution.py:35
  11.8 0.5 edges.1
  12.3 5.2 %collective-permute-start.4 = (bf16[18,8,320]{2,1,0:T(8,128)(2,1)S(1)}, bf16[18,8,320]{2,1,0:T(8,128)(2,1)S(1)}, u32[]{:S(2)}, u32[]{:S(2)}) collective-permute-start(bf16[18,8,320]{2,1,0:T(8,128)(2,1)S(1)} %get-tuple-element.40), channel_id=1, source_target_pairs={{0,2},{1,3},{2,0},{3,1},{4,6},{5,7},{6,4},{7,5},{8,10},{9,11},{10,... | collective-permute-start | bytes 276488 | tf_op jit(solution)/shard_map/ppermute | solution.py:35
  17.5 0.4 collective-permute-start.6
  17.9 0.3 collective-permute-start.5
  18.2 1.1 %turn.1.turned = bf16[320,2048]{1,0:T(8,128)(2,1)S(1)} custom-call(bf16[8,8,16,320]{3,2,1,0:T(8,128)(2,1)S(1)} %copy-done.3, bf16[8,8,16,320]{3,2,1,0:T(8,128)(2,1)S(1)} %collective-permute-done.2.other), custom_call_target="tpu_custom_call" | custom-call | flops 1 | bytes 1 | tf_op jit(solution)/shard_map/turn/pallas_call | solution.py:121
  19.2 4.6 %collective-permute-done.5.corner = bf16[18,320]{1,0:T(8,128)(2,1)S(1)} collective-permute-done((bf16[18,320]{1,0:T(8,128)(2,1)S(1)}, bf16[18,320]{1,0:T(8,128)(2,1)S(1)}, u32[]{:S(2)}, u32[]{:S(2)}) %collective-permute-start.5) | collective-permute-done | bytes 11552 | tf_op jit(solution)/shard_map/ppermute | solution.py:35
  23.8 0.4 collective-permute-start.10
  24.2 0.5 collective-permute-start.8
  24.7 1.2 %collective-permute-done.9.corner_other = bf16[18,320]{1,0:T(8,128)(2,1)S(1)} collective-permute-done((bf16[18,320]{1,0:T(8,128)(2,1)S(1)}, bf16[18,320]{1,0:T(8,128)(2,1)S(1)}, u32[]{:S(2)}, u32[]{:S(2)}) %collective-permute-start.9) | collective-permute-done | bytes 11552 | tf_op jit(solution)/shard_map/ppermute | solution.py:35
  25.9 8.3 %tiles.1 = (bf16[10,18,16,1024]{3,2,1,0:T(8,128)(2,1)S(1)}, f32[9,80,512]{2,1,0:T(8,128)S(1)}, bf16[9,80,512]{2,1,0:T(8,128)(2,1)S(1)}, bf16[9,80,512]{2,1,0:T(8,128)(2,1)S(1)}, bf16[9,80,512]{2,1,0:T(8,128)(2,1)S(1)}) custom-call(bf16[8,8,16,320]{3,2,1,0:T(8,128)(2,1)S(1)} %copy-done.2, bf16[8,8,16,320]{3,2,1,0:T(8,128)(2,1)S(1)} %collective-permute-done.1.other, ...), custom_call_target="tpu_custom_call" | custom-call | flops 1 | bytes 1 | tf_op jit(solution)/shard_map/tiles/pallas_call | solution.py:191
  34.2 0.3 collective-permute-start.13
  34.4 1.6 %collective-permute-start.14 = (bf16[9,80,512]{2,1,0:T(8,128)(2,1)S(1)}, bf16[9,80,512]{2,1,0:T(8,128)(2,1)S(1)}, u32[]{:S(2)}, u32[]{:S(2)}) collective-permute-start(bf16[9,80,512]{2,1,0:T(8,128)(2,1)S(1)} %get-tuple-element.55), channel_id=1, source_target_pairs={{0,32},{1,33},{2,34},{3,35},{4,36},{5,37},{6,38},{7,39},{8,40},{9,... | collective-permute-start | bytes 2211848 | tf_op jit(solution)/shard_map/ppermute | solution.py:35
  36.1 1.6 %collective-permute-start.15 = (bf16[9,80,512]{2,1,0:T(8,128)(2,1)S(1)}, bf16[9,80,512]{2,1,0:T(8,128)(2,1)S(1)}, u32[]{:S(2)}, u32[]{:S(2)}) collective-permute-start(bf16[9,80,512]{2,1,0:T(8,128)(2,1)S(1)} %get-tuple-element.56), channel_id=1, source_target_pairs={{0,96},{1,97},{2,98},{3,99},{4,100},{5,101},{6,102},{7,103},{8,104... | collective-permute-start | bytes 2211848 | tf_op jit(solution)/shard_map/ppermute | solution.py:35
  37.7 5.2 %own_half.1.partial = f32[320,1024]{1,0:T(8,128)S(1)} custom-call(bf16[10,18,16,1024]{3,2,1,0:T(8,128)(2,1)S(1)} %get-tuple-element.50.shifted, bf16[27,160,320]{2,1,0:T(8,128)(2,1)S(1)} %copy-done.1), custom_call_target="tpu_custom_call" | custom-call | flops 1 | bytes 1 | tf_op jit(solution)/shard_map/own_half/pallas_call | solution.py:249
  42.9 0.7 collective-permute-done.10.far
  43.5 0.1 fusion
  43.6 0.6 collective-permute-start.12
  44.2 0.1 collective-permute-start.11
  44.3 1.7 %collective-permute-done.12.near_high = bf16[9,80,480]{2,1,0:T(8,128)(2,1)S(1)} collective-permute-done((bf16[9,80,480]{2,1,0:T(8,128)(2,1)S(1)}, bf16[9,80,480]{2,1,0:T(8,128)(2,1)S(1)}, u32[]{:S(2)}, u32[]{:S(2)}) %collective-permute-start.12) | collective-permute-done | bytes 691232 | tf_op jit(solution)/shard_map/ppermute | solution.py:35
  46.1 1.1 %collective-permute-done.11.near_low = bf16[9,80,480]{2,1,0:T(8,128)(2,1)S(1)} collective-permute-done((bf16[9,80,480]{2,1,0:T(8,128)(2,1)S(1)}, bf16[9,80,480]{2,1,0:T(8,128)(2,1)S(1)}, u32[]{:S(2)}, u32[]{:S(2)}) %collective-permute-start.11) | collective-permute-done | bytes 691232 | tf_op jit(solution)/shard_map/ppermute | solution.py:35
  47.1 4.2 %other_half.1 = bf16[8,8,16,320]{3,2,1,0:T(8,128)(2,1)} custom-call(bf16[10,18,16,1024]{3,2,1,0:T(8,128)(2,1)S(1)} %get-tuple-element.50.shifted, bf16[9,160,512]{2,1,0:T(8,128)(2,1)S(1)} %collective-permute-done.10.far, bf16[9,80,480]{2,1,0:T(8,128)(2,1)S(1)} %collective-permute-done.11.near_low, bf16[9,80,480]{2,1,0:T(8,128)(2,1)S(1)} %collective-permute-done.12.near_high, ...), custom_call_target="tpu_custom_call" | custom-call | flops 1 | bytes 1 | tf_op jit(solution)/shard_map/other_half/pallas_call | solution.py:280
  51.3 1.8 %collective-permute-done.14.one = bf16[9,80,512]{2,1,0:T(8,128)(2,1)S(1)} collective-permute-done((bf16[9,80,512]{2,1,0:T(8,128)(2,1)S(1)}, bf16[9,80,512]{2,1,0:T(8,128)(2,1)S(1)}, u32[]{:S(2)}, u32[]{:S(2)}) %collective-permute-start.14) | collective-permute-done | bytes 737312 | tf_op jit(solution)/shard_map/ppermute | solution.py:35
  53.1 1.3 %collective-permute-done.15.three = bf16[9,80,512]{2,1,0:T(8,128)(2,1)S(1)} collective-permute-done((bf16[9,80,512]{2,1,0:T(8,128)(2,1)S(1)}, bf16[9,80,512]{2,1,0:T(8,128)(2,1)S(1)}, u32[]{:S(2)}, u32[]{:S(2)}) %collective-permute-start.15) | collective-permute-done | bytes 737312 | tf_op jit(solution)/shard_map/ppermute | solution.py:35
  54.4 0.4 fold.1
  54.8 1.2 %collective-permute-start.16 = (bf16[180,512]{1,0:T(8,128)(2,1)S(1)}, bf16[180,512]{1,0:T(8,128)(2,1)S(1)}, u32[]{:S(2)}, u32[]{:S(2)}) collective-permute-start(bf16[180,512]{1,0:T(8,128)(2,1)S(1)} %get-tuple-element.63), channel_id=1, source_target_pairs={{0,4},{1,5},{2,6},{3,7},{4,0},{5,1},{6,2},{7,3},{8,12},{9,13},{10,... | collective-permute-start | bytes 552968 | tf_op jit(solution)/shard_map/ppermute | solution.py:35
  56.0 1.2 %collective-permute-start.17 = (bf16[180,512]{1,0:T(8,128)(2,1)S(1)}, bf16[180,512]{1,0:T(8,128)(2,1)S(1)}, u32[]{:S(2)}, u32[]{:S(2)}) collective-permute-start(bf16[180,512]{1,0:T(8,128)(2,1)S(1)} %get-tuple-element.64), channel_id=1, source_target_pairs={{0,2},{1,3},{2,0},{3,1},{4,6},{5,7},{6,4},{7,5},{8,10},{9,11},{10,... | collective-permute-start | bytes 552968 | tf_op jit(solution)/shard_map/ppermute | solution.py:35
  57.3 0.9 %collective-permute-start.18 = (bf16[180,512]{1,0:T(8,128)(2,1)S(1)}, bf16[180,512]{1,0:T(8,128)(2,1)S(1)}, u32[]{:S(2)}, u32[]{:S(2)}) collective-permute-start(bf16[180,512]{1,0:T(8,128)(2,1)S(1)} %get-tuple-element.65), channel_id=1, source_target_pairs={{0,6},{1,7},{2,4},{3,5},{4,2},{5,3},{6,0},{7,1},{8,14},{9,15},{10,... | collective-permute-start | bytes 552968 | tf_op jit(solution)/shard_map/ppermute | solution.py:35
  58.1 3.0 %collective-permute-done.16.r1 = bf16[180,512]{1,0:T(8,128)(2,1)S(1)} collective-permute-done((bf16[180,512]{1,0:T(8,128)(2,1)S(1)}, bf16[180,512]{1,0:T(8,128)(2,1)S(1)}, u32[]{:S(2)}, u32[]{:S(2)}) %collective-permute-start.16) | collective-permute-done | bytes 184352 | tf_op jit(solution)/shard_map/ppermute | solution.py:35
  61.1 1.4 %collective-permute-done.17.r2 = bf16[180,512]{1,0:T(8,128)(2,1)S(1)} collective-permute-done((bf16[180,512]{1,0:T(8,128)(2,1)S(1)}, bf16[180,512]{1,0:T(8,128)(2,1)S(1)}, u32[]{:S(2)}, u32[]{:S(2)}) %collective-permute-start.17) | collective-permute-done | bytes 184352 | tf_op jit(solution)/shard_map/ppermute | solution.py:35
  62.6 0.7 collective-permute-done.18.r3
  63.2 0.1 cut.1
  63.4 1.3 %collective-permute-start.19 = (bf16[90,512]{1,0:T(8,128)(2,1)S(1)}, bf16[90,512]{1,0:T(8,128)(2,1)S(1)}, u32[]{:S(2)}, u32[]{:S(2)}) collective-permute-start(bf16[90,512]{1,0:T(8,128)(2,1)S(1)} %get-tuple-element.67), channel_id=1, source_target_pairs={{0,8},{1,9},{2,10},{3,11},{4,12},{5,13},{6,14},{7,15},{8,0},{9,1},... | collective-permute-start | bytes 276488 | tf_op jit(solution)/shard_map/ppermute | solution.py:35
  64.7 1.6 %collective-permute-start.20 = (bf16[90,512]{1,0:T(8,128)(2,1)S(1)}, bf16[90,512]{1,0:T(8,128)(2,1)S(1)}, u32[]{:S(2)}, u32[]{:S(2)}) collective-permute-start(bf16[90,512]{1,0:T(8,128)(2,1)S(1)} %get-tuple-element.68), channel_id=1, source_target_pairs={{0,1},{1,0},{2,3},{3,2},{4,5},{5,4},{6,7},{7,6},{8,9},{9,8},{10,11... | collective-permute-start | bytes 276488 | tf_op jit(solution)/shard_map/ppermute | solution.py:35
  66.3 0.4 collective-permute-start.21
  66.7 1.7 %collective-permute-done.19.r1 = bf16[90,512]{1,0:T(8,128)(2,1)S(1)} collective-permute-done((bf16[90,512]{1,0:T(8,128)(2,1)S(1)}, bf16[90,512]{1,0:T(8,128)(2,1)S(1)}, u32[]{:S(2)}, u32[]{:S(2)}) %collective-permute-start.19) | collective-permute-done | bytes 92192 | tf_op jit(solution)/shard_map/ppermute | solution.py:35
  68.4 0.9 %collective-permute-done.20.r2 = bf16[90,512]{1,0:T(8,128)(2,1)S(1)} collective-permute-done((bf16[90,512]{1,0:T(8,128)(2,1)S(1)}, bf16[90,512]{1,0:T(8,128)(2,1)S(1)}, u32[]{:S(2)}, u32[]{:S(2)}) %collective-permute-start.20) | collective-permute-done | bytes 92192 | tf_op jit(solution)/shard_map/ppermute | solution.py:35
  69.4 2.5 %collective-permute-done.21.r3 = bf16[90,512]{1,0:T(8,128)(2,1)S(1)} collective-permute-done((bf16[90,512]{1,0:T(8,128)(2,1)S(1)}, bf16[90,512]{1,0:T(8,128)(2,1)S(1)}, u32[]{:S(2)}, u32[]{:S(2)}) %collective-permute-start.21) | collective-permute-done | bytes 92192 | tf_op jit(solution)/shard_map/ppermute | solution.py:35
  71.9 2.9 %collective-permute-start.22 = (f32[45,512]{1,0:T(8,128)S(1)}, f32[45,512]{1,0:T(8,128)S(1)}, u32[]{:S(2)}, u32[]{:S(2)}) collective-permute-start(f32[45,512]{1,0:T(8,128)S(1)} %get-tuple-element.71), channel_id=1, source_target_pairs={{0,16},{1,17},{2,18},{3,19},{4,20},{5,21},{6,22},{7,23},{8,24},{9,... | collective-permute-start | bytes 276488 | tf_op jit(solution)/shard_map/ppermute | solution.py:35
  74.8 0.9 %collective-permute-done.22.theirs = f32[45,512]{1,0:T(8,128)S(1)} collective-permute-done((f32[45,512]{1,0:T(8,128)S(1)}, f32[45,512]{1,0:T(8,128)S(1)}, u32[]{:S(2)}, u32[]{:S(2)}) %collective-permute-start.22) | collective-permute-done | bytes 92192 | tf_op jit(solution)/shard_map/ppermute | solution.py:35
  75.8 0.8 %last.1 = f32[5,27,160]{2,1,0:T(8,128)} custom-call(f32[45,512]{1,0:T(8,128)S(1)} %get-tuple-element.70.mine, f32[45,512]{1,0:T(8,128)S(1)} %collective-permute-done.22.theirs), custom_call_target="tpu_custom_call" | custom-call | flops 1 | bytes 1 | tf_op jit(solution)/shard_map/last/pallas_call | solution.py:365
  (18 shorter events, 0.1 us)
Async XLA Ops:
  0.6 7.9 %collective-permute-start.2 = (bf16[8,8,16,320]{3,2,1,0:T(8,128)(2,1)}, bf16[8,8,16,320]{3,2,1,0:T(8,128)(2,1)S(1)}, u32[]{:S(2)}, u32[]{:S(2)}) collective-permute-start(bf16[8,8,16,320]{3,2,1,0:T(8,128)(2,1)} %own.2), channel_id=1, source_target_pairs={{0,16},{1,17},{2,18},{3,19},{4,20},{5,21},{6,22},{7,23},{8,24},{9,... | collective-permute-start | bytes 1966088 | tf_op jit(solution)/shard_map/ppermute | solution.py:35
  2.1 6.4 %collective-permute-start.1 = (bf16[8,8,16,320]{3,2,1,0:T(8,128)(2,1)}, bf16[8,8,16,320]{3,2,1,0:T(8,128)(2,1)S(1)}, u32[]{:S(2)}, u32[]{:S(2)}) collective-permute-start(bf16[8,8,16,320]{3,2,1,0:T(8,128)(2,1)} %g.3), channel_id=1, source_target_pairs={{0,16},{1,17},{2,18},{3,19},{4,20},{5,21},{6,22},{7,23},{8,24},{9,... | collective-permute-start | bytes 1966088 | tf_op jit(solution)/shard_map/ppermute | solution.py:35
  3.1 5.4 %collective-permute-start = (bf16[8,16,320]{2,1,0:T(8,128)(2,1)S(1)}, bf16[8,16,320]{2,1,0:T(8,128)(2,1)S(1)}, u32[]{:S(2)}, u32[]{:S(2)}) collective-permute-start(bf16[8,16,320]{2,1,0:T(8,128)(2,1)S(1)} %dynamic-slice_bitcast_fusion), channel_id=1, source_target_pairs={{0,112},{1,113},{2,114},{3,115},{4,116},{5,117},{6,118},{7,119},{8... | collective-permute-start | bytes 245768 | tf_op jit(solution)/shard_map/ppermute | solution.py:35
  5.2 1.9 %copy-start = (bf16[27,160,320]{2,1,0:T(8,128)(2,1)S(1)}, bf16[27,160,320]{2,1,0:T(8,128)(2,1)}, u32[]{:S(2)}) copy-start(bf16[27,160,320]{2,1,0:T(8,128)(2,1)} %own.3) | copy-start | bytes 8294404
  7.2 4.6 %copy-start.2 = (bf16[8,8,16,320]{3,2,1,0:T(8,128)(2,1)S(1)}, bf16[8,8,16,320]{3,2,1,0:T(8,128)(2,1)}, u32[]{:S(2)}) copy-start(bf16[8,8,16,320]{3,2,1,0:T(8,128)(2,1)} %g.3) | copy-start | bytes 1966084
  8.5 9.6 %copy-start.3 = (bf16[8,8,16,320]{3,2,1,0:T(8,128)(2,1)S(1)}, bf16[8,8,16,320]{3,2,1,0:T(8,128)(2,1)}, u32[]{:S(2)}) copy-start(bf16[8,8,16,320]{3,2,1,0:T(8,128)(2,1)} %own.2) | copy-start | bytes 1966084
  8.6 3.2 %collective-permute-start.3 = (bf16[8,16,320]{2,1,0:T(8,128)(2,1)S(1)}, bf16[8,16,320]{2,1,0:T(8,128)(2,1)S(1)}, u32[]{:S(2)}, u32[]{:S(2)}) collective-permute-start(bf16[8,16,320]{2,1,0:T(8,128)(2,1)S(1)} %collective-permute-done.alpha), channel_id=1, source_target_pairs={{0,16},{1,17},{2,18},{3,19},{4,20},{5,21},{6,22},{7,23},{8,24},{9,... | collective-permute-start | bytes 245768 | tf_op jit(solution)/shard_map/ppermute | solution.py:35
  12.3 11.5 %collective-permute-start.4 = (bf16[18,8,320]{2,1,0:T(8,128)(2,1)S(1)}, bf16[18,8,320]{2,1,0:T(8,128)(2,1)S(1)}, u32[]{:S(2)}, u32[]{:S(2)}) collective-permute-start(bf16[18,8,320]{2,1,0:T(8,128)(2,1)S(1)} %get-tuple-element.40), channel_id=1, source_target_pairs={{0,2},{1,3},{2,0},{3,1},{4,6},{5,7},{6,4},{7,5},{8,10},{9,11},{10,... | collective-permute-start | bytes 276488 | tf_op jit(solution)/shard_map/ppermute | solution.py:35
  17.5 6.3 %collective-permute-start.6 = (bf16[9,16,320]{2,1,0:T(8,128)(2,1)S(1)}, bf16[9,16,320]{2,1,0:T(8,128)(2,1)S(1)}, u32[]{:S(2)}, u32[]{:S(2)}) collective-permute-start(bf16[9,16,320]{2,1,0:T(8,128)(2,1)S(1)} %get-tuple-element.42), channel_id=1, source_target_pairs={{0,1},{1,0},{2,3},{3,2},{4,5},{5,4},{6,7},{7,6},{8,9},{9,8},{10,11... | collective-permute-start | bytes 276488 | tf_op jit(solution)/shard_map/ppermute | solution.py:35
  17.9 5.9 %collective-permute-start.5 = (bf16[18,320]{1,0:T(8,128)(2,1)S(1)}, bf16[18,320]{1,0:T(8,128)(2,1)S(1)}, u32[]{:S(2)}, u32[]{:S(2)}) collective-permute-start(bf16[18,320]{1,0:T(8,128)(2,1)S(1)} %get-tuple-element.41), channel_id=1, source_target_pairs={{0,3},{1,2},{2,1},{3,0},{4,7},{5,6},{6,5},{7,4},{8,11},{9,10},{10,... | collective-permute-start | bytes 34568 | tf_op jit(solution)/shard_map/ppermute | solution.py:35
  23.8 19.7 %collective-permute-start.10 = (bf16[9,160,512]{2,1,0:T(8,128)(2,1)S(1)}, bf16[9,160,512]{2,1,0:T(8,128)(2,1)S(1)}, u32[]{:S(2)}, u32[]{:S(2)}) collective-permute-start(bf16[9,160,512]{2,1,0:T(8,128)(2,1)S(1)} %flip.1), channel_id=1, source_target_pairs={{0,1},{1,0},{2,3},{3,2},{4,5},{5,4},{6,7},{7,6},{8,9},{9,8},{10,11... | collective-permute-start | bytes 4423688 | tf_op jit(solution)/shard_map/ppermute | solution.py:35
  24.2 1.7 %collective-permute-start.7 = (bf16[18,8,320]{2,1,0:T(8,128)(2,1)S(1)}, bf16[18,8,320]{2,1,0:T(8,128)(2,1)S(1)}, u32[]{:S(2)}, u32[]{:S(2)}) collective-permute-start(bf16[18,8,320]{2,1,0:T(8,128)(2,1)S(1)} %collective-permute-done.4.line), channel_id=1, source_target_pairs={{0,16},{1,17},{2,18},{3,19},{4,20},{5,21},{6,22},{7,23},{8,24},{9,... | collective-permute-start | bytes 276488 | tf_op jit(solution)/shard_map/ppermute | solution.py:35
  24.2 1.7 %collective-permute-start.8 = (bf16[9,16,320]{2,1,0:T(8,128)(2,1)S(1)}, bf16[9,16,320]{2,1,0:T(8,128)(2,1)S(1)}, u32[]{:S(2)}, u32[]{:S(2)}) collective-permute-start(bf16[9,16,320]{2,1,0:T(8,128)(2,1)S(1)} %collective-permute-done.6.half), channel_id=1, source_target_pairs={{0,16},{1,17},{2,18},{3,19},{4,20},{5,21},{6,22},{7,23},{8,24},{9,... | collective-permute-start | bytes 276488 | tf_op jit(solution)/shard_map/ppermute | solution.py:35
  24.7 1.2 %collective-permute-start.9 = (bf16[18,320]{1,0:T(8,128)(2,1)S(1)}, bf16[18,320]{1,0:T(8,128)(2,1)S(1)}, u32[]{:S(2)}, u32[]{:S(2)}) collective-permute-start(bf16[18,320]{1,0:T(8,128)(2,1)S(1)} %collective-permute-done.5.corner), channel_id=1, source_target_pairs={{0,16},{1,17},{2,18},{3,19},{4,20},{5,21},{6,22},{7,23},{8,24},{9,... | collective-permute-start | bytes 34568 | tf_op jit(solution)/shard_map/ppermute | solution.py:35
  25.9 11.8 %copy-start.1 = (bf16[27,160,320]{2,1,0:T(8,128)(2,1)S(1)}, bf16[27,160,320]{2,1,0:T(8,128)(2,1)}, u32[]{:S(2)}) copy-start(bf16[27,160,320]{2,1,0:T(8,128)(2,1)} %own.3) | copy-start | bytes 8294404
  34.2 17.2 %collective-permute-start.13 = (bf16[9,80,512]{2,1,0:T(8,128)(2,1)S(1)}, bf16[9,80,512]{2,1,0:T(8,128)(2,1)S(1)}, u32[]{:S(2)}, u32[]{:S(2)}) collective-permute-start(bf16[9,80,512]{2,1,0:T(8,128)(2,1)S(1)} %get-tuple-element.54), channel_id=1, source_target_pairs={{0,64},{1,65},{2,66},{3,67},{4,68},{5,69},{6,70},{7,71},{8,72},{9,... | collective-permute-start | bytes 2211848 | tf_op jit(solution)/shard_map/ppermute | solution.py:35
  34.4 18.7 %collective-permute-start.14 = (bf16[9,80,512]{2,1,0:T(8,128)(2,1)S(1)}, bf16[9,80,512]{2,1,0:T(8,128)(2,1)S(1)}, u32[]{:S(2)}, u32[]{:S(2)}) collective-permute-start(bf16[9,80,512]{2,1,0:T(8,128)(2,1)S(1)} %get-tuple-element.55), channel_id=1, source_target_pairs={{0,32},{1,33},{2,34},{3,35},{4,36},{5,37},{6,38},{7,39},{8,40},{9,... | collective-permute-start | bytes 2211848 | tf_op jit(solution)/shard_map/ppermute | solution.py:35
  36.1 18.4 %collective-permute-start.15 = (bf16[9,80,512]{2,1,0:T(8,128)(2,1)S(1)}, bf16[9,80,512]{2,1,0:T(8,128)(2,1)S(1)}, u32[]{:S(2)}, u32[]{:S(2)}) collective-permute-start(bf16[9,80,512]{2,1,0:T(8,128)(2,1)S(1)} %get-tuple-element.56), channel_id=1, source_target_pairs={{0,96},{1,97},{2,98},{3,99},{4,100},{5,101},{6,102},{7,103},{8,104... | collective-permute-start | bytes 2211848 | tf_op jit(solution)/shard_map/ppermute | solution.py:35
  43.6 2.4 %collective-permute-start.12 = (bf16[9,80,480]{2,1,0:T(8,128)(2,1)S(1)}, bf16[9,80,480]{2,1,0:T(8,128)(2,1)S(1)}, u32[]{:S(2)}, u32[]{:S(2)}) collective-permute-start(bf16[9,80,480]{2,1,0:T(8,128)(2,1)S(1)} %get-tuple-element.72), channel_id=1, source_target_pairs={{0,16},{1,17},{2,18},{3,19},{4,20},{5,21},{6,22},{7,23},{8,24},{9,... | collective-permute-start | bytes 2073608 | tf_op jit(solution)/shard_map/ppermute | solution.py:35
  44.2 2.9 %collective-permute-start.11 = (bf16[9,80,480]{2,1,0:T(8,128)(2,1)S(1)}, bf16[9,80,480]{2,1,0:T(8,128)(2,1)S(1)}, u32[]{:S(2)}, u32[]{:S(2)}) collective-permute-start(bf16[9,80,480]{2,1,0:T(8,128)(2,1)S(1)} %get-tuple-element.73), channel_id=1, source_target_pairs={{0,16},{1,17},{2,18},{3,19},{4,20},{5,21},{6,22},{7,23},{8,24},{9,... | collective-permute-start | bytes 2073608 | tf_op jit(solution)/shard_map/ppermute | solution.py:35
  54.8 6.3 %collective-permute-start.16 = (bf16[180,512]{1,0:T(8,128)(2,1)S(1)}, bf16[180,512]{1,0:T(8,128)(2,1)S(1)}, u32[]{:S(2)}, u32[]{:S(2)}) collective-permute-start(bf16[180,512]{1,0:T(8,128)(2,1)S(1)} %get-tuple-element.63), channel_id=1, source_target_pairs={{0,4},{1,5},{2,6},{3,7},{4,0},{5,1},{6,2},{7,3},{8,12},{9,13},{10,... | collective-permute-start | bytes 552968 | tf_op jit(solution)/shard_map/ppermute | solution.py:35
  56.0 6.5 %collective-permute-start.17 = (bf16[180,512]{1,0:T(8,128)(2,1)S(1)}, bf16[180,512]{1,0:T(8,128)(2,1)S(1)}, u32[]{:S(2)}, u32[]{:S(2)}) collective-permute-start(bf16[180,512]{1,0:T(8,128)(2,1)S(1)} %get-tuple-element.64), channel_id=1, source_target_pairs={{0,2},{1,3},{2,0},{3,1},{4,6},{5,7},{6,4},{7,5},{8,10},{9,11},{10,... | collective-permute-start | bytes 552968 | tf_op jit(solution)/shard_map/ppermute | solution.py:35
  57.3 5.9 %collective-permute-start.18 = (bf16[180,512]{1,0:T(8,128)(2,1)S(1)}, bf16[180,512]{1,0:T(8,128)(2,1)S(1)}, u32[]{:S(2)}, u32[]{:S(2)}) collective-permute-start(bf16[180,512]{1,0:T(8,128)(2,1)S(1)} %get-tuple-element.65), channel_id=1, source_target_pairs={{0,6},{1,7},{2,4},{3,5},{4,2},{5,3},{6,0},{7,1},{8,14},{9,15},{10,... | collective-permute-start | bytes 552968 | tf_op jit(solution)/shard_map/ppermute | solution.py:35
  63.4 5.1 %collective-permute-start.19 = (bf16[90,512]{1,0:T(8,128)(2,1)S(1)}, bf16[90,512]{1,0:T(8,128)(2,1)S(1)}, u32[]{:S(2)}, u32[]{:S(2)}) collective-permute-start(bf16[90,512]{1,0:T(8,128)(2,1)S(1)} %get-tuple-element.67), channel_id=1, source_target_pairs={{0,8},{1,9},{2,10},{3,11},{4,12},{5,13},{6,14},{7,15},{8,0},{9,1},... | collective-permute-start | bytes 276488 | tf_op jit(solution)/shard_map/ppermute | solution.py:35
  64.7 4.6 %collective-permute-start.20 = (bf16[90,512]{1,0:T(8,128)(2,1)S(1)}, bf16[90,512]{1,0:T(8,128)(2,1)S(1)}, u32[]{:S(2)}, u32[]{:S(2)}) collective-permute-start(bf16[90,512]{1,0:T(8,128)(2,1)S(1)} %get-tuple-element.68), channel_id=1, source_target_pairs={{0,1},{1,0},{2,3},{3,2},{4,5},{5,4},{6,7},{7,6},{8,9},{9,8},{10,11... | collective-permute-start | bytes 276488 | tf_op jit(solution)/shard_map/ppermute | solution.py:35
  66.3 5.6 %collective-permute-start.21 = (bf16[90,512]{1,0:T(8,128)(2,1)S(1)}, bf16[90,512]{1,0:T(8,128)(2,1)S(1)}, u32[]{:S(2)}, u32[]{:S(2)}) collective-permute-start(bf16[90,512]{1,0:T(8,128)(2,1)S(1)} %get-tuple-element.69), channel_id=1, source_target_pairs={{0,9},{1,8},{2,11},{3,10},{4,13},{5,12},{6,15},{7,14},{8,1},{9,0},... | collective-permute-start | bytes 276488 | tf_op jit(solution)/shard_map/ppermute | solution.py:35
  71.9 3.8 %collective-permute-start.22 = (f32[45,512]{1,0:T(8,128)S(1)}, f32[45,512]{1,0:T(8,128)S(1)}, u32[]{:S(2)}, u32[]{:S(2)}) collective-permute-start(f32[45,512]{1,0:T(8,128)S(1)} %get-tuple-element.71), channel_id=1, source_target_pairs={{0,16},{1,17},{2,18},{3,19},{4,20},{5,21},{6,22},{7,23},{8,24},{9,... | collective-permute-start | bytes 276488 | tf_op jit(solution)/shard_map/ppermute | solution.py:35

commit v5 on v4

--- a/solution.py
+++ b/solution.py
@@ -207,20 +207,23 @@
     return jnp.concatenate([turned.astype(BF), jnp.zeros((rows, HALF - 480), BF)], axis=1)
 
 
-def flip_kernel(weight, out):
+def flip_kernel(weight, after, out):
     core = lax.axis_index("lx") % 2
     for pq in range(9):
         out[pq] = flipped(weight, pq, core * 160, 160)
 
 
-def flip(weight):
+def flip(weight, after):
+    vmem, hbm = pl.BlockSpec(memory_space=pltpu.VMEM), pl.BlockSpec(memory_space=pl.ANY)
     return pl.pallas_call(
         flip_kernel,
         out_shape=sds((9, 160, HALF), BF),
+        in_specs=[vmem, hbm],
+        out_specs=vmem,
         compiler_params=params(20),
         cost_estimate=BRIEF,
         name="flip",
-    )(weight)
+    )(weight, after)
 
 
 def half_sum(shifted, taps, first, emit):
@@ -310,52 +313,36 @@
     )(*operands)
 
 
-def cut_kernel(keep, r1, r2, r3, out, low, high, same):
+def cut_kernel(keep, r1, r2, r3, mine, s1, s2, s3, s4):
+    home = lax.axis_index("af") == lax.axis_index("lx") % 2
     total = keep[...]
     for ref in (r1, r2, r3):
         total = total + ref[...].astype(F32)
-    tens = [total[10 * n : 10 * n + 10] for n in range(18)]
-    part = jnp.concatenate([v[:5] for v in tens], axis=0)
-    out[...] = part
-    low[...] = part.astype(BF)
-    part = jnp.concatenate([v[5:] for v in tens], axis=0).astype(BF)
-    high[...] = part
-    same[...] = part
+    same, far_same, other, far_other = (
+        jnp.concatenate([total[20 * n + at : 20 * n + at + 5] for n in range(9)], axis=0)
+        for at in (0, 5, 10, 15)
+    )
+    mine[...] = same
+    s1[...] = jnp.where(home, other, same).astype(BF)
+    s2[...] = jnp.where(home, far_other, far_same).astype(BF)
+    s3[...] = jnp.where(home, far_same, other).astype(BF)
+    s4[...] = far_other.astype(BF)
 
 
 def cut(*operands):
     return pl.pallas_call(
         cut_kernel,
-        out_shape=(sds((90, HALF), F32),) + (sds((90, HALF), BF),) * 3,
+        out_shape=(sds((45, HALF), F32),) + (sds((45, HALF), BF),) * 4,
         compiler_params=params(),
         cost_estimate=BRIEF,
         name="cut",
     )(*operands)
 
 
-def close_kernel(keep, r1, r2, r3, mine, theirs):
-    total = keep[...]
-    for ref in (r1, r2, r3):
-        total = total + ref[...].astype(F32)
-    tens = [total[10 * n : 10 * n + 10] for n in range(9)]
-    mine[...] = jnp.concatenate([v[:5] for v in tens], axis=0)
-    theirs[...] = jnp.concatenate([v[5:] for v in tens], axis=0)
-
-
-def close(*operands):
-    piece = sds((45, HALF), F32)
-    return pl.pallas_call(
-        close_kernel,
-        out_shape=(piece, piece),
-        compiler_params=params(),
-        cost_estimate=BRIEF,
-        name="close",
-    )(*operands)
-
-
-def last_kernel(scale, mine, theirs, out):
-    owner = lax.axis_index("af") == lax.axis_index("lx") % 2
-    total = jnp.where(owner, mine[...], theirs[...]) * scale
+def last_kernel(scale, mine, r1, r2, r3, r4, out):
+    home = lax.axis_index("af") == lax.axis_index("lx") % 2
+    total = r1[...].astype(F32) + r2[...].astype(F32) + r3[...].astype(F32)
+    total = (total + jnp.where(home, mine[...], r4[...].astype(F32))) * scale
     for pq in range(9):
         for r in range(3):
             out[:, 3 * pq + r, :] = total[5 * pq : 5 * pq + 5, 160 * r : 160 * r + 160]
@@ -379,13 +366,12 @@
     inputs_other = swap_core(inputs)
     outer = lax.dynamic_slice_in_dim(grad_out, core * 7, 1, 1).reshape(8, 16, C)
     alpha = send(outer, lambda a, b, c: ((a + 2 * (a % 2) - 1) % 8, b, c))
-    quarter = flip(weight)
-    alpha, grad_other, inputs_other, quarter = lax.optimization_barrier(
-        (alpha, grad_other, inputs_other, quarter)
-    )
-    beta = swap_core(alpha)
+    beta = send(outer, lambda a, b, c: ((a + 4 * (a % 2) - 2) % 8, b, c))
+    turned = turn(inputs, inputs_other)
+    alpha, beta, grad_other, turned = lax.optimization_barrier((alpha, beta, grad_other, turned))
 
     line, plane, corner, outer = edges(grad_out, grad_other, alpha, beta)
+    quarter = flip(weight, corner)
 
     def side(a, b):
         return b ^ 1 if a % 2 == 0 else (b + 2 * (b % 2) - 1) % 8
@@ -393,11 +379,9 @@
     line = send(line, lambda a, b, c: (a, side(a, b), c))
     corner = send(corner, lambda a, b, c: (a, side(a, b), c ^ 1))
     plane = send(plane, lambda a, b, c: (a, b, c ^ 1))
-    turned = turn(inputs, inputs_other)
-    line, corner, plane, turned = lax.optimization_barrier((line, corner, plane, turned))
+    line, corner, plane, quarter = lax.optimization_barrier((line, corner, plane, quarter))
     line_other, corner_other, plane_other = swap_core(line), swap_core(corner), swap_core(plane)
 
-    quarter, turned = lax.optimization_barrier((quarter, turned))
     far = send(quarter, lambda a, b, c: (a, b ^ (4 * (a % 2)), c ^ 1))
 
     shifted, keep, one, three, opposite = tiles(
@@ -417,12 +401,19 @@
 
     keep, one, three, far = fold(keep, one, three, opposite)
     far, one, three = send(far, ring(2, 1)), send(one, ring(1, 1)), send(three, ring(3, 1))
-    keep, low, high, same = cut(keep, far, one, three)
-    far = send(high, lambda a, b, c: (a, b ^ 4, c))
-    one = send(low, lambda a, b, c: (a, b, c ^ 1))
-    three = send(same, lambda a, b, c: (a, b ^ 4, c ^ 1))
-    mine, theirs = close(keep, far, one, three)
-    grad_weight = last(scale, mine, swap_core(theirs))
+    mine, *sums = cut(keep, far, one, three)
+
+    def either(home, away):
+        return lambda a, b, c: home(a, b, c) if a % 2 == c else away(a, b, c)
+
+    steps = (
+        either(lambda a, b, c: (a ^ 1, b, c), lambda a, b, c: (a, b, c ^ 1)),
+        either(lambda a, b, c: (a ^ 1, b ^ 4, c), lambda a, b, c: (a, b ^ 4, c ^ 1)),
+        either(lambda a, b, c: (a, b ^ 4, c), lambda a, b, c: (a ^ 1, b, c ^ 1)),
+        either(lambda a, b, c: (a, b, c), lambda a, b, c: (a ^ 1, b ^ 4, c ^ 1)),
+    )
+    sums = [send(v, to) for v, to in zip(sums, steps)]
+    grad_weight = last(scale, mine, *sums)
     return (grad_input, jnp.transpose(grad_weight, (1, 2, 0)))
 
 

time: 76.8 us -> 74.8 us (0.974)
  waiting for transfers between devices: 24.5 us -> 21.7 us
  starting transfers between devices: 26.5 us -> 28.3 us
  local copies, waits for them, and re-layouts: 2.97 us -> 2.16 us
    ppermute x23, waiting for transfers between devices: 24.5 us -> 21.7 us  [send(): return lax.ppermute(value, AXES, routes(to))]
    ppermute x23, starting transfers between devices: 26.5 us -> 28.3 us  [send(): return lax.ppermute(value, AXES, routes(to))]
    unnamed x8 -> x6, local copies, waits for them, and re-layouts: 1.95 us -> 1.14 us
    pallas_call x3 -> x2, Pallas kernels: 1.54 us -> 1.49 us  [the longest x1 1.33 us: flip(): pl.pallas_call(flip_kernel, out_shape=sds((9, 160, HALF), BF), in_specs=[...]
  transfers between devices with their start and end apart: 23 -> 23, of which waited for: 15 -> 13; matrix products, arithmetic and copies ran while one was open for 1% -> 1% of each run, Pallas kernels for 26% -> 27%
where the time goes in v5:
time: 74.8 us; the launch traced here: 74.7 us
  starting transfers between devices  28.3 us (38%)
  Pallas kernels  21.8 us (29%)
  waiting for transfers between devices  21.7 us (29%)
  local copies, waits for them, and re-layouts  2.16 us (3%)
  between operations  0.75 us (1%)
    ppermute x23, starting transfers between devices, send(): return lax.ppermute(value, AXES, routes(to))  28.3 us
    ppermute x23, waiting for transfers between devices, send(): return lax.ppermute(value, AXES, routes(to))  21.7 us
    pallas_call x1, Pallas kernels, tiles(): pl.pallas_call(tiles_kernel, out_shape=(sds((10, 18, 16, LANES), BF), sds...  8.24 us
    pallas_call x1, Pallas kernels, own_half(): pl.pallas_call(own_kernel, out_shape=sds((C, 1024), F32), compiler_params...  5.16 us
    pallas_call x1, Pallas kernels, other_half(): pl.pallas_call(other_kernel, out_shape=sds((8, 8, 16, C), BF), scratch_sh...  4.21 us
  transfers between devices with their start and end apart: 23, of which 13 were waited for; matrix products, arithmetic and copies ran while one was open for 1% of the time, Pallas kernels for 27%

profile of v5, /device:TPU:1, one launch (start us, length us, event | category | flops | bytes accessed | tf_op | source)
XLA Modules:
  0.0 74.7 jit_solution(7568606609541094570)
XLA Ops:
  0.6 1.5 %collective-permute-start.3 = (bf16[8,8,16,320]{3,2,1,0:T(8,128)(2,1)}, bf16[8,8,16,320]{3,2,1,0:T(8,128)(2,1)S(1)}, u32[]{:S(2)}, u32[]{:S(2)}) collective-permute-start(bf16[8,8,16,320]{3,2,1,0:T(8,128)(2,1)} %own.2), channel_id=1, source_target_pairs={{0,16},{1,17},{2,18},{3,19},{4,20},{5,21},{6,22},{7,23},{8,24},{9,... | collective-permute-start | bytes 1966088 | tf_op jit(solution)/shard_map/ppermute | solution.py:35
  2.1 0.1 collective-permute-start.2
  2.2 0.9 %dynamic-slice_bitcast_fusion = bf16[8,16,320]{2,1,0:T(8,128)(2,1)S(1)} fusion(bf16[8,8,16,320]{3,2,1,0:T(8,128)(2,1)} %g.3, s32[]{:T(128)S(6)} %select_n.11), kind=kLoop, calls=%fused_computation | loop fusion | bytes 163844 | tf_op jit(solution)/shard_map/reshape | solution.py:367
  3.1 0.0 copy-start.1
  3.1 1.8 %collective-permute-start.1 = (bf16[8,16,320]{2,1,0:T(8,128)(2,1)S(1)}, bf16[8,16,320]{2,1,0:T(8,128)(2,1)S(1)}, u32[]{:S(2)}, u32[]{:S(2)}) collective-permute-start(bf16[8,16,320]{2,1,0:T(8,128)(2,1)S(1)} %dynamic-slice_bitcast_fusion), channel_id=1, source_target_pairs={{0,96},{1,97},{2,98},{3,99},{4,100},{5,101},{6,102},{7,103},{8,104... | collective-permute-start | bytes 245768 | tf_op jit(solution)/shard_map/ppermute | solution.py:35
  4.9 0.4 collective-permute-start
  5.3 1.1 %copy-done.2 = bf16[8,8,16,320]{3,2,1,0:T(8,128)(2,1)S(1)} copy-done((bf16[8,8,16,320]{3,2,1,0:T(8,128)(2,1)S(1)}, bf16[8,8,16,320]{3,2,1,0:T(8,128)(2,1)}, u32[]{:S(2)}) %copy-start.2) | copy-done | bytes 655384
  6.5 1.1 %turn.1.turned = bf16[320,2048]{1,0:T(8,128)(2,1)S(1)} custom-call(bf16[8,8,16,320]{3,2,1,0:T(8,128)(2,1)S(1)} %copy-done.2, bf16[8,8,16,320]{3,2,1,0:T(8,128)(2,1)S(1)} %collective-permute-done.3.other), custom_call_target="tpu_custom_call" | custom-call | flops 1 | bytes 1 | tf_op jit(solution)/shard_map/turn/pallas_call | solution.py:121
  7.5 1.5 %collective-permute-done.1.beta = bf16[8,16,320]{2,1,0:T(8,128)(2,1)S(1)} collective-permute-done((bf16[8,16,320]{2,1,0:T(8,128)(2,1)S(1)}, bf16[8,16,320]{2,1,0:T(8,128)(2,1)S(1)}, u32[]{:S(2)}, u32[]{:S(2)}) %collective-permute-start.1) | collective-permute-done | bytes 81952 | tf_op jit(solution)/shard_map/ppermute | solution.py:35
  9.1 0.0 collective-permute-done.alpha
  9.1 0.5 edges.1
  9.6 5.2 %collective-permute-start.4 = (bf16[18,8,320]{2,1,0:T(8,128)(2,1)S(1)}, bf16[18,8,320]{2,1,0:T(8,128)(2,1)S(1)}, u32[]{:S(2)}, u32[]{:S(2)}) collective-permute-start(bf16[18,8,320]{2,1,0:T(8,128)(2,1)S(1)} %get-tuple-element.38), channel_id=1, source_target_pairs={{0,2},{1,3},{2,0},{3,1},{4,6},{5,7},{6,4},{7,5},{8,10},{9,11},{10,... | collective-permute-start | bytes 276488 | tf_op jit(solution)/shard_map/ppermute | solution.py:35
  14.7 0.4 collective-permute-start.6
  15.1 0.3 collective-permute-start.5
  15.4 1.3 %flip.1 = bf16[9,160,512]{2,1,0:T(8,128)(2,1)S(1)} custom-call(bf16[27,160,320]{2,1,0:T(8,128)(2,1)S(1)} %copy-done, bf16[18,320]{1,0:T(8,128)(2,1)S(1)} %get-tuple-element.39.after), custom_call_target="tpu_custom_call" | custom-call | flops 1 | bytes 1 | tf_op jit(solution)/shard_map/flip/pallas_call | solution.py:218
  16.8 4.3 %collective-permute-done.5.corner = bf16[18,320]{1,0:T(8,128)(2,1)S(1)} collective-permute-done((bf16[18,320]{1,0:T(8,128)(2,1)S(1)}, bf16[18,320]{1,0:T(8,128)(2,1)S(1)}, u32[]{:S(2)}, u32[]{:S(2)}) %collective-permute-start.5) | collective-permute-done | bytes 11552 | tf_op jit(solution)/shard_map/ppermute | solution.py:35
  21.1 0.0 collective-permute-done.4.line
  21.1 0.4 collective-permute-start.10
  21.5 0.3 collective-permute-start.7
  21.8 0.2 collective-permute-start.8
  22.0 0.3 collective-permute-start.9
  22.3 0.8 %collective-permute-done.9.corner_other = bf16[18,320]{1,0:T(8,128)(2,1)S(1)} collective-permute-done((bf16[18,320]{1,0:T(8,128)(2,1)S(1)}, bf16[18,320]{1,0:T(8,128)(2,1)S(1)}, u32[]{:S(2)}, u32[]{:S(2)}) %collective-permute-start.9) | collective-permute-done | bytes 11552 | tf_op jit(solution)/shard_map/ppermute | solution.py:35
  23.2 8.2 %tiles.1 = (bf16[10,18,16,1024]{3,2,1,0:T(8,128)(2,1)S(1)}, f32[9,80,512]{2,1,0:T(8,128)S(1)}, bf16[9,80,512]{2,1,0:T(8,128)(2,1)S(1)}, bf16[9,80,512]{2,1,0:T(8,128)(2,1)S(1)}, bf16[9,80,512]{2,1,0:T(8,128)(2,1)S(1)}) custom-call(bf16[8,8,16,320]{3,2,1,0:T(8,128)(2,1)S(1)} %copy-done.1, bf16[8,8,16,320]{3,2,1,0:T(8,128)(2,1)S(1)} %collective-permute-done.2.other, ...), custom_call_target="tpu_custom_call" | custom-call | flops 1 | bytes 1 | tf_op jit(solution)/shard_map/tiles/pallas_call | solution.py:191
  31.4 2.7 %collective-permute-start.13 = (bf16[9,80,512]{2,1,0:T(8,128)(2,1)S(1)}, bf16[9,80,512]{2,1,0:T(8,128)(2,1)S(1)}, u32[]{:S(2)}, u32[]{:S(2)}) collective-permute-start(bf16[9,80,512]{2,1,0:T(8,128)(2,1)S(1)} %get-tuple-element.49), channel_id=1, source_target_pairs={{0,64},{1,65},{2,66},{3,67},{4,68},{5,69},{6,70},{7,71},{8,72},{9,... | collective-permute-start | bytes 2211848 | tf_op jit(solution)/shard_map/ppermute | solution.py:35
  34.1 0.9 %collective-permute-start.15 = (bf16[9,80,512]{2,1,0:T(8,128)(2,1)S(1)}, bf16[9,80,512]{2,1,0:T(8,128)(2,1)S(1)}, u32[]{:S(2)}, u32[]{:S(2)}) collective-permute-start(bf16[9,80,512]{2,1,0:T(8,128)(2,1)S(1)} %get-tuple-element.51), channel_id=1, source_target_pairs={{0,96},{1,97},{2,98},{3,99},{4,100},{5,101},{6,102},{7,103},{8,104... | collective-permute-start | bytes 2211848 | tf_op jit(solution)/shard_map/ppermute | solution.py:35
  34.9 5.2 %own_half.1.partial = f32[320,1024]{1,0:T(8,128)S(1)} custom-call(bf16[10,18,16,1024]{3,2,1,0:T(8,128)(2,1)S(1)} %get-tuple-element.45.shifted, bf16[27,160,320]{2,1,0:T(8,128)(2,1)S(1)} %copy-done), custom_call_target="tpu_custom_call" | custom-call | flops 1 | bytes 1 | tf_op jit(solution)/shard_map/own_half/pallas_call | solution.py:252
  40.1 0.7 collective-permute-done.10.far
  40.8 0.1 fusion
  40.9 2.2 %collective-permute-start.12 = (bf16[9,80,480]{2,1,0:T(8,128)(2,1)S(1)}, bf16[9,80,480]{2,1,0:T(8,128)(2,1)S(1)}, u32[]{:S(2)}, u32[]{:S(2)}) collective-permute-start(bf16[9,80,480]{2,1,0:T(8,128)(2,1)S(1)} %get-tuple-element.66), channel_id=1, source_target_pairs={{0,16},{1,17},{2,18},{3,19},{4,20},{5,21},{6,22},{7,23},{8,24},{9,... | collective-permute-start | bytes 2073608 | tf_op jit(solution)/shard_map/ppermute | solution.py:35
  43.1 0.1 collective-permute-start.11
  43.2 1.7 %collective-permute-done.12.near_high = bf16[9,80,480]{2,1,0:T(8,128)(2,1)S(1)} collective-permute-done((bf16[9,80,480]{2,1,0:T(8,128)(2,1)S(1)}, bf16[9,80,480]{2,1,0:T(8,128)(2,1)S(1)}, u32[]{:S(2)}, u32[]{:S(2)}) %collective-permute-start.12) | collective-permute-done | bytes 691232 | tf_op jit(solution)/shard_map/ppermute | solution.py:35
  44.9 1.1 %collective-permute-done.11.near_low = bf16[9,80,480]{2,1,0:T(8,128)(2,1)S(1)} collective-permute-done((bf16[9,80,480]{2,1,0:T(8,128)(2,1)S(1)}, bf16[9,80,480]{2,1,0:T(8,128)(2,1)S(1)}, u32[]{:S(2)}, u32[]{:S(2)}) %collective-permute-start.11) | collective-permute-done | bytes 691232 | tf_op jit(solution)/shard_map/ppermute | solution.py:35
  46.0 4.2 %other_half.1 = bf16[8,8,16,320]{3,2,1,0:T(8,128)(2,1)} custom-call(bf16[10,18,16,1024]{3,2,1,0:T(8,128)(2,1)S(1)} %get-tuple-element.45.shifted, bf16[9,160,512]{2,1,0:T(8,128)(2,1)S(1)} %collective-permute-done.10.far, bf16[9,80,480]{2,1,0:T(8,128)(2,1)S(1)} %collective-permute-done.11.near_low, bf16[9,80,480]{2,1,0:T(8,128)(2,1)S(1)} %collective-permute-done.12.near_high, ...), custom_call_target="tpu_custom_call" | custom-call | flops 1 | bytes 1 | tf_op jit(solution)/shard_map/other_half/pallas_call | solution.py:283
  50.2 0.9 %collective-permute-done.14.one = bf16[9,80,512]{2,1,0:T(8,128)(2,1)S(1)} collective-permute-done((bf16[9,80,512]{2,1,0:T(8,128)(2,1)S(1)}, bf16[9,80,512]{2,1,0:T(8,128)(2,1)S(1)}, u32[]{:S(2)}, u32[]{:S(2)}) %collective-permute-start.14) | collective-permute-done | bytes 737312 | tf_op jit(solution)/shard_map/ppermute | solution.py:35
  51.1 0.6 collective-permute-done.15.three
  51.7 0.4 fold.1
  52.1 3.0 %collective-permute-start.16 = (bf16[180,512]{1,0:T(8,128)(2,1)S(1)}, bf16[180,512]{1,0:T(8,128)(2,1)S(1)}, u32[]{:S(2)}, u32[]{:S(2)}) collective-permute-start(bf16[180,512]{1,0:T(8,128)(2,1)S(1)} %get-tuple-element.58), channel_id=1, source_target_pairs={{0,4},{1,5},{2,6},{3,7},{4,0},{5,1},{6,2},{7,3},{8,12},{9,13},{10,... | collective-permute-start | bytes 552968 | tf_op jit(solution)/shard_map/ppermute | solution.py:35
  55.1 2.2 %collective-permute-start.17 = (bf16[180,512]{1,0:T(8,128)(2,1)S(1)}, bf16[180,512]{1,0:T(8,128)(2,1)S(1)}, u32[]{:S(2)}, u32[]{:S(2)}) collective-permute-start(bf16[180,512]{1,0:T(8,128)(2,1)S(1)} %get-tuple-element.59), channel_id=1, source_target_pairs={{0,2},{1,3},{2,0},{3,1},{4,6},{5,7},{6,4},{7,5},{8,10},{9,11},{10,... | collective-permute-start | bytes 552968 | tf_op jit(solution)/shard_map/ppermute | solution.py:35
  57.3 0.8 %collective-permute-done.16.r1 = bf16[180,512]{1,0:T(8,128)(2,1)S(1)} collective-permute-done((bf16[180,512]{1,0:T(8,128)(2,1)S(1)}, bf16[180,512]{1,0:T(8,128)(2,1)S(1)}, u32[]{:S(2)}, u32[]{:S(2)}) %collective-permute-start.16) | collective-permute-done | bytes 184352 | tf_op jit(solution)/shard_map/ppermute | solution.py:35
  58.1 4.5 %collective-permute-done.17.r2 = bf16[180,512]{1,0:T(8,128)(2,1)S(1)} collective-permute-done((bf16[180,512]{1,0:T(8,128)(2,1)S(1)}, bf16[180,512]{1,0:T(8,128)(2,1)S(1)}, u32[]{:S(2)}, u32[]{:S(2)}) %collective-permute-start.17) | collective-permute-done | bytes 184352 | tf_op jit(solution)/shard_map/ppermute | solution.py:35
  62.6 0.6 collective-permute-done.18.r3
  63.2 0.2 cut.1
  63.4 0.1 collective-permute-start.19
  63.5 3.7 %collective-permute-start.20 = (bf16[45,512]{1,0:T(8,128)(2,1)S(1)}, bf16[45,512]{1,0:T(8,128)(2,1)S(1)}, u32[]{:S(2)}, u32[]{:S(2)}) collective-permute-start(bf16[45,512]{1,0:T(8,128)(2,1)S(1)} %get-tuple-element.63), channel_id=1, source_target_pairs={{0,24},{1,8},{2,26},{3,10},{4,28},{5,12},{6,30},{7,14},{8,16},{9,0... | collective-permute-start | bytes 138248 | tf_op jit(solution)/shard_map/ppermute | solution.py:35
  67.2 2.5 %collective-permute-start.22 = (bf16[45,512]{1,0:T(8,128)(2,1)S(1)}, bf16[45,512]{1,0:T(8,128)(2,1)S(1)}, u32[]{:S(2)}, u32[]{:S(2)}) collective-permute-start(bf16[45,512]{1,0:T(8,128)(2,1)S(1)} %get-tuple-element.65), channel_id=1, source_target_pairs={{0,0},{1,24},{2,2},{3,26},{4,4},{5,28},{6,6},{7,30},{8,8},{9,16},{... | collective-permute-start | bytes 138248 | tf_op jit(solution)/shard_map/ppermute | solution.py:35
  69.8 1.2 %collective-permute-done.21.r3 = bf16[45,512]{1,0:T(8,128)(2,1)S(1)} collective-permute-done((bf16[45,512]{1,0:T(8,128)(2,1)S(1)}, bf16[45,512]{1,0:T(8,128)(2,1)S(1)}, u32[]{:S(2)}, u32[]{:S(2)}) %collective-permute-start.21) | collective-permute-done | bytes 46112 | tf_op jit(solution)/shard_map/ppermute | solution.py:35
  71.0 2.8 %collective-permute-done.22.r4 = bf16[45,512]{1,0:T(8,128)(2,1)S(1)} collective-permute-done((bf16[45,512]{1,0:T(8,128)(2,1)S(1)}, bf16[45,512]{1,0:T(8,128)(2,1)S(1)}, u32[]{:S(2)}, u32[]{:S(2)}) %collective-permute-start.22) | collective-permute-done | bytes 46112 | tf_op jit(solution)/shard_map/ppermute | solution.py:35
  73.8 0.8 %last.1 = f32[5,27,160]{2,1,0:T(8,128)} custom-call(f32[45,512]{1,0:T(8,128)S(1)} %get-tuple-element.61.mine, bf16[45,512]{1,0:T(8,128)(2,1)S(1)} %collective-permute-done.19.r1, bf16[45,512]{1,0:T(8,128)(2,1)S(1)} %collective-permute-done.20.r2, bf16[45,512]{1,0:T(8,128)(2,1)S(1)} %collective-permute-done.21.r3, bf16[45,512]{1,0:T(8,128)(2,1)S(1)} %collective-permute-done.22.r4), custom_call_target="tpu_custom_call" | custom-call | flops 1 | bytes 1 | tf_op jit(solution)/shard_map/last/pallas_call | solution.py:352
  (15 shorter events, 0.0 us)
Async XLA Ops:
  0.6 4.7 %collective-permute-start.3 = (bf16[8,8,16,320]{3,2,1,0:T(8,128)(2,1)}, bf16[8,8,16,320]{3,2,1,0:T(8,128)(2,1)S(1)}, u32[]{:S(2)}, u32[]{:S(2)}) collective-permute-start(bf16[8,8,16,320]{3,2,1,0:T(8,128)(2,1)} %own.2), channel_id=1, source_target_pairs={{0,16},{1,17},{2,18},{3,19},{4,20},{5,21},{6,22},{7,23},{8,24},{9,... | collective-permute-start | bytes 1966088 | tf_op jit(solution)/shard_map/ppermute | solution.py:35
  2.1 6.9 %collective-permute-start.2 = (bf16[8,8,16,320]{3,2,1,0:T(8,128)(2,1)}, bf16[8,8,16,320]{3,2,1,0:T(8,128)(2,1)S(1)}, u32[]{:S(2)}, u32[]{:S(2)}) collective-permute-start(bf16[8,8,16,320]{3,2,1,0:T(8,128)(2,1)} %g.3), channel_id=1, source_target_pairs={{0,16},{1,17},{2,18},{3,19},{4,20},{5,21},{6,22},{7,23},{8,24},{9,... | collective-permute-start | bytes 1966088 | tf_op jit(solution)/shard_map/ppermute | solution.py:35
  3.1 5.9 %copy-start.1 = (bf16[8,8,16,320]{3,2,1,0:T(8,128)(2,1)S(1)}, bf16[8,8,16,320]{3,2,1,0:T(8,128)(2,1)}, u32[]{:S(2)}) copy-start(bf16[8,8,16,320]{3,2,1,0:T(8,128)(2,1)} %g.3) | copy-start | bytes 1966084
  3.1 5.9 %collective-permute-start.1 = (bf16[8,16,320]{2,1,0:T(8,128)(2,1)S(1)}, bf16[8,16,320]{2,1,0:T(8,128)(2,1)S(1)}, u32[]{:S(2)}, u32[]{:S(2)}) collective-permute-start(bf16[8,16,320]{2,1,0:T(8,128)(2,1)S(1)} %dynamic-slice_bitcast_fusion), channel_id=1, source_target_pairs={{0,96},{1,97},{2,98},{3,99},{4,100},{5,101},{6,102},{7,103},{8,104... | collective-permute-start | bytes 245768 | tf_op jit(solution)/shard_map/ppermute | solution.py:35
  4.9 4.1 %collective-permute-start = (bf16[8,16,320]{2,1,0:T(8,128)(2,1)S(1)}, bf16[8,16,320]{2,1,0:T(8,128)(2,1)S(1)}, u32[]{:S(2)}, u32[]{:S(2)}) collective-permute-start(bf16[8,16,320]{2,1,0:T(8,128)(2,1)S(1)} %dynamic-slice_bitcast_fusion), channel_id=1, source_target_pairs={{0,112},{1,113},{2,114},{3,115},{4,116},{5,117},{6,118},{7,119},{8... | collective-permute-start | bytes 245768 | tf_op jit(solution)/shard_map/ppermute | solution.py:35
  5.3 1.1 %copy-start.2 = (bf16[8,8,16,320]{3,2,1,0:T(8,128)(2,1)S(1)}, bf16[8,8,16,320]{3,2,1,0:T(8,128)(2,1)}, u32[]{:S(2)}) copy-start(bf16[8,8,16,320]{3,2,1,0:T(8,128)(2,1)} %own.2) | copy-start | bytes 1966084
  6.5 9.0 %copy-start = (bf16[27,160,320]{2,1,0:T(8,128)(2,1)S(1)}, bf16[27,160,320]{2,1,0:T(8,128)(2,1)}, u32[]{:S(2)}) copy-start(bf16[27,160,320]{2,1,0:T(8,128)(2,1)} %own.3) | copy-start | bytes 8294404
  9.6 11.5 %collective-permute-start.4 = (bf16[18,8,320]{2,1,0:T(8,128)(2,1)S(1)}, bf16[18,8,320]{2,1,0:T(8,128)(2,1)S(1)}, u32[]{:S(2)}, u32[]{:S(2)}) collective-permute-start(bf16[18,8,320]{2,1,0:T(8,128)(2,1)S(1)} %get-tuple-element.38), channel_id=1, source_target_pairs={{0,2},{1,3},{2,0},{3,1},{4,6},{5,7},{6,4},{7,5},{8,10},{9,11},{10,... | collective-permute-start | bytes 276488 | tf_op jit(solution)/shard_map/ppermute | solution.py:35
  14.7 6.3 %collective-permute-start.6 = (bf16[9,16,320]{2,1,0:T(8,128)(2,1)S(1)}, bf16[9,16,320]{2,1,0:T(8,128)(2,1)S(1)}, u32[]{:S(2)}, u32[]{:S(2)}) collective-permute-start(bf16[9,16,320]{2,1,0:T(8,128)(2,1)S(1)} %get-tuple-element.40), channel_id=1, source_target_pairs={{0,1},{1,0},{2,3},{3,2},{4,5},{5,4},{6,7},{7,6},{8,9},{9,8},{10,11... | collective-permute-start | bytes 276488 | tf_op jit(solution)/shard_map/ppermute | solution.py:35
  15.1 5.9 %collective-permute-start.5 = (bf16[18,320]{1,0:T(8,128)(2,1)S(1)}, bf16[18,320]{1,0:T(8,128)(2,1)S(1)}, u32[]{:S(2)}, u32[]{:S(2)}) collective-permute-start(bf16[18,320]{1,0:T(8,128)(2,1)S(1)} %get-tuple-element.39.after), channel_id=1, source_target_pairs={{0,3},{1,2},{2,1},{3,0},{4,7},{5,6},{6,5},{7,4},{8,11},{9,10},{10,... | collective-permute-start | bytes 34568 | tf_op jit(solution)/shard_map/ppermute | solution.py:35
  21.1 19.7 %collective-permute-start.10 = (bf16[9,160,512]{2,1,0:T(8,128)(2,1)S(1)}, bf16[9,160,512]{2,1,0:T(8,128)(2,1)S(1)}, u32[]{:S(2)}, u32[]{:S(2)}) collective-permute-start(bf16[9,160,512]{2,1,0:T(8,128)(2,1)S(1)} %flip.1), channel_id=1, source_target_pairs={{0,1},{1,0},{2,3},{3,2},{4,5},{5,4},{6,7},{7,6},{8,9},{9,8},{10,11... | collective-permute-start | bytes 4423688 | tf_op jit(solution)/shard_map/ppermute | solution.py:35
  21.5 1.7 %collective-permute-start.7 = (bf16[18,8,320]{2,1,0:T(8,128)(2,1)S(1)}, bf16[18,8,320]{2,1,0:T(8,128)(2,1)S(1)}, u32[]{:S(2)}, u32[]{:S(2)}) collective-permute-start(bf16[18,8,320]{2,1,0:T(8,128)(2,1)S(1)} %collective-permute-done.4.line), channel_id=1, source_target_pairs={{0,16},{1,17},{2,18},{3,19},{4,20},{5,21},{6,22},{7,23},{8,24},{9,... | collective-permute-start | bytes 276488 | tf_op jit(solution)/shard_map/ppermute | solution.py:35
  21.8 1.4 %collective-permute-start.8 = (bf16[9,16,320]{2,1,0:T(8,128)(2,1)S(1)}, bf16[9,16,320]{2,1,0:T(8,128)(2,1)S(1)}, u32[]{:S(2)}, u32[]{:S(2)}) collective-permute-start(bf16[9,16,320]{2,1,0:T(8,128)(2,1)S(1)} %collective-permute-done.6.half), channel_id=1, source_target_pairs={{0,16},{1,17},{2,18},{3,19},{4,20},{5,21},{6,22},{7,23},{8,24},{9,... | collective-permute-start | bytes 276488 | tf_op jit(solution)/shard_map/ppermute | solution.py:35
  22.0 1.2 %collective-permute-start.9 = (bf16[18,320]{1,0:T(8,128)(2,1)S(1)}, bf16[18,320]{1,0:T(8,128)(2,1)S(1)}, u32[]{:S(2)}, u32[]{:S(2)}) collective-permute-start(bf16[18,320]{1,0:T(8,128)(2,1)S(1)} %collective-permute-done.5.corner), channel_id=1, source_target_pairs={{0,16},{1,17},{2,18},{3,19},{4,20},{5,21},{6,22},{7,23},{8,24},{9,... | collective-permute-start | bytes 34568 | tf_op jit(solution)/shard_map/ppermute | solution.py:35
  31.4 18.8 %collective-permute-start.13 = (bf16[9,80,512]{2,1,0:T(8,128)(2,1)S(1)}, bf16[9,80,512]{2,1,0:T(8,128)(2,1)S(1)}, u32[]{:S(2)}, u32[]{:S(2)}) collective-permute-start(bf16[9,80,512]{2,1,0:T(8,128)(2,1)S(1)} %get-tuple-element.49), channel_id=1, source_target_pairs={{0,64},{1,65},{2,66},{3,67},{4,68},{5,69},{6,70},{7,71},{8,72},{9,... | collective-permute-start | bytes 2211848 | tf_op jit(solution)/shard_map/ppermute | solution.py:35
  34.1 17.0 %collective-permute-start.14 = (bf16[9,80,512]{2,1,0:T(8,128)(2,1)S(1)}, bf16[9,80,512]{2,1,0:T(8,128)(2,1)S(1)}, u32[]{:S(2)}, u32[]{:S(2)}) collective-permute-start(bf16[9,80,512]{2,1,0:T(8,128)(2,1)S(1)} %get-tuple-element.50), channel_id=1, source_target_pairs={{0,32},{1,33},{2,34},{3,35},{4,36},{5,37},{6,38},{7,39},{8,40},{9,... | collective-permute-start | bytes 2211848 | tf_op jit(solution)/shard_map/ppermute | solution.py:35
  34.1 17.6 %collective-permute-start.15 = (bf16[9,80,512]{2,1,0:T(8,128)(2,1)S(1)}, bf16[9,80,512]{2,1,0:T(8,128)(2,1)S(1)}, u32[]{:S(2)}, u32[]{:S(2)}) collective-permute-start(bf16[9,80,512]{2,1,0:T(8,128)(2,1)S(1)} %get-tuple-element.51), channel_id=1, source_target_pairs={{0,96},{1,97},{2,98},{3,99},{4,100},{5,101},{6,102},{7,103},{8,104... | collective-permute-start | bytes 2211848 | tf_op jit(solution)/shard_map/ppermute | solution.py:35
  40.9 4.0 %collective-permute-start.12 = (bf16[9,80,480]{2,1,0:T(8,128)(2,1)S(1)}, bf16[9,80,480]{2,1,0:T(8,128)(2,1)S(1)}, u32[]{:S(2)}, u32[]{:S(2)}) collective-permute-start(bf16[9,80,480]{2,1,0:T(8,128)(2,1)S(1)} %get-tuple-element.66), channel_id=1, source_target_pairs={{0,16},{1,17},{2,18},{3,19},{4,20},{5,21},{6,22},{7,23},{8,24},{9,... | collective-permute-start | bytes 2073608 | tf_op jit(solution)/shard_map/ppermute | solution.py:35
  43.1 2.9 %collective-permute-start.11 = (bf16[9,80,480]{2,1,0:T(8,128)(2,1)S(1)}, bf16[9,80,480]{2,1,0:T(8,128)(2,1)S(1)}, u32[]{:S(2)}, u32[]{:S(2)}) collective-permute-start(bf16[9,80,480]{2,1,0:T(8,128)(2,1)S(1)} %get-tuple-element.67), channel_id=1, source_target_pairs={{0,16},{1,17},{2,18},{3,19},{4,20},{5,21},{6,22},{7,23},{8,24},{9,... | collective-permute-start | bytes 2073608 | tf_op jit(solution)/shard_map/ppermute | solution.py:35
  52.1 6.0 %collective-permute-start.16 = (bf16[180,512]{1,0:T(8,128)(2,1)S(1)}, bf16[180,512]{1,0:T(8,128)(2,1)S(1)}, u32[]{:S(2)}, u32[]{:S(2)}) collective-permute-start(bf16[180,512]{1,0:T(8,128)(2,1)S(1)} %get-tuple-element.58), channel_id=1, source_target_pairs={{0,4},{1,5},{2,6},{3,7},{4,0},{5,1},{6,2},{7,3},{8,12},{9,13},{10,... | collective-permute-start | bytes 552968 | tf_op jit(solution)/shard_map/ppermute | solution.py:35
  55.1 7.5 %collective-permute-start.17 = (bf16[180,512]{1,0:T(8,128)(2,1)S(1)}, bf16[180,512]{1,0:T(8,128)(2,1)S(1)}, u32[]{:S(2)}, u32[]{:S(2)}) collective-permute-start(bf16[180,512]{1,0:T(8,128)(2,1)S(1)} %get-tuple-element.59), channel_id=1, source_target_pairs={{0,2},{1,3},{2,0},{3,1},{4,6},{5,7},{6,4},{7,5},{8,10},{9,11},{10,... | collective-permute-start | bytes 552968 | tf_op jit(solution)/shard_map/ppermute | solution.py:35
  57.3 5.9 %collective-permute-start.18 = (bf16[180,512]{1,0:T(8,128)(2,1)S(1)}, bf16[180,512]{1,0:T(8,128)(2,1)S(1)}, u32[]{:S(2)}, u32[]{:S(2)}) collective-permute-start(bf16[180,512]{1,0:T(8,128)(2,1)S(1)} %get-tuple-element.60), channel_id=1, source_target_pairs={{0,6},{1,7},{2,4},{3,5},{4,2},{5,3},{6,0},{7,1},{8,14},{9,15},{10,... | collective-permute-start | bytes 552968 | tf_op jit(solution)/shard_map/ppermute | solution.py:35
  63.4 6.3 %collective-permute-start.19 = (bf16[45,512]{1,0:T(8,128)(2,1)S(1)}, bf16[45,512]{1,0:T(8,128)(2,1)S(1)}, u32[]{:S(2)}, u32[]{:S(2)}) collective-permute-start(bf16[45,512]{1,0:T(8,128)(2,1)S(1)} %get-tuple-element.62), channel_id=1, source_target_pairs={{0,16},{1,0},{2,18},{3,2},{4,20},{5,4},{6,22},{7,6},{8,24},{9,8},{... | collective-permute-start | bytes 138248 | tf_op jit(solution)/shard_map/ppermute | solution.py:35
  63.5 6.3 %collective-permute-start.20 = (bf16[45,512]{1,0:T(8,128)(2,1)S(1)}, bf16[45,512]{1,0:T(8,128)(2,1)S(1)}, u32[]{:S(2)}, u32[]{:S(2)}) collective-permute-start(bf16[45,512]{1,0:T(8,128)(2,1)S(1)} %get-tuple-element.63), channel_id=1, source_target_pairs={{0,24},{1,8},{2,26},{3,10},{4,28},{5,12},{6,30},{7,14},{8,16},{9,0... | collective-permute-start | bytes 138248 | tf_op jit(solution)/shard_map/ppermute | solution.py:35
  67.2 3.8 %collective-permute-start.21 = (bf16[45,512]{1,0:T(8,128)(2,1)S(1)}, bf16[45,512]{1,0:T(8,128)(2,1)S(1)}, u32[]{:S(2)}, u32[]{:S(2)}) collective-permute-start(bf16[45,512]{1,0:T(8,128)(2,1)S(1)} %get-tuple-element.64), channel_id=1, source_target_pairs={{0,8},{1,16},{2,10},{3,18},{4,12},{5,20},{6,14},{7,22},{8,0},{9,24... | collective-permute-start | bytes 138248 | tf_op jit(solution)/shard_map/ppermute | solution.py:35
  67.2 6.6 %collective-permute-start.22 = (bf16[45,512]{1,0:T(8,128)(2,1)S(1)}, bf16[45,512]{1,0:T(8,128)(2,1)S(1)}, u32[]{:S(2)}, u32[]{:S(2)}) collective-permute-start(bf16[45,512]{1,0:T(8,128)(2,1)S(1)} %get-tuple-element.65), channel_id=1, source_target_pairs={{0,0},{1,24},{2,2},{3,26},{4,4},{5,28},{6,6},{7,30},{8,8},{9,16},{... | collective-permute-start | bytes 138248 | tf_op jit(solution)/shard_map/ppermute | solution.py:35

commit v6 on v5

--- a/solution.py
+++ b/solution.py
@@ -44,6 +44,7 @@
 
 
 BRIEF = pl.CostEstimate(flops=1, bytes_accessed=1, transcendentals=0)
+LONG = pl.CostEstimate(flops=4 * 10**10, bytes_accessed=10**7, transcendentals=0)
 
 
 def sds(shape, dtype):
@@ -193,7 +194,7 @@
         out_shape=(sds((10, 18, 16, LANES), BF), sds((9, 80, HALF), F32), piece, piece, piece),
         scratch_shapes=[pltpu.VMEM((18, 16, C), BF)],
         compiler_params=params(28),
-        cost_estimate=BRIEF,
+        cost_estimate=LONG,
         name="tiles",
     )(*operands)
 

time: 74.8 us -> 73.8 us (0.987)
  waiting for transfers between devices: 21.7 us -> 20.8 us
    ppermute x23, waiting for transfers between devices: 21.7 us -> 20.8 us  [send(): return lax.ppermute(value, AXES, routes(to))]
  transfers between devices with their start and end apart: 23 -> 23, of which waited for: 13 -> 11; matrix products, arithmetic and copies ran while one was open for 1% -> 1% of each run, Pallas kernels for 27% -> 27%
where the time goes in v6:
time: 73.8 us; the launch traced here: 73.7 us
  starting transfers between devices  28 us (38%)
  Pallas kernels  21.9 us (30%)
  waiting for transfers between devices  20.8 us (28%)
  local copies, waits for them, and re-layouts  2.16 us (3%)
  between operations  0.76 us (1%)
    ppermute x23, starting transfers between devices, send(): return lax.ppermute(value, AXES, routes(to))  28 us
    ppermute x23, waiting for transfers between devices, send(): return lax.ppermute(value, AXES, routes(to))  20.8 us
    pallas_call x1, Pallas kernels, tiles(): pl.pallas_call(tiles_kernel, out_shape=(sds((10, 18, 16, LANES), BF), sds...  8.26 us
    pallas_call x1, Pallas kernels, own_half(): pl.pallas_call(own_kernel, out_shape=sds((C, 1024), F32), compiler_params...  5.16 us
    pallas_call x1, Pallas kernels, other_half(): pl.pallas_call(other_kernel, out_shape=sds((8, 8, 16, C), BF), scratch_sh...  4.21 us
  transfers between devices with their start and end apart: 23, of which 11 were waited for; matrix products, arithmetic and copies ran while one was open for 1% of the time, Pallas kernels for 27%

profile of v6, /device:TPU:1, one launch (start us, length us, event | category | flops | bytes accessed | tf_op | source)
XLA Modules:
  0.0 73.7 jit_solution(15696497361682755508)
XLA Ops:
  0.6 1.5 %collective-permute-start.3 = (bf16[8,8,16,320]{3,2,1,0:T(8,128)(2,1)}, bf16[8,8,16,320]{3,2,1,0:T(8,128)(2,1)S(1)}, u32[]{:S(2)}, u32[]{:S(2)}) collective-permute-start(bf16[8,8,16,320]{3,2,1,0:T(8,128)(2,1)} %own.2), channel_id=1, source_target_pairs={{0,16},{1,17},{2,18},{3,19},{4,20},{5,21},{6,22},{7,23},{8,24},{9,... | collective-permute-start | bytes 1966088 | tf_op jit(solution)/shard_map/ppermute | solution.py:35
  2.1 0.1 collective-permute-start.2
  2.2 0.9 %dynamic-slice_bitcast_fusion = bf16[8,16,320]{2,1,0:T(8,128)(2,1)S(1)} fusion(bf16[8,8,16,320]{3,2,1,0:T(8,128)(2,1)} %g.3, s32[]{:T(128)S(6)} %select_n.11), kind=kLoop, calls=%fused_computation | loop fusion | bytes 163844 | tf_op jit(solution)/shard_map/reshape | solution.py:368
  3.1 0.0 copy-start.1
  3.1 1.8 %collective-permute-start.1 = (bf16[8,16,320]{2,1,0:T(8,128)(2,1)S(1)}, bf16[8,16,320]{2,1,0:T(8,128)(2,1)S(1)}, u32[]{:S(2)}, u32[]{:S(2)}) collective-permute-start(bf16[8,16,320]{2,1,0:T(8,128)(2,1)S(1)} %dynamic-slice_bitcast_fusion), channel_id=1, source_target_pairs={{0,96},{1,97},{2,98},{3,99},{4,100},{5,101},{6,102},{7,103},{8,104... | collective-permute-start | bytes 245768 | tf_op jit(solution)/shard_map/ppermute | solution.py:35
  4.9 0.4 collective-permute-start
  5.3 0.0 collective-permute-done.3.other
  5.3 1.1 %copy-done.2 = bf16[8,8,16,320]{3,2,1,0:T(8,128)(2,1)S(1)} copy-done((bf16[8,8,16,320]{3,2,1,0:T(8,128)(2,1)S(1)}, bf16[8,8,16,320]{3,2,1,0:T(8,128)(2,1)}, u32[]{:S(2)}) %copy-start.2) | copy-done | bytes 655384
  6.5 1.1 %turn.1.turned = bf16[320,2048]{1,0:T(8,128)(2,1)S(1)} custom-call(bf16[8,8,16,320]{3,2,1,0:T(8,128)(2,1)S(1)} %copy-done.2, bf16[8,8,16,320]{3,2,1,0:T(8,128)(2,1)S(1)} %collective-permute-done.3.other), custom_call_target="tpu_custom_call" | custom-call | flops 1 | bytes 1 | tf_op jit(solution)/shard_map/turn/pallas_call | solution.py:122
  7.5 1.5 %collective-permute-done.1.beta = bf16[8,16,320]{2,1,0:T(8,128)(2,1)S(1)} collective-permute-done((bf16[8,16,320]{2,1,0:T(8,128)(2,1)S(1)}, bf16[8,16,320]{2,1,0:T(8,128)(2,1)S(1)}, u32[]{:S(2)}, u32[]{:S(2)}) %collective-permute-start.1) | collective-permute-done | bytes 81952 | tf_op jit(solution)/shard_map/ppermute | solution.py:35
  9.1 0.0 collective-permute-done.alpha
  9.1 0.0 collective-permute-done.2.other
  9.1 0.5 edges.1
  9.6 5.2 %collective-permute-start.4 = (bf16[18,8,320]{2,1,0:T(8,128)(2,1)S(1)}, bf16[18,8,320]{2,1,0:T(8,128)(2,1)S(1)}, u32[]{:S(2)}, u32[]{:S(2)}) collective-permute-start(bf16[18,8,320]{2,1,0:T(8,128)(2,1)S(1)} %get-tuple-element.38), channel_id=1, source_target_pairs={{0,2},{1,3},{2,0},{3,1},{4,6},{5,7},{6,4},{7,5},{8,10},{9,11},{10,... | collective-permute-start | bytes 276488 | tf_op jit(solution)/shard_map/ppermute | solution.py:35
  14.7 0.4 collective-permute-start.6
  15.1 0.3 collective-permute-start.5
  15.4 1.3 %flip.1 = bf16[9,160,512]{2,1,0:T(8,128)(2,1)S(1)} custom-call(bf16[27,160,320]{2,1,0:T(8,128)(2,1)S(1)} %copy-done, bf16[18,320]{1,0:T(8,128)(2,1)S(1)} %get-tuple-element.39.after), custom_call_target="tpu_custom_call" | custom-call | flops 1 | bytes 1 | tf_op jit(solution)/shard_map/flip/pallas_call | solution.py:219
  16.8 4.3 %collective-permute-done.5.corner = bf16[18,320]{1,0:T(8,128)(2,1)S(1)} collective-permute-done((bf16[18,320]{1,0:T(8,128)(2,1)S(1)}, bf16[18,320]{1,0:T(8,128)(2,1)S(1)}, u32[]{:S(2)}, u32[]{:S(2)}) %collective-permute-start.5) | collective-permute-done | bytes 11552 | tf_op jit(solution)/shard_map/ppermute | solution.py:35
  21.1 0.2 collective-permute-start.7
  21.3 0.3 collective-permute-start.8
  21.6 0.2 collective-permute-start.9
  21.8 1.9 %collective-permute-start.10 = (bf16[9,160,512]{2,1,0:T(8,128)(2,1)S(1)}, bf16[9,160,512]{2,1,0:T(8,128)(2,1)S(1)}, u32[]{:S(2)}, u32[]{:S(2)}) collective-permute-start(bf16[9,160,512]{2,1,0:T(8,128)(2,1)S(1)} %flip.1), channel_id=1, source_target_pairs={{0,1},{1,0},{2,3},{3,2},{4,5},{5,4},{6,7},{7,6},{8,9},{9,8},{10,11... | collective-permute-start | bytes 4423688 | tf_op jit(solution)/shard_map/ppermute | solution.py:35
  23.7 8.3 %tiles.1 = (bf16[10,18,16,1024]{3,2,1,0:T(8,128)(2,1)S(1)}, f32[9,80,512]{2,1,0:T(8,128)S(1)}, bf16[9,80,512]{2,1,0:T(8,128)(2,1)S(1)}, bf16[9,80,512]{2,1,0:T(8,128)(2,1)S(1)}, bf16[9,80,512]{2,1,0:T(8,128)(2,1)S(1)}) custom-call(bf16[8,8,16,320]{3,2,1,0:T(8,128)(2,1)S(1)} %copy-done.1, bf16[8,8,16,320]{3,2,1,0:T(8,128)(2,1)S(1)} %collective-permute-done.2.other, ...), custom_call_target="tpu_custom_call" | custom-call | flops 40000000000 | bytes 10000000 | tf_op jit(solution)/shard_map/tiles/pallas_call | solution.py:192
  32.0 2.7 %collective-permute-start.13 = (bf16[9,80,512]{2,1,0:T(8,128)(2,1)S(1)}, bf16[9,80,512]{2,1,0:T(8,128)(2,1)S(1)}, u32[]{:S(2)}, u32[]{:S(2)}) collective-permute-start(bf16[9,80,512]{2,1,0:T(8,128)(2,1)S(1)} %get-tuple-element.49), channel_id=1, source_target_pairs={{0,64},{1,65},{2,66},{3,67},{4,68},{5,69},{6,70},{7,71},{8,72},{9,... | collective-permute-start | bytes 2211848 | tf_op jit(solution)/shard_map/ppermute | solution.py:35
  34.7 0.8 %collective-permute-start.15 = (bf16[9,80,512]{2,1,0:T(8,128)(2,1)S(1)}, bf16[9,80,512]{2,1,0:T(8,128)(2,1)S(1)}, u32[]{:S(2)}, u32[]{:S(2)}) collective-permute-start(bf16[9,80,512]{2,1,0:T(8,128)(2,1)S(1)} %get-tuple-element.51), channel_id=1, source_target_pairs={{0,96},{1,97},{2,98},{3,99},{4,100},{5,101},{6,102},{7,103},{8,104... | collective-permute-start | bytes 2211848 | tf_op jit(solution)/shard_map/ppermute | solution.py:35
  35.5 5.2 %own_half.1.partial = f32[320,1024]{1,0:T(8,128)S(1)} custom-call(bf16[10,18,16,1024]{3,2,1,0:T(8,128)(2,1)S(1)} %get-tuple-element.45.shifted, bf16[27,160,320]{2,1,0:T(8,128)(2,1)S(1)} %copy-done), custom_call_target="tpu_custom_call" | custom-call | flops 1 | bytes 1 | tf_op jit(solution)/shard_map/own_half/pallas_call | solution.py:253
  40.7 0.9 %collective-permute-done.10.far = bf16[9,160,512]{2,1,0:T(8,128)(2,1)S(1)} collective-permute-done((bf16[9,160,512]{2,1,0:T(8,128)(2,1)S(1)}, bf16[9,160,512]{2,1,0:T(8,128)(2,1)S(1)}, u32[]{:S(2)}, u32[]{:S(2)}) %collective-permute-start.10) | collective-permute-done | bytes 1474592 | tf_op jit(solution)/shard_map/ppermute | solution.py:35
  41.5 0.1 fusion
  41.7 1.1 %collective-permute-start.12 = (bf16[9,80,480]{2,1,0:T(8,128)(2,1)S(1)}, bf16[9,80,480]{2,1,0:T(8,128)(2,1)S(1)}, u32[]{:S(2)}, u32[]{:S(2)}) collective-permute-start(bf16[9,80,480]{2,1,0:T(8,128)(2,1)S(1)} %get-tuple-element.66), channel_id=1, source_target_pairs={{0,16},{1,17},{2,18},{3,19},{4,20},{5,21},{6,22},{7,23},{8,24},{9,... | collective-permute-start | bytes 2073608 | tf_op jit(solution)/shard_map/ppermute | solution.py:35
  42.7 0.1 collective-permute-start.11
  42.8 1.7 %collective-permute-done.12.near_high = bf16[9,80,480]{2,1,0:T(8,128)(2,1)S(1)} collective-permute-done((bf16[9,80,480]{2,1,0:T(8,128)(2,1)S(1)}, bf16[9,80,480]{2,1,0:T(8,128)(2,1)S(1)}, u32[]{:S(2)}, u32[]{:S(2)}) %collective-permute-start.12) | collective-permute-done | bytes 691232 | tf_op jit(solution)/shard_map/ppermute | solution.py:35
  44.6 1.1 %collective-permute-done.11.near_low = bf16[9,80,480]{2,1,0:T(8,128)(2,1)S(1)} collective-permute-done((bf16[9,80,480]{2,1,0:T(8,128)(2,1)S(1)}, bf16[9,80,480]{2,1,0:T(8,128)(2,1)S(1)}, u32[]{:S(2)}, u32[]{:S(2)}) %collective-permute-start.11) | collective-permute-done | bytes 691232 | tf_op jit(solution)/shard_map/ppermute | solution.py:35
  45.6 4.2 %other_half.1 = bf16[8,8,16,320]{3,2,1,0:T(8,128)(2,1)} custom-call(bf16[10,18,16,1024]{3,2,1,0:T(8,128)(2,1)S(1)} %get-tuple-element.45.shifted, bf16[9,160,512]{2,1,0:T(8,128)(2,1)S(1)} %collective-permute-done.10.far, bf16[9,80,480]{2,1,0:T(8,128)(2,1)S(1)} %collective-permute-done.11.near_low, bf16[9,80,480]{2,1,0:T(8,128)(2,1)S(1)} %collective-permute-done.12.near_high, ...), custom_call_target="tpu_custom_call" | custom-call | flops 1 | bytes 1 | tf_op jit(solution)/shard_map/other_half/pallas_call | solution.py:284
  49.8 1.9 %collective-permute-done.14.one = bf16[9,80,512]{2,1,0:T(8,128)(2,1)S(1)} collective-permute-done((bf16[9,80,512]{2,1,0:T(8,128)(2,1)S(1)}, bf16[9,80,512]{2,1,0:T(8,128)(2,1)S(1)}, u32[]{:S(2)}, u32[]{:S(2)}) %collective-permute-start.14) | collective-permute-done | bytes 737312 | tf_op jit(solution)/shard_map/ppermute | solution.py:35
  51.7 0.4 collective-permute-done.15.three
  52.2 0.4 fold.1
  52.6 2.1 %collective-permute-start.16 = (bf16[180,512]{1,0:T(8,128)(2,1)S(1)}, bf16[180,512]{1,0:T(8,128)(2,1)S(1)}, u32[]{:S(2)}, u32[]{:S(2)}) collective-permute-start(bf16[180,512]{1,0:T(8,128)(2,1)S(1)} %get-tuple-element.58), channel_id=1, source_target_pairs={{0,4},{1,5},{2,6},{3,7},{4,0},{5,1},{6,2},{7,3},{8,12},{9,13},{10,... | collective-permute-start | bytes 552968 | tf_op jit(solution)/shard_map/ppermute | solution.py:35
  54.7 2.2 %collective-permute-start.17 = (bf16[180,512]{1,0:T(8,128)(2,1)S(1)}, bf16[180,512]{1,0:T(8,128)(2,1)S(1)}, u32[]{:S(2)}, u32[]{:S(2)}) collective-permute-start(bf16[180,512]{1,0:T(8,128)(2,1)S(1)} %get-tuple-element.59), channel_id=1, source_target_pairs={{0,2},{1,3},{2,0},{3,1},{4,6},{5,7},{6,4},{7,5},{8,10},{9,11},{10,... | collective-permute-start | bytes 552968 | tf_op jit(solution)/shard_map/ppermute | solution.py:35
  57.0 1.6 %collective-permute-done.16.r1 = bf16[180,512]{1,0:T(8,128)(2,1)S(1)} collective-permute-done((bf16[180,512]{1,0:T(8,128)(2,1)S(1)}, bf16[180,512]{1,0:T(8,128)(2,1)S(1)}, u32[]{:S(2)}, u32[]{:S(2)}) %collective-permute-start.16) | collective-permute-done | bytes 184352 | tf_op jit(solution)/shard_map/ppermute | solution.py:35
  58.6 3.7 %collective-permute-done.17.r2 = bf16[180,512]{1,0:T(8,128)(2,1)S(1)} collective-permute-done((bf16[180,512]{1,0:T(8,128)(2,1)S(1)}, bf16[180,512]{1,0:T(8,128)(2,1)S(1)}, u32[]{:S(2)}, u32[]{:S(2)}) %collective-permute-start.17) | collective-permute-done | bytes 184352 | tf_op jit(solution)/shard_map/ppermute | solution.py:35
  62.3 0.6 collective-permute-done.18.r3
  62.9 0.2 cut.1
  63.0 0.1 collective-permute-start.19
  63.1 2.0 %collective-permute-start.20 = (bf16[45,512]{1,0:T(8,128)(2,1)S(1)}, bf16[45,512]{1,0:T(8,128)(2,1)S(1)}, u32[]{:S(2)}, u32[]{:S(2)}) collective-permute-start(bf16[45,512]{1,0:T(8,128)(2,1)S(1)} %get-tuple-element.63), channel_id=1, source_target_pairs={{0,24},{1,8},{2,26},{3,10},{4,28},{5,12},{6,30},{7,14},{8,16},{9,0... | collective-permute-start | bytes 138248 | tf_op jit(solution)/shard_map/ppermute | solution.py:35
  65.1 1.1 %collective-permute-start.21 = (bf16[45,512]{1,0:T(8,128)(2,1)S(1)}, bf16[45,512]{1,0:T(8,128)(2,1)S(1)}, u32[]{:S(2)}, u32[]{:S(2)}) collective-permute-start(bf16[45,512]{1,0:T(8,128)(2,1)S(1)} %get-tuple-element.64), channel_id=1, source_target_pairs={{0,8},{1,16},{2,10},{3,18},{4,12},{5,20},{6,14},{7,22},{8,0},{9,24... | collective-permute-start | bytes 138248 | tf_op jit(solution)/shard_map/ppermute | solution.py:35
  66.2 3.6 %collective-permute-start.22 = (bf16[45,512]{1,0:T(8,128)(2,1)S(1)}, bf16[45,512]{1,0:T(8,128)(2,1)S(1)}, u32[]{:S(2)}, u32[]{:S(2)}) collective-permute-start(bf16[45,512]{1,0:T(8,128)(2,1)S(1)} %get-tuple-element.65), channel_id=1, source_target_pairs={{0,0},{1,24},{2,2},{3,26},{4,4},{5,28},{6,6},{7,30},{8,8},{9,16},{... | collective-permute-start | bytes 138248 | tf_op jit(solution)/shard_map/ppermute | solution.py:35
  69.8 3.0 %collective-permute-done.22.r4 = bf16[45,512]{1,0:T(8,128)(2,1)S(1)} collective-permute-done((bf16[45,512]{1,0:T(8,128)(2,1)S(1)}, bf16[45,512]{1,0:T(8,128)(2,1)S(1)}, u32[]{:S(2)}, u32[]{:S(2)}) %collective-permute-start.22) | collective-permute-done | bytes 46112 | tf_op jit(solution)/shard_map/ppermute | solution.py:35
  72.8 0.8 %last.1 = f32[5,27,160]{2,1,0:T(8,128)} custom-call(f32[45,512]{1,0:T(8,128)S(1)} %get-tuple-element.61.mine, bf16[45,512]{1,0:T(8,128)(2,1)S(1)} %collective-permute-done.19.r1, bf16[45,512]{1,0:T(8,128)(2,1)S(1)} %collective-permute-done.20.r2, bf16[45,512]{1,0:T(8,128)(2,1)S(1)} %collective-permute-done.21.r3, bf16[45,512]{1,0:T(8,128)(2,1)S(1)} %collective-permute-done.22.r4), custom_call_target="tpu_custom_call" | custom-call | flops 1 | bytes 1 | tf_op jit(solution)/shard_map/last/pallas_call | solution.py:353
  (15 shorter events, 0.0 us)
Async XLA Ops:
  0.6 4.7 %collective-permute-start.3 = (bf16[8,8,16,320]{3,2,1,0:T(8,128)(2,1)}, bf16[8,8,16,320]{3,2,1,0:T(8,128)(2,1)S(1)}, u32[]{:S(2)}, u32[]{:S(2)}) collective-permute-start(bf16[8,8,16,320]{3,2,1,0:T(8,128)(2,1)} %own.2), channel_id=1, source_target_pairs={{0,16},{1,17},{2,18},{3,19},{4,20},{5,21},{6,22},{7,23},{8,24},{9,... | collective-permute-start | bytes 1966088 | tf_op jit(solution)/shard_map/ppermute | solution.py:35
  2.1 6.9 %collective-permute-start.2 = (bf16[8,8,16,320]{3,2,1,0:T(8,128)(2,1)}, bf16[8,8,16,320]{3,2,1,0:T(8,128)(2,1)S(1)}, u32[]{:S(2)}, u32[]{:S(2)}) collective-permute-start(bf16[8,8,16,320]{3,2,1,0:T(8,128)(2,1)} %g.3), channel_id=1, source_target_pairs={{0,16},{1,17},{2,18},{3,19},{4,20},{5,21},{6,22},{7,23},{8,24},{9,... | collective-permute-start | bytes 1966088 | tf_op jit(solution)/shard_map/ppermute | solution.py:35
  3.1 5.9 %copy-start.1 = (bf16[8,8,16,320]{3,2,1,0:T(8,128)(2,1)S(1)}, bf16[8,8,16,320]{3,2,1,0:T(8,128)(2,1)}, u32[]{:S(2)}) copy-start(bf16[8,8,16,320]{3,2,1,0:T(8,128)(2,1)} %g.3) | copy-start | bytes 1966084
  3.1 5.9 %collective-permute-start.1 = (bf16[8,16,320]{2,1,0:T(8,128)(2,1)S(1)}, bf16[8,16,320]{2,1,0:T(8,128)(2,1)S(1)}, u32[]{:S(2)}, u32[]{:S(2)}) collective-permute-start(bf16[8,16,320]{2,1,0:T(8,128)(2,1)S(1)} %dynamic-slice_bitcast_fusion), channel_id=1, source_target_pairs={{0,96},{1,97},{2,98},{3,99},{4,100},{5,101},{6,102},{7,103},{8,104... | collective-permute-start | bytes 245768 | tf_op jit(solution)/shard_map/ppermute | solution.py:35
  4.9 4.1 %collective-permute-start = (bf16[8,16,320]{2,1,0:T(8,128)(2,1)S(1)}, bf16[8,16,320]{2,1,0:T(8,128)(2,1)S(1)}, u32[]{:S(2)}, u32[]{:S(2)}) collective-permute-start(bf16[8,16,320]{2,1,0:T(8,128)(2,1)S(1)} %dynamic-slice_bitcast_fusion), channel_id=1, source_target_pairs={{0,112},{1,113},{2,114},{3,115},{4,116},{5,117},{6,118},{7,119},{8... | collective-permute-start | bytes 245768 | tf_op jit(solution)/shard_map/ppermute | solution.py:35
  5.3 1.1 %copy-start.2 = (bf16[8,8,16,320]{3,2,1,0:T(8,128)(2,1)S(1)}, bf16[8,8,16,320]{3,2,1,0:T(8,128)(2,1)}, u32[]{:S(2)}) copy-start(bf16[8,8,16,320]{3,2,1,0:T(8,128)(2,1)} %own.2) | copy-start | bytes 1966084
  6.5 9.0 %copy-start = (bf16[27,160,320]{2,1,0:T(8,128)(2,1)S(1)}, bf16[27,160,320]{2,1,0:T(8,128)(2,1)}, u32[]{:S(2)}) copy-start(bf16[27,160,320]{2,1,0:T(8,128)(2,1)} %own.3) | copy-start | bytes 8294404
  9.6 11.5 %collective-permute-start.4 = (bf16[18,8,320]{2,1,0:T(8,128)(2,1)S(1)}, bf16[18,8,320]{2,1,0:T(8,128)(2,1)S(1)}, u32[]{:S(2)}, u32[]{:S(2)}) collective-permute-start(bf16[18,8,320]{2,1,0:T(8,128)(2,1)S(1)} %get-tuple-element.38), channel_id=1, source_target_pairs={{0,2},{1,3},{2,0},{3,1},{4,6},{5,7},{6,4},{7,5},{8,10},{9,11},{10,... | collective-permute-start | bytes 276488 | tf_op jit(solution)/shard_map/ppermute | solution.py:35
  14.7 6.3 %collective-permute-start.6 = (bf16[9,16,320]{2,1,0:T(8,128)(2,1)S(1)}, bf16[9,16,320]{2,1,0:T(8,128)(2,1)S(1)}, u32[]{:S(2)}, u32[]{:S(2)}) collective-permute-start(bf16[9,16,320]{2,1,0:T(8,128)(2,1)S(1)} %get-tuple-element.40), channel_id=1, source_target_pairs={{0,1},{1,0},{2,3},{3,2},{4,5},{5,4},{6,7},{7,6},{8,9},{9,8},{10,11... | collective-permute-start | bytes 276488 | tf_op jit(solution)/shard_map/ppermute | solution.py:35
  15.1 5.9 %collective-permute-start.5 = (bf16[18,320]{1,0:T(8,128)(2,1)S(1)}, bf16[18,320]{1,0:T(8,128)(2,1)S(1)}, u32[]{:S(2)}, u32[]{:S(2)}) collective-permute-start(bf16[18,320]{1,0:T(8,128)(2,1)S(1)} %get-tuple-element.39.after), channel_id=1, source_target_pairs={{0,3},{1,2},{2,1},{3,0},{4,7},{5,6},{6,5},{7,4},{8,11},{9,10},{10,... | collective-permute-start | bytes 34568 | tf_op jit(solution)/shard_map/ppermute | solution.py:35
  21.1 2.6 %collective-permute-start.7 = (bf16[18,8,320]{2,1,0:T(8,128)(2,1)S(1)}, bf16[18,8,320]{2,1,0:T(8,128)(2,1)S(1)}, u32[]{:S(2)}, u32[]{:S(2)}) collective-permute-start(bf16[18,8,320]{2,1,0:T(8,128)(2,1)S(1)} %collective-permute-done.4.line), channel_id=1, source_target_pairs={{0,16},{1,17},{2,18},{3,19},{4,20},{5,21},{6,22},{7,23},{8,24},{9,... | collective-permute-start | bytes 276488 | tf_op jit(solution)/shard_map/ppermute | solution.py:35
  21.3 2.4 %collective-permute-start.8 = (bf16[9,16,320]{2,1,0:T(8,128)(2,1)S(1)}, bf16[9,16,320]{2,1,0:T(8,128)(2,1)S(1)}, u32[]{:S(2)}, u32[]{:S(2)}) collective-permute-start(bf16[9,16,320]{2,1,0:T(8,128)(2,1)S(1)} %collective-permute-done.6.half), channel_id=1, source_target_pairs={{0,16},{1,17},{2,18},{3,19},{4,20},{5,21},{6,22},{7,23},{8,24},{9,... | collective-permute-start | bytes 276488 | tf_op jit(solution)/shard_map/ppermute | solution.py:35
  21.6 2.1 %collective-permute-start.9 = (bf16[18,320]{1,0:T(8,128)(2,1)S(1)}, bf16[18,320]{1,0:T(8,128)(2,1)S(1)}, u32[]{:S(2)}, u32[]{:S(2)}) collective-permute-start(bf16[18,320]{1,0:T(8,128)(2,1)S(1)} %collective-permute-done.5.corner), channel_id=1, source_target_pairs={{0,16},{1,17},{2,18},{3,19},{4,20},{5,21},{6,22},{7,23},{8,24},{9,... | collective-permute-start | bytes 34568 | tf_op jit(solution)/shard_map/ppermute | solution.py:35
  21.8 19.7 %collective-permute-start.10 = (bf16[9,160,512]{2,1,0:T(8,128)(2,1)S(1)}, bf16[9,160,512]{2,1,0:T(8,128)(2,1)S(1)}, u32[]{:S(2)}, u32[]{:S(2)}) collective-permute-start(bf16[9,160,512]{2,1,0:T(8,128)(2,1)S(1)} %flip.1), channel_id=1, source_target_pairs={{0,1},{1,0},{2,3},{3,2},{4,5},{5,4},{6,7},{7,6},{8,9},{9,8},{10,11... | collective-permute-start | bytes 4423688 | tf_op jit(solution)/shard_map/ppermute | solution.py:35
  32.0 17.8 %collective-permute-start.13 = (bf16[9,80,512]{2,1,0:T(8,128)(2,1)S(1)}, bf16[9,80,512]{2,1,0:T(8,128)(2,1)S(1)}, u32[]{:S(2)}, u32[]{:S(2)}) collective-permute-start(bf16[9,80,512]{2,1,0:T(8,128)(2,1)S(1)} %get-tuple-element.49), channel_id=1, source_target_pairs={{0,64},{1,65},{2,66},{3,67},{4,68},{5,69},{6,70},{7,71},{8,72},{9,... | collective-permute-start | bytes 2211848 | tf_op jit(solution)/shard_map/ppermute | solution.py:35
  34.7 17.0 %collective-permute-start.14 = (bf16[9,80,512]{2,1,0:T(8,128)(2,1)S(1)}, bf16[9,80,512]{2,1,0:T(8,128)(2,1)S(1)}, u32[]{:S(2)}, u32[]{:S(2)}) collective-permute-start(bf16[9,80,512]{2,1,0:T(8,128)(2,1)S(1)} %get-tuple-element.50), channel_id=1, source_target_pairs={{0,32},{1,33},{2,34},{3,35},{4,36},{5,37},{6,38},{7,39},{8,40},{9,... | collective-permute-start | bytes 2211848 | tf_op jit(solution)/shard_map/ppermute | solution.py:35
  34.7 17.5 %collective-permute-start.15 = (bf16[9,80,512]{2,1,0:T(8,128)(2,1)S(1)}, bf16[9,80,512]{2,1,0:T(8,128)(2,1)S(1)}, u32[]{:S(2)}, u32[]{:S(2)}) collective-permute-start(bf16[9,80,512]{2,1,0:T(8,128)(2,1)S(1)} %get-tuple-element.51), channel_id=1, source_target_pairs={{0,96},{1,97},{2,98},{3,99},{4,100},{5,101},{6,102},{7,103},{8,104... | collective-permute-start | bytes 2211848 | tf_op jit(solution)/shard_map/ppermute | solution.py:35
  41.7 2.9 %collective-permute-start.12 = (bf16[9,80,480]{2,1,0:T(8,128)(2,1)S(1)}, bf16[9,80,480]{2,1,0:T(8,128)(2,1)S(1)}, u32[]{:S(2)}, u32[]{:S(2)}) collective-permute-start(bf16[9,80,480]{2,1,0:T(8,128)(2,1)S(1)} %get-tuple-element.66), channel_id=1, source_target_pairs={{0,16},{1,17},{2,18},{3,19},{4,20},{5,21},{6,22},{7,23},{8,24},{9,... | collective-permute-start | bytes 2073608 | tf_op jit(solution)/shard_map/ppermute | solution.py:35
  42.7 2.9 %collective-permute-start.11 = (bf16[9,80,480]{2,1,0:T(8,128)(2,1)S(1)}, bf16[9,80,480]{2,1,0:T(8,128)(2,1)S(1)}, u32[]{:S(2)}, u32[]{:S(2)}) collective-permute-start(bf16[9,80,480]{2,1,0:T(8,128)(2,1)S(1)} %get-tuple-element.67), channel_id=1, source_target_pairs={{0,16},{1,17},{2,18},{3,19},{4,20},{5,21},{6,22},{7,23},{8,24},{9,... | collective-permute-start | bytes 2073608 | tf_op jit(solution)/shard_map/ppermute | solution.py:35
  52.6 6.0 %collective-permute-start.16 = (bf16[180,512]{1,0:T(8,128)(2,1)S(1)}, bf16[180,512]{1,0:T(8,128)(2,1)S(1)}, u32[]{:S(2)}, u32[]{:S(2)}) collective-permute-start(bf16[180,512]{1,0:T(8,128)(2,1)S(1)} %get-tuple-element.58), channel_id=1, source_target_pairs={{0,4},{1,5},{2,6},{3,7},{4,0},{5,1},{6,2},{7,3},{8,12},{9,13},{10,... | collective-permute-start | bytes 552968 | tf_op jit(solution)/shard_map/ppermute | solution.py:35
  54.7 7.5 %collective-permute-start.17 = (bf16[180,512]{1,0:T(8,128)(2,1)S(1)}, bf16[180,512]{1,0:T(8,128)(2,1)S(1)}, u32[]{:S(2)}, u32[]{:S(2)}) collective-permute-start(bf16[180,512]{1,0:T(8,128)(2,1)S(1)} %get-tuple-element.59), channel_id=1, source_target_pairs={{0,2},{1,3},{2,0},{3,1},{4,6},{5,7},{6,4},{7,5},{8,10},{9,11},{10,... | collective-permute-start | bytes 552968 | tf_op jit(solution)/shard_map/ppermute | solution.py:35
  57.0 5.9 %collective-permute-start.18 = (bf16[180,512]{1,0:T(8,128)(2,1)S(1)}, bf16[180,512]{1,0:T(8,128)(2,1)S(1)}, u32[]{:S(2)}, u32[]{:S(2)}) collective-permute-start(bf16[180,512]{1,0:T(8,128)(2,1)S(1)} %get-tuple-element.60), channel_id=1, source_target_pairs={{0,6},{1,7},{2,4},{3,5},{4,2},{5,3},{6,0},{7,1},{8,14},{9,15},{10,... | collective-permute-start | bytes 552968 | tf_op jit(solution)/shard_map/ppermute | solution.py:35
  63.0 6.7 %collective-permute-start.19 = (bf16[45,512]{1,0:T(8,128)(2,1)S(1)}, bf16[45,512]{1,0:T(8,128)(2,1)S(1)}, u32[]{:S(2)}, u32[]{:S(2)}) collective-permute-start(bf16[45,512]{1,0:T(8,128)(2,1)S(1)} %get-tuple-element.62), channel_id=1, source_target_pairs={{0,16},{1,0},{2,18},{3,2},{4,20},{5,4},{6,22},{7,6},{8,24},{9,8},{... | collective-permute-start | bytes 138248 | tf_op jit(solution)/shard_map/ppermute | solution.py:35
  63.1 6.6 %collective-permute-start.20 = (bf16[45,512]{1,0:T(8,128)(2,1)S(1)}, bf16[45,512]{1,0:T(8,128)(2,1)S(1)}, u32[]{:S(2)}, u32[]{:S(2)}) collective-permute-start(bf16[45,512]{1,0:T(8,128)(2,1)S(1)} %get-tuple-element.63), channel_id=1, source_target_pairs={{0,24},{1,8},{2,26},{3,10},{4,28},{5,12},{6,30},{7,14},{8,16},{9,0... | collective-permute-start | bytes 138248 | tf_op jit(solution)/shard_map/ppermute | solution.py:35
  65.1 4.7 %collective-permute-start.21 = (bf16[45,512]{1,0:T(8,128)(2,1)S(1)}, bf16[45,512]{1,0:T(8,128)(2,1)S(1)}, u32[]{:S(2)}, u32[]{:S(2)}) collective-permute-start(bf16[45,512]{1,0:T(8,128)(2,1)S(1)} %get-tuple-element.64), channel_id=1, source_target_pairs={{0,8},{1,16},{2,10},{3,18},{4,12},{5,20},{6,14},{7,22},{8,0},{9,24... | collective-permute-start | bytes 138248 | tf_op jit(solution)/shard_map/ppermute | solution.py:35
  66.2 6.6 %collective-permute-start.22 = (bf16[45,512]{1,0:T(8,128)(2,1)S(1)}, bf16[45,512]{1,0:T(8,128)(2,1)S(1)}, u32[]{:S(2)}, u32[]{:S(2)}) collective-permute-start(bf16[45,512]{1,0:T(8,128)(2,1)S(1)} %get-tuple-element.65), channel_id=1, source_target_pairs={{0,0},{1,24},{2,2},{3,26},{4,4},{5,28},{6,6},{7,30},{8,8},{9,16},{... | collective-permute-start | bytes 138248 | tf_op jit(solution)/shard_map/ppermute | solution.py:35

commit v7 on v6

--- a/solution.py
+++ b/solution.py
@@ -124,7 +124,7 @@
         out_shape=sds((C, 2048), BF),
         scratch_shapes=[pltpu.VMEM((8, 16, 16, C), BF)],
         compiler_params=params(12),
-        cost_estimate=BRIEF,
+        cost_estimate=LONG,
         name="turn",
     )(own, other)
 
@@ -169,7 +169,7 @@
             put(src[:, pl.ds(n, 1)].reshape(8, 16, C), at + n)
             return carry
 
-        lax.fori_loop(0, 8, row, 0, unroll=4)
+        lax.fori_loop(0, 8, row, 0, unroll=8)
     put(outer[0], core * 17)
     put(outer[1], 17 - core * 17)
     plane[pl.ds(9 * core, 9)] = half[...]
@@ -413,7 +413,7 @@
         either(lambda a, b, c: (a, b ^ 4, c), lambda a, b, c: (a ^ 1, b, c ^ 1)),
         either(lambda a, b, c: (a, b, c), lambda a, b, c: (a ^ 1, b ^ 4, c ^ 1)),
     )
-    sums = [send(v, to) for v, to in zip(sums, steps)]
+    sums = [send(sums[n], steps[n]) for n in (2, 1, 0, 3)]
     grad_weight = last(scale, mine, *sums)
     return (grad_input, jnp.transpose(grad_weight, (1, 2, 0)))
 

time: 73.8 us -> 73.2 us (level)
  waiting for transfers between devices: 20.8 us -> 18.8 us
  starting transfers between devices: 28 us -> 29.3 us
    ppermute x23, waiting for transfers between devices: 20.8 us -> 18.8 us  [send(): return lax.ppermute(value, AXES, routes(to))]
    ppermute x23, starting transfers between devices: 28 us -> 29.3 us  [send(): return lax.ppermute(value, AXES, routes(to))]
where the time goes in v7:
time: 73.2 us; the launch traced here: 73 us
  starting transfers between devices  29.3 us (40%)
  Pallas kernels  21.9 us (30%)
  waiting for transfers between devices  18.8 us (26%)
  local copies, waits for them, and re-layouts  2.16 us (3%)
  between operations  0.79 us (1%)
    ppermute x23, starting transfers between devices, send(): return lax.ppermute(value, AXES, routes(to))  29.3 us
    ppermute x23, waiting for transfers between devices, send(): return lax.ppermute(value, AXES, routes(to))  18.8 us
    pallas_call x1, Pallas kernels, tiles(): pl.pallas_call(tiles_kernel, out_shape=(sds((10, 18, 16, LANES), BF), sds...  8.25 us
    pallas_call x1, Pallas kernels, own_half(): pl.pallas_call(own_kernel, out_shape=sds((C, 1024), F32), compiler_params...  5.16 us
    pallas_call x1, Pallas kernels, other_half(): pl.pallas_call(other_kernel, out_shape=sds((8, 8, 16, C), BF), scratch_sh...  4.21 us
  transfers between devices with their start and end apart: 23, of which 11 were waited for; matrix products, arithmetic and copies ran while one was open for 1% of the time, Pallas kernels for 27%

profile of v7, /device:TPU:1, one launch (start us, length us, event | category | flops | bytes accessed | tf_op | source)
XLA Modules:
  0.0 73.0 jit_solution(18111307161144106139)
XLA Ops:
  0.6 1.5 %collective-permute-start.3 = (bf16[8,8,16,320]{3,2,1,0:T(8,128)(2,1)}, bf16[8,8,16,320]{3,2,1,0:T(8,128)(2,1)S(1)}, u32[]{:S(2)}, u32[]{:S(2)}) collective-permute-start(bf16[8,8,16,320]{3,2,1,0:T(8,128)(2,1)} %own.2), channel_id=1, source_target_pairs={{0,16},{1,17},{2,18},{3,19},{4,20},{5,21},{6,22},{7,23},{8,24},{9,... | collective-permute-start | bytes 1966088 | tf_op jit(solution)/shard_map/ppermute | solution.py:35
  2.1 0.9 %dynamic-slice_bitcast_fusion = bf16[8,16,320]{2,1,0:T(8,128)(2,1)S(1)} fusion(bf16[8,8,16,320]{3,2,1,0:T(8,128)(2,1)} %g.3, s32[]{:T(128)S(6)} %select_n.11), kind=kLoop, calls=%fused_computation | loop fusion | bytes 163844 | tf_op jit(solution)/shard_map/reshape | solution.py:368
  3.0 0.0 copy-start.1
  3.0 1.8 %collective-permute-start.1 = (bf16[8,16,320]{2,1,0:T(8,128)(2,1)S(1)}, bf16[8,16,320]{2,1,0:T(8,128)(2,1)S(1)}, u32[]{:S(2)}, u32[]{:S(2)}) collective-permute-start(bf16[8,16,320]{2,1,0:T(8,128)(2,1)S(1)} %dynamic-slice_bitcast_fusion), channel_id=1, source_target_pairs={{0,96},{1,97},{2,98},{3,99},{4,100},{5,101},{6,102},{7,103},{8,104... | collective-permute-start | bytes 245768 | tf_op jit(solution)/shard_map/ppermute | solution.py:35
  4.8 0.0 collective-permute-start
  4.9 2.6 %collective-permute-start.2 = (bf16[8,8,16,320]{3,2,1,0:T(8,128)(2,1)}, bf16[8,8,16,320]{3,2,1,0:T(8,128)(2,1)S(1)}, u32[]{:S(2)}, u32[]{:S(2)}) collective-permute-start(bf16[8,8,16,320]{3,2,1,0:T(8,128)(2,1)} %g.3), channel_id=1, source_target_pairs={{0,16},{1,17},{2,18},{3,19},{4,20},{5,21},{6,22},{7,23},{8,24},{9,... | collective-permute-start | bytes 1966088 | tf_op jit(solution)/shard_map/ppermute | solution.py:35
  7.4 0.0 collective-permute-done.3.other
  7.5 1.1 %copy-done.2 = bf16[8,8,16,320]{3,2,1,0:T(8,128)(2,1)S(1)} copy-done((bf16[8,8,16,320]{3,2,1,0:T(8,128)(2,1)S(1)}, bf16[8,8,16,320]{3,2,1,0:T(8,128)(2,1)}, u32[]{:S(2)}) %copy-start.2) | copy-done | bytes 655384
  8.6 1.1 %turn.1.turned = bf16[320,2048]{1,0:T(8,128)(2,1)S(1)} custom-call(bf16[8,8,16,320]{3,2,1,0:T(8,128)(2,1)S(1)} %copy-done.2, bf16[8,8,16,320]{3,2,1,0:T(8,128)(2,1)S(1)} %collective-permute-done.3.other), custom_call_target="tpu_custom_call" | custom-call | flops 40000000000 | bytes 10000000 | tf_op jit(solution)/shard_map/turn/pallas_call | solution.py:122
  9.7 0.0 collective-permute-done.alpha
  9.7 0.5 edges.1
  10.2 5.2 %collective-permute-start.4 = (bf16[18,8,320]{2,1,0:T(8,128)(2,1)S(1)}, bf16[18,8,320]{2,1,0:T(8,128)(2,1)S(1)}, u32[]{:S(2)}, u32[]{:S(2)}) collective-permute-start(bf16[18,8,320]{2,1,0:T(8,128)(2,1)S(1)} %get-tuple-element.38), channel_id=1, source_target_pairs={{0,2},{1,3},{2,0},{3,1},{4,6},{5,7},{6,4},{7,5},{8,10},{9,11},{10,... | collective-permute-start | bytes 276488 | tf_op jit(solution)/shard_map/ppermute | solution.py:35
  15.4 0.4 collective-permute-start.6
  15.8 0.3 collective-permute-start.5
  16.1 1.3 %flip.1 = bf16[9,160,512]{2,1,0:T(8,128)(2,1)S(1)} custom-call(bf16[27,160,320]{2,1,0:T(8,128)(2,1)S(1)} %copy-done, bf16[18,320]{1,0:T(8,128)(2,1)S(1)} %get-tuple-element.39.after), custom_call_target="tpu_custom_call" | custom-call | flops 1 | bytes 1 | tf_op jit(solution)/shard_map/flip/pallas_call | solution.py:219
  17.4 4.3 %collective-permute-done.5.corner = bf16[18,320]{1,0:T(8,128)(2,1)S(1)} collective-permute-done((bf16[18,320]{1,0:T(8,128)(2,1)S(1)}, bf16[18,320]{1,0:T(8,128)(2,1)S(1)}, u32[]{:S(2)}, u32[]{:S(2)}) %collective-permute-start.5) | collective-permute-done | bytes 11552 | tf_op jit(solution)/shard_map/ppermute | solution.py:35
  21.7 0.0 collective-permute-done.4.line
  21.7 0.0 collective-permute-done.6.half
  21.7 0.5 collective-permute-start.8
  22.2 0.1 collective-permute-start.9
  22.3 1.0 %collective-permute-start.10 = (bf16[9,160,512]{2,1,0:T(8,128)(2,1)S(1)}, bf16[9,160,512]{2,1,0:T(8,128)(2,1)S(1)}, u32[]{:S(2)}, u32[]{:S(2)}) collective-permute-start(bf16[9,160,512]{2,1,0:T(8,128)(2,1)S(1)} %flip.1), channel_id=1, source_target_pairs={{0,1},{1,0},{2,3},{3,2},{4,5},{5,4},{6,7},{7,6},{8,9},{9,8},{10,11... | collective-permute-start | bytes 4423688 | tf_op jit(solution)/shard_map/ppermute | solution.py:35
  23.2 0.1 collective-permute-done.9.corner_other
  23.4 8.2 %tiles.1 = (bf16[10,18,16,1024]{3,2,1,0:T(8,128)(2,1)S(1)}, f32[9,80,512]{2,1,0:T(8,128)S(1)}, bf16[9,80,512]{2,1,0:T(8,128)(2,1)S(1)}, bf16[9,80,512]{2,1,0:T(8,128)(2,1)S(1)}, bf16[9,80,512]{2,1,0:T(8,128)(2,1)S(1)}) custom-call(bf16[8,8,16,320]{3,2,1,0:T(8,128)(2,1)S(1)} %copy-done.1, bf16[8,8,16,320]{3,2,1,0:T(8,128)(2,1)S(1)} %collective-permute-done.2.other, ...), custom_call_target="tpu_custom_call" | custom-call | flops 40000000000 | bytes 10000000 | tf_op jit(solution)/shard_map/tiles/pallas_call | solution.py:192
  31.7 2.6 %collective-permute-start.13 = (bf16[9,80,512]{2,1,0:T(8,128)(2,1)S(1)}, bf16[9,80,512]{2,1,0:T(8,128)(2,1)S(1)}, u32[]{:S(2)}, u32[]{:S(2)}) collective-permute-start(bf16[9,80,512]{2,1,0:T(8,128)(2,1)S(1)} %get-tuple-element.49), channel_id=1, source_target_pairs={{0,64},{1,65},{2,66},{3,67},{4,68},{5,69},{6,70},{7,71},{8,72},{9,... | collective-permute-start | bytes 2211848 | tf_op jit(solution)/shard_map/ppermute | solution.py:35
  34.2 0.9 %collective-permute-start.15 = (bf16[9,80,512]{2,1,0:T(8,128)(2,1)S(1)}, bf16[9,80,512]{2,1,0:T(8,128)(2,1)S(1)}, u32[]{:S(2)}, u32[]{:S(2)}) collective-permute-start(bf16[9,80,512]{2,1,0:T(8,128)(2,1)S(1)} %get-tuple-element.51), channel_id=1, source_target_pairs={{0,96},{1,97},{2,98},{3,99},{4,100},{5,101},{6,102},{7,103},{8,104... | collective-permute-start | bytes 2211848 | tf_op jit(solution)/shard_map/ppermute | solution.py:35
  35.2 5.2 %own_half.1.partial = f32[320,1024]{1,0:T(8,128)S(1)} custom-call(bf16[10,18,16,1024]{3,2,1,0:T(8,128)(2,1)S(1)} %get-tuple-element.45.shifted, bf16[27,160,320]{2,1,0:T(8,128)(2,1)S(1)} %copy-done), custom_call_target="tpu_custom_call" | custom-call | flops 1 | bytes 1 | tf_op jit(solution)/shard_map/own_half/pallas_call | solution.py:253
  40.3 1.7 %collective-permute-done.10.far = bf16[9,160,512]{2,1,0:T(8,128)(2,1)S(1)} collective-permute-done((bf16[9,160,512]{2,1,0:T(8,128)(2,1)S(1)}, bf16[9,160,512]{2,1,0:T(8,128)(2,1)S(1)}, u32[]{:S(2)}, u32[]{:S(2)}) %collective-permute-start.10) | collective-permute-done | bytes 1474592 | tf_op jit(solution)/shard_map/ppermute | solution.py:35
  42.0 0.1 fusion
  42.1 0.1 collective-permute-start.12
  42.3 0.4 collective-permute-start.11
  42.7 1.7 %collective-permute-done.12.near_high = bf16[9,80,480]{2,1,0:T(8,128)(2,1)S(1)} collective-permute-done((bf16[9,80,480]{2,1,0:T(8,128)(2,1)S(1)}, bf16[9,80,480]{2,1,0:T(8,128)(2,1)S(1)}, u32[]{:S(2)}, u32[]{:S(2)}) %collective-permute-start.12) | collective-permute-done | bytes 691232 | tf_op jit(solution)/shard_map/ppermute | solution.py:35
  44.4 1.1 %collective-permute-done.11.near_low = bf16[9,80,480]{2,1,0:T(8,128)(2,1)S(1)} collective-permute-done((bf16[9,80,480]{2,1,0:T(8,128)(2,1)S(1)}, bf16[9,80,480]{2,1,0:T(8,128)(2,1)S(1)}, u32[]{:S(2)}, u32[]{:S(2)}) %collective-permute-start.11) | collective-permute-done | bytes 691232 | tf_op jit(solution)/shard_map/ppermute | solution.py:35
  45.5 4.2 %other_half.1 = bf16[8,8,16,320]{3,2,1,0:T(8,128)(2,1)} custom-call(bf16[10,18,16,1024]{3,2,1,0:T(8,128)(2,1)S(1)} %get-tuple-element.45.shifted, bf16[9,160,512]{2,1,0:T(8,128)(2,1)S(1)} %collective-permute-done.10.far, bf16[9,80,480]{2,1,0:T(8,128)(2,1)S(1)} %collective-permute-done.11.near_low, bf16[9,80,480]{2,1,0:T(8,128)(2,1)S(1)} %collective-permute-done.12.near_high, ...), custom_call_target="tpu_custom_call" | custom-call | flops 1 | bytes 1 | tf_op jit(solution)/shard_map/other_half/pallas_call | solution.py:284
  49.7 1.6 %collective-permute-done.14.one = bf16[9,80,512]{2,1,0:T(8,128)(2,1)S(1)} collective-permute-done((bf16[9,80,512]{2,1,0:T(8,128)(2,1)S(1)}, bf16[9,80,512]{2,1,0:T(8,128)(2,1)S(1)}, u32[]{:S(2)}, u32[]{:S(2)}) %collective-permute-start.14) | collective-permute-done | bytes 737312 | tf_op jit(solution)/shard_map/ppermute | solution.py:35
  51.3 0.7 collective-permute-done.15.three
  51.9 0.4 fold.1
  52.3 2.3 %collective-permute-start.16 = (bf16[180,512]{1,0:T(8,128)(2,1)S(1)}, bf16[180,512]{1,0:T(8,128)(2,1)S(1)}, u32[]{:S(2)}, u32[]{:S(2)}) collective-permute-start(bf16[180,512]{1,0:T(8,128)(2,1)S(1)} %get-tuple-element.58), channel_id=1, source_target_pairs={{0,4},{1,5},{2,6},{3,7},{4,0},{5,1},{6,2},{7,3},{8,12},{9,13},{10,... | collective-permute-start | bytes 552968 | tf_op jit(solution)/shard_map/ppermute | solution.py:35
  54.6 1.9 %collective-permute-start.17 = (bf16[180,512]{1,0:T(8,128)(2,1)S(1)}, bf16[180,512]{1,0:T(8,128)(2,1)S(1)}, u32[]{:S(2)}, u32[]{:S(2)}) collective-permute-start(bf16[180,512]{1,0:T(8,128)(2,1)S(1)} %get-tuple-element.59), channel_id=1, source_target_pairs={{0,2},{1,3},{2,0},{3,1},{4,6},{5,7},{6,4},{7,5},{8,10},{9,11},{10,... | collective-permute-start | bytes 552968 | tf_op jit(solution)/shard_map/ppermute | solution.py:35
  56.5 1.9 %collective-permute-done.16.r1 = bf16[180,512]{1,0:T(8,128)(2,1)S(1)} collective-permute-done((bf16[180,512]{1,0:T(8,128)(2,1)S(1)}, bf16[180,512]{1,0:T(8,128)(2,1)S(1)}, u32[]{:S(2)}, u32[]{:S(2)}) %collective-permute-start.16) | collective-permute-done | bytes 184352 | tf_op jit(solution)/shard_map/ppermute | solution.py:35
  58.4 3.4 %collective-permute-done.17.r2 = bf16[180,512]{1,0:T(8,128)(2,1)S(1)} collective-permute-done((bf16[180,512]{1,0:T(8,128)(2,1)S(1)}, bf16[180,512]{1,0:T(8,128)(2,1)S(1)}, u32[]{:S(2)}, u32[]{:S(2)}) %collective-permute-start.17) | collective-permute-done | bytes 184352 | tf_op jit(solution)/shard_map/ppermute | solution.py:35
  61.8 0.6 collective-permute-done.18.r3
  62.4 0.2 cut.1
  62.6 2.1 %collective-permute-start.19 = (bf16[45,512]{1,0:T(8,128)(2,1)S(1)}, bf16[45,512]{1,0:T(8,128)(2,1)S(1)}, u32[]{:S(2)}, u32[]{:S(2)}) collective-permute-start(bf16[45,512]{1,0:T(8,128)(2,1)S(1)} %get-tuple-element.62), channel_id=1, source_target_pairs={{0,8},{1,16},{2,10},{3,18},{4,12},{5,20},{6,14},{7,22},{8,0},{9,24... | collective-permute-start | bytes 138248 | tf_op jit(solution)/shard_map/ppermute | solution.py:35
  64.6 0.3 collective-permute-start.20
  64.9 0.0 collective-permute-start.21
  64.9 5.4 %collective-permute-start.22 = (bf16[45,512]{1,0:T(8,128)(2,1)S(1)}, bf16[45,512]{1,0:T(8,128)(2,1)S(1)}, u32[]{:S(2)}, u32[]{:S(2)}) collective-permute-start(bf16[45,512]{1,0:T(8,128)(2,1)S(1)} %get-tuple-element.65), channel_id=1, source_target_pairs={{0,0},{1,24},{2,2},{3,26},{4,4},{5,28},{6,6},{7,30},{8,8},{9,16},{... | collective-permute-start | bytes 138248 | tf_op jit(solution)/shard_map/ppermute | solution.py:35
  70.4 1.7 %collective-permute-done.22.r4 = bf16[45,512]{1,0:T(8,128)(2,1)S(1)} collective-permute-done((bf16[45,512]{1,0:T(8,128)(2,1)S(1)}, bf16[45,512]{1,0:T(8,128)(2,1)S(1)}, u32[]{:S(2)}, u32[]{:S(2)}) %collective-permute-start.22) | collective-permute-done | bytes 46112 | tf_op jit(solution)/shard_map/ppermute | solution.py:35
  72.1 0.8 %last.1 = f32[5,27,160]{2,1,0:T(8,128)} custom-call(f32[45,512]{1,0:T(8,128)S(1)} %get-tuple-element.61.mine, bf16[45,512]{1,0:T(8,128)(2,1)S(1)} %collective-permute-done.19.r1, bf16[45,512]{1,0:T(8,128)(2,1)S(1)} %collective-permute-done.20.r2, bf16[45,512]{1,0:T(8,128)(2,1)S(1)} %collective-permute-done.21.r3, bf16[45,512]{1,0:T(8,128)(2,1)S(1)} %collective-permute-done.22.r4), custom_call_target="tpu_custom_call" | custom-call | flops 1 | bytes 1 | tf_op jit(solution)/shard_map/last/pallas_call | solution.py:353
  (15 shorter events, 0.0 us)
Async XLA Ops:
  0.6 6.8 %collective-permute-start.3 = (bf16[8,8,16,320]{3,2,1,0:T(8,128)(2,1)}, bf16[8,8,16,320]{3,2,1,0:T(8,128)(2,1)S(1)}, u32[]{:S(2)}, u32[]{:S(2)}) collective-permute-start(bf16[8,8,16,320]{3,2,1,0:T(8,128)(2,1)} %own.2), channel_id=1, source_target_pairs={{0,16},{1,17},{2,18},{3,19},{4,20},{5,21},{6,22},{7,23},{8,24},{9,... | collective-permute-start | bytes 1966088 | tf_op jit(solution)/shard_map/ppermute | solution.py:35
  3.0 6.6 %copy-start.1 = (bf16[8,8,16,320]{3,2,1,0:T(8,128)(2,1)S(1)}, bf16[8,8,16,320]{3,2,1,0:T(8,128)(2,1)}, u32[]{:S(2)}) copy-start(bf16[8,8,16,320]{3,2,1,0:T(8,128)(2,1)} %g.3) | copy-start | bytes 1966084
  3.0 6.6 %collective-permute-start.1 = (bf16[8,16,320]{2,1,0:T(8,128)(2,1)S(1)}, bf16[8,16,320]{2,1,0:T(8,128)(2,1)S(1)}, u32[]{:S(2)}, u32[]{:S(2)}) collective-permute-start(bf16[8,16,320]{2,1,0:T(8,128)(2,1)S(1)} %dynamic-slice_bitcast_fusion), channel_id=1, source_target_pairs={{0,96},{1,97},{2,98},{3,99},{4,100},{5,101},{6,102},{7,103},{8,104... | collective-permute-start | bytes 245768 | tf_op jit(solution)/shard_map/ppermute | solution.py:35
  4.8 4.8 %collective-permute-start = (bf16[8,16,320]{2,1,0:T(8,128)(2,1)S(1)}, bf16[8,16,320]{2,1,0:T(8,128)(2,1)S(1)}, u32[]{:S(2)}, u32[]{:S(2)}) collective-permute-start(bf16[8,16,320]{2,1,0:T(8,128)(2,1)S(1)} %dynamic-slice_bitcast_fusion), channel_id=1, source_target_pairs={{0,112},{1,113},{2,114},{3,115},{4,116},{5,117},{6,118},{7,119},{8... | collective-permute-start | bytes 245768 | tf_op jit(solution)/shard_map/ppermute | solution.py:35
  4.9 4.8 %collective-permute-start.2 = (bf16[8,8,16,320]{3,2,1,0:T(8,128)(2,1)}, bf16[8,8,16,320]{3,2,1,0:T(8,128)(2,1)S(1)}, u32[]{:S(2)}, u32[]{:S(2)}) collective-permute-start(bf16[8,8,16,320]{3,2,1,0:T(8,128)(2,1)} %g.3), channel_id=1, source_target_pairs={{0,16},{1,17},{2,18},{3,19},{4,20},{5,21},{6,22},{7,23},{8,24},{9,... | collective-permute-start | bytes 1966088 | tf_op jit(solution)/shard_map/ppermute | solution.py:35
  7.5 1.1 %copy-start.2 = (bf16[8,8,16,320]{3,2,1,0:T(8,128)(2,1)S(1)}, bf16[8,8,16,320]{3,2,1,0:T(8,128)(2,1)}, u32[]{:S(2)}) copy-start(bf16[8,8,16,320]{3,2,1,0:T(8,128)(2,1)} %own.2) | copy-start | bytes 1966084
  8.6 7.5 %copy-start = (bf16[27,160,320]{2,1,0:T(8,128)(2,1)S(1)}, bf16[27,160,320]{2,1,0:T(8,128)(2,1)}, u32[]{:S(2)}) copy-start(bf16[27,160,320]{2,1,0:T(8,128)(2,1)} %own.3) | copy-start | bytes 8294404
  10.2 11.5 %collective-permute-start.4 = (bf16[18,8,320]{2,1,0:T(8,128)(2,1)S(1)}, bf16[18,8,320]{2,1,0:T(8,128)(2,1)S(1)}, u32[]{:S(2)}, u32[]{:S(2)}) collective-permute-start(bf16[18,8,320]{2,1,0:T(8,128)(2,1)S(1)} %get-tuple-element.38), channel_id=1, source_target_pairs={{0,2},{1,3},{2,0},{3,1},{4,6},{5,7},{6,4},{7,5},{8,10},{9,11},{10,... | collective-permute-start | bytes 276488 | tf_op jit(solution)/shard_map/ppermute | solution.py:35
  15.4 6.3 %collective-permute-start.6 = (bf16[9,16,320]{2,1,0:T(8,128)(2,1)S(1)}, bf16[9,16,320]{2,1,0:T(8,128)(2,1)S(1)}, u32[]{:S(2)}, u32[]{:S(2)}) collective-permute-start(bf16[9,16,320]{2,1,0:T(8,128)(2,1)S(1)} %get-tuple-element.40), channel_id=1, source_target_pairs={{0,1},{1,0},{2,3},{3,2},{4,5},{5,4},{6,7},{7,6},{8,9},{9,8},{10,11... | collective-permute-start | bytes 276488 | tf_op jit(solution)/shard_map/ppermute | solution.py:35
  15.8 5.9 %collective-permute-start.5 = (bf16[18,320]{1,0:T(8,128)(2,1)S(1)}, bf16[18,320]{1,0:T(8,128)(2,1)S(1)}, u32[]{:S(2)}, u32[]{:S(2)}) collective-permute-start(bf16[18,320]{1,0:T(8,128)(2,1)S(1)} %get-tuple-element.39.after), channel_id=1, source_target_pairs={{0,3},{1,2},{2,1},{3,0},{4,7},{5,6},{6,5},{7,4},{8,11},{9,10},{10,... | collective-permute-start | bytes 34568 | tf_op jit(solution)/shard_map/ppermute | solution.py:35
  21.7 1.7 %collective-permute-start.7 = (bf16[18,8,320]{2,1,0:T(8,128)(2,1)S(1)}, bf16[18,8,320]{2,1,0:T(8,128)(2,1)S(1)}, u32[]{:S(2)}, u32[]{:S(2)}) collective-permute-start(bf16[18,8,320]{2,1,0:T(8,128)(2,1)S(1)} %collective-permute-done.4.line), channel_id=1, source_target_pairs={{0,16},{1,17},{2,18},{3,19},{4,20},{5,21},{6,22},{7,23},{8,24},{9,... | collective-permute-start | bytes 276488 | tf_op jit(solution)/shard_map/ppermute | solution.py:35
  21.7 1.7 %collective-permute-start.8 = (bf16[9,16,320]{2,1,0:T(8,128)(2,1)S(1)}, bf16[9,16,320]{2,1,0:T(8,128)(2,1)S(1)}, u32[]{:S(2)}, u32[]{:S(2)}) collective-permute-start(bf16[9,16,320]{2,1,0:T(8,128)(2,1)S(1)} %collective-permute-done.6.half), channel_id=1, source_target_pairs={{0,16},{1,17},{2,18},{3,19},{4,20},{5,21},{6,22},{7,23},{8,24},{9,... | collective-permute-start | bytes 276488 | tf_op jit(solution)/shard_map/ppermute | solution.py:35
  22.2 1.2 %collective-permute-start.9 = (bf16[18,320]{1,0:T(8,128)(2,1)S(1)}, bf16[18,320]{1,0:T(8,128)(2,1)S(1)}, u32[]{:S(2)}, u32[]{:S(2)}) collective-permute-start(bf16[18,320]{1,0:T(8,128)(2,1)S(1)} %collective-permute-done.5.corner), channel_id=1, source_target_pairs={{0,16},{1,17},{2,18},{3,19},{4,20},{5,21},{6,22},{7,23},{8,24},{9,... | collective-permute-start | bytes 34568 | tf_op jit(solution)/shard_map/ppermute | solution.py:35
  22.3 19.7 %collective-permute-start.10 = (bf16[9,160,512]{2,1,0:T(8,128)(2,1)S(1)}, bf16[9,160,512]{2,1,0:T(8,128)(2,1)S(1)}, u32[]{:S(2)}, u32[]{:S(2)}) collective-permute-start(bf16[9,160,512]{2,1,0:T(8,128)(2,1)S(1)} %flip.1), channel_id=1, source_target_pairs={{0,1},{1,0},{2,3},{3,2},{4,5},{5,4},{6,7},{7,6},{8,9},{9,8},{10,11... | collective-permute-start | bytes 4423688 | tf_op jit(solution)/shard_map/ppermute | solution.py:35
  31.7 18.0 %collective-permute-start.13 = (bf16[9,80,512]{2,1,0:T(8,128)(2,1)S(1)}, bf16[9,80,512]{2,1,0:T(8,128)(2,1)S(1)}, u32[]{:S(2)}, u32[]{:S(2)}) collective-permute-start(bf16[9,80,512]{2,1,0:T(8,128)(2,1)S(1)} %get-tuple-element.49), channel_id=1, source_target_pairs={{0,64},{1,65},{2,66},{3,67},{4,68},{5,69},{6,70},{7,71},{8,72},{9,... | collective-permute-start | bytes 2211848 | tf_op jit(solution)/shard_map/ppermute | solution.py:35
  34.2 17.0 %collective-permute-start.14 = (bf16[9,80,512]{2,1,0:T(8,128)(2,1)S(1)}, bf16[9,80,512]{2,1,0:T(8,128)(2,1)S(1)}, u32[]{:S(2)}, u32[]{:S(2)}) collective-permute-start(bf16[9,80,512]{2,1,0:T(8,128)(2,1)S(1)} %get-tuple-element.50), channel_id=1, source_target_pairs={{0,32},{1,33},{2,34},{3,35},{4,36},{5,37},{6,38},{7,39},{8,40},{9,... | collective-permute-start | bytes 2211848 | tf_op jit(solution)/shard_map/ppermute | solution.py:35
  34.2 17.7 %collective-permute-start.15 = (bf16[9,80,512]{2,1,0:T(8,128)(2,1)S(1)}, bf16[9,80,512]{2,1,0:T(8,128)(2,1)S(1)}, u32[]{:S(2)}, u32[]{:S(2)}) collective-permute-start(bf16[9,80,512]{2,1,0:T(8,128)(2,1)S(1)} %get-tuple-element.51), channel_id=1, source_target_pairs={{0,96},{1,97},{2,98},{3,99},{4,100},{5,101},{6,102},{7,103},{8,104... | collective-permute-start | bytes 2211848 | tf_op jit(solution)/shard_map/ppermute | solution.py:35
  42.1 2.3 %collective-permute-start.12 = (bf16[9,80,480]{2,1,0:T(8,128)(2,1)S(1)}, bf16[9,80,480]{2,1,0:T(8,128)(2,1)S(1)}, u32[]{:S(2)}, u32[]{:S(2)}) collective-permute-start(bf16[9,80,480]{2,1,0:T(8,128)(2,1)S(1)} %get-tuple-element.66), channel_id=1, source_target_pairs={{0,16},{1,17},{2,18},{3,19},{4,20},{5,21},{6,22},{7,23},{8,24},{9,... | collective-permute-start | bytes 2073608 | tf_op jit(solution)/shard_map/ppermute | solution.py:35
  42.3 3.2 %collective-permute-start.11 = (bf16[9,80,480]{2,1,0:T(8,128)(2,1)S(1)}, bf16[9,80,480]{2,1,0:T(8,128)(2,1)S(1)}, u32[]{:S(2)}, u32[]{:S(2)}) collective-permute-start(bf16[9,80,480]{2,1,0:T(8,128)(2,1)S(1)} %get-tuple-element.67), channel_id=1, source_target_pairs={{0,16},{1,17},{2,18},{3,19},{4,20},{5,21},{6,22},{7,23},{8,24},{9,... | collective-permute-start | bytes 2073608 | tf_op jit(solution)/shard_map/ppermute | solution.py:35
  52.3 6.0 %collective-permute-start.16 = (bf16[180,512]{1,0:T(8,128)(2,1)S(1)}, bf16[180,512]{1,0:T(8,128)(2,1)S(1)}, u32[]{:S(2)}, u32[]{:S(2)}) collective-permute-start(bf16[180,512]{1,0:T(8,128)(2,1)S(1)} %get-tuple-element.58), channel_id=1, source_target_pairs={{0,4},{1,5},{2,6},{3,7},{4,0},{5,1},{6,2},{7,3},{8,12},{9,13},{10,... | collective-permute-start | bytes 552968 | tf_op jit(solution)/shard_map/ppermute | solution.py:35
  54.6 7.2 %collective-permute-start.17 = (bf16[180,512]{1,0:T(8,128)(2,1)S(1)}, bf16[180,512]{1,0:T(8,128)(2,1)S(1)}, u32[]{:S(2)}, u32[]{:S(2)}) collective-permute-start(bf16[180,512]{1,0:T(8,128)(2,1)S(1)} %get-tuple-element.59), channel_id=1, source_target_pairs={{0,2},{1,3},{2,0},{3,1},{4,6},{5,7},{6,4},{7,5},{8,10},{9,11},{10,... | collective-permute-start | bytes 552968 | tf_op jit(solution)/shard_map/ppermute | solution.py:35
  56.5 5.9 %collective-permute-start.18 = (bf16[180,512]{1,0:T(8,128)(2,1)S(1)}, bf16[180,512]{1,0:T(8,128)(2,1)S(1)}, u32[]{:S(2)}, u32[]{:S(2)}) collective-permute-start(bf16[180,512]{1,0:T(8,128)(2,1)S(1)} %get-tuple-element.60), channel_id=1, source_target_pairs={{0,6},{1,7},{2,4},{3,5},{4,2},{5,3},{6,0},{7,1},{8,14},{9,15},{10,... | collective-permute-start | bytes 552968 | tf_op jit(solution)/shard_map/ppermute | solution.py:35
  62.6 7.8 %collective-permute-start.19 = (bf16[45,512]{1,0:T(8,128)(2,1)S(1)}, bf16[45,512]{1,0:T(8,128)(2,1)S(1)}, u32[]{:S(2)}, u32[]{:S(2)}) collective-permute-start(bf16[45,512]{1,0:T(8,128)(2,1)S(1)} %get-tuple-element.62), channel_id=1, source_target_pairs={{0,8},{1,16},{2,10},{3,18},{4,12},{5,20},{6,14},{7,22},{8,0},{9,24... | collective-permute-start | bytes 138248 | tf_op jit(solution)/shard_map/ppermute | solution.py:35
  64.6 5.7 %collective-permute-start.20 = (bf16[45,512]{1,0:T(8,128)(2,1)S(1)}, bf16[45,512]{1,0:T(8,128)(2,1)S(1)}, u32[]{:S(2)}, u32[]{:S(2)}) collective-permute-start(bf16[45,512]{1,0:T(8,128)(2,1)S(1)} %get-tuple-element.63), channel_id=1, source_target_pairs={{0,24},{1,8},{2,26},{3,10},{4,28},{5,12},{6,30},{7,14},{8,16},{9,0... | collective-permute-start | bytes 138248 | tf_op jit(solution)/shard_map/ppermute | solution.py:35
  64.9 5.5 %collective-permute-start.21 = (bf16[45,512]{1,0:T(8,128)(2,1)S(1)}, bf16[45,512]{1,0:T(8,128)(2,1)S(1)}, u32[]{:S(2)}, u32[]{:S(2)}) collective-permute-start(bf16[45,512]{1,0:T(8,128)(2,1)S(1)} %get-tuple-element.64), channel_id=1, source_target_pairs={{0,16},{1,0},{2,18},{3,2},{4,20},{5,4},{6,22},{7,6},{8,24},{9,8},{... | collective-permute-start | bytes 138248 | tf_op jit(solution)/shard_map/ppermute | solution.py:35
  64.9 7.2 %collective-permute-start.22 = (bf16[45,512]{1,0:T(8,128)(2,1)S(1)}, bf16[45,512]{1,0:T(8,128)(2,1)S(1)}, u32[]{:S(2)}, u32[]{:S(2)}) collective-permute-start(bf16[45,512]{1,0:T(8,128)(2,1)S(1)} %get-tuple-element.65), channel_id=1, source_target_pairs={{0,0},{1,24},{2,2},{3,26},{4,4},{5,28},{6,6},{7,30},{8,8},{9,16},{... | collective-permute-start | bytes 138248 | tf_op jit(solution)/shard_map/ppermute | solution.py:35

commit v8 on v7

--- a/solution.py
+++ b/solution.py
@@ -377,10 +377,10 @@
     def side(a, b):
         return b ^ 1 if a % 2 == 0 else (b + 2 * (b % 2) - 1) % 8
 
+    plane = send(plane, lambda a, b, c: (a, b, c ^ 1))
     line = send(line, lambda a, b, c: (a, side(a, b), c))
     corner = send(corner, lambda a, b, c: (a, side(a, b), c ^ 1))
-    plane = send(plane, lambda a, b, c: (a, b, c ^ 1))
-    line, corner, plane, quarter = lax.optimization_barrier((line, corner, plane, quarter))
+    plane, line, corner, quarter = lax.optimization_barrier((plane, line, corner, quarter))
     line_other, corner_other, plane_other = swap_core(line), swap_core(corner), swap_core(plane)
 
     far = send(quarter, lambda a, b, c: (a, b ^ (4 * (a % 2)), c ^ 1))

time: 73.2 us -> 73.8 us (level)
  waiting for transfers between devices: 18.8 us -> 19.7 us
    ppermute x23, waiting for transfers between devices: 18.8 us -> 19.7 us  [send(): return lax.ppermute(value, AXES, routes(to))]
where the time goes in v8:
time: 73.8 us; the launch traced here: 73.6 us
  starting transfers between devices  29.1 us (39%)
  Pallas kernels  21.9 us (30%)
  waiting for transfers between devices  19.7 us (27%)
  local copies, waits for them, and re-layouts  2.16 us (3%)
  between operations  0.79 us (1%)
    ppermute x23, starting transfers between devices, send(): return lax.ppermute(value, AXES, routes(to))  29.1 us
    ppermute x23, waiting for transfers between devices, send(): return lax.ppermute(value, AXES, routes(to))  19.7 us
    pallas_call x1, Pallas kernels, tiles(): pl.pallas_call(tiles_kernel, out_shape=(sds((10, 18, 16, LANES), BF), sds...  8.25 us
    pallas_call x1, Pallas kernels, own_half(): pl.pallas_call(own_kernel, out_shape=sds((C, 1024), F32), compiler_params...  5.16 us
    pallas_call x1, Pallas kernels, other_half(): pl.pallas_call(other_kernel, out_shape=sds((8, 8, 16, C), BF), scratch_sh...  4.21 us
  transfers between devices with their start and end apart: 23, of which 11 were waited for; matrix products, arithmetic and copies ran while one was open for 1% of the time, Pallas kernels for 27%

profile of v8, /device:TPU:1, one launch (start us, length us, event | category | flops | bytes accessed | tf_op | source)
XLA Modules:
  0.0 73.6 jit_solution(3016227108329075235)
XLA Ops:
  0.6 1.5 %collective-permute-start.3 = (bf16[8,8,16,320]{3,2,1,0:T(8,128)(2,1)}, bf16[8,8,16,320]{3,2,1,0:T(8,128)(2,1)S(1)}, u32[]{:S(2)}, u32[]{:S(2)}) collective-permute-start(bf16[8,8,16,320]{3,2,1,0:T(8,128)(2,1)} %own.2), channel_id=1, source_target_pairs={{0,16},{1,17},{2,18},{3,19},{4,20},{5,21},{6,22},{7,23},{8,24},{9,... | collective-permute-start | bytes 1966088 | tf_op jit(solution)/shard_map/ppermute | solution.py:35
  2.1 0.9 %dynamic-slice_bitcast_fusion = bf16[8,16,320]{2,1,0:T(8,128)(2,1)S(1)} fusion(bf16[8,8,16,320]{3,2,1,0:T(8,128)(2,1)} %g.3, s32[]{:T(128)S(6)} %select_n.11), kind=kLoop, calls=%fused_computation | loop fusion | bytes 163844 | tf_op jit(solution)/shard_map/reshape | solution.py:368
  3.0 0.0 copy-start.1
  3.0 1.8 %collective-permute-start.1 = (bf16[8,16,320]{2,1,0:T(8,128)(2,1)S(1)}, bf16[8,16,320]{2,1,0:T(8,128)(2,1)S(1)}, u32[]{:S(2)}, u32[]{:S(2)}) collective-permute-start(bf16[8,16,320]{2,1,0:T(8,128)(2,1)S(1)} %dynamic-slice_bitcast_fusion), channel_id=1, source_target_pairs={{0,96},{1,97},{2,98},{3,99},{4,100},{5,101},{6,102},{7,103},{8,104... | collective-permute-start | bytes 245768 | tf_op jit(solution)/shard_map/ppermute | solution.py:35
  4.8 0.0 collective-permute-start
  4.9 2.6 %collective-permute-start.2 = (bf16[8,8,16,320]{3,2,1,0:T(8,128)(2,1)}, bf16[8,8,16,320]{3,2,1,0:T(8,128)(2,1)S(1)}, u32[]{:S(2)}, u32[]{:S(2)}) collective-permute-start(bf16[8,8,16,320]{3,2,1,0:T(8,128)(2,1)} %g.3), channel_id=1, source_target_pairs={{0,16},{1,17},{2,18},{3,19},{4,20},{5,21},{6,22},{7,23},{8,24},{9,... | collective-permute-start | bytes 1966088 | tf_op jit(solution)/shard_map/ppermute | solution.py:35
  7.4 0.0 collective-permute-done.3.other
  7.5 1.1 %copy-done.2 = bf16[8,8,16,320]{3,2,1,0:T(8,128)(2,1)S(1)} copy-done((bf16[8,8,16,320]{3,2,1,0:T(8,128)(2,1)S(1)}, bf16[8,8,16,320]{3,2,1,0:T(8,128)(2,1)}, u32[]{:S(2)}) %copy-start.2) | copy-done | bytes 655384
  8.6 1.1 %turn.1.turned = bf16[320,2048]{1,0:T(8,128)(2,1)S(1)} custom-call(bf16[8,8,16,320]{3,2,1,0:T(8,128)(2,1)S(1)} %copy-done.2, bf16[8,8,16,320]{3,2,1,0:T(8,128)(2,1)S(1)} %collective-permute-done.3.other), custom_call_target="tpu_custom_call" | custom-call | flops 40000000000 | bytes 10000000 | tf_op jit(solution)/shard_map/turn/pallas_call | solution.py:122
  9.7 0.0 collective-permute-done.alpha
  9.7 0.5 edges.1
  10.2 1.4 %collective-permute-start.4 = (bf16[9,16,320]{2,1,0:T(8,128)(2,1)S(1)}, bf16[9,16,320]{2,1,0:T(8,128)(2,1)S(1)}, u32[]{:S(2)}, u32[]{:S(2)}) collective-permute-start(bf16[9,16,320]{2,1,0:T(8,128)(2,1)S(1)} %get-tuple-element.38), channel_id=1, source_target_pairs={{0,1},{1,0},{2,3},{3,2},{4,5},{5,4},{6,7},{7,6},{8,9},{9,8},{10,11... | collective-permute-start | bytes 276488 | tf_op jit(solution)/shard_map/ppermute | solution.py:35
  11.5 4.8 %collective-permute-start.5 = (bf16[18,8,320]{2,1,0:T(8,128)(2,1)S(1)}, bf16[18,8,320]{2,1,0:T(8,128)(2,1)S(1)}, u32[]{:S(2)}, u32[]{:S(2)}) collective-permute-start(bf16[18,8,320]{2,1,0:T(8,128)(2,1)S(1)} %get-tuple-element.39), channel_id=1, source_target_pairs={{0,2},{1,3},{2,0},{3,1},{4,6},{5,7},{6,4},{7,5},{8,10},{9,11},{10,... | collective-permute-start | bytes 276488 | tf_op jit(solution)/shard_map/ppermute | solution.py:35
  16.4 0.0 collective-permute-start.6
  16.4 1.3 %flip.1 = bf16[9,160,512]{2,1,0:T(8,128)(2,1)S(1)} custom-call(bf16[27,160,320]{2,1,0:T(8,128)(2,1)S(1)} %copy-done, bf16[18,320]{1,0:T(8,128)(2,1)S(1)} %get-tuple-element.40.after), custom_call_target="tpu_custom_call" | custom-call | flops 1 | bytes 1 | tf_op jit(solution)/shard_map/flip/pallas_call | solution.py:219
  17.7 4.6 %collective-permute-done.6.corner = bf16[18,320]{1,0:T(8,128)(2,1)S(1)} collective-permute-done((bf16[18,320]{1,0:T(8,128)(2,1)S(1)}, bf16[18,320]{1,0:T(8,128)(2,1)S(1)}, u32[]{:S(2)}, u32[]{:S(2)}) %collective-permute-start.6) | collective-permute-done | bytes 11552 | tf_op jit(solution)/shard_map/ppermute | solution.py:35
  22.3 0.0 collective-permute-start.7
  22.3 0.5 collective-permute-start.8
  22.8 0.1 collective-permute-start.9
  22.9 0.3 collective-permute-start.10
  23.2 0.8 %collective-permute-done.9.corner_other = bf16[18,320]{1,0:T(8,128)(2,1)S(1)} collective-permute-done((bf16[18,320]{1,0:T(8,128)(2,1)S(1)}, bf16[18,320]{1,0:T(8,128)(2,1)S(1)}, u32[]{:S(2)}, u32[]{:S(2)}) %collective-permute-start.9) | collective-permute-done | bytes 11552 | tf_op jit(solution)/shard_map/ppermute | solution.py:35
  24.0 0.0 collective-permute-done.7.line_other
  24.0 8.2 %tiles.1 = (bf16[10,18,16,1024]{3,2,1,0:T(8,128)(2,1)S(1)}, f32[9,80,512]{2,1,0:T(8,128)S(1)}, bf16[9,80,512]{2,1,0:T(8,128)(2,1)S(1)}, bf16[9,80,512]{2,1,0:T(8,128)(2,1)S(1)}, bf16[9,80,512]{2,1,0:T(8,128)(2,1)S(1)}) custom-call(bf16[8,8,16,320]{3,2,1,0:T(8,128)(2,1)S(1)} %copy-done.1, bf16[8,8,16,320]{3,2,1,0:T(8,128)(2,1)S(1)} %collective-permute-done.2.other, ...), custom_call_target="tpu_custom_call" | custom-call | flops 40000000000 | bytes 10000000 | tf_op jit(solution)/shard_map/tiles/pallas_call | solution.py:192
  32.3 2.0 %collective-permute-start.13 = (bf16[9,80,512]{2,1,0:T(8,128)(2,1)S(1)}, bf16[9,80,512]{2,1,0:T(8,128)(2,1)S(1)}, u32[]{:S(2)}, u32[]{:S(2)}) collective-permute-start(bf16[9,80,512]{2,1,0:T(8,128)(2,1)S(1)} %get-tuple-element.49), channel_id=1, source_target_pairs={{0,64},{1,65},{2,66},{3,67},{4,68},{5,69},{6,70},{7,71},{8,72},{9,... | collective-permute-start | bytes 2211848 | tf_op jit(solution)/shard_map/ppermute | solution.py:35
  34.2 0.1 collective-permute-start.14
  34.3 1.4 %collective-permute-start.15 = (bf16[9,80,512]{2,1,0:T(8,128)(2,1)S(1)}, bf16[9,80,512]{2,1,0:T(8,128)(2,1)S(1)}, u32[]{:S(2)}, u32[]{:S(2)}) collective-permute-start(bf16[9,80,512]{2,1,0:T(8,128)(2,1)S(1)} %get-tuple-element.51), channel_id=1, source_target_pairs={{0,96},{1,97},{2,98},{3,99},{4,100},{5,101},{6,102},{7,103},{8,104... | collective-permute-start | bytes 2211848 | tf_op jit(solution)/shard_map/ppermute | solution.py:35
  35.8 5.2 %own_half.1.partial = f32[320,1024]{1,0:T(8,128)S(1)} custom-call(bf16[10,18,16,1024]{3,2,1,0:T(8,128)(2,1)S(1)} %get-tuple-element.45.shifted, bf16[27,160,320]{2,1,0:T(8,128)(2,1)S(1)} %copy-done), custom_call_target="tpu_custom_call" | custom-call | flops 1 | bytes 1 | tf_op jit(solution)/shard_map/own_half/pallas_call | solution.py:253
  40.9 1.7 %collective-permute-done.10.far = bf16[9,160,512]{2,1,0:T(8,128)(2,1)S(1)} collective-permute-done((bf16[9,160,512]{2,1,0:T(8,128)(2,1)S(1)}, bf16[9,160,512]{2,1,0:T(8,128)(2,1)S(1)}, u32[]{:S(2)}, u32[]{:S(2)}) %collective-permute-start.10) | collective-permute-done | bytes 1474592 | tf_op jit(solution)/shard_map/ppermute | solution.py:35
  42.6 0.1 fusion
  42.7 0.1 collective-permute-start.12
  42.9 0.4 collective-permute-start.11
  43.3 1.7 %collective-permute-done.12.near_high = bf16[9,80,480]{2,1,0:T(8,128)(2,1)S(1)} collective-permute-done((bf16[9,80,480]{2,1,0:T(8,128)(2,1)S(1)}, bf16[9,80,480]{2,1,0:T(8,128)(2,1)S(1)}, u32[]{:S(2)}, u32[]{:S(2)}) %collective-permute-start.12) | collective-permute-done | bytes 691232 | tf_op jit(solution)/shard_map/ppermute | solution.py:35
  45.0 1.1 %collective-permute-done.11.near_low = bf16[9,80,480]{2,1,0:T(8,128)(2,1)S(1)} collective-permute-done((bf16[9,80,480]{2,1,0:T(8,128)(2,1)S(1)}, bf16[9,80,480]{2,1,0:T(8,128)(2,1)S(1)}, u32[]{:S(2)}, u32[]{:S(2)}) %collective-permute-start.11) | collective-permute-done | bytes 691232 | tf_op jit(solution)/shard_map/ppermute | solution.py:35
  46.1 4.2 %other_half.1 = bf16[8,8,16,320]{3,2,1,0:T(8,128)(2,1)} custom-call(bf16[10,18,16,1024]{3,2,1,0:T(8,128)(2,1)S(1)} %get-tuple-element.45.shifted, bf16[9,160,512]{2,1,0:T(8,128)(2,1)S(1)} %collective-permute-done.10.far, bf16[9,80,480]{2,1,0:T(8,128)(2,1)S(1)} %collective-permute-done.11.near_low, bf16[9,80,480]{2,1,0:T(8,128)(2,1)S(1)} %collective-permute-done.12.near_high, ...), custom_call_target="tpu_custom_call" | custom-call | flops 1 | bytes 1 | tf_op jit(solution)/shard_map/other_half/pallas_call | solution.py:284
  50.3 1.1 %collective-permute-done.14.one = bf16[9,80,512]{2,1,0:T(8,128)(2,1)S(1)} collective-permute-done((bf16[9,80,512]{2,1,0:T(8,128)(2,1)S(1)}, bf16[9,80,512]{2,1,0:T(8,128)(2,1)S(1)}, u32[]{:S(2)}, u32[]{:S(2)}) %collective-permute-start.14) | collective-permute-done | bytes 737312 | tf_op jit(solution)/shard_map/ppermute | solution.py:35
  51.4 1.1 %collective-permute-done.15.three = bf16[9,80,512]{2,1,0:T(8,128)(2,1)S(1)} collective-permute-done((bf16[9,80,512]{2,1,0:T(8,128)(2,1)S(1)}, bf16[9,80,512]{2,1,0:T(8,128)(2,1)S(1)}, u32[]{:S(2)}, u32[]{:S(2)}) %collective-permute-start.15) | collective-permute-done | bytes 737312 | tf_op jit(solution)/shard_map/ppermute | solution.py:35
  52.5 0.4 fold.1
  52.9 2.3 %collective-permute-start.16 = (bf16[180,512]{1,0:T(8,128)(2,1)S(1)}, bf16[180,512]{1,0:T(8,128)(2,1)S(1)}, u32[]{:S(2)}, u32[]{:S(2)}) collective-permute-start(bf16[180,512]{1,0:T(8,128)(2,1)S(1)} %get-tuple-element.58), channel_id=1, source_target_pairs={{0,4},{1,5},{2,6},{3,7},{4,0},{5,1},{6,2},{7,3},{8,12},{9,13},{10,... | collective-permute-start | bytes 552968 | tf_op jit(solution)/shard_map/ppermute | solution.py:35
  55.2 1.9 %collective-permute-start.17 = (bf16[180,512]{1,0:T(8,128)(2,1)S(1)}, bf16[180,512]{1,0:T(8,128)(2,1)S(1)}, u32[]{:S(2)}, u32[]{:S(2)}) collective-permute-start(bf16[180,512]{1,0:T(8,128)(2,1)S(1)} %get-tuple-element.59), channel_id=1, source_target_pairs={{0,2},{1,3},{2,0},{3,1},{4,6},{5,7},{6,4},{7,5},{8,10},{9,11},{10,... | collective-permute-start | bytes 552968 | tf_op jit(solution)/shard_map/ppermute | solution.py:35
  57.1 1.9 %collective-permute-done.16.r1 = bf16[180,512]{1,0:T(8,128)(2,1)S(1)} collective-permute-done((bf16[180,512]{1,0:T(8,128)(2,1)S(1)}, bf16[180,512]{1,0:T(8,128)(2,1)S(1)}, u32[]{:S(2)}, u32[]{:S(2)}) %collective-permute-start.16) | collective-permute-done | bytes 184352 | tf_op jit(solution)/shard_map/ppermute | solution.py:35
  59.0 3.5 %collective-permute-done.17.r2 = bf16[180,512]{1,0:T(8,128)(2,1)S(1)} collective-permute-done((bf16[180,512]{1,0:T(8,128)(2,1)S(1)}, bf16[180,512]{1,0:T(8,128)(2,1)S(1)}, u32[]{:S(2)}, u32[]{:S(2)}) %collective-permute-start.17) | collective-permute-done | bytes 184352 | tf_op jit(solution)/shard_map/ppermute | solution.py:35
  62.4 0.6 collective-permute-done.18.r3
  63.0 0.2 cut.1
  63.2 2.0 %collective-permute-start.19 = (bf16[45,512]{1,0:T(8,128)(2,1)S(1)}, bf16[45,512]{1,0:T(8,128)(2,1)S(1)}, u32[]{:S(2)}, u32[]{:S(2)}) collective-permute-start(bf16[45,512]{1,0:T(8,128)(2,1)S(1)} %get-tuple-element.62), channel_id=1, source_target_pairs={{0,8},{1,16},{2,10},{3,18},{4,12},{5,20},{6,14},{7,22},{8,0},{9,24... | collective-permute-start | bytes 138248 | tf_op jit(solution)/shard_map/ppermute | solution.py:35
  65.3 0.1 collective-permute-start.21
  65.3 5.7 %collective-permute-start.22 = (bf16[45,512]{1,0:T(8,128)(2,1)S(1)}, bf16[45,512]{1,0:T(8,128)(2,1)S(1)}, u32[]{:S(2)}, u32[]{:S(2)}) collective-permute-start(bf16[45,512]{1,0:T(8,128)(2,1)S(1)} %get-tuple-element.65), channel_id=1, source_target_pairs={{0,0},{1,24},{2,2},{3,26},{4,4},{5,28},{6,6},{7,30},{8,8},{9,16},{... | collective-permute-start | bytes 138248 | tf_op jit(solution)/shard_map/ppermute | solution.py:35
  71.0 1.7 %collective-permute-done.22.r4 = bf16[45,512]{1,0:T(8,128)(2,1)S(1)} collective-permute-done((bf16[45,512]{1,0:T(8,128)(2,1)S(1)}, bf16[45,512]{1,0:T(8,128)(2,1)S(1)}, u32[]{:S(2)}, u32[]{:S(2)}) %collective-permute-start.22) | collective-permute-done | bytes 46112 | tf_op jit(solution)/shard_map/ppermute | solution.py:35
  72.7 0.8 %last.1 = f32[5,27,160]{2,1,0:T(8,128)} custom-call(f32[45,512]{1,0:T(8,128)S(1)} %get-tuple-element.61.mine, bf16[45,512]{1,0:T(8,128)(2,1)S(1)} %collective-permute-done.19.r1, bf16[45,512]{1,0:T(8,128)(2,1)S(1)} %collective-permute-done.20.r2, bf16[45,512]{1,0:T(8,128)(2,1)S(1)} %collective-permute-done.21.r3, bf16[45,512]{1,0:T(8,128)(2,1)S(1)} %collective-permute-done.22.r4), custom_call_target="tpu_custom_call" | custom-call | flops 1 | bytes 1 | tf_op jit(solution)/shard_map/last/pallas_call | solution.py:353
  (15 shorter events, 0.0 us)
Async XLA Ops:
  0.6 6.8 %collective-permute-start.3 = (bf16[8,8,16,320]{3,2,1,0:T(8,128)(2,1)}, bf16[8,8,16,320]{3,2,1,0:T(8,128)(2,1)S(1)}, u32[]{:S(2)}, u32[]{:S(2)}) collective-permute-start(bf16[8,8,16,320]{3,2,1,0:T(8,128)(2,1)} %own.2), channel_id=1, source_target_pairs={{0,16},{1,17},{2,18},{3,19},{4,20},{5,21},{6,22},{7,23},{8,24},{9,... | collective-permute-start | bytes 1966088 | tf_op jit(solution)/shard_map/ppermute | solution.py:35
  3.0 6.6 %copy-start.1 = (bf16[8,8,16,320]{3,2,1,0:T(8,128)(2,1)S(1)}, bf16[8,8,16,320]{3,2,1,0:T(8,128)(2,1)}, u32[]{:S(2)}) copy-start(bf16[8,8,16,320]{3,2,1,0:T(8,128)(2,1)} %g.3) | copy-start | bytes 1966084
  3.0 6.6 %collective-permute-start.1 = (bf16[8,16,320]{2,1,0:T(8,128)(2,1)S(1)}, bf16[8,16,320]{2,1,0:T(8,128)(2,1)S(1)}, u32[]{:S(2)}, u32[]{:S(2)}) collective-permute-start(bf16[8,16,320]{2,1,0:T(8,128)(2,1)S(1)} %dynamic-slice_bitcast_fusion), channel_id=1, source_target_pairs={{0,96},{1,97},{2,98},{3,99},{4,100},{5,101},{6,102},{7,103},{8,104... | collective-permute-start | bytes 245768 | tf_op jit(solution)/shard_map/ppermute | solution.py:35
  4.8 4.8 %collective-permute-start = (bf16[8,16,320]{2,1,0:T(8,128)(2,1)S(1)}, bf16[8,16,320]{2,1,0:T(8,128)(2,1)S(1)}, u32[]{:S(2)}, u32[]{:S(2)}) collective-permute-start(bf16[8,16,320]{2,1,0:T(8,128)(2,1)S(1)} %dynamic-slice_bitcast_fusion), channel_id=1, source_target_pairs={{0,112},{1,113},{2,114},{3,115},{4,116},{5,117},{6,118},{7,119},{8... | collective-permute-start | bytes 245768 | tf_op jit(solution)/shard_map/ppermute | solution.py:35
  4.9 4.8 %collective-permute-start.2 = (bf16[8,8,16,320]{3,2,1,0:T(8,128)(2,1)}, bf16[8,8,16,320]{3,2,1,0:T(8,128)(2,1)S(1)}, u32[]{:S(2)}, u32[]{:S(2)}) collective-permute-start(bf16[8,8,16,320]{3,2,1,0:T(8,128)(2,1)} %g.3), channel_id=1, source_target_pairs={{0,16},{1,17},{2,18},{3,19},{4,20},{5,21},{6,22},{7,23},{8,24},{9,... | collective-permute-start | bytes 1966088 | tf_op jit(solution)/shard_map/ppermute | solution.py:35
  7.5 1.1 %copy-start.2 = (bf16[8,8,16,320]{3,2,1,0:T(8,128)(2,1)S(1)}, bf16[8,8,16,320]{3,2,1,0:T(8,128)(2,1)}, u32[]{:S(2)}) copy-start(bf16[8,8,16,320]{3,2,1,0:T(8,128)(2,1)} %own.2) | copy-start | bytes 1966084
  8.6 7.8 %copy-start = (bf16[27,160,320]{2,1,0:T(8,128)(2,1)S(1)}, bf16[27,160,320]{2,1,0:T(8,128)(2,1)}, u32[]{:S(2)}) copy-start(bf16[27,160,320]{2,1,0:T(8,128)(2,1)} %own.3) | copy-start | bytes 8294404
  10.2 12.1 %collective-permute-start.4 = (bf16[9,16,320]{2,1,0:T(8,128)(2,1)S(1)}, bf16[9,16,320]{2,1,0:T(8,128)(2,1)S(1)}, u32[]{:S(2)}, u32[]{:S(2)}) collective-permute-start(bf16[9,16,320]{2,1,0:T(8,128)(2,1)S(1)} %get-tuple-element.38), channel_id=1, source_target_pairs={{0,1},{1,0},{2,3},{3,2},{4,5},{5,4},{6,7},{7,6},{8,9},{9,8},{10,11... | collective-permute-start | bytes 276488 | tf_op jit(solution)/shard_map/ppermute | solution.py:35
  11.5 10.8 %collective-permute-start.5 = (bf16[18,8,320]{2,1,0:T(8,128)(2,1)S(1)}, bf16[18,8,320]{2,1,0:T(8,128)(2,1)S(1)}, u32[]{:S(2)}, u32[]{:S(2)}) collective-permute-start(bf16[18,8,320]{2,1,0:T(8,128)(2,1)S(1)} %get-tuple-element.39), channel_id=1, source_target_pairs={{0,2},{1,3},{2,0},{3,1},{4,6},{5,7},{6,4},{7,5},{8,10},{9,11},{10,... | collective-permute-start | bytes 276488 | tf_op jit(solution)/shard_map/ppermute | solution.py:35
  16.4 5.9 %collective-permute-start.6 = (bf16[18,320]{1,0:T(8,128)(2,1)S(1)}, bf16[18,320]{1,0:T(8,128)(2,1)S(1)}, u32[]{:S(2)}, u32[]{:S(2)}) collective-permute-start(bf16[18,320]{1,0:T(8,128)(2,1)S(1)} %get-tuple-element.40.after), channel_id=1, source_target_pairs={{0,3},{1,2},{2,1},{3,0},{4,7},{5,6},{6,5},{7,4},{8,11},{9,10},{10,... | collective-permute-start | bytes 34568 | tf_op jit(solution)/shard_map/ppermute | solution.py:35
  22.3 1.7 %collective-permute-start.7 = (bf16[18,8,320]{2,1,0:T(8,128)(2,1)S(1)}, bf16[18,8,320]{2,1,0:T(8,128)(2,1)S(1)}, u32[]{:S(2)}, u32[]{:S(2)}) collective-permute-start(bf16[18,8,320]{2,1,0:T(8,128)(2,1)S(1)} %collective-permute-done.5.line), channel_id=1, source_target_pairs={{0,16},{1,17},{2,18},{3,19},{4,20},{5,21},{6,22},{7,23},{8,24},{9,... | collective-permute-start | bytes 276488 | tf_op jit(solution)/shard_map/ppermute | solution.py:35
  22.3 1.7 %collective-permute-start.8 = (bf16[9,16,320]{2,1,0:T(8,128)(2,1)S(1)}, bf16[9,16,320]{2,1,0:T(8,128)(2,1)S(1)}, u32[]{:S(2)}, u32[]{:S(2)}) collective-permute-start(bf16[9,16,320]{2,1,0:T(8,128)(2,1)S(1)} %collective-permute-done.4.half), channel_id=1, source_target_pairs={{0,16},{1,17},{2,18},{3,19},{4,20},{5,21},{6,22},{7,23},{8,24},{9,... | collective-permute-start | bytes 276488 | tf_op jit(solution)/shard_map/ppermute | solution.py:35
  22.8 1.2 %collective-permute-start.9 = (bf16[18,320]{1,0:T(8,128)(2,1)S(1)}, bf16[18,320]{1,0:T(8,128)(2,1)S(1)}, u32[]{:S(2)}, u32[]{:S(2)}) collective-permute-start(bf16[18,320]{1,0:T(8,128)(2,1)S(1)} %collective-permute-done.6.corner), channel_id=1, source_target_pairs={{0,16},{1,17},{2,18},{3,19},{4,20},{5,21},{6,22},{7,23},{8,24},{9,... | collective-permute-start | bytes 34568 | tf_op jit(solution)/shard_map/ppermute | solution.py:35
  22.9 19.7 %collective-permute-start.10 = (bf16[9,160,512]{2,1,0:T(8,128)(2,1)S(1)}, bf16[9,160,512]{2,1,0:T(8,128)(2,1)S(1)}, u32[]{:S(2)}, u32[]{:S(2)}) collective-permute-start(bf16[9,160,512]{2,1,0:T(8,128)(2,1)S(1)} %flip.1), channel_id=1, source_target_pairs={{0,1},{1,0},{2,3},{3,2},{4,5},{5,4},{6,7},{7,6},{8,9},{9,8},{10,11... | collective-permute-start | bytes 4423688 | tf_op jit(solution)/shard_map/ppermute | solution.py:35
  32.3 18.0 %collective-permute-start.13 = (bf16[9,80,512]{2,1,0:T(8,128)(2,1)S(1)}, bf16[9,80,512]{2,1,0:T(8,128)(2,1)S(1)}, u32[]{:S(2)}, u32[]{:S(2)}) collective-permute-start(bf16[9,80,512]{2,1,0:T(8,128)(2,1)S(1)} %get-tuple-element.49), channel_id=1, source_target_pairs={{0,64},{1,65},{2,66},{3,67},{4,68},{5,69},{6,70},{7,71},{8,72},{9,... | collective-permute-start | bytes 2211848 | tf_op jit(solution)/shard_map/ppermute | solution.py:35
  34.2 17.2 %collective-permute-start.14 = (bf16[9,80,512]{2,1,0:T(8,128)(2,1)S(1)}, bf16[9,80,512]{2,1,0:T(8,128)(2,1)S(1)}, u32[]{:S(2)}, u32[]{:S(2)}) collective-permute-start(bf16[9,80,512]{2,1,0:T(8,128)(2,1)S(1)} %get-tuple-element.50), channel_id=1, source_target_pairs={{0,32},{1,33},{2,34},{3,35},{4,36},{5,37},{6,38},{7,39},{8,40},{9,... | collective-permute-start | bytes 2211848 | tf_op jit(solution)/shard_map/ppermute | solution.py:35
  34.3 18.2 %collective-permute-start.15 = (bf16[9,80,512]{2,1,0:T(8,128)(2,1)S(1)}, bf16[9,80,512]{2,1,0:T(8,128)(2,1)S(1)}, u32[]{:S(2)}, u32[]{:S(2)}) collective-permute-start(bf16[9,80,512]{2,1,0:T(8,128)(2,1)S(1)} %get-tuple-element.51), channel_id=1, source_target_pairs={{0,96},{1,97},{2,98},{3,99},{4,100},{5,101},{6,102},{7,103},{8,104... | collective-permute-start | bytes 2211848 | tf_op jit(solution)/shard_map/ppermute | solution.py:35
  42.7 2.3 %collective-permute-start.12 = (bf16[9,80,480]{2,1,0:T(8,128)(2,1)S(1)}, bf16[9,80,480]{2,1,0:T(8,128)(2,1)S(1)}, u32[]{:S(2)}, u32[]{:S(2)}) collective-permute-start(bf16[9,80,480]{2,1,0:T(8,128)(2,1)S(1)} %get-tuple-element.66), channel_id=1, source_target_pairs={{0,16},{1,17},{2,18},{3,19},{4,20},{5,21},{6,22},{7,23},{8,24},{9,... | collective-permute-start | bytes 2073608 | tf_op jit(solution)/shard_map/ppermute | solution.py:35
  42.9 3.2 %collective-permute-start.11 = (bf16[9,80,480]{2,1,0:T(8,128)(2,1)S(1)}, bf16[9,80,480]{2,1,0:T(8,128)(2,1)S(1)}, u32[]{:S(2)}, u32[]{:S(2)}) collective-permute-start(bf16[9,80,480]{2,1,0:T(8,128)(2,1)S(1)} %get-tuple-element.67), channel_id=1, source_target_pairs={{0,16},{1,17},{2,18},{3,19},{4,20},{5,21},{6,22},{7,23},{8,24},{9,... | collective-permute-start | bytes 2073608 | tf_op jit(solution)/shard_map/ppermute | solution.py:35
  52.9 6.0 %collective-permute-start.16 = (bf16[180,512]{1,0:T(8,128)(2,1)S(1)}, bf16[180,512]{1,0:T(8,128)(2,1)S(1)}, u32[]{:S(2)}, u32[]{:S(2)}) collective-permute-start(bf16[180,512]{1,0:T(8,128)(2,1)S(1)} %get-tuple-element.58), channel_id=1, source_target_pairs={{0,4},{1,5},{2,6},{3,7},{4,0},{5,1},{6,2},{7,3},{8,12},{9,13},{10,... | collective-permute-start | bytes 552968 | tf_op jit(solution)/shard_map/ppermute | solution.py:35
  55.2 7.2 %collective-permute-start.17 = (bf16[180,512]{1,0:T(8,128)(2,1)S(1)}, bf16[180,512]{1,0:T(8,128)(2,1)S(1)}, u32[]{:S(2)}, u32[]{:S(2)}) collective-permute-start(bf16[180,512]{1,0:T(8,128)(2,1)S(1)} %get-tuple-element.59), channel_id=1, source_target_pairs={{0,2},{1,3},{2,0},{3,1},{4,6},{5,7},{6,4},{7,5},{8,10},{9,11},{10,... | collective-permute-start | bytes 552968 | tf_op jit(solution)/shard_map/ppermute | solution.py:35
  57.1 5.9 %collective-permute-start.18 = (bf16[180,512]{1,0:T(8,128)(2,1)S(1)}, bf16[180,512]{1,0:T(8,128)(2,1)S(1)}, u32[]{:S(2)}, u32[]{:S(2)}) collective-permute-start(bf16[180,512]{1,0:T(8,128)(2,1)S(1)} %get-tuple-element.60), channel_id=1, source_target_pairs={{0,6},{1,7},{2,4},{3,5},{4,2},{5,3},{6,0},{7,1},{8,14},{9,15},{10,... | collective-permute-start | bytes 552968 | tf_op jit(solution)/shard_map/ppermute | solution.py:35
  63.2 7.8 %collective-permute-start.19 = (bf16[45,512]{1,0:T(8,128)(2,1)S(1)}, bf16[45,512]{1,0:T(8,128)(2,1)S(1)}, u32[]{:S(2)}, u32[]{:S(2)}) collective-permute-start(bf16[45,512]{1,0:T(8,128)(2,1)S(1)} %get-tuple-element.62), channel_id=1, source_target_pairs={{0,8},{1,16},{2,10},{3,18},{4,12},{5,20},{6,14},{7,22},{8,0},{9,24... | collective-permute-start | bytes 138248 | tf_op jit(solution)/shard_map/ppermute | solution.py:35
  65.3 5.7 %collective-permute-start.20 = (bf16[45,512]{1,0:T(8,128)(2,1)S(1)}, bf16[45,512]{1,0:T(8,128)(2,1)S(1)}, u32[]{:S(2)}, u32[]{:S(2)}) collective-permute-start(bf16[45,512]{1,0:T(8,128)(2,1)S(1)} %get-tuple-element.63), channel_id=1, source_target_pairs={{0,24},{1,8},{2,26},{3,10},{4,28},{5,12},{6,30},{7,14},{8,16},{9,0... | collective-permute-start | bytes 138248 | tf_op jit(solution)/shard_map/ppermute | solution.py:35
  65.3 5.7 %collective-permute-start.21 = (bf16[45,512]{1,0:T(8,128)(2,1)S(1)}, bf16[45,512]{1,0:T(8,128)(2,1)S(1)}, u32[]{:S(2)}, u32[]{:S(2)}) collective-permute-start(bf16[45,512]{1,0:T(8,128)(2,1)S(1)} %get-tuple-element.64), channel_id=1, source_target_pairs={{0,16},{1,0},{2,18},{3,2},{4,20},{5,4},{6,22},{7,6},{8,24},{9,8},{... | collective-permute-start | bytes 138248 | tf_op jit(solution)/shard_map/ppermute | solution.py:35
  65.3 7.4 %collective-permute-start.22 = (bf16[45,512]{1,0:T(8,128)(2,1)S(1)}, bf16[45,512]{1,0:T(8,128)(2,1)S(1)}, u32[]{:S(2)}, u32[]{:S(2)}) collective-permute-start(bf16[45,512]{1,0:T(8,128)(2,1)S(1)} %get-tuple-element.65), channel_id=1, source_target_pairs={{0,0},{1,24},{2,2},{3,26},{4,4},{5,28},{6,6},{7,30},{8,8},{9,16},{... | collective-permute-start | bytes 138248 | tf_op jit(solution)/shard_map/ppermute | solution.py:35
